TPU v7x, 256 devices: a whole 4x4x8 slice. The times are simulated.
256 devices in a mesh: pipe: 16 (over y, x_lo, core), tensor: 8 (over z), dp: 2 (over x_hi).
Axes of the slice: x: 4 (x_hi: 2, x_lo: 2; x = x_hi * 2 + x_lo), y: 4, z: 8, core: 2. Of those that a mesh axis runs over, the one named last changes fastest.
Arguments:
- hidden: bfloat16 [512, 8192], P(('dp', 'pipe', 'tensor')), parts along dimension 0, may hold values from -9 to 9
- lm_weight: bfloat16 [8192, 65536], P(None, ('pipe', 'tensor')), may hold values from -0.150893068 to 0.150893068
- targets: int32 [512], P('dp'), parts along dimension 0, may hold values from 0 to 65535
- loss_grad: float32 [512], P('dp'), parts along dimension 0, may hold values from 8 to 64
Outputs:
- ce_loss: float32 [512], P(('dp', 'pipe', 'tensor')), parts along dimension 0
- z_term: float32 [512], P(('dp', 'pipe', 'tensor')), parts along dimension 0
- hidden_grad: bfloat16 [512, 8192], P(('dp', 'pipe', 'tensor')), parts along dimension 0
There are 2 independent parts, one for each index of `dp`. A program takes and returns all parts, laid end to end along the dimension named above; an argument that names none is the same for every part. Nothing has to cross between parts.
All inputs are finite; a program needn't handle non-finite values.
Results may differ from a plain program's by a relative error of at most 0.0045.
Values may be sent and summed in bfloat16 or wider, within the bound.
No kernel may reach another device: no remote copies, remote signals or barrier semaphores. Data moves between devices by JAX's collectives and lax.ppermute only.
A program may use at most 64 MiB of HBM per device.

v0:
```python
import jax
import jax.numpy as jnp
from jax import lax
from jax.sharding import PartitionSpec as P

zloss_coef = 0.0001


def shards(hidden, lm_weight, targets, loss_grad):
    own_count = hidden.shape[0]
    voc_width = lm_weight.shape[1]
    position = lax.axis_index(("pipe", "tensor"))
    logits = jnp.dot(
        lax.all_gather(hidden, ("pipe", "tensor"), axis=0, tiled=True),
        lm_weight,
        preferred_element_type=jnp.float32,
    )
    columns = jnp.arange(voc_width, dtype=jnp.int32) + position * voc_width
    onehot = (columns[None, :] == targets[:, None]).astype(jnp.float32)
    picked = jnp.sum(logits * onehot, axis=1)
    local_top = jnp.max(logits, axis=1)
    row_top = lax.pmax(local_top, ("pipe", "tensor"))
    local_sum = jnp.sum(jnp.exp(logits - row_top[:, None]), axis=1)
    sum_exp, target_logit = lax.psum((local_sum, picked), ("pipe", "tensor"))
    log_total = row_top + jnp.log(sum_exp)
    ce_full = log_total - target_logit
    z_full = zloss_coef * log_total * log_total
    factor = 1.0 + 2.0 * zloss_coef * log_total
    probs = jnp.exp(logits - log_total[:, None])
    logit_grad = (loss_grad[:, None] * (probs * factor[:, None] - onehot)).astype(jnp.bfloat16)
    summed = lax.psum_scatter(
        lax.dot_general(
            logit_grad, lm_weight, (((1,), (1,)), ((), ())), preferred_element_type=jnp.float32
        ),
        ("pipe", "tensor"),
        scatter_dimension=0,
        tiled=True,
    )
    offset = position * own_count
    ce_loss = lax.dynamic_slice_in_dim(ce_full, offset, own_count, 0)
    z_term = lax.dynamic_slice_in_dim(z_full, offset, own_count, 0)
    return (ce_loss, z_term, summed.astype(jnp.bfloat16))


def solution(mesh):
    in_specs = (P(("dp", "pipe", "tensor"), None), P(None, ("pipe", "tensor")), P("dp"), P("dp"))
    out_specs = (
        P(("dp", "pipe", "tensor")),
        P(("dp", "pipe", "tensor")),
        P(("dp", "pipe", "tensor"), None),
    )
    return jax.shard_map(shards, mesh=mesh, in_specs=in_specs, out_specs=out_specs, check_vma=False)
```

profile of v0, /device:TPU:4, one launch (start us, length us, event | category | flops | bytes accessed | tf_op | source)
XLA Modules:
  0.0 1610.8 jit_solution(15767751598662972643)
XLA Ops:
  7.2 0.0 all-gather.3.cloned.1.call-start
  7.2 0.7 all-gather.3.cloned.1.call-update
  7.9 1.3 dynamic-slice
  9.8 364.6 %all-gather.3.cloned.1.call-done = bf16[128,2,8192]{2,1,0:T(2,128)(2,1)} async-done(((bf16[1,2,8192]{2,1,0:T(2,128)(2,1)}), bf16[128,2,8192]{2,1,0:T(2,128)(2,1)}) %all-gather.3.cloned.1.call-update) | async-done | bytes 4194320 | tf_op jit(solution)/shard_map/all_gather | solution.py:14
  374.4 7.2 reshape.16
  381.6 0.0 copy-start
  381.7 0.0 copy-start.1
  381.7 7.1 fusion.11
  388.7 279.0 %pmax.7 = f32[256]{0:T(256)S(1)} all-reduce(f32[256]{0:T(256)S(1)} %get-tuple-element.9), channel_id=1, replica_groups=mesh['pipe'=16,'tensor'=8,'dp'=2] {'pipe','tensor'}, use_global_device_ids=true, to_apply=%region_1.0 | all-reduce | flops 256 | bytes 2048 | tf_op jit(solution)/shard_map/pmax | solution.py:22
  667.7 0.0 copy-done
  667.7 0.3 fusion
  668.0 275.6 %psum.14 = f32[256]{0:T(256)S(1)} all-reduce(f32[256]{0:T(256)S(1)} %get-tuple-element.4), channel_id=1, replica_groups=mesh['pipe'=16,'tensor'=8,'dp'=2] {'pipe','tensor'}, use_global_device_ids=true, to_apply=%region_3.0 | all-reduce | flops 256 | bytes 2048 | tf_op jit(solution)/shard_map/psum | solution.py:24
  943.6 0.0 copy-done.1
  943.6 9.1 fusion.4
  952.7 648.6 %all-reduce.3 = (f32[256]{0:T(256)S(1)}, bf16[256,8192]{1,0:T(8,128)(2,1)}) all-reduce(f32[256]{0:T(256)S(1)} %get-tuple-element.3, f32[256,8192]{1,0:T(8,128)} %fusion.4), channel_id=1, replica_groups=mesh['pipe'=16,'tensor'=8,'dp'=2] {'pipe','tensor'}, use_global_device_ids=true, to_apply=%region_5.0 | all-reduce | flops 2097408 | bytes 12584960 | tf_op jit(solution)/shard_map/psum | solution.py:24
  1601.3 0.6 dynamic_slice.7
  1601.8 0.6 dynamic_slice.6
  1602.4 1.6 dynamic-slice_convert_fusion
  (4 shorter events, 0.0 us)
Async XLA Ops:
  7.2 367.3 %all-gather.3.cloned.1.call-start = ((), (), s32[]{:S(2)}) async-start(), calls=%async_computation | async-start | bytes 4227072 | tf_op jit(solution)/shard_map/all_gather | solution.py:14
  381.6 286.1 %copy-start = (s32[256]{0:T(256)S(1)}, s32[256]{0:T(256)}, u32[]{:S(2)}) copy-start(s32[256]{0:T(256)} %param.6) | copy-start | bytes 3076
  381.7 562.0 %copy-start.1 = (f32[256]{0:T(256)S(1)}, f32[256]{0:T(256)}, u32[]{:S(2)}) copy-start(f32[256]{0:T(256)} %param.7) | copy-start | bytes 3076
Sparse Core Ops, SparseCore 0:
  9.8 364.5 all-gather.2
where the time goes:
time: 1610 us
  blocking collectives  1200 us (75%)
  waiting for transfers between devices  365 us (23%)
  matrix products  16.1 us (1%)
    psum x2, blocking collectives, shards(): sum_exp, target_logit = lax.psum((local_sum, picked), ('pipe', 'tensor'))  924 us
    all_gather x1, waiting for transfers between devices, shards(): lax.all_gather(hidden, ('pipe', 'tensor'), axis=0, tiled=True)  365 us
    pmax x1, blocking collectives, shards(): row_top = lax.pmax(local_top, ('pipe', 'tensor'))  279 us
  transfers between devices with their start and end apart: 1, of which 1 were waited for; matrix products, arithmetic and copies ran while one was open for 0% of the time, Pallas kernels for 0%

commit v1 on v0

v1 whole, which is shorter than its diff:
```python
import jax
import jax.numpy as jnp
from jax import lax
from jax.sharding import Mesh
from jax.sharding import PartitionSpec as P

zloss_coef = 0.0001
NY, NX, NC, NZ = 4, 2, 2, 8
GROUP = ("y", "x", "c", "z")
OFFSETS = (0, 1, -1, 2)


def index_of(y, x, c, z):
    return (((y % NY) * NX + x % NX) * NC + c % NC) * NZ + z % NZ


def pairs(route):
    every = [(y, x, c, z) for y in range(NY) for x in range(NX) for c in range(NC) for z in range(NZ)]
    return [(index_of(*p), index_of(*route(*p))) for p in every]


def to_x(y, x, c, z):
    return y, x + 1, c, z


def to_c(y, x, c, z):
    return y, x, c + 1, z


def to_z4(y, x, c, z):
    return y, x, c, z + 4


def to_first(step):
    return lambda y, x, c, z: (y, x, c, z + step) if c == 0 else (y + step, x, c, z)


def to_second(step):
    return lambda y, x, c, z: (y + step, x, c, z) if c == 0 else (y, x, c, z + step)


def send(value, route):
    return lax.ppermute(value, GROUP, pairs(route))


def row_numbers(own_rows):
    y, x, c, z = (lax.axis_index(a) for a in GROUP)
    at = jnp.arange(256, dtype=jnp.int32)
    r, xr, z4, q1, q2, cr = at & 1, (at >> 1) & 1, (at >> 2) & 1, (at >> 3) & 3, (at >> 5) & 3, at >> 7
    o1 = jnp.where(q1 == 2, -1, jnp.where(q1 == 3, 2, q1))
    o2 = jnp.where(q2 == 2, -1, jnp.where(q2 == 3, 2, q2))
    core = c ^ cr
    zo = jnp.where(core == 0, o1, o2) + 4 * z4
    yo = jnp.where(core == 0, o2, o1)
    return ((((y + yo) & 3) * 2 + (x ^ xr)) * 2 + core) * 16 + ((z + zo) & 7) * 2 + r


def merge(stats, axis):
    top, total, picked = stats
    highest = jnp.max(top, axis=axis, keepdims=True)
    total = jnp.sum(total * jnp.exp(top - highest), axis=axis)
    return jnp.stack([jnp.squeeze(highest, axis), total, jnp.sum(picked, axis=axis)])


def shards(hidden, lm_weight, targets, loss_grad):
    f32 = jnp.float32
    voc_width = lm_weight.shape[1]
    depth = hidden.shape[1]
    position = lax.axis_index(GROUP)

    rows = row_numbers(hidden.shape[0])
    place = rows[:, None] == jnp.arange(256, dtype=jnp.int32)[None, :]
    own_targets = jnp.sum(jnp.where(place, targets[None, :], 0), axis=1)
    own_grad = jnp.sum(jnp.where(place, loss_grad[None, :], 0.0), axis=1)

    block = jnp.concatenate([hidden, send(hidden, to_x)])
    block = jnp.concatenate([block, send(block, to_z4)])
    block = jnp.concatenate([block] + [send(block, to_first(-o)) for o in OFFSETS[1:]])
    block = jnp.concatenate([block] + [send(block, to_second(-o)) for o in OFFSETS[1:]])
    block = jnp.concatenate([block, send(block, to_c)])

    logits = jnp.dot(block, lm_weight, preferred_element_type=f32)
    columns = jnp.arange(voc_width, dtype=jnp.int32) + position * voc_width
    hit = columns[None, :] == own_targets[:, None]
    top = jnp.max(logits, axis=1)
    total = jnp.sum(jnp.exp(logits - top[:, None]), axis=1)
    picked = jnp.sum(jnp.where(hit, logits, 0.0), axis=1)
    local = jnp.stack([top, total, picked])
    stats = jnp.sum(jnp.where(place[None], local[:, :, None], 0.0), axis=1)
    stats = merge(jnp.stack([stats, send(stats, to_c)], axis=1), 0)
    stats = merge(jnp.stack([stats, send(stats, to_x)], axis=1), 0)
    spread = lax.all_to_all(jnp.broadcast_to(stats[None], (32, 3, 256)), ("y", "z"), 0, 0)
    stats = merge(jnp.swapaxes(spread, 0, 1), 0)
    log_can = stats[0] + jnp.log(stats[1])
    both = jnp.stack([log_can, stats[2]])
    both = jnp.sum(jnp.where(place[None], both[:, None, :], 0.0), axis=2)
    log_total, target_logit = both[0], both[1]

    ce_loss = (log_total - target_logit)[:2]
    z_term = (zloss_coef * log_total * log_total)[:2]
    factor = 1.0 + 2.0 * zloss_coef * log_total
    probs = jnp.exp(logits - log_total[:, None])
    grad = (own_grad[:, None] * (probs * factor[:, None] - hit.astype(f32))).astype(jnp.bfloat16)
    part = lax.dot_general(grad, lm_weight, (((1,), (1,)), ((), ())), preferred_element_type=f32)

    part = part.reshape(2, 128, depth)
    part = part[0] + send(part[1].astype(jnp.bfloat16), to_c).astype(f32)
    part = part.reshape(4, 32, depth)
    part = part[0] + sum(
        send(part[k].astype(jnp.bfloat16), to_second(OFFSETS[k])).astype(f32) for k in (1, 2, 3)
    )
    part = part.reshape(4, 8, depth)
    part = part[0] + sum(
        send(part[k].astype(jnp.bfloat16), to_first(OFFSETS[k])).astype(f32) for k in (1, 2, 3)
    )
    part = part.reshape(2, 4, depth)
    part = part[0] + send(part[1], to_z4)
    part = part.reshape(2, 2, depth)
    part = part[0] + send(part[1], to_x)
    return ce_loss, z_term, part.astype(jnp.bfloat16)


def solution(mesh):
    mesh = Mesh(mesh.devices.reshape(NY, NX, NC, NZ, 2), (*GROUP, "dp"))
    own = ("dp", *GROUP)
    in_specs = (P(own, None), P(None, GROUP), P("dp"), P("dp"))
    out_specs = (P(own), P(own), P(own, None))
    return jax.shard_map(shards, mesh=mesh, in_specs=in_specs, out_specs=out_specs, check_vma=False)
```

time: 1610 us -> 162 us (0.10)
  blocking collectives: 1200 us -> 0 us
  waiting for transfers between devices: 365 us -> 67.6 us
  starting transfers between devices: 0.04 us -> 47.2 us
    psum x2 -> x0, blocking collectives: 924 us -> none  [shards(): sum_exp, target_logit = lax.psum((local_sum, picked), ('pipe', 'tensor'))]
    all_gather x1 -> x0, waiting for transfers between devices: 365 us -> none  [shards(): lax.all_gather(hidden, ('pipe', 'tensor'), axis=0, tiled=True)]
    pmax x1 -> x0, blocking collectives: 279 us -> none  [shards(): row_top = lax.pmax(local_top, ('pipe', 'tensor'))]
    ppermute x0 -> x20, waiting for transfers between devices: none -> 57.6 us  [send(): return lax.ppermute(value, GROUP, pairs(route))]
    ppermute x0 -> x20, starting transfers between devices: none -> 38.6 us  [send(): return lax.ppermute(value, GROUP, pairs(route))]
    concatenate x0 -> x3, local copies, waits for them, and re-layouts: none -> 23.2 us  [the longest x1 19 us: shards(): block = jnp.concatenate([block, send(block, to_c)])]
  transfers between devices with their start and end apart: 1 -> 21, of which waited for: 1 -> 18; matrix products, arithmetic and copies ran while one was open for 0% -> 1% of each run, Pallas kernels for 0% -> 0%
where the time goes in v1:
time: 162 us; the launch traced here: 159 us
  waiting for transfers between devices  67.6 us (42%)
  starting transfers between devices  47.2 us (29%)
  local copies, waits for them, and re-layouts  25.4 us (16%)
  matrix products  12.9 us (8%)
  other arithmetic  5.37 us (3%)
    ppermute x20, waiting for transfers between devices, send(): return lax.ppermute(value, GROUP, pairs(route))  57.6 us
    ppermute x20, starting transfers between devices, send(): return lax.ppermute(value, GROUP, pairs(route))  38.6 us
    concatenate x1, local copies, waits for them, and re-layouts, shards(): block = jnp.concatenate([block, send(block, to_c)])  19 us
    all_to_all x1, waiting for transfers between devices, shards(): lax.all_to_all(jnp.broadcast_to(stats[None], (32, 3, 256)), ('y', 'z'), 0...  10 us
    all_to_all x1, starting transfers between devices, shards(): lax.all_to_all(jnp.broadcast_to(stats[None], (32, 3, 256)), ('y', 'z'), 0...  8.64 us
    dot_general x1, matrix products, shards(): logits = jnp.dot(block, lm_weight, preferred_element_type=f32)  7.08 us
    dot_general x1, matrix products, shards(): lax.dot_general(grad, lm_weight, (((1,), (1,)), ((), ())), preferred_elem...  5.83 us
    concatenate x1, local copies, waits for them, and re-layouts, shards(): jnp.concatenate([block] + [send(block, to_second(-o)) for o in OFFSETS[1:]])  3.26 us
  transfers between devices with their start and end apart: 21, of which 18 were waited for; matrix products, arithmetic and copies ran while one was open for 1% of the time, Pallas kernels for 0%

profile of v1, /device:TPU:4, one launch (start us, length us, event | category | flops | bytes accessed | tf_op | source)
XLA Modules:
  0.0 159.3 jit_solution(12802015504856507927)
XLA Ops:
  0.6 1.3 collective-permute-start
  1.9 2.9 %collective-permute-done = bf16[2,8192]{1,0:T(2,128)(2,1)S(1)} collective-permute-done((bf16[2,8192]{1,0:T(2,128)(2,1)}, bf16[2,8192]{1,0:T(2,128)(2,1)S(1)}, u32[]{:S(2)}, u32[]{:S(2)}) %collective-permute-start) | collective-permute-done | bytes 32800 | tf_op jit(solution)/shard_map/ppermute | solution.py:43
  4.9 0.8 pad_maximum_fusion.1
  5.7 7.3 %collective-permute-start.1 = (bf16[4,8192]{1,0:T(4,128)(2,1)S(1)}, bf16[4,8192]{1,0:T(4,128)(2,1)S(1)}, u32[]{:S(2)}, u32[]{:S(2)}) collective-permute-start(bf16[4,8192]{1,0:T(4,128)(2,1)S(1)} %pad_maximum_fusion.1), channel_id=1, source_target_pairs={{0,8},{2,10},{4,12},{6,14},{8,0},{10,2},{12,4},{14,6},{16,24},{18,... | collective-permute-start | bytes 196616 | tf_op jit(solution)/shard_map/ppermute | solution.py:43
  13.0 2.3 %collective-permute-done.1 = bf16[4,8192]{1,0:T(4,128)(2,1)S(1)} collective-permute-done((bf16[4,8192]{1,0:T(4,128)(2,1)S(1)}, bf16[4,8192]{1,0:T(4,128)(2,1)S(1)}, u32[]{:S(2)}, u32[]{:S(2)}) %collective-permute-start.1) | collective-permute-done | bytes 65568 | tf_op jit(solution)/shard_map/ppermute | solution.py:43
  15.3 0.9 pad_maximum_fusion
  16.2 5.0 %collective-permute-start.4 = (bf16[8,8192]{1,0:T(8,128)(2,1)S(1)}, bf16[8,8192]{1,0:T(8,128)(2,1)S(1)}, u32[]{:S(2)}, u32[]{:S(2)}) collective-permute-start(bf16[8,8192]{1,0:T(8,128)(2,1)S(1)} %pad_maximum_fusion), channel_id=1, source_target_pairs={{0,12},{2,14},{4,0},{6,2},{8,4},{10,6},{12,8},{14,10},{16,144},{18... | collective-permute-start | bytes 393224 | tf_op jit(solution)/shard_map/ppermute | solution.py:43
  21.2 1.0 collective-permute-start.3
  22.2 2.2 %collective-permute-start.2 = (bf16[8,8192]{1,0:T(8,128)(2,1)S(1)}, bf16[8,8192]{1,0:T(8,128)(2,1)S(1)}, u32[]{:S(2)}, u32[]{:S(2)}) collective-permute-start(bf16[8,8192]{1,0:T(8,128)(2,1)S(1)} %pad_maximum_fusion), channel_id=1, source_target_pairs={{0,14},{2,0},{4,2},{6,4},{8,6},{10,8},{12,10},{14,12},{16,208},{18... | collective-permute-start | bytes 393224 | tf_op jit(solution)/shard_map/ppermute | solution.py:43
  24.4 0.7 collective-permute-done.4
  25.1 2.3 %collective-permute-done.3 = bf16[8,8192]{1,0:T(8,128)(2,1)S(1)} collective-permute-done((bf16[8,8192]{1,0:T(8,128)(2,1)S(1)}, bf16[8,8192]{1,0:T(8,128)(2,1)S(1)}, u32[]{:S(2)}, u32[]{:S(2)}) %collective-permute-start.3) | collective-permute-done | bytes 131104 | tf_op jit(solution)/shard_map/ppermute | solution.py:43
  27.4 0.5 collective-permute-done.2
  27.9 0.9 concatenate.21
  28.8 5.7 %collective-permute-start.7 = (bf16[32,8192]{1,0:T(8,128)(2,1)S(1)}, bf16[32,8192]{1,0:T(8,128)(2,1)S(1)}, u32[]{:S(2)}, u32[]{:S(2)}) collective-permute-start(bf16[32,8192]{1,0:T(8,128)(2,1)S(1)} %concatenate.21), channel_id=1, source_target_pairs={{0,128},{2,130},{4,132},{6,134},{8,136},{10,138},{12,140},{14,142}... | collective-permute-start | bytes 1572872 | tf_op jit(solution)/shard_map/ppermute | solution.py:43
  34.5 0.0 collective-permute-start.6
  34.5 3.2 %collective-permute-start.5 = (bf16[32,8192]{1,0:T(8,128)(2,1)S(1)}, bf16[32,8192]{1,0:T(8,128)(2,1)}, u32[]{:S(2)}, u32[]{:S(2)}) collective-permute-start(bf16[32,8192]{1,0:T(8,128)(2,1)S(1)} %concatenate.21), channel_id=1, source_target_pairs={{0,192},{2,194},{4,196},{6,198},{8,200},{10,202},{12,204},{14,206}... | collective-permute-start | bytes 1572872 | tf_op jit(solution)/shard_map/ppermute | solution.py:43
  37.8 4.0 %collective-permute-done.7 = bf16[32,8192]{1,0:T(8,128)(2,1)S(1)} collective-permute-done((bf16[32,8192]{1,0:T(8,128)(2,1)S(1)}, bf16[32,8192]{1,0:T(8,128)(2,1)S(1)}, u32[]{:S(2)}, u32[]{:S(2)}) %collective-permute-start.7) | collective-permute-done | bytes 524320 | tf_op jit(solution)/shard_map/ppermute | solution.py:43
  41.8 5.5 %collective-permute-done.6 = bf16[32,8192]{1,0:T(8,128)(2,1)S(1)} collective-permute-done((bf16[32,8192]{1,0:T(8,128)(2,1)S(1)}, bf16[32,8192]{1,0:T(8,128)(2,1)S(1)}, u32[]{:S(2)}, u32[]{:S(2)}) %collective-permute-start.6) | collective-permute-done | bytes 524320 | tf_op jit(solution)/shard_map/ppermute | solution.py:43
  47.3 0.0 collective-permute-done.5
  47.3 3.3 %concatenate.22 = bf16[128,8192]{1,0:T(8,128)(2,1)S(1)} concatenate(bf16[2,8192]{1,0:T(2,128)(2,1)} %param.4, bf16[2,8192]{1,0:T(2,128)(2,1)} %copy-done.1, bf16[4,8192]{1,0:T(4,128)(2,1)} %copy-done, bf16[8,8192]{1,0:T(8,128)(2,1)S(1)} %collective-permute-done.2, bf16[8,8192]{1,0:T(8,128)(2,1)S(1)} %collective-permute-done.3, bf16[8,8192]{1,0:T(8,128)(2,1)S(1)} %collective-permute-done.4, ...), dimensions={0} | concatenate | bytes 4194304 | tf_op jit(solution)/shard_map/concatenate | solution.py:79
  50.6 0.1 collective-permute-start.8
  50.8 0.2 select_reduce_fusion.3
  50.9 0.7 iota_compare_fusion
  51.7 3.3 %collective-permute-done.8 = bf16[128,8192]{1,0:T(8,128)(2,1)} collective-permute-done((bf16[128,8192]{1,0:T(8,128)(2,1)S(1)}, bf16[128,8192]{1,0:T(8,128)(2,1)}, u32[]{:S(2)}, u32[]{:S(2)}) %collective-permute-start.8) | collective-permute-done | bytes 2097184 | tf_op jit(solution)/shard_map/ppermute | solution.py:43
  55.0 19.0 %concatenate.23 = bf16[256,8192]{1,0:T(8,128)(2,1)} concatenate(bf16[2,8192]{1,0:T(2,128)(2,1)} %param.4, bf16[2,8192]{1,0:T(2,128)(2,1)} %copy-done.1, bf16[4,8192]{1,0:T(4,128)(2,1)} %copy-done, bf16[8,8192]{1,0:T(8,128)(2,1)S(1)} %collective-permute-done.2, bf16[8,8192]{1,0:T(8,128)(2,1)S(1)} %collective-permute-done.3, bf16[8,8192]{1,0:T(8,128)(2,1)S(1)} %collective-permute-done.4, ...), dimensions={0} | concatenate | bytes 8388608 | tf_op jit(solution)/shard_map/concatenate | solution.py:80
  74.0 7.1 %fusion.36 = (f32[256]{0:T(256)S(1)}, f32[256,512]{1,0:T(8,128)S(1)}) fusion(bf16[256,8192]{1,0:T(8,128)(2,1)} %concatenate.23, bf16[8192,512]{1,0:T(8,128)(2,1)} %param.5), kind=kOutput, calls=%fused_computation.76 | convolution fusion | flops 2147614464 | bytes 13108224 | tf_op jit(solution)/shard_map/dot_general | solution.py:82
  81.1 0.3 exponential_reduce_fusion
  81.4 0.2 select_reduce_fusion
  81.6 0.2 collective-permute-start.9
  81.8 1.0 collective-permute-done.9
  82.9 1.3 collective-permute-start.10
  84.2 2.4 %collective-permute-done.10 = f32[3,256]{1,0:T(4,128)S(1)} collective-permute-done((f32[3,256]{1,0:T(4,128)S(1)}, f32[3,256]{1,0:T(4,128)S(1)}, u32[]{:S(2)}, u32[]{:S(2)}) %collective-permute-start.10) | collective-permute-done | bytes 3104 | tf_op jit(solution)/shard_map/ppermute | solution.py:43
  86.7 0.7 broadcast_in_dim.111
  87.3 8.6 %all-to-all-start = ((f32[32,3,256]{2,1,0:T(4,128)}), f32[32,3,256]{2,1,0:T(4,128)S(1)}, u32[]{:S(2)}, u32[]{:S(2)}) async-start(f32[32,3,256]{2,1,0:T(4,128)} %broadcast_in_dim.111), calls=%async_computation | async-start | bytes 262144 | tf_op jit(solution)/shard_map/all_to_all | solution.py:92
  96.0 0.2 select_reduce_fusion.2
  96.2 10.0 %all-to-all-done = f32[32,3,256]{2,1,0:T(4,128)S(1)} async-done(((f32[32,3,256]{2,1,0:T(4,128)}), f32[32,3,256]{2,1,0:T(4,128)S(1)}, u32[]{:S(2)}, u32[]{:S(2)}) %all-to-all-start) | async-done | bytes 98336 | tf_op jit(solution)/shard_map/all_to_all | solution.py:92
  106.2 0.1 slice_reduce_fusion.1
  106.4 0.2 select_reduce_fusion.1
  106.6 5.8 %fusion.4 = f32[256,8192]{1,0:T(8,128)S(1)} fusion(bf16[8192,512]{1,0:T(8,128)(2,1)} %param.5, f32[256,512]{1,0:T(8,128)S(1)} %get-tuple-element.34, f32[256]{0:T(256)S(1)} %get-tuple-element.30, f32[256]{0:T(256)S(1)} %bitcast.59, f32[256]{0:T(256)S(1)} %select_reduce_fusion.2, s32[512]{0:T(512)S(1)} %iota_add_fusion, s32[256]{0:T(256)S(1)} %select_reduce_fusion.3), kind=kOutput, calls=%fused_computation.12 | convolution fusion | flops 2148401152 | bytes 17307648 | tf_op jit(solution)/shard_map/dot_general | solution.py:104
  112.4 0.2 slice.117
  112.6 0.1 collective-permute-start.11
  112.7 4.1 %collective-permute-done.11 = bf16[128,8192]{1,0:T(8,128)(2,1)S(1)} collective-permute-done((bf16[128,8192]{1,0:T(8,128)(2,1)S(1)}, bf16[128,8192]{1,0:T(8,128)(2,1)S(1)}, u32[]{:S(2)}, u32[]{:S(2)}) %collective-permute-start.11) | collective-permute-done | bytes 2097184 | tf_op jit(solution)/shard_map/ppermute | solution.py:43
  116.9 0.6 fusion.29
  117.5 0.1 fusion.33
  117.6 0.7 collective-permute-start.12
  118.3 2.0 %collective-permute-start.14 = (bf16[32,8192]{1,0:T(8,128)(2,1)S(1)}, bf16[32,8192]{1,0:T(8,128)(2,1)S(1)}, u32[]{:S(2)}, u32[]{:S(2)}) collective-permute-start(bf16[32,8192]{1,0:T(8,128)(2,1)S(1)} %get-tuple-element.16), channel_id=1, source_target_pairs={{0,128},{2,130},{4,132},{6,134},{8,136},{10,138},{12,140},{14,142}... | collective-permute-start | bytes 1572872 | tf_op jit(solution)/shard_map/ppermute | solution.py:43
  120.4 1.3 collective-permute-start.13
  121.7 12.1 %collective-permute-done.12 = bf16[32,8192]{1,0:T(8,128)(2,1)S(1)} collective-permute-done((bf16[32,8192]{1,0:T(8,128)(2,1)S(1)}, bf16[32,8192]{1,0:T(8,128)(2,1)S(1)}, u32[]{:S(2)}, u32[]{:S(2)}) %collective-permute-start.12) | collective-permute-done | bytes 524320 | tf_op jit(solution)/shard_map/ppermute | solution.py:43
  133.7 0.0 collective-permute-done.14
  133.7 0.9 collective-permute-done.13
  134.6 0.3 fusion.28
  134.9 1.1 collective-permute-start.15
  136.1 0.6 collective-permute-start.17
  136.7 2.9 %collective-permute-start.16 = (bf16[8,8192]{1,0:T(8,128)(2,1)S(1)}, bf16[8,8192]{1,0:T(8,128)(2,1)S(1)}, u32[]{:S(2)}, u32[]{:S(2)}) collective-permute-start(bf16[8,8192]{1,0:T(8,128)(2,1)S(1)} %get-tuple-element.20), channel_id=1, source_target_pairs={{0,14},{2,0},{4,2},{6,4},{8,6},{10,8},{12,10},{14,12},{16,208},{18... | collective-permute-start | bytes 393224 | tf_op jit(solution)/shard_map/ppermute | solution.py:43
  139.5 1.7 %collective-permute-done.15 = bf16[8,8192]{1,0:T(8,128)(2,1)S(1)} collective-permute-done((bf16[8,8192]{1,0:T(8,128)(2,1)S(1)}, bf16[8,8192]{1,0:T(8,128)(2,1)S(1)}, u32[]{:S(2)}, u32[]{:S(2)}) %collective-permute-start.15) | collective-permute-done | bytes 131104 | tf_op jit(solution)/shard_map/ppermute | solution.py:43
  141.2 3.4 %collective-permute-done.17 = bf16[8,8192]{1,0:T(8,128)(2,1)S(1)} collective-permute-done((bf16[8,8192]{1,0:T(8,128)(2,1)S(1)}, bf16[8,8192]{1,0:T(8,128)(2,1)S(1)}, u32[]{:S(2)}, u32[]{:S(2)}) %collective-permute-start.17) | collective-permute-done | bytes 131104 | tf_op jit(solution)/shard_map/ppermute | solution.py:43
  144.5 0.1 slice_add_fusion.2
  144.7 1.2 collective-permute-start.18
  145.9 8.4 %collective-permute-done.18 = f32[4,8192]{1,0:T(4,128)S(1)} collective-permute-done((f32[4,8192]{1,0:T(4,128)S(1)}, f32[4,8192]{1,0:T(4,128)S(1)}, u32[]{:S(2)}, u32[]{:S(2)}) %collective-permute-start.18) | collective-permute-done | bytes 131104 | tf_op jit(solution)/shard_map/ppermute | solution.py:43
  154.3 1.3 collective-permute-start.19
  155.6 0.5 slice.78
  156.1 0.5 slice.77
  156.6 2.0 %collective-permute-done.19 = f32[2,8192]{1,0:T(2,128)S(1)} collective-permute-done((f32[2,8192]{1,0:T(2,128)S(1)}, f32[2,8192]{1,0:T(2,128)S(1)}, u32[]{:S(2)}, u32[]{:S(2)}) %collective-permute-start.19) | collective-permute-done | bytes 65568 | tf_op jit(solution)/shard_map/ppermute | solution.py:43
  158.7 0.7 fusion.11
  (31 shorter events, 0.4 us)
Async XLA Ops:
  0.6 50.1 %copy-start.3 = (s32[256]{0:T(256)S(1)}, s32[256]{0:T(256)}, u32[]{:S(2)}) copy-start(s32[256]{0:T(256)} %param.6) | copy-start | bytes 3076
  0.6 4.2 %collective-permute-start = (bf16[2,8192]{1,0:T(2,128)(2,1)}, bf16[2,8192]{1,0:T(2,128)(2,1)S(1)}, u32[]{:S(2)}, u32[]{:S(2)}) collective-permute-start(bf16[2,8192]{1,0:T(2,128)(2,1)} %param.4), channel_id=1, source_target_pairs={{0,32},{2,34},{4,36},{6,38},{8,40},{10,42},{12,44},{14,46},{16,48}... | collective-permute-start | bytes 98312 | tf_op jit(solution)/shard_map/ppermute | solution.py:43
  4.9 23.1 %copy-start.1 = (bf16[2,8192]{1,0:T(2,128)(2,1)}, bf16[2,8192]{1,0:T(2,128)(2,1)S(1)}, u32[]{:S(2)}) copy-start(bf16[2,8192]{1,0:T(2,128)(2,1)S(1)} %collective-permute-done) | copy-start | bytes 98308
  5.7 9.6 %collective-permute-start.1 = (bf16[4,8192]{1,0:T(4,128)(2,1)S(1)}, bf16[4,8192]{1,0:T(4,128)(2,1)S(1)}, u32[]{:S(2)}, u32[]{:S(2)}) collective-permute-start(bf16[4,8192]{1,0:T(4,128)(2,1)S(1)} %pad_maximum_fusion.1), channel_id=1, source_target_pairs={{0,8},{2,10},{4,12},{6,14},{8,0},{10,2},{12,4},{14,6},{16,24},{18,... | collective-permute-start | bytes 196616 | tf_op jit(solution)/shard_map/ppermute | solution.py:43
  15.3 12.6 %copy-start = (bf16[4,8192]{1,0:T(4,128)(2,1)}, bf16[4,8192]{1,0:T(4,128)(2,1)S(1)}, u32[]{:S(2)}) copy-start(bf16[4,8192]{1,0:T(4,128)(2,1)S(1)} %collective-permute-done.1) | copy-start | bytes 196612
  16.2 8.9 %collective-permute-start.4 = (bf16[8,8192]{1,0:T(8,128)(2,1)S(1)}, bf16[8,8192]{1,0:T(8,128)(2,1)S(1)}, u32[]{:S(2)}, u32[]{:S(2)}) collective-permute-start(bf16[8,8192]{1,0:T(8,128)(2,1)S(1)} %pad_maximum_fusion), channel_id=1, source_target_pairs={{0,12},{2,14},{4,0},{6,2},{8,4},{10,6},{12,8},{14,10},{16,144},{18... | collective-permute-start | bytes 393224 | tf_op jit(solution)/shard_map/ppermute | solution.py:43
  21.2 6.2 %collective-permute-start.3 = (bf16[8,8192]{1,0:T(8,128)(2,1)S(1)}, bf16[8,8192]{1,0:T(8,128)(2,1)S(1)}, u32[]{:S(2)}, u32[]{:S(2)}) collective-permute-start(bf16[8,8192]{1,0:T(8,128)(2,1)S(1)} %pad_maximum_fusion), channel_id=1, source_target_pairs={{0,2},{2,4},{4,6},{6,8},{8,10},{10,12},{12,14},{14,0},{16,80},{18,... | collective-permute-start | bytes 393224 | tf_op jit(solution)/shard_map/ppermute | solution.py:43
  22.2 5.7 %collective-permute-start.2 = (bf16[8,8192]{1,0:T(8,128)(2,1)S(1)}, bf16[8,8192]{1,0:T(8,128)(2,1)S(1)}, u32[]{:S(2)}, u32[]{:S(2)}) collective-permute-start(bf16[8,8192]{1,0:T(8,128)(2,1)S(1)} %pad_maximum_fusion), channel_id=1, source_target_pairs={{0,14},{2,0},{4,2},{6,4},{8,6},{10,8},{12,10},{14,12},{16,208},{18... | collective-permute-start | bytes 393224 | tf_op jit(solution)/shard_map/ppermute | solution.py:43
  28.8 13.0 %collective-permute-start.7 = (bf16[32,8192]{1,0:T(8,128)(2,1)S(1)}, bf16[32,8192]{1,0:T(8,128)(2,1)S(1)}, u32[]{:S(2)}, u32[]{:S(2)}) collective-permute-start(bf16[32,8192]{1,0:T(8,128)(2,1)S(1)} %concatenate.21), channel_id=1, source_target_pairs={{0,128},{2,130},{4,132},{6,134},{8,136},{10,138},{12,140},{14,142}... | collective-permute-start | bytes 1572872 | tf_op jit(solution)/shard_map/ppermute | solution.py:43
  34.5 12.8 %collective-permute-start.6 = (bf16[32,8192]{1,0:T(8,128)(2,1)S(1)}, bf16[32,8192]{1,0:T(8,128)(2,1)S(1)}, u32[]{:S(2)}, u32[]{:S(2)}) collective-permute-start(bf16[32,8192]{1,0:T(8,128)(2,1)S(1)} %concatenate.21), channel_id=1, source_target_pairs={{0,64},{2,66},{4,68},{6,70},{8,72},{10,74},{12,76},{14,78},{16,18}... | collective-permute-start | bytes 1572872 | tf_op jit(solution)/shard_map/ppermute | solution.py:43
  34.5 12.8 %collective-permute-start.5 = (bf16[32,8192]{1,0:T(8,128)(2,1)S(1)}, bf16[32,8192]{1,0:T(8,128)(2,1)}, u32[]{:S(2)}, u32[]{:S(2)}) collective-permute-start(bf16[32,8192]{1,0:T(8,128)(2,1)S(1)} %concatenate.21), channel_id=1, source_target_pairs={{0,192},{2,194},{4,196},{6,198},{8,200},{10,202},{12,204},{14,206}... | collective-permute-start | bytes 1572872 | tf_op jit(solution)/shard_map/ppermute | solution.py:43
  50.6 4.4 %collective-permute-start.8 = (bf16[128,8192]{1,0:T(8,128)(2,1)S(1)}, bf16[128,8192]{1,0:T(8,128)(2,1)}, u32[]{:S(2)}, u32[]{:S(2)}) collective-permute-start(bf16[128,8192]{1,0:T(8,128)(2,1)S(1)} %concatenate.22), channel_id=1, source_target_pairs={{0,16},{2,18},{4,20},{6,22},{8,24},{10,26},{12,28},{14,30},{16,0},... | collective-permute-start | bytes 6291464 | tf_op jit(solution)/shard_map/ppermute | solution.py:43
  74.0 7.4 %copy-start.2 = (pred[256,256]{1,0:T(8,128)(4,1)S(1)}, pred[256,256]{1,0:T(8,128)(4,1)}, u32[]{:S(2)}) copy-start(pred[256,256]{1,0:T(8,128)(4,1)} %iota_compare_fusion) | copy-start | bytes 196612
  74.0 22.0 %copy-start.4 = (f32[256]{0:T(256)S(1)}, f32[256]{0:T(256)}, u32[]{:S(2)}) copy-start(f32[256]{0:T(256)} %param.7) | copy-start | bytes 3076
  81.6 1.3 collective-permute-start.9
  82.9 3.7 %collective-permute-start.10 = (f32[3,256]{1,0:T(4,128)S(1)}, f32[3,256]{1,0:T(4,128)S(1)}, u32[]{:S(2)}, u32[]{:S(2)}) collective-permute-start(f32[3,256]{1,0:T(4,128)S(1)} %get-tuple-element.27), channel_id=1, source_target_pairs={{0,32},{2,34},{4,36},{6,38},{8,40},{10,42},{12,44},{14,46},{16,48}... | collective-permute-start | bytes 9224 | tf_op jit(solution)/shard_map/ppermute | solution.py:43
  87.3 18.9 %all-to-all-start = ((f32[32,3,256]{2,1,0:T(4,128)}), f32[32,3,256]{2,1,0:T(4,128)S(1)}, u32[]{:S(2)}, u32[]{:S(2)}) async-start(f32[32,3,256]{2,1,0:T(4,128)} %broadcast_in_dim.111), calls=%async_computation | async-start | bytes 262144 | tf_op jit(solution)/shard_map/all_to_all | solution.py:92
  112.6 4.2 %collective-permute-start.11 = (bf16[128,8192]{1,0:T(8,128)(2,1)S(1)}, bf16[128,8192]{1,0:T(8,128)(2,1)S(1)}, u32[]{:S(2)}, u32[]{:S(2)}) collective-permute-start(bf16[128,8192]{1,0:T(8,128)(2,1)S(1)} %slice.117), channel_id=1, source_target_pairs={{0,16},{2,18},{4,20},{6,22},{8,24},{10,26},{12,28},{14,30},{16,0},... | collective-permute-start | bytes 6291464 | tf_op jit(solution)/shard_map/ppermute | solution.py:43
  117.6 16.1 %collective-permute-start.12 = (bf16[32,8192]{1,0:T(8,128)(2,1)S(1)}, bf16[32,8192]{1,0:T(8,128)(2,1)S(1)}, u32[]{:S(2)}, u32[]{:S(2)}) collective-permute-start(bf16[32,8192]{1,0:T(8,128)(2,1)S(1)} %get-tuple-element.15), channel_id=1, source_target_pairs={{0,64},{2,66},{4,68},{6,70},{8,72},{10,74},{12,76},{14,78},{16,18}... | collective-permute-start | bytes 1572872 | tf_op jit(solution)/shard_map/ppermute | solution.py:43
  118.3 15.4 %collective-permute-start.14 = (bf16[32,8192]{1,0:T(8,128)(2,1)S(1)}, bf16[32,8192]{1,0:T(8,128)(2,1)S(1)}, u32[]{:S(2)}, u32[]{:S(2)}) collective-permute-start(bf16[32,8192]{1,0:T(8,128)(2,1)S(1)} %get-tuple-element.16), channel_id=1, source_target_pairs={{0,128},{2,130},{4,132},{6,134},{8,136},{10,138},{12,140},{14,142}... | collective-permute-start | bytes 1572872 | tf_op jit(solution)/shard_map/ppermute | solution.py:43
  120.4 14.3 %collective-permute-start.13 = (bf16[32,8192]{1,0:T(8,128)(2,1)S(1)}, bf16[32,8192]{1,0:T(8,128)(2,1)S(1)}, u32[]{:S(2)}, u32[]{:S(2)}) collective-permute-start(bf16[32,8192]{1,0:T(8,128)(2,1)S(1)} %get-tuple-element.17), channel_id=1, source_target_pairs={{0,192},{2,194},{4,196},{6,198},{8,200},{10,202},{12,204},{14,206}... | collective-permute-start | bytes 1572872 | tf_op jit(solution)/shard_map/ppermute | solution.py:43
  134.9 6.3 %collective-permute-start.15 = (bf16[8,8192]{1,0:T(8,128)(2,1)S(1)}, bf16[8,8192]{1,0:T(8,128)(2,1)S(1)}, u32[]{:S(2)}, u32[]{:S(2)}) collective-permute-start(bf16[8,8192]{1,0:T(8,128)(2,1)S(1)} %get-tuple-element.18), channel_id=1, source_target_pairs={{0,2},{2,4},{4,6},{6,8},{8,10},{10,12},{12,14},{14,0},{16,80},{18,... | collective-permute-start | bytes 393224 | tf_op jit(solution)/shard_map/ppermute | solution.py:43
  136.1 8.5 %collective-permute-start.17 = (bf16[8,8192]{1,0:T(8,128)(2,1)S(1)}, bf16[8,8192]{1,0:T(8,128)(2,1)S(1)}, u32[]{:S(2)}, u32[]{:S(2)}) collective-permute-start(bf16[8,8192]{1,0:T(8,128)(2,1)S(1)} %get-tuple-element.19), channel_id=1, source_target_pairs={{0,4},{2,6},{4,8},{6,10},{8,12},{10,14},{12,0},{14,2},{16,144},{18... | collective-permute-start | bytes 393224 | tf_op jit(solution)/shard_map/ppermute | solution.py:43
  136.7 7.9 %collective-permute-start.16 = (bf16[8,8192]{1,0:T(8,128)(2,1)S(1)}, bf16[8,8192]{1,0:T(8,128)(2,1)S(1)}, u32[]{:S(2)}, u32[]{:S(2)}) collective-permute-start(bf16[8,8192]{1,0:T(8,128)(2,1)S(1)} %get-tuple-element.20), channel_id=1, source_target_pairs={{0,14},{2,0},{4,2},{6,4},{8,6},{10,8},{12,10},{14,12},{16,208},{18... | collective-permute-start | bytes 393224 | tf_op jit(solution)/shard_map/ppermute | solution.py:43
  144.7 9.6 %collective-permute-start.18 = (f32[4,8192]{1,0:T(4,128)S(1)}, f32[4,8192]{1,0:T(4,128)S(1)}, u32[]{:S(2)}, u32[]{:S(2)}) collective-permute-start(f32[4,8192]{1,0:T(4,128)S(1)} %slice.106), channel_id=1, source_target_pairs={{0,8},{2,10},{4,12},{6,14},{8,0},{10,2},{12,4},{14,6},{16,24},{18,... | collective-permute-start | bytes 393224 | tf_op jit(solution)/shard_map/ppermute | solution.py:43
  154.3 4.4 %collective-permute-start.19 = (f32[2,8192]{1,0:T(2,128)S(1)}, f32[2,8192]{1,0:T(2,128)S(1)}, u32[]{:S(2)}, u32[]{:S(2)}) collective-permute-start(f32[2,8192]{1,0:T(2,128)S(1)} %slice.108), channel_id=1, source_target_pairs={{0,32},{2,34},{4,36},{6,38},{8,40},{10,42},{12,44},{14,46},{16,48}... | collective-permute-start | bytes 196616 | tf_op jit(solution)/shard_map/ppermute | solution.py:43

commit v2 on v1

v2 whole, which is shorter than its diff:
```python
import functools

import jax
import jax.numpy as jnp
from jax import lax
from jax.experimental import pallas as pl
from jax.experimental.pallas import tpu as pltpu
from jax.sharding import Mesh
from jax.sharding import PartitionSpec as P

zloss_coef = 0.0001
NY, NX, NC, NZ = 4, 2, 2, 8
GROUP = ("y", "x", "c", "z")
OFFSETS = (0, 1, -1, 2)
BF, F32 = jnp.bfloat16, jnp.float32
ROWS, DEPTH, WIDTH = 256, 8192, 512
CHUNK = 1024
VMEM = pl.BlockSpec(memory_space=pltpu.VMEM)
SMEM = pl.BlockSpec(memory_space=pltpu.SMEM)


def index_of(y, x, c, z):
    return (((y % NY) * NX + x % NX) * NC + c % NC) * NZ + z % NZ


def pairs(route):
    every = [(y, x, c, z) for y in range(NY) for x in range(NX) for c in range(NC) for z in range(NZ)]
    return [(index_of(*p), index_of(*route(*p))) for p in every]


def to_x(y, x, c, z):
    return y, x + 1, c, z


def to_c(y, x, c, z):
    return y, x, c + 1, z


def to_z4(y, x, c, z):
    return y, x, c, z + 4


def to_xz4(y, x, c, z):
    return y, x + 1, c, z + 4


def to_first(step):
    return lambda y, x, c, z: (y, x, c, z + step) if c == 0 else (y + step, x, c, z)


def to_second(step):
    return lambda y, x, c, z: (y + step, x, c, z) if c == 0 else (y, x, c, z + step)


def send(value, route):
    return lax.ppermute(value, GROUP, pairs(route))


def row_numbers():
    y, x, c, z = (lax.axis_index(a) for a in GROUP)
    at = jnp.arange(ROWS, dtype=jnp.int32)
    r, xr, z4, q1, q2, cr = at & 1, (at >> 1) & 1, (at >> 2) & 1, (at >> 3) & 3, (at >> 5) & 3, at >> 7
    o1 = jnp.where(q1 == 2, -1, jnp.where(q1 == 3, 2, q1))
    o2 = jnp.where(q2 == 2, -1, jnp.where(q2 == 3, 2, q2))
    core = c ^ cr
    zo = jnp.where(core == 0, o1, o2) + 4 * z4
    yo = jnp.where(core == 0, o2, o1)
    return ((((y + yo) & 3) * 2 + (x ^ xr)) * 2 + core) * 16 + ((z + zo) & 7) * 2 + r


def params(mib=40):
    return pltpu.CompilerParams(vmem_limit_bytes=mib << 20)


def placed(rows_ref):
    return rows_ref[...] == lax.broadcasted_iota(jnp.int32, (ROWS, ROWS), 1)


def logits_kernel(rows_ref, hit_ref, p0, p1, p2, p3, p4, p5, p6, p7, w_ref, logits_ref, stats_ref):
    pieces = (p0, p1, p2, p3, p4, p5, p6, p7)
    acc = jnp.zeros((ROWS, WIDTH), F32)
    for k in range(0, DEPTH, CHUNK):
        left = jnp.concatenate([p[:, k : k + CHUNK] for p in pieces], axis=0)
        acc += jnp.dot(left, w_ref[k : k + CHUNK, :], preferred_element_type=F32)
    logits_ref[...] = acc
    top = jnp.max(acc, axis=1, keepdims=True)
    total = jnp.sum(jnp.exp(acc - top), axis=1, keepdims=True)
    hit = lax.broadcasted_iota(jnp.int32, (ROWS, WIDTH), 1) == hit_ref[...]
    picked = jnp.sum(jnp.where(hit, acc, 0.0), axis=1, keepdims=True)
    place = placed(rows_ref)
    for i, column in enumerate((top, total, picked)):
        stats_ref[i : i + 1, :] = jnp.sum(jnp.where(place, column, 0.0), axis=0, keepdims=True)


def grad_kernel(start, dtype, rows_ref, hit_ref, top_ref, logits_ref, w_ref, soft_ref, target_ref):
    half = ROWS // 2
    place = placed(rows_ref)[start : start + half]
    top = jnp.sum(jnp.where(place, top_ref[...], 0.0), axis=1, keepdims=True)
    hit = lax.broadcasted_iota(jnp.int32, (half, WIDTH), 1) == hit_ref[start : start + half, :]
    soft = jnp.where(hit, 0.0, jnp.exp(logits_ref[start : start + half, :] - top)).astype(BF)
    left = jnp.concatenate([soft, jnp.where(hit, 1.0, 0.0).astype(BF)], axis=0)
    for k in range(0, DEPTH, CHUNK):
        both = lax.dot_general(left, w_ref[k : k + CHUNK, :], (((1,), (1,)), ((), ())), preferred_element_type=F32)
        soft_ref[:, k : k + CHUNK] = both[:half].astype(dtype)
        target_ref[:, k : k + CHUNK] = both[half:].astype(BF)


def combine_kernel(rows_ref, grad_ref, top_ref, stats_ref, soft_own, soft_in, target_own, target_in, o0, o1, o2, o3, log_ref):
    place = placed(rows_ref)[: ROWS // 2]

    def ordered(row):
        return jnp.sum(jnp.where(place, row, 0.0), axis=1, keepdims=True)

    log_total = ordered(stats_ref[0:1, :] + jnp.log(stats_ref[1:2, :]))
    picked = ordered(stats_ref[2:3, :])
    top = ordered(top_ref[...])
    lane = lax.broadcasted_iota(jnp.int32, (8, 128), 1)
    log_ref[...] = jnp.where(lane == 0, log_total[:8], picked[:8])
    factor = 1.0 + 2.0 * zloss_coef * log_total
    grad = grad_ref[: ROWS // 2, :]
    scale = grad * factor * jnp.exp(top - log_total)
    target = (grad * (jnp.exp(picked - log_total) * factor - 1.0)).astype(BF).astype(F32)
    for q, out in enumerate((o0, o1, o2, o3)):
        at = slice(32 * q, 32 * q + 32)
        for k in range(0, DEPTH, CHUNK):
            cut = slice(k, k + CHUNK)
            soft = soft_own[at, cut] + soft_in[at, cut].astype(F32)
            chosen = target_own[at, cut].astype(F32) + target_in[at, cut].astype(F32)
            out[:, cut] = (scale[at] * soft + target[at] * chosen).astype(out.dtype)


def merge(stats, axis):
    top, total, picked = stats
    highest = jnp.max(top, axis=axis, keepdims=True)
    total = jnp.sum(total * jnp.exp(top - highest), axis=axis)
    return jnp.stack([jnp.squeeze(highest, axis), total, jnp.sum(picked, axis=axis)])


def shards(hidden, lm_weight, targets, loss_grad):
    position = lax.axis_index(GROUP)
    half = ROWS // 2

    rows = row_numbers()[:, None]
    place = rows == jnp.arange(ROWS, dtype=jnp.int32)[None, :]
    own_hit = jnp.sum(jnp.where(place, targets[None, :], 0), axis=1, keepdims=True) - position * WIDTH
    own_grad = jnp.sum(jnp.where(place, loss_grad[None, :], 0.0), axis=1, keepdims=True)

    block = jnp.concatenate([hidden] + [send(hidden, to) for to in (to_x, to_z4, to_xz4)])
    block = jnp.concatenate([block] + [send(block, to_first(-o)) for o in OFFSETS[1:]])
    pieces = [block] + [send(block, to_second(-o)) for o in OFFSETS[1:]]
    pieces = pieces + [send(p, to_c) for p in pieces]

    logits, stats = pl.pallas_call(
        logits_kernel,
        out_shape=(jax.ShapeDtypeStruct((ROWS, WIDTH), F32), jax.ShapeDtypeStruct((3, ROWS), F32)),
        in_specs=[VMEM] * 11,
        out_specs=(VMEM, VMEM),
        compiler_params=params(),
        cost_estimate=pl.CostEstimate(flops=2 * ROWS * DEPTH * WIDTH, bytes_accessed=13 << 20, transcendentals=ROWS * WIDTH),
        name="logits",
    )(rows, own_hit, *pieces, lm_weight)
    stats = merge(jnp.stack([stats, send(stats, to_c)], axis=1), 0)
    top = stats[:1]

    def product(start, dtype):
        return pl.pallas_call(
            functools.partial(grad_kernel, start, dtype),
            out_shape=(jax.ShapeDtypeStruct((half, DEPTH), dtype), jax.ShapeDtypeStruct((half, DEPTH), BF)),
            in_specs=[VMEM] * 5,
            out_specs=(VMEM, VMEM),
            compiler_params=params(),
            cost_estimate=pl.CostEstimate(flops=2 * ROWS * DEPTH * WIDTH, bytes_accessed=12 << 20, transcendentals=half * WIDTH),
            name="product",
        )(rows, own_hit, top, logits, lm_weight)

    soft_out, target_out = product(half, BF)
    soft_in, target_in = send(soft_out, to_c), send(target_out, to_c)
    soft_own, target_own = product(0, F32)

    stats = merge(jnp.stack([stats, send(stats, to_x)], axis=1), 0)
    spread = lax.all_to_all(jnp.broadcast_to(stats[None], (32, 3, ROWS)), ("y", "z"), 0, 0)
    stats = merge(jnp.swapaxes(spread, 0, 1), 0)

    *pieces, logs = pl.pallas_call(
        combine_kernel,
        out_shape=[jax.ShapeDtypeStruct((32, DEPTH), F32)]
        + [jax.ShapeDtypeStruct((32, DEPTH), BF)] * 3
        + [jax.ShapeDtypeStruct((8, 128), F32)],
        in_specs=[VMEM] * 8,
        out_specs=[VMEM] * 5,
        compiler_params=params(),
        cost_estimate=pl.CostEstimate(flops=6 * half * DEPTH, bytes_accessed=13 << 20, transcendentals=0),
        name="combine",
    )(rows, own_grad, top, stats, soft_own, soft_in, target_own, target_in)
    log_total, target_logit = logs[:2, 0], logs[:2, 1]
    ce_loss = log_total - target_logit
    z_term = zloss_coef * log_total * log_total

    part = pieces[0] + sum(send(pieces[k], to_second(OFFSETS[k])).astype(F32) for k in (1, 2, 3))
    part = part.reshape(4, 8, DEPTH)
    part = part[0] + sum(send(part[k].astype(BF), to_first(OFFSETS[k])).astype(F32) for k in (1, 2, 3))
    part = [part[0:2]] + [send(part[2 * k : 2 * k + 2], to) for k, to in ((1, to_x), (2, to_z4), (3, to_xz4))]
    part = (part[0] + part[1]) + (part[2] + part[3])
    return ce_loss, z_term, part.astype(BF)


def solution(mesh):
    mesh = Mesh(mesh.devices.reshape(NY, NX, NC, NZ, 2), (*GROUP, "dp"))
    own = ("dp", *GROUP)
    in_specs = (P(own, None), P(None, GROUP), P("dp"), P("dp"))
    out_specs = (P(own), P(own), P(own, None))
    return jax.shard_map(shards, mesh=mesh, in_specs=in_specs, out_specs=out_specs, check_vma=False)
```

time: 162 us -> 133 us (0.82); the launches traced: 159 us -> 133 us
  waiting for transfers between devices: 67.6 us -> 45.6 us
  Pallas kernels: 0 us -> 17.7 us
  matrix products: 12.9 us -> 0 us
  local copies, waits for them, and re-layouts: 25.4 us -> 14.5 us
  starting transfers between devices: 47.2 us -> 50.2 us
    concatenate x2 -> x0, local copies, waits for them, and re-layouts: 22.3 us -> none  [the longest x1 19 us: shards(): block = jnp.concatenate([block, send(block, to_c)])]
    pallas_call x0 -> x4, Pallas kernels: none -> 17.7 us  [the longest x2 10.4 us: product(): pl.pallas_call(functools.partial(grad_kernel, start, dtype), out_shape=(j...]
    ppermute x20 -> x26, waiting for transfers between devices: 57.6 us -> 44.4 us  [send(): return lax.ppermute(value, GROUP, pairs(route))]
    dot_general x2 -> x0, matrix products: 12.9 us -> none  [the longest x1 7.08 us: shards(): logits = jnp.dot(block, lm_weight, preferred_element_type=f32)]
    unnamed x10 -> x18, local copies, waits for them, and re-layouts: 0.02 us -> 12.3 us
    all_to_all x1, waiting for transfers between devices: 10 us -> 1.22 us  [shards(): lax.all_to_all(jnp.broadcast_to(stats[None], (32, 3, ROWS)), ('y', 'z'),...]
    ppermute x20 -> x26, starting transfers between devices: 38.6 us -> 42.4 us  [send(): return lax.ppermute(value, GROUP, pairs(route))]
  transfers between devices with their start and end apart: 21 -> 27, of which waited for: 18 -> 17; matrix products, arithmetic and copies ran while one was open for 1% -> 2% of each run, Pallas kernels for 0% -> 4%
where the time goes in v2:
time: 133 us
  starting transfers between devices  50.2 us (38%)
  waiting for transfers between devices  45.6 us (34%)
  Pallas kernels  17.7 us (13%)
  local copies, waits for them, and re-layouts  14.5 us (11%)
  other arithmetic  3.87 us (3%)
    ppermute x26, waiting for transfers between devices, send(): return lax.ppermute(value, GROUP, pairs(route))  44.4 us
    ppermute x26, starting transfers between devices, send(): return lax.ppermute(value, GROUP, pairs(route))  42.4 us
    unnamed x18, local copies, waits for them, and re-layouts  12.3 us
    pallas_call x2, Pallas kernels, product(): pl.pallas_call(functools.partial(grad_kernel, start, dtype), out_shape=(j...  10.4 us
    all_to_all x1, starting transfers between devices, shards(): lax.all_to_all(jnp.broadcast_to(stats[None], (32, 3, ROWS)), ('y', 'z'),...  7.82 us
    pallas_call x1, Pallas kernels, shards(): pl.pallas_call(logits_kernel, out_shape=(jax.ShapeDtypeStruct((ROWS, WIDT...  4.1 us
    pallas_call x1, Pallas kernels, shards(): pl.pallas_call(combine_kernel, out_shape=[jax.ShapeDtypeStruct((32, DEPTH...  3.21 us
  transfers between devices with their start and end apart: 27, of which 17 were waited for; matrix products, arithmetic and copies ran while one was open for 2% of the time, Pallas kernels for 4%

profile of v2, /device:TPU:4, one launch (start us, length us, event | category | flops | bytes accessed | tf_op | source)
XLA Modules:
  0.0 132.7 jit_solution(4512439669987242823)
XLA Ops:
  0.6 7.9 %collective-permute-start.2 = (bf16[2,8192]{1,0:T(2,128)(2,1)}, bf16[2,8192]{1,0:T(2,128)(2,1)S(1)}, u32[]{:S(2)}, u32[]{:S(2)}) collective-permute-start(bf16[2,8192]{1,0:T(2,128)(2,1)} %param.4), channel_id=1, source_target_pairs={{0,40},{2,42},{4,44},{6,46},{8,32},{10,34},{12,36},{14,38},{16,56}... | collective-permute-start | bytes 98312 | tf_op jit(solution)/shard_map/ppermute | solution.py:56
  8.5 0.8 collective-permute-start
  9.4 1.4 %collective-permute-done.2 = bf16[2,8192]{1,0:T(2,128)(2,1)S(1)} collective-permute-done((bf16[2,8192]{1,0:T(2,128)(2,1)}, bf16[2,8192]{1,0:T(2,128)(2,1)S(1)}, u32[]{:S(2)}, u32[]{:S(2)}) %collective-permute-start.2) | collective-permute-done | bytes 32800 | tf_op jit(solution)/shard_map/ppermute | solution.py:56
  10.7 6.1 %collective-permute-done.1 = bf16[2,8192]{1,0:T(2,128)(2,1)S(1)} collective-permute-done((bf16[2,8192]{1,0:T(2,128)(2,1)}, bf16[2,8192]{1,0:T(2,128)(2,1)S(1)}, u32[]{:S(2)}, u32[]{:S(2)}) %collective-permute-start.1) | collective-permute-done | bytes 32800 | tf_op jit(solution)/shard_map/ppermute | solution.py:56
  16.8 0.9 pad_maximum_fusion
  17.8 0.9 collective-permute-start.5
  18.7 1.0 collective-permute-start.4
  19.7 2.2 %collective-permute-start.3 = (bf16[8,8192]{1,0:T(8,128)(2,1)S(1)}, bf16[8,8192]{1,0:T(8,128)(2,1)S(1)}, u32[]{:S(2)}, u32[]{:S(2)}) collective-permute-start(bf16[8,8192]{1,0:T(8,128)(2,1)S(1)} %pad_maximum_fusion), channel_id=1, source_target_pairs={{0,14},{2,0},{4,2},{6,4},{8,6},{10,8},{12,10},{14,12},{16,208},{18... | collective-permute-start | bytes 393224 | tf_op jit(solution)/shard_map/ppermute | solution.py:56
  21.9 3.3 %collective-permute-done.5 = bf16[8,8192]{1,0:T(8,128)(2,1)S(1)} collective-permute-done((bf16[8,8192]{1,0:T(8,128)(2,1)S(1)}, bf16[8,8192]{1,0:T(8,128)(2,1)S(1)}, u32[]{:S(2)}, u32[]{:S(2)}) %collective-permute-start.5) | collective-permute-done | bytes 131104 | tf_op jit(solution)/shard_map/ppermute | solution.py:56
  25.2 0.6 collective-permute-done.3
  25.8 1.0 concatenate.8.p0
  26.8 3.3 %collective-permute-start.8 = (bf16[32,8192]{1,0:T(8,128)(2,1)S(1)}, bf16[32,8192]{1,0:T(8,128)(2,1)S(1)}, u32[]{:S(2)}, u32[]{:S(2)}) collective-permute-start(bf16[32,8192]{1,0:T(8,128)(2,1)S(1)} %concatenate.8.p0), channel_id=1, source_target_pairs={{0,128},{2,130},{4,132},{6,134},{8,136},{10,138},{12,140},{14,142}... | collective-permute-start | bytes 1572872 | tf_op jit(solution)/shard_map/ppermute | solution.py:56
  30.0 0.7 collective-permute-start.7
  30.7 2.6 %collective-permute-start.6 = (bf16[32,8192]{1,0:T(8,128)(2,1)S(1)}, bf16[32,8192]{1,0:T(8,128)(2,1)S(1)}, u32[]{:S(2)}, u32[]{:S(2)}) collective-permute-start(bf16[32,8192]{1,0:T(8,128)(2,1)S(1)} %concatenate.8.p0), channel_id=1, source_target_pairs={{0,192},{2,194},{4,196},{6,198},{8,200},{10,202},{12,204},{14,206}... | collective-permute-start | bytes 1572872 | tf_op jit(solution)/shard_map/ppermute | solution.py:56
  33.3 4.4 %collective-permute-done.8.p3 = bf16[32,8192]{1,0:T(8,128)(2,1)S(1)} collective-permute-done((bf16[32,8192]{1,0:T(8,128)(2,1)S(1)}, bf16[32,8192]{1,0:T(8,128)(2,1)S(1)}, u32[]{:S(2)}, u32[]{:S(2)}) %collective-permute-start.8) | collective-permute-done | bytes 524320 | tf_op jit(solution)/shard_map/ppermute | solution.py:56
  37.6 2.7 %collective-permute-start.12 = (bf16[32,8192]{1,0:T(8,128)(2,1)S(1)}, bf16[32,8192]{1,0:T(8,128)(2,1)}, u32[]{:S(2)}, u32[]{:S(2)}) collective-permute-start(bf16[32,8192]{1,0:T(8,128)(2,1)S(1)} %collective-permute-done.8.p3), channel_id=1, source_target_pairs={{0,16},{2,18},{4,20},{6,22},{8,24},{10,26},{12,28},{14,30},{16,0},... | collective-permute-start | bytes 1572872 | tf_op jit(solution)/shard_map/ppermute | solution.py:56
  40.3 2.8 %collective-permute-done.7.p2 = bf16[32,8192]{1,0:T(8,128)(2,1)S(1)} collective-permute-done((bf16[32,8192]{1,0:T(8,128)(2,1)S(1)}, bf16[32,8192]{1,0:T(8,128)(2,1)S(1)}, u32[]{:S(2)}, u32[]{:S(2)}) %collective-permute-start.7) | collective-permute-done | bytes 524320 | tf_op jit(solution)/shard_map/ppermute | solution.py:56
  43.2 0.4 collective-permute-done.6.p1
  43.5 1.5 %collective-permute-start.10 = (bf16[32,8192]{1,0:T(8,128)(2,1)S(1)}, bf16[32,8192]{1,0:T(8,128)(2,1)}, u32[]{:S(2)}, u32[]{:S(2)}) collective-permute-start(bf16[32,8192]{1,0:T(8,128)(2,1)S(1)} %collective-permute-done.6.p1), channel_id=1, source_target_pairs={{0,16},{2,18},{4,20},{6,22},{8,24},{10,26},{12,28},{14,30},{16,0},... | collective-permute-start | bytes 1572872 | tf_op jit(solution)/shard_map/ppermute | solution.py:56
  45.0 0.9 select_reduce_fusion
  45.9 0.1 copy.32.hit_ref
  46.0 0.2 and_add_fusion.rows_ref
  46.2 0.8 copy-done.6
  47.0 3.4 %copy-done = bf16[8192,512]{1,0:T(8,128)(2,1)S(1)} copy-done((bf16[8192,512]{1,0:T(8,128)(2,1)S(1)}, bf16[8192,512]{1,0:T(8,128)(2,1)}, u32[]{:S(2)}) %copy-start) | copy-done | bytes 8388632
  50.4 1.0 copy-done.7
  51.5 4.1 %logits.1 = (f32[256,512]{1,0:T(8,128)S(1)}, f32[3,256]{1,0:T(4,128)S(1)}) custom-call(s32[256,1]{1,0:T(8,128)S(1)} %and_add_fusion.rows_ref, s32[256,1]{1,0:T(8,128)S(1)} %copy.32.hit_ref, bf16[32,8192]{1,0:T(8,128)(2,1)S(1)} %concatenate.8.p0, bf16[32,8192]{1,0:T(8,128)(2,1)S(1)} %collective-permute-done.6.p1, ...), custom_call_target="tpu_custom_call" | custom-call | flops 2147483648 | bytes 13631488 | tf_op jit(solution)/shard_map/logits/pallas_call | solution.py:153
  55.6 0.3 collective-permute-start.13
  55.8 1.2 collective-permute-done.13
  57.0 4.5 %product.3 = (bf16[128,8192]{1,0:T(8,128)(2,1)}, bf16[128,8192]{1,0:T(8,128)(2,1)}) custom-call(s32[256,1]{1,0:T(8,128)S(1)} %and_add_fusion.rows_ref, s32[256,1]{1,0:T(8,128)S(1)} %copy.32.hit_ref, f32[1,256]{1,0:T(1,128)S(1)} %bitcast.57, f32[256,512]{1,0:T(8,128)S(1)} %get-tuple-element.15.logits_ref, bf16[8192,512]{1,0:T(8,128)(2,1)S(1)} %copy-done.1), custom_call_target="tpu_custom_call" | custom-call | flops 2147483648 | bytes 12582912 | tf_op jit(solution)/shard_map/product/pallas_call | solution.py:166
  61.6 0.2 collective-permute-start.15
  61.7 0.3 collective-permute-start.16
  62.1 0.6 collective-permute-start.14
  62.8 0.2 select_reduce_fusion.1
  63.0 0.1 copy.39.grad_ref
  63.1 2.7 %collective-permute-done.14 = f32[3,256]{1,0:T(4,128)S(1)} collective-permute-done((f32[3,256]{1,0:T(4,128)S(1)}, f32[3,256]{1,0:T(4,128)S(1)}, u32[]{:S(2)}, u32[]{:S(2)}) %collective-permute-start.14) | collective-permute-done | bytes 3104 | tf_op jit(solution)/shard_map/ppermute | solution.py:56
  65.9 0.7 broadcast_in_dim.65
  66.6 7.8 %all-to-all-start = ((f32[32,3,256]{2,1,0:T(4,128)}), f32[32,3,256]{2,1,0:T(4,128)S(1)}, u32[]{:S(2)}, u32[]{:S(2)}) async-start(f32[32,3,256]{2,1,0:T(4,128)} %broadcast_in_dim.65), calls=%async_computation | async-start | bytes 262144 | tf_op jit(solution)/shard_map/all_to_all | solution.py:181
  74.4 5.9 %product.2 = (f32[128,8192]{1,0:T(8,128)S(1)}, bf16[128,8192]{1,0:T(8,128)(2,1)S(1)}) custom-call(s32[256,1]{1,0:T(8,128)S(1)} %and_add_fusion.rows_ref, s32[256,1]{1,0:T(8,128)S(1)} %copy.32.hit_ref, f32[1,256]{1,0:T(1,128)S(1)} %bitcast.59, f32[256,512]{1,0:T(8,128)S(1)} %get-tuple-element.15.logits_ref, bf16[8192,512]{1,0:T(8,128)(2,1)} %w_ref.5), custom_call_target="tpu_custom_call" | custom-call | flops 2147483648 | bytes 12582912 | tf_op jit(solution)/shard_map/product/pallas_call | solution.py:166
  80.3 1.9 %copy-done.2 = f32[128,8192]{1,0:T(8,128)} copy-done((f32[128,8192]{1,0:T(8,128)}, f32[128,8192]{1,0:T(8,128)S(1)}, u32[]{:S(2)}) %copy-start.2) | copy-done | bytes 4194328
  82.3 1.3 copy-done.4
  83.6 1.2 all-to-all-done
  85.0 2.2 %copy-done.3 = f32[128,8192]{1,0:T(8,128)S(1)} copy-done((f32[128,8192]{1,0:T(8,128)S(1)}, f32[128,8192]{1,0:T(8,128)}, u32[]{:S(2)}) %copy-start.3) | copy-done | bytes 4194328
  87.2 1.6 %copy-done.5 = bf16[128,8192]{1,0:T(8,128)(2,1)S(1)} copy-done((bf16[128,8192]{1,0:T(8,128)(2,1)S(1)}, bf16[128,8192]{1,0:T(8,128)(2,1)}, u32[]{:S(2)}) %copy-start.5) | copy-done | bytes 2097176
  88.8 3.2 %combine.1 = (f32[32,8192]{1,0:T(8,128)S(1)}, bf16[32,8192]{1,0:T(8,128)(2,1)S(1)}, bf16[32,8192]{1,0:T(8,128)(2,1)S(1)}, bf16[32,8192]{1,0:T(8,128)(2,1)S(1)}, f32[8,128]{1,0:T(8,128)S(1)}) custom-call(s32[256,1]{1,0:T(8,128)S(1)} %and_add_fusion.rows_ref, f32[256,1]{1,0:T(8,128)S(1)} %copy.39.grad_ref, f32[1,256]{1,0:T(1,128)S(1)} %bitcast.60, ...), custom_call_target="tpu_custom_call" | custom-call | flops 6291456 | bytes 13631488 | tf_op jit(solution)/shard_map/combine/pallas_call | solution.py:184
  92.0 0.7 collective-permute-start.17
  92.7 2.6 %collective-permute-start.18 = (bf16[32,8192]{1,0:T(8,128)(2,1)S(1)}, bf16[32,8192]{1,0:T(8,128)(2,1)S(1)}, u32[]{:S(2)}, u32[]{:S(2)}) collective-permute-start(bf16[32,8192]{1,0:T(8,128)(2,1)S(1)} %get-tuple-element.23), channel_id=1, source_target_pairs={{0,192},{2,194},{4,196},{6,198},{8,200},{10,202},{12,204},{14,206}... | collective-permute-start | bytes 1572872 | tf_op jit(solution)/shard_map/ppermute | solution.py:56
  95.3 0.9 collective-permute-start.19
  96.2 6.3 %collective-permute-done.17 = bf16[32,8192]{1,0:T(8,128)(2,1)S(1)} collective-permute-done((bf16[32,8192]{1,0:T(8,128)(2,1)S(1)}, bf16[32,8192]{1,0:T(8,128)(2,1)S(1)}, u32[]{:S(2)}, u32[]{:S(2)}) %collective-permute-start.17) | collective-permute-done | bytes 524320 | tf_op jit(solution)/shard_map/ppermute | solution.py:56
  102.4 5.2 %collective-permute-done.18 = bf16[32,8192]{1,0:T(8,128)(2,1)S(1)} collective-permute-done((bf16[32,8192]{1,0:T(8,128)(2,1)S(1)}, bf16[32,8192]{1,0:T(8,128)(2,1)S(1)}, u32[]{:S(2)}, u32[]{:S(2)}) %collective-permute-start.18) | collective-permute-done | bytes 524320 | tf_op jit(solution)/shard_map/ppermute | solution.py:56
  107.6 0.5 collective-permute-done.19
  108.1 0.2 fusion.21
  108.4 1.5 %collective-permute-start.20 = (bf16[8,8192]{1,0:T(8,128)(2,1)S(1)}, bf16[8,8192]{1,0:T(8,128)(2,1)S(1)}, u32[]{:S(2)}, u32[]{:S(2)}) collective-permute-start(bf16[8,8192]{1,0:T(8,128)(2,1)S(1)} %get-tuple-element.35), channel_id=1, source_target_pairs={{0,2},{2,4},{4,6},{6,8},{8,10},{10,12},{12,14},{14,0},{16,80},{18,... | collective-permute-start | bytes 393224 | tf_op jit(solution)/shard_map/ppermute | solution.py:56
  109.9 2.4 %collective-permute-start.22 = (bf16[8,8192]{1,0:T(8,128)(2,1)S(1)}, bf16[8,8192]{1,0:T(8,128)(2,1)S(1)}, u32[]{:S(2)}, u32[]{:S(2)}) collective-permute-start(bf16[8,8192]{1,0:T(8,128)(2,1)S(1)} %get-tuple-element.36), channel_id=1, source_target_pairs={{0,4},{2,6},{4,8},{6,10},{8,12},{10,14},{12,0},{14,2},{16,144},{18... | collective-permute-start | bytes 393224 | tf_op jit(solution)/shard_map/ppermute | solution.py:56
  112.3 1.8 %collective-permute-start.21 = (bf16[8,8192]{1,0:T(8,128)(2,1)S(1)}, bf16[8,8192]{1,0:T(8,128)(2,1)S(1)}, u32[]{:S(2)}, u32[]{:S(2)}) collective-permute-start(bf16[8,8192]{1,0:T(8,128)(2,1)S(1)} %get-tuple-element.37), channel_id=1, source_target_pairs={{0,14},{2,0},{4,2},{6,4},{8,6},{10,8},{12,10},{14,12},{16,208},{18... | collective-permute-start | bytes 393224 | tf_op jit(solution)/shard_map/ppermute | solution.py:56
  114.1 0.2 slice_reduce_fusion.1
  114.3 0.4 collective-permute-done.20
  114.6 3.4 %collective-permute-done.22 = bf16[8,8192]{1,0:T(8,128)(2,1)S(1)} collective-permute-done((bf16[8,8192]{1,0:T(8,128)(2,1)S(1)}, bf16[8,8192]{1,0:T(8,128)(2,1)S(1)}, u32[]{:S(2)}, u32[]{:S(2)}) %collective-permute-start.22) | collective-permute-done | bytes 131104 | tf_op jit(solution)/shard_map/ppermute | solution.py:56
  118.1 5.4 %collective-permute-start.25 = (f32[2,8192]{1,0:T(2,128)S(1)}, f32[2,8192]{1,0:T(2,128)S(1)}, u32[]{:S(2)}, u32[]{:S(2)}) collective-permute-start(f32[2,8192]{1,0:T(2,128)S(1)} %get-tuple-element.38), channel_id=1, source_target_pairs={{0,40},{2,42},{4,44},{6,46},{8,32},{10,34},{12,36},{14,38},{16,56}... | collective-permute-start | bytes 196616 | tf_op jit(solution)/shard_map/ppermute | solution.py:56
  123.6 1.0 collective-permute-start.24
  124.6 1.1 collective-permute-start.23
  125.6 0.5 multiply_multiply_fusion
  126.1 3.0 %collective-permute-done.25 = f32[2,8192]{1,0:T(2,128)S(1)} collective-permute-done((f32[2,8192]{1,0:T(2,128)S(1)}, f32[2,8192]{1,0:T(2,128)S(1)}, u32[]{:S(2)}, u32[]{:S(2)}) %collective-permute-start.25) | collective-permute-done | bytes 65568 | tf_op jit(solution)/shard_map/ppermute | solution.py:56
  129.1 2.9 %collective-permute-done.24 = f32[2,8192]{1,0:T(2,128)S(1)} collective-permute-done((f32[2,8192]{1,0:T(2,128)S(1)}, f32[2,8192]{1,0:T(2,128)S(1)}, u32[]{:S(2)}, u32[]{:S(2)}) %collective-permute-start.24) | collective-permute-done | bytes 65568 | tf_op jit(solution)/shard_map/ppermute | solution.py:56
  132.0 0.7 fusion.5
  (38 shorter events, 0.5 us)
Async XLA Ops:
  0.6 10.1 %collective-permute-start.2 = (bf16[2,8192]{1,0:T(2,128)(2,1)}, bf16[2,8192]{1,0:T(2,128)(2,1)S(1)}, u32[]{:S(2)}, u32[]{:S(2)}) collective-permute-start(bf16[2,8192]{1,0:T(2,128)(2,1)} %param.4), channel_id=1, source_target_pairs={{0,40},{2,42},{4,44},{6,46},{8,32},{10,34},{12,36},{14,38},{16,56}... | collective-permute-start | bytes 98312 | tf_op jit(solution)/shard_map/ppermute | solution.py:56
  8.5 8.3 %collective-permute-start.1 = (bf16[2,8192]{1,0:T(2,128)(2,1)}, bf16[2,8192]{1,0:T(2,128)(2,1)S(1)}, u32[]{:S(2)}, u32[]{:S(2)}) collective-permute-start(bf16[2,8192]{1,0:T(2,128)(2,1)} %param.4), channel_id=1, source_target_pairs={{0,8},{2,10},{4,12},{6,14},{8,0},{10,2},{12,4},{14,6},{16,24},{18,... | collective-permute-start | bytes 98312 | tf_op jit(solution)/shard_map/ppermute | solution.py:56
  8.5 8.3 %collective-permute-start = (bf16[2,8192]{1,0:T(2,128)(2,1)}, bf16[2,8192]{1,0:T(2,128)(2,1)S(1)}, u32[]{:S(2)}, u32[]{:S(2)}) collective-permute-start(bf16[2,8192]{1,0:T(2,128)(2,1)} %param.4), channel_id=1, source_target_pairs={{0,32},{2,34},{4,36},{6,38},{8,40},{10,42},{12,44},{14,46},{16,48}... | collective-permute-start | bytes 98312 | tf_op jit(solution)/shard_map/ppermute | solution.py:56
  17.8 7.5 %collective-permute-start.5 = (bf16[8,8192]{1,0:T(8,128)(2,1)S(1)}, bf16[8,8192]{1,0:T(8,128)(2,1)S(1)}, u32[]{:S(2)}, u32[]{:S(2)}) collective-permute-start(bf16[8,8192]{1,0:T(8,128)(2,1)S(1)} %pad_maximum_fusion), channel_id=1, source_target_pairs={{0,12},{2,14},{4,0},{6,2},{8,4},{10,6},{12,8},{14,10},{16,144},{18... | collective-permute-start | bytes 393224 | tf_op jit(solution)/shard_map/ppermute | solution.py:56
  18.7 6.5 %collective-permute-start.4 = (bf16[8,8192]{1,0:T(8,128)(2,1)S(1)}, bf16[8,8192]{1,0:T(8,128)(2,1)S(1)}, u32[]{:S(2)}, u32[]{:S(2)}) collective-permute-start(bf16[8,8192]{1,0:T(8,128)(2,1)S(1)} %pad_maximum_fusion), channel_id=1, source_target_pairs={{0,2},{2,4},{4,6},{6,8},{8,10},{10,12},{12,14},{14,0},{16,80},{18,... | collective-permute-start | bytes 393224 | tf_op jit(solution)/shard_map/ppermute | solution.py:56
  19.7 6.1 %collective-permute-start.3 = (bf16[8,8192]{1,0:T(8,128)(2,1)S(1)}, bf16[8,8192]{1,0:T(8,128)(2,1)S(1)}, u32[]{:S(2)}, u32[]{:S(2)}) collective-permute-start(bf16[8,8192]{1,0:T(8,128)(2,1)S(1)} %pad_maximum_fusion), channel_id=1, source_target_pairs={{0,14},{2,0},{4,2},{6,4},{8,6},{10,8},{12,10},{14,12},{16,208},{18... | collective-permute-start | bytes 393224 | tf_op jit(solution)/shard_map/ppermute | solution.py:56
  26.8 10.9 %collective-permute-start.8 = (bf16[32,8192]{1,0:T(8,128)(2,1)S(1)}, bf16[32,8192]{1,0:T(8,128)(2,1)S(1)}, u32[]{:S(2)}, u32[]{:S(2)}) collective-permute-start(bf16[32,8192]{1,0:T(8,128)(2,1)S(1)} %concatenate.8.p0), channel_id=1, source_target_pairs={{0,128},{2,130},{4,132},{6,134},{8,136},{10,138},{12,140},{14,142}... | collective-permute-start | bytes 1572872 | tf_op jit(solution)/shard_map/ppermute | solution.py:56
  30.0 13.1 %collective-permute-start.7 = (bf16[32,8192]{1,0:T(8,128)(2,1)S(1)}, bf16[32,8192]{1,0:T(8,128)(2,1)S(1)}, u32[]{:S(2)}, u32[]{:S(2)}) collective-permute-start(bf16[32,8192]{1,0:T(8,128)(2,1)S(1)} %concatenate.8.p0), channel_id=1, source_target_pairs={{0,64},{2,66},{4,68},{6,70},{8,72},{10,74},{12,76},{14,78},{16,18}... | collective-permute-start | bytes 1572872 | tf_op jit(solution)/shard_map/ppermute | solution.py:56
  30.7 12.8 %collective-permute-start.6 = (bf16[32,8192]{1,0:T(8,128)(2,1)S(1)}, bf16[32,8192]{1,0:T(8,128)(2,1)S(1)}, u32[]{:S(2)}, u32[]{:S(2)}) collective-permute-start(bf16[32,8192]{1,0:T(8,128)(2,1)S(1)} %concatenate.8.p0), channel_id=1, source_target_pairs={{0,192},{2,194},{4,196},{6,198},{8,200},{10,202},{12,204},{14,206}... | collective-permute-start | bytes 1572872 | tf_op jit(solution)/shard_map/ppermute | solution.py:56
  33.3 12.9 %collective-permute-start.9 = (bf16[32,8192]{1,0:T(8,128)(2,1)S(1)}, bf16[32,8192]{1,0:T(8,128)(2,1)S(1)}, u32[]{:S(2)}, u32[]{:S(2)}) collective-permute-start(bf16[32,8192]{1,0:T(8,128)(2,1)S(1)} %concatenate.8.p0), channel_id=1, source_target_pairs={{0,16},{2,18},{4,20},{6,22},{8,24},{10,26},{12,28},{14,30},{16,0},... | collective-permute-start | bytes 1572872 | tf_op jit(solution)/shard_map/ppermute | solution.py:56
  37.6 9.4 %collective-permute-start.12 = (bf16[32,8192]{1,0:T(8,128)(2,1)S(1)}, bf16[32,8192]{1,0:T(8,128)(2,1)}, u32[]{:S(2)}, u32[]{:S(2)}) collective-permute-start(bf16[32,8192]{1,0:T(8,128)(2,1)S(1)} %collective-permute-done.8.p3), channel_id=1, source_target_pairs={{0,16},{2,18},{4,20},{6,22},{8,24},{10,26},{12,28},{14,30},{16,0},... | collective-permute-start | bytes 1572872 | tf_op jit(solution)/shard_map/ppermute | solution.py:56
  43.2 3.9 %collective-permute-start.11 = (bf16[32,8192]{1,0:T(8,128)(2,1)S(1)}, bf16[32,8192]{1,0:T(8,128)(2,1)}, u32[]{:S(2)}, u32[]{:S(2)}) collective-permute-start(bf16[32,8192]{1,0:T(8,128)(2,1)S(1)} %collective-permute-done.7.p2), channel_id=1, source_target_pairs={{0,16},{2,18},{4,20},{6,22},{8,24},{10,26},{12,28},{14,30},{16,0},... | collective-permute-start | bytes 1572872 | tf_op jit(solution)/shard_map/ppermute | solution.py:56
  43.5 3.5 %collective-permute-start.10 = (bf16[32,8192]{1,0:T(8,128)(2,1)S(1)}, bf16[32,8192]{1,0:T(8,128)(2,1)}, u32[]{:S(2)}, u32[]{:S(2)}) collective-permute-start(bf16[32,8192]{1,0:T(8,128)(2,1)S(1)} %collective-permute-done.6.p1), channel_id=1, source_target_pairs={{0,16},{2,18},{4,20},{6,22},{8,24},{10,26},{12,28},{14,30},{16,0},... | collective-permute-start | bytes 1572872 | tf_op jit(solution)/shard_map/ppermute | solution.py:56
  46.2 0.8 copy-start.6
  47.0 3.4 %copy-start = (bf16[8192,512]{1,0:T(8,128)(2,1)S(1)}, bf16[8192,512]{1,0:T(8,128)(2,1)}, u32[]{:S(2)}) copy-start(bf16[8192,512]{1,0:T(8,128)(2,1)} %w_ref.5) | copy-start | bytes 25165828
  50.4 1.0 copy-start.7
  51.5 5.6 %copy-start.1 = (bf16[8192,512]{1,0:T(8,128)(2,1)S(1)}, bf16[8192,512]{1,0:T(8,128)(2,1)}, u32[]{:S(2)}) copy-start(bf16[8192,512]{1,0:T(8,128)(2,1)} %w_ref.5) | copy-start | bytes 25165828
  55.6 1.4 %collective-permute-start.13 = (f32[3,256]{1,0:T(4,128)S(1)}, f32[3,256]{1,0:T(4,128)S(1)}, u32[]{:S(2)}, u32[]{:S(2)}) collective-permute-start(f32[3,256]{1,0:T(4,128)S(1)} %get-tuple-element.14), channel_id=1, source_target_pairs={{0,16},{2,18},{4,20},{6,22},{8,24},{10,26},{12,28},{14,30},{16,0},... | collective-permute-start | bytes 9224 | tf_op jit(solution)/shard_map/ppermute | solution.py:56
  57.0 5.7 %copy-start.8 = (f32[256]{0:T(256)S(1)}, f32[256]{0:T(256)}, u32[]{:S(2)}) copy-start(f32[256]{0:T(256)} %param.7) | copy-start | bytes 3076
  61.6 23.4 %collective-permute-start.15 = (bf16[128,8192]{1,0:T(8,128)(2,1)}, bf16[128,8192]{1,0:T(8,128)(2,1)S(1)}, u32[]{:S(2)}, u32[]{:S(2)}) collective-permute-start(bf16[128,8192]{1,0:T(8,128)(2,1)} %get-tuple-element.17), channel_id=1, source_target_pairs={{0,16},{2,18},{4,20},{6,22},{8,24},{10,26},{12,28},{14,30},{16,0},... | collective-permute-start | bytes 6291464 | tf_op jit(solution)/shard_map/ppermute | solution.py:56
  61.7 23.2 %collective-permute-start.16 = (bf16[128,8192]{1,0:T(8,128)(2,1)}, bf16[128,8192]{1,0:T(8,128)(2,1)}, u32[]{:S(2)}, u32[]{:S(2)}) collective-permute-start(bf16[128,8192]{1,0:T(8,128)(2,1)} %get-tuple-element.19), channel_id=1, source_target_pairs={{0,16},{2,18},{4,20},{6,22},{8,24},{10,26},{12,28},{14,30},{16,0},... | collective-permute-start | bytes 6291464 | tf_op jit(solution)/shard_map/ppermute | solution.py:56
  62.1 3.7 %collective-permute-start.14 = (f32[3,256]{1,0:T(4,128)S(1)}, f32[3,256]{1,0:T(4,128)S(1)}, u32[]{:S(2)}, u32[]{:S(2)}) collective-permute-start(f32[3,256]{1,0:T(4,128)S(1)} %get-tuple-element.48), channel_id=1, source_target_pairs={{0,32},{2,34},{4,36},{6,38},{8,40},{10,42},{12,44},{14,46},{16,48}... | collective-permute-start | bytes 9224 | tf_op jit(solution)/shard_map/ppermute | solution.py:56
  66.6 18.2 %all-to-all-start = ((f32[32,3,256]{2,1,0:T(4,128)}), f32[32,3,256]{2,1,0:T(4,128)S(1)}, u32[]{:S(2)}, u32[]{:S(2)}) async-start(f32[32,3,256]{2,1,0:T(4,128)} %broadcast_in_dim.65), calls=%async_computation | async-start | bytes 262144 | tf_op jit(solution)/shard_map/all_to_all | solution.py:181
  80.3 2.0 %copy-start.2 = (f32[128,8192]{1,0:T(8,128)}, f32[128,8192]{1,0:T(8,128)S(1)}, u32[]{:S(2)}) copy-start(f32[128,8192]{1,0:T(8,128)S(1)} %get-tuple-element.16.soft_own) | copy-start | bytes 12582916
  82.3 1.3 copy-start.4
  85.0 2.2 %copy-start.3 = (f32[128,8192]{1,0:T(8,128)S(1)}, f32[128,8192]{1,0:T(8,128)}, u32[]{:S(2)}) copy-start(f32[128,8192]{1,0:T(8,128)} %copy-done.2) | copy-start | bytes 12582916
  87.2 1.6 %copy-start.5 = (bf16[128,8192]{1,0:T(8,128)(2,1)S(1)}, bf16[128,8192]{1,0:T(8,128)(2,1)}, u32[]{:S(2)}) copy-start(bf16[128,8192]{1,0:T(8,128)(2,1)} %copy-done.4) | copy-start | bytes 6291460
  92.0 10.5 %collective-permute-start.17 = (bf16[32,8192]{1,0:T(8,128)(2,1)S(1)}, bf16[32,8192]{1,0:T(8,128)(2,1)S(1)}, u32[]{:S(2)}, u32[]{:S(2)}) collective-permute-start(bf16[32,8192]{1,0:T(8,128)(2,1)S(1)} %get-tuple-element.22), channel_id=1, source_target_pairs={{0,64},{2,66},{4,68},{6,70},{8,72},{10,74},{12,76},{14,78},{16,18}... | collective-permute-start | bytes 1572872 | tf_op jit(solution)/shard_map/ppermute | solution.py:56
  92.7 15.0 %collective-permute-start.18 = (bf16[32,8192]{1,0:T(8,128)(2,1)S(1)}, bf16[32,8192]{1,0:T(8,128)(2,1)S(1)}, u32[]{:S(2)}, u32[]{:S(2)}) collective-permute-start(bf16[32,8192]{1,0:T(8,128)(2,1)S(1)} %get-tuple-element.23), channel_id=1, source_target_pairs={{0,192},{2,194},{4,196},{6,198},{8,200},{10,202},{12,204},{14,206}... | collective-permute-start | bytes 1572872 | tf_op jit(solution)/shard_map/ppermute | solution.py:56
  95.3 12.8 %collective-permute-start.19 = (bf16[32,8192]{1,0:T(8,128)(2,1)S(1)}, bf16[32,8192]{1,0:T(8,128)(2,1)S(1)}, u32[]{:S(2)}, u32[]{:S(2)}) collective-permute-start(bf16[32,8192]{1,0:T(8,128)(2,1)S(1)} %get-tuple-element.24), channel_id=1, source_target_pairs={{0,128},{2,130},{4,132},{6,134},{8,136},{10,138},{12,140},{14,142}... | collective-permute-start | bytes 1572872 | tf_op jit(solution)/shard_map/ppermute | solution.py:56
  108.4 6.3 %collective-permute-start.20 = (bf16[8,8192]{1,0:T(8,128)(2,1)S(1)}, bf16[8,8192]{1,0:T(8,128)(2,1)S(1)}, u32[]{:S(2)}, u32[]{:S(2)}) collective-permute-start(bf16[8,8192]{1,0:T(8,128)(2,1)S(1)} %get-tuple-element.35), channel_id=1, source_target_pairs={{0,2},{2,4},{4,6},{6,8},{8,10},{10,12},{12,14},{14,0},{16,80},{18,... | collective-permute-start | bytes 393224 | tf_op jit(solution)/shard_map/ppermute | solution.py:56
  109.9 8.1 %collective-permute-start.22 = (bf16[8,8192]{1,0:T(8,128)(2,1)S(1)}, bf16[8,8192]{1,0:T(8,128)(2,1)S(1)}, u32[]{:S(2)}, u32[]{:S(2)}) collective-permute-start(bf16[8,8192]{1,0:T(8,128)(2,1)S(1)} %get-tuple-element.36), channel_id=1, source_target_pairs={{0,4},{2,6},{4,8},{6,10},{8,12},{10,14},{12,0},{14,2},{16,144},{18... | collective-permute-start | bytes 393224 | tf_op jit(solution)/shard_map/ppermute | solution.py:56
  112.3 5.7 %collective-permute-start.21 = (bf16[8,8192]{1,0:T(8,128)(2,1)S(1)}, bf16[8,8192]{1,0:T(8,128)(2,1)S(1)}, u32[]{:S(2)}, u32[]{:S(2)}) collective-permute-start(bf16[8,8192]{1,0:T(8,128)(2,1)S(1)} %get-tuple-element.37), channel_id=1, source_target_pairs={{0,14},{2,0},{4,2},{6,4},{8,6},{10,8},{12,10},{14,12},{16,208},{18... | collective-permute-start | bytes 393224 | tf_op jit(solution)/shard_map/ppermute | solution.py:56
  118.1 11.0 %collective-permute-start.25 = (f32[2,8192]{1,0:T(2,128)S(1)}, f32[2,8192]{1,0:T(2,128)S(1)}, u32[]{:S(2)}, u32[]{:S(2)}) collective-permute-start(f32[2,8192]{1,0:T(2,128)S(1)} %get-tuple-element.38), channel_id=1, source_target_pairs={{0,40},{2,42},{4,44},{6,46},{8,32},{10,34},{12,36},{14,38},{16,56}... | collective-permute-start | bytes 196616 | tf_op jit(solution)/shard_map/ppermute | solution.py:56
  123.6 8.4 %collective-permute-start.24 = (f32[2,8192]{1,0:T(2,128)S(1)}, f32[2,8192]{1,0:T(2,128)S(1)}, u32[]{:S(2)}, u32[]{:S(2)}) collective-permute-start(f32[2,8192]{1,0:T(2,128)S(1)} %get-tuple-element.39), channel_id=1, source_target_pairs={{0,8},{2,10},{4,12},{6,14},{8,0},{10,2},{12,4},{14,6},{16,24},{18,... | collective-permute-start | bytes 196616 | tf_op jit(solution)/shard_map/ppermute | solution.py:56
  124.6 7.5 %collective-permute-start.23 = (f32[2,8192]{1,0:T(2,128)S(1)}, f32[2,8192]{1,0:T(2,128)S(1)}, u32[]{:S(2)}, u32[]{:S(2)}) collective-permute-start(f32[2,8192]{1,0:T(2,128)S(1)} %get-tuple-element.40), channel_id=1, source_target_pairs={{0,32},{2,34},{4,36},{6,38},{8,40},{10,42},{12,44},{14,46},{16,48}... | collective-permute-start | bytes 196616 | tf_op jit(solution)/shard_map/ppermute | solution.py:56

commit v3 on v2

v3 whole, which is shorter than its diff:
```python
import functools

import jax
import jax.numpy as jnp
from jax import lax
from jax.experimental import pallas as pl
from jax.experimental.pallas import tpu as pltpu
from jax.sharding import Mesh
from jax.sharding import PartitionSpec as P

zloss_coef = 0.0001
NY, NX, NC, NZ = 4, 2, 2, 8
GROUP = ("y", "x", "c", "z")
OFFSETS = (0, 1, -1, 2)
BF, F32 = jnp.bfloat16, jnp.float32
ROWS, DEPTH, WIDTH = 256, 8192, 512
CHUNK = 1024
VMEM = pl.BlockSpec(memory_space=pltpu.VMEM)
SMEM = pl.BlockSpec(memory_space=pltpu.SMEM)


def index_of(y, x, c, z):
    return (((y % NY) * NX + x % NX) * NC + c % NC) * NZ + z % NZ


def pairs(route):
    every = [(y, x, c, z) for y in range(NY) for x in range(NX) for c in range(NC) for z in range(NZ)]
    return [(index_of(*p), index_of(*route(*p))) for p in every]


def to_x(y, x, c, z):
    return y, x + 1, c, z


def to_c(y, x, c, z):
    return y, x, c + 1, z


def to_z4(y, x, c, z):
    return y, x, c, z + 4


def to_xc(y, x, c, z):
    return y, x + 1, c + 1, z


def to_xz4(y, x, c, z):
    return y, x + 1, c, z + 4


def to_first(step):
    return lambda y, x, c, z: (y, x, c, z + step) if c == 0 else (y + step, x, c, z)


def to_second(step):
    return lambda y, x, c, z: (y + step, x, c, z) if c == 0 else (y, x, c, z + step)


def send(value, route):
    return lax.ppermute(value, GROUP, pairs(route))


def row_numbers():
    y, x, c, z = (lax.axis_index(a) for a in GROUP)
    at = jnp.arange(ROWS, dtype=jnp.int32)
    r, xr, z4, q1, q2, cr = at & 1, (at >> 1) & 1, (at >> 2) & 1, (at >> 3) & 3, (at >> 5) & 3, at >> 7
    o1 = jnp.where(q1 == 2, -1, jnp.where(q1 == 3, 2, q1))
    o2 = jnp.where(q2 == 2, -1, jnp.where(q2 == 3, 2, q2))
    core = c ^ cr
    zo = jnp.where(core == 0, o1, o2) + 4 * z4
    yo = jnp.where(core == 0, o2, o1)
    return ((((y + yo) & 3) * 2 + (x ^ xr)) * 2 + core) * 16 + ((z + zo) & 7) * 2 + r


def params(mib=8):
    return pltpu.CompilerParams(vmem_limit_bytes=mib << 20)


def placed(rows_ref):
    return rows_ref[...] == lax.broadcasted_iota(jnp.int32, (ROWS, ROWS), 1)


def logits_kernel(rows_ref, hit_ref, p0, p1, p2, p3, p4, p5, p6, p7, w_ref, logits_ref, stats_ref):
    pieces = (p0, p1, p2, p3, p4, p5, p6, p7)
    acc = jnp.zeros((ROWS, WIDTH), F32)
    for k in range(0, DEPTH, CHUNK):
        left = jnp.concatenate([p[:, k : k + CHUNK] for p in pieces], axis=0)
        acc += jnp.dot(left, w_ref[k : k + CHUNK, :], preferred_element_type=F32)
    logits_ref[...] = acc
    top = jnp.max(acc, axis=1, keepdims=True)
    total = jnp.sum(jnp.exp(acc - top), axis=1, keepdims=True)
    hit = lax.broadcasted_iota(jnp.int32, (ROWS, WIDTH), 1) == hit_ref[...]
    picked = jnp.sum(jnp.where(hit, acc, 0.0), axis=1, keepdims=True)
    place = placed(rows_ref)
    for i, column in enumerate((top, total, picked)):
        stats_ref[i : i + 1, :] = jnp.sum(jnp.where(place, column, 0.0), axis=0, keepdims=True)


def product(left, w_ref, out_refs):
    for k in range(0, DEPTH, CHUNK):
        part = lax.dot_general(left, w_ref[k : k + CHUNK, :], (((1,), (1,)), ((), ())), preferred_element_type=F32)
        at = 0
        for out in out_refs:
            out[:, k : k + CHUNK] = part[at : at + out.shape[0]].astype(out.dtype)
            at += out.shape[0]


def target_kernel(hit_ref, w_ref, own_ref, other_ref):
    hit = lax.broadcasted_iota(jnp.int32, (ROWS, WIDTH), 1) == hit_ref[...]
    product(jnp.where(hit, 1.0, 0.0).astype(BF), w_ref, (own_ref, other_ref))


def soft_kernel(start, rows_ref, hit_ref, merged_ref, logits_ref, w_ref, soft_ref):
    half = ROWS // 2
    cut = slice(start, start + half)
    top = jnp.sum(jnp.where(placed(rows_ref)[cut], merged_ref[0, 0:1, :], 0.0), axis=1, keepdims=True)
    hit = lax.broadcasted_iota(jnp.int32, (half, WIDTH), 1) == hit_ref[cut, :]
    product(jnp.where(hit, 0.0, jnp.exp(logits_ref[cut, :] - top)).astype(BF), w_ref, (soft_ref,))


def merge_kernel(own_ref, core_ref, x_ref, both_ref, out_ref):
    refs = (own_ref, core_ref, x_ref, both_ref)
    tops = [r[0:1, :] for r in refs]
    top = jnp.maximum(jnp.maximum(tops[0], tops[1]), jnp.maximum(tops[2], tops[3]))
    total = sum(r[1:2, :] * jnp.exp(t - top) for r, t in zip(refs, tops))
    picked = sum(r[2:3, :] for r in refs)
    merged = jnp.concatenate([top, total, picked], axis=0)
    for i in range(out_ref.shape[0]):
        out_ref[i] = merged


def scales_kernel(rows_ref, grad_ref, merged_ref, spread_ref, out_ref):
    place = placed(rows_ref)[: ROWS // 2]

    def ordered(row):
        return jnp.sum(jnp.where(place, row, 0.0), axis=1, keepdims=True)

    tops = spread_ref[:, 0, :]
    highest = jnp.max(tops, axis=0, keepdims=True)
    total = jnp.sum(spread_ref[:, 1, :] * jnp.exp(tops - highest), axis=0, keepdims=True)
    log_total = ordered(highest + jnp.log(total))
    picked = ordered(jnp.sum(spread_ref[:, 2, :], axis=0, keepdims=True))
    top = ordered(merged_ref[0, 0:1, :])
    factor = 1.0 + 2.0 * zloss_coef * log_total
    grad = grad_ref[: ROWS // 2, :]
    scale = grad * factor * jnp.exp(top - log_total)
    target = (grad * (jnp.exp(picked - log_total) * factor - 1.0)).astype(BF).astype(F32)
    lane = lax.broadcasted_iota(jnp.int32, (ROWS // 2, 128), 1)
    out_ref[...] = jnp.where(lane == 0, scale, jnp.where(lane == 1, target, jnp.where(lane == 2, log_total, picked)))


def combine_kernel(parts, scales_ref, soft_own, soft_in, target_own, target_in, *outs):
    for q, out in zip(parts, outs):
        at = slice(32 * q, 32 * q + 32)
        scale, target = scales_ref[at, 0:1], scales_ref[at, 1:2]
        for k in range(0, DEPTH, CHUNK):
            cut = slice(k, k + CHUNK)
            soft = soft_own[at, cut] + soft_in[at, cut].astype(F32)
            chosen = target_own[at, cut].astype(F32) + target_in[at, cut].astype(F32)
            out[:, cut] = (scale * soft + target * chosen).astype(out.dtype)


def shards(hidden, lm_weight, targets, loss_grad):
    position = lax.axis_index(GROUP)
    half = ROWS // 2

    rows = row_numbers()[:, None]
    place = rows == jnp.arange(ROWS, dtype=jnp.int32)[None, :]
    own_hit = jnp.sum(jnp.where(place, targets[None, :], 0), axis=1, keepdims=True) - position * WIDTH
    own_grad = jnp.sum(jnp.where(place, loss_grad[None, :], 0.0), axis=1, keepdims=True)

    block = jnp.concatenate([hidden] + [send(hidden, to) for to in (to_x, to_z4, to_xz4)])
    block = jnp.concatenate([block] + [send(block, to_first(-o)) for o in OFFSETS[1:]])
    pieces = [block] + [send(block, to_second(-o)) for o in OFFSETS[1:]]
    pieces = pieces + [send(p, to_c) for p in pieces]

    hit, block = lax.optimization_barrier((own_hit, block))
    target_own, target_out = pl.pallas_call(
        target_kernel,
        out_shape=[jax.ShapeDtypeStruct((half, DEPTH), BF)] * 2,
        in_specs=[VMEM] * 2,
        out_specs=[VMEM] * 2,
        compiler_params=params(),
        cost_estimate=pl.CostEstimate(flops=2 * ROWS * DEPTH * WIDTH, bytes_accessed=12 << 20, transcendentals=0),
        name="target",
    )(hit, lm_weight)
    target_in = send(target_out, to_c)
    pieces[0], target_own = lax.optimization_barrier((pieces[0], target_own))

    logits, stats = pl.pallas_call(
        logits_kernel,
        out_shape=(jax.ShapeDtypeStruct((ROWS, WIDTH), F32), jax.ShapeDtypeStruct((3, ROWS), F32)),
        in_specs=[VMEM] * 11,
        out_specs=(VMEM, VMEM),
        compiler_params=params(),
        cost_estimate=pl.CostEstimate(flops=2 * ROWS * DEPTH * WIDTH, bytes_accessed=13 << 20, transcendentals=ROWS * WIDTH),
        name="logits",
    )(rows, own_hit, *pieces, lm_weight)
    stats = [stats] + [send(stats, to) for to in (to_c, to_x, to_xc)]

    merged = pl.pallas_call(
        merge_kernel,
        out_shape=jax.ShapeDtypeStruct((32, 3, ROWS), F32),
        in_specs=[VMEM] * 4,
        out_specs=VMEM,
        compiler_params=params(),
        name="merge",
    )(*stats)

    def soft(start, dtype):
        return pl.pallas_call(
            functools.partial(soft_kernel, start),
            out_shape=jax.ShapeDtypeStruct((half, DEPTH), dtype),
            in_specs=[VMEM] * 5,
            out_specs=VMEM,
            compiler_params=params(),
            cost_estimate=pl.CostEstimate(flops=ROWS * DEPTH * WIDTH, bytes_accessed=10 << 20, transcendentals=half * WIDTH),
            name="soft",
        )(rows, own_hit, merged, logits, lm_weight)

    spread = lax.all_to_all(merged, ("y", "z"), 0, 0)
    soft_in = send(soft(half, BF), to_c)
    soft_own = soft(0, F32)
    scales = pl.pallas_call(
        scales_kernel,
        out_shape=jax.ShapeDtypeStruct((half, 128), F32),
        in_specs=[VMEM] * 4,
        out_specs=VMEM,
        compiler_params=params(),
        name="scales",
    )(rows, own_grad, merged, spread)

    def combine(parts, dtype):
        return pl.pallas_call(
            functools.partial(combine_kernel, parts),
            out_shape=[jax.ShapeDtypeStruct((32, DEPTH), dtype)] * len(parts),
            in_specs=[VMEM] * 5,
            out_specs=[VMEM] * len(parts),
            compiler_params=params(),
            cost_estimate=pl.CostEstimate(flops=6 * 32 * DEPTH, bytes_accessed=2 << 20, transcendentals=0),
            name="combine",
        )(scales, soft_own, soft_in, target_own, target_in)

    pieces = [None, None, None, combine((3,), BF)[0]]
    pieces[1], pieces[2] = combine((1, 2), BF)
    pieces[0] = combine((0,), F32)[0]
    log_total, target_logit = scales[:2, 2], scales[:2, 3]
    ce_loss = log_total - target_logit
    z_term = zloss_coef * log_total * log_total

    part = pieces[0] + sum(send(pieces[k], to_second(OFFSETS[k])).astype(F32) for k in (1, 2, 3))
    part = part.reshape(4, 8, DEPTH)
    part = part[0] + sum(send(part[k].astype(BF), to_first(OFFSETS[k])).astype(F32) for k in (1, 2, 3))
    part = [part[0:2]] + [
        send(part[2 * k : 2 * k + 2].astype(BF), to).astype(F32) for k, to in ((1, to_x), (2, to_z4), (3, to_xz4))
    ]
    part = (part[0] + part[1]) + (part[2] + part[3])
    return ce_loss, z_term, part.astype(BF)


def solution(mesh):
    mesh = Mesh(mesh.devices.reshape(NY, NX, NC, NZ, 2), (*GROUP, "dp"))
    own = ("dp", *GROUP)
    in_specs = (P(own, None), P(None, GROUP), P("dp"), P("dp"))
    out_specs = (P(own), P(own), P(own, None))
    return jax.shard_map(shards, mesh=mesh, in_specs=in_specs, out_specs=out_specs, check_vma=False)
```

time: 133 us -> 140 us (1.053); the launches traced: 133 us -> 138 us
  Pallas kernels: 17.7 us -> 27.3 us
  starting transfers between devices: 50.2 us -> 41.3 us
  waiting for transfers between devices: 45.6 us -> 52.6 us
  local copies, waits for them, and re-layouts: 14.5 us -> 12.6 us
    pallas_call x3 -> x8, Pallas kernels: 13.6 us -> 22.7 us  [the longest x2 9.06 us: soft(): pl.pallas_call(functools.partial(soft_kernel, start), out_shape=jax.Shape...]
    ppermute x26 -> x27, starting transfers between devices: 42.4 us -> 35.1 us  [send(): return lax.ppermute(value, GROUP, pairs(route))]
    ppermute x26 -> x27, waiting for transfers between devices: 44.4 us -> 51.3 us  [send(): return lax.ppermute(value, GROUP, pairs(route))]
    all_to_all x1, starting transfers between devices: 7.82 us -> 6.2 us  [shards(): spread = lax.all_to_all(merged, ('y', 'z'), 0, 0)]
    unnamed x18 -> x12, local copies, waits for them, and re-layouts: 12.3 us -> 10.9 us
  transfers between devices with their start and end apart: 27 -> 28, of which waited for: 17 -> 17; matrix products, arithmetic and copies ran while one was open for 2% -> 2% of each run, Pallas kernels for 4% -> 14%
where the time goes in v3:
time: 140 us; the launch traced here: 138 us
  waiting for transfers between devices  52.6 us (38%)
  starting transfers between devices  41.3 us (30%)
  Pallas kernels  27.3 us (20%)
  local copies, waits for them, and re-layouts  12.6 us (9%)
  other arithmetic  3.63 us (3%)
    ppermute x27, waiting for transfers between devices, send(): return lax.ppermute(value, GROUP, pairs(route))  51.3 us
    ppermute x27, starting transfers between devices, send(): return lax.ppermute(value, GROUP, pairs(route))  35.1 us
    unnamed x12, local copies, waits for them, and re-layouts  10.9 us
    pallas_call x2, Pallas kernels, soft(): pl.pallas_call(functools.partial(soft_kernel, start), out_shape=jax.Shape...  9.06 us
    pallas_call x3, Pallas kernels, combine(): pl.pallas_call(functools.partial(combine_kernel, parts), out_shape=[jax.S...  8 us
    all_to_all x1, starting transfers between devices, shards(): spread = lax.all_to_all(merged, ('y', 'z'), 0, 0)  6.2 us
    pallas_call x1, Pallas kernels, shards(): pl.pallas_call(logits_kernel, out_shape=(jax.ShapeDtypeStruct((ROWS, WIDT...  4.61 us
    pallas_call x1, Pallas kernels, shards(): pl.pallas_call(target_kernel, out_shape=[jax.ShapeDtypeStruct((half, DEPT...  3.76 us
  transfers between devices with their start and end apart: 28, of which 17 were waited for; matrix products, arithmetic and copies ran while one was open for 2% of the time, Pallas kernels for 14%

profile of v3, /device:TPU:4, one launch (start us, length us, event | category | flops | bytes accessed | tf_op | source)
XLA Modules:
  0.0 138.3 jit_solution(1943963179872756713)
XLA Ops:
  0.6 1.3 collective-permute-start
  1.9 7.2 %collective-permute-start.1 = (bf16[2,8192]{1,0:T(2,128)(2,1)}, bf16[2,8192]{1,0:T(2,128)(2,1)S(1)}, u32[]{:S(2)}, u32[]{:S(2)}) collective-permute-start(bf16[2,8192]{1,0:T(2,128)(2,1)} %param.4), channel_id=1, source_target_pairs={{0,8},{2,10},{4,12},{6,14},{8,0},{10,2},{12,4},{14,6},{16,24},{18,... | collective-permute-start | bytes 98312 | tf_op jit(solution)/shard_map/ppermute | solution.py:60
  9.1 0.3 collective-permute-start.2
  9.4 1.9 %collective-permute-done.1 = bf16[2,8192]{1,0:T(2,128)(2,1)S(1)} collective-permute-done((bf16[2,8192]{1,0:T(2,128)(2,1)}, bf16[2,8192]{1,0:T(2,128)(2,1)S(1)}, u32[]{:S(2)}, u32[]{:S(2)}) %collective-permute-start.1) | collective-permute-done | bytes 32800 | tf_op jit(solution)/shard_map/ppermute | solution.py:60
  11.2 6.8 %collective-permute-done.2 = bf16[2,8192]{1,0:T(2,128)(2,1)S(1)} collective-permute-done((bf16[2,8192]{1,0:T(2,128)(2,1)}, bf16[2,8192]{1,0:T(2,128)(2,1)S(1)}, u32[]{:S(2)}, u32[]{:S(2)}) %collective-permute-start.2) | collective-permute-done | bytes 32800 | tf_op jit(solution)/shard_map/ppermute | solution.py:60
  18.0 0.9 pad_maximum_fusion
  18.9 0.2 collective-permute-start.3
  19.1 1.9 %collective-permute-start.4 = (bf16[8,8192]{1,0:T(8,128)(2,1)S(1)}, bf16[8,8192]{1,0:T(8,128)(2,1)S(1)}, u32[]{:S(2)}, u32[]{:S(2)}) collective-permute-start(bf16[8,8192]{1,0:T(8,128)(2,1)S(1)} %pad_maximum_fusion), channel_id=1, source_target_pairs={{0,2},{2,4},{4,6},{6,8},{8,10},{10,12},{12,14},{14,0},{16,80},{18,... | collective-permute-start | bytes 393224 | tf_op jit(solution)/shard_map/ppermute | solution.py:60
  21.1 2.9 %collective-permute-done.3 = bf16[8,8192]{1,0:T(8,128)(2,1)S(1)} collective-permute-done((bf16[8,8192]{1,0:T(8,128)(2,1)S(1)}, bf16[8,8192]{1,0:T(8,128)(2,1)S(1)}, u32[]{:S(2)}, u32[]{:S(2)}) %collective-permute-start.3) | collective-permute-done | bytes 131104 | tf_op jit(solution)/shard_map/ppermute | solution.py:60
  24.0 1.3 collective-permute-done.4
  25.3 3.0 %collective-permute-done.5 = bf16[8,8192]{1,0:T(8,128)(2,1)S(1)} collective-permute-done((bf16[8,8192]{1,0:T(8,128)(2,1)S(1)}, bf16[8,8192]{1,0:T(8,128)(2,1)S(1)}, u32[]{:S(2)}, u32[]{:S(2)}) %collective-permute-start.5) | collective-permute-done | bytes 131104 | tf_op jit(solution)/shard_map/ppermute | solution.py:60
  28.3 1.0 concatenate.8.p0
  29.3 3.1 %collective-permute-start.6 = (bf16[32,8192]{1,0:T(8,128)(2,1)S(1)}, bf16[32,8192]{1,0:T(8,128)(2,1)}, u32[]{:S(2)}, u32[]{:S(2)}) collective-permute-start(bf16[32,8192]{1,0:T(8,128)(2,1)S(1)} %concatenate.8.p0), channel_id=1, source_target_pairs={{0,192},{2,194},{4,196},{6,198},{8,200},{10,202},{12,204},{14,206}... | collective-permute-start | bytes 1572872 | tf_op jit(solution)/shard_map/ppermute | solution.py:60
  32.4 2.4 %collective-permute-start.8 = (bf16[32,8192]{1,0:T(8,128)(2,1)S(1)}, bf16[32,8192]{1,0:T(8,128)(2,1)}, u32[]{:S(2)}, u32[]{:S(2)}) collective-permute-start(bf16[32,8192]{1,0:T(8,128)(2,1)S(1)} %concatenate.8.p0), channel_id=1, source_target_pairs={{0,128},{2,130},{4,132},{6,134},{8,136},{10,138},{12,140},{14,142}... | collective-permute-start | bytes 1572872 | tf_op jit(solution)/shard_map/ppermute | solution.py:60
  34.8 0.9 select_reduce_fusion
  35.8 8.9 %collective-permute-done.6.p1 = bf16[32,8192]{1,0:T(8,128)(2,1)} collective-permute-done((bf16[32,8192]{1,0:T(8,128)(2,1)S(1)}, bf16[32,8192]{1,0:T(8,128)(2,1)}, u32[]{:S(2)}, u32[]{:S(2)}) %collective-permute-start.6) | collective-permute-done | bytes 524320 | tf_op jit(solution)/shard_map/ppermute | solution.py:60
  44.7 3.8 %collective-permute-done.7.p2 = bf16[32,8192]{1,0:T(8,128)(2,1)} collective-permute-done((bf16[32,8192]{1,0:T(8,128)(2,1)S(1)}, bf16[32,8192]{1,0:T(8,128)(2,1)}, u32[]{:S(2)}, u32[]{:S(2)}) %collective-permute-start.7) | collective-permute-done | bytes 524320 | tf_op jit(solution)/shard_map/ppermute | solution.py:60
  48.5 0.5 collective-permute-start.12
  49.0 0.1 copy.19.hit_ref
  49.2 0.2 and_add_fusion.rows_ref
  49.3 0.1 copy.18.hit_ref
  49.5 3.4 %copy-done = bf16[8192,512]{1,0:T(8,128)(2,1)S(1)} copy-done((bf16[8192,512]{1,0:T(8,128)(2,1)S(1)}, bf16[8192,512]{1,0:T(8,128)(2,1)}, u32[]{:S(2)}) %copy-start) | copy-done | bytes 8388632
  52.9 3.8 %target.1 = (bf16[128,8192]{1,0:T(8,128)(2,1)S(1)}, bf16[128,8192]{1,0:T(8,128)(2,1)}) custom-call(s32[256,1]{1,0:T(8,128)S(1)} %copy.18.hit_ref, bf16[8192,512]{1,0:T(8,128)(2,1)S(1)} %copy-done), custom_call_target="tpu_custom_call" | custom-call | flops 2147483648 | bytes 12582912 | tf_op jit(solution)/shard_map/target/pallas_call | solution.py:178
  56.7 4.6 %logits.1 = (f32[256,512]{1,0:T(8,128)S(1)}, f32[3,256]{1,0:T(4,128)S(1)}) custom-call(s32[256,1]{1,0:T(8,128)S(1)} %and_add_fusion.rows_ref, s32[256,1]{1,0:T(8,128)S(1)} %copy.19.hit_ref, bf16[32,8192]{1,0:T(8,128)(2,1)S(1)} %concatenate.8.p0, bf16[32,8192]{1,0:T(8,128)(2,1)} %collective-permute-done.6.p1, bf16[32,8192]{1,0:T(8,128)(2,1)} %collective-permute-done.7.p2, ...), custom_call_target="tpu_custom_call" | custom-call | flops 2147483648 | bytes 13631488 | tf_op jit(solution)/shard_map/logits/pallas_call | solution.py:190
  61.4 1.1 collective-permute-start.14
  62.4 0.8 collective-permute-start.15
  63.3 0.4 collective-permute-start.17
  63.6 1.5 %collective-permute-done.14.x_ref = f32[3,256]{1,0:T(4,128)S(1)} collective-permute-done((f32[3,256]{1,0:T(4,128)S(1)}, f32[3,256]{1,0:T(4,128)S(1)}, u32[]{:S(2)}, u32[]{:S(2)}) %collective-permute-start.14) | collective-permute-done | bytes 3104 | tf_op jit(solution)/shard_map/ppermute | solution.py:60
  65.1 0.4 collective-permute-done.15.both_ref
  65.5 0.7 merge.1.merged_ref
  66.2 5.2 %soft.3 = bf16[128,8192]{1,0:T(8,128)(2,1)} custom-call(s32[256,1]{1,0:T(8,128)S(1)} %and_add_fusion.rows_ref, s32[256,1]{1,0:T(8,128)S(1)} %copy.19.hit_ref, f32[32,3,256]{2,1,0:T(4,128)} %merge.1.merged_ref, f32[256,512]{1,0:T(8,128)S(1)} %get-tuple-element.16.logits_ref, bf16[8192,512]{1,0:T(8,128)(2,1)S(1)} %copy-done.1), custom_call_target="tpu_custom_call" | custom-call | flops 1073741824 | bytes 10485760 | tf_op jit(solution)/shard_map/soft/pallas_call | solution.py:211
  71.4 0.1 collective-permute-start.16
  71.5 6.2 %all-to-all-start = ((f32[32,3,256]{2,1,0:T(4,128)}), f32[32,3,256]{2,1,0:T(4,128)S(1)}, u32[]{:S(2)}, u32[]{:S(2)}) async-start(f32[32,3,256]{2,1,0:T(4,128)} %merge.1.merged_ref), calls=%async_computation | async-start | bytes 262144 | tf_op jit(solution)/shard_map/all_to_all | solution.py:221
  77.8 0.2 select_reduce_fusion.1
  77.9 0.1 copy.20.grad_ref
  78.1 3.4 %copy-done.2 = bf16[8192,512]{1,0:T(8,128)(2,1)S(1)} copy-done((bf16[8192,512]{1,0:T(8,128)(2,1)S(1)}, bf16[8192,512]{1,0:T(8,128)(2,1)}, u32[]{:S(2)}) %copy-start.2) | copy-done | bytes 8388632
  81.5 3.8 %soft.2.soft_own = f32[128,8192]{1,0:T(8,128)S(1)} custom-call(s32[256,1]{1,0:T(8,128)S(1)} %and_add_fusion.rows_ref, s32[256,1]{1,0:T(8,128)S(1)} %copy.19.hit_ref, f32[32,3,256]{2,1,0:T(4,128)} %merge.1.merged_ref, f32[256,512]{1,0:T(8,128)S(1)} %get-tuple-element.16.logits_ref, bf16[8192,512]{1,0:T(8,128)(2,1)S(1)} %copy-done.2), custom_call_target="tpu_custom_call" | custom-call | flops 1073741824 | bytes 10485760 | tf_op jit(solution)/shard_map/soft/pallas_call | solution.py:211
  85.3 2.0 %copy-done.3 = f32[128,8192]{1,0:T(8,128)} copy-done((f32[128,8192]{1,0:T(8,128)}, f32[128,8192]{1,0:T(8,128)S(1)}, u32[]{:S(2)}) %copy-start.3) | copy-done | bytes 4194328
  87.3 1.3 all-to-all-done.spread_ref
  88.6 1.2 scales.1.scales_ref
  89.8 2.2 %copy-done.4 = f32[128,8192]{1,0:T(8,128)S(1)} copy-done((f32[128,8192]{1,0:T(8,128)S(1)}, f32[128,8192]{1,0:T(8,128)}, u32[]{:S(2)}) %copy-start.4) | copy-done | bytes 4194328
  92.0 2.9 %combine.4 = (bf16[32,8192]{1,0:T(8,128)(2,1)S(1)}, bf16[32,8192]{1,0:T(8,128)(2,1)S(1)}) custom-call(f32[128,128]{1,0:T(8,128)S(1)} %scales.1.scales_ref, f32[128,8192]{1,0:T(8,128)S(1)} %copy-done.4, bf16[128,8192]{1,0:T(8,128)(2,1)} %collective-permute-done.16.soft_in, bf16[128,8192]{1,0:T(8,128)(2,1)S(1)} %get-tuple-element.17.target_own, ...), custom_call_target="tpu_custom_call" | custom-call | flops 1572864 | bytes 2097152 | tf_op jit(solution)/shard_map/combine/pallas_call | solution.py:234
  94.9 0.7 collective-permute-start.18
  95.5 2.6 %collective-permute-start.19 = (bf16[32,8192]{1,0:T(8,128)(2,1)S(1)}, bf16[32,8192]{1,0:T(8,128)(2,1)S(1)}, u32[]{:S(2)}, u32[]{:S(2)}) collective-permute-start(bf16[32,8192]{1,0:T(8,128)(2,1)S(1)} %get-tuple-element.20), channel_id=1, source_target_pairs={{0,192},{2,194},{4,196},{6,198},{8,200},{10,202},{12,204},{14,206}... | collective-permute-start | bytes 1572872 | tf_op jit(solution)/shard_map/ppermute | solution.py:60
  98.2 2.6 %combine.5 = bf16[32,8192]{1,0:T(8,128)(2,1)S(1)} custom-call(f32[128,128]{1,0:T(8,128)S(1)} %scales.1.scales_ref, f32[128,8192]{1,0:T(8,128)S(1)} %copy-done.4, bf16[128,8192]{1,0:T(8,128)(2,1)} %collective-permute-done.16.soft_in, bf16[128,8192]{1,0:T(8,128)(2,1)S(1)} %get-tuple-element.17.target_own, bf16[128,8192]{1,0:T(8,128)(2,1)} %collective-permute-done.17.target_in), custom_call_target="tpu_custom_call" | custom-call | flops 1572864 | bytes 2097152 | tf_op jit(solution)/shard_map/combine/pallas_call | solution.py:234
  100.7 0.9 collective-permute-start.20
  101.6 2.6 %combine.3 = f32[32,8192]{1,0:T(8,128)S(1)} custom-call(f32[128,128]{1,0:T(8,128)S(1)} %scales.1.scales_ref, f32[128,8192]{1,0:T(8,128)S(1)} %copy-done.4, bf16[128,8192]{1,0:T(8,128)(2,1)} %collective-permute-done.16.soft_in, bf16[128,8192]{1,0:T(8,128)(2,1)S(1)} %get-tuple-element.17.target_own, bf16[128,8192]{1,0:T(8,128)(2,1)} %collective-permute-done.17.target_in), custom_call_target="tpu_custom_call" | custom-call | flops 1572864 | bytes 2097152 | tf_op jit(solution)/shard_map/combine/pallas_call | solution.py:234
  104.2 1.1 collective-permute-done.18
  105.3 5.2 %collective-permute-done.19 = bf16[32,8192]{1,0:T(8,128)(2,1)S(1)} collective-permute-done((bf16[32,8192]{1,0:T(8,128)(2,1)S(1)}, bf16[32,8192]{1,0:T(8,128)(2,1)S(1)}, u32[]{:S(2)}, u32[]{:S(2)}) %collective-permute-start.19) | collective-permute-done | bytes 524320 | tf_op jit(solution)/shard_map/ppermute | solution.py:60
  110.5 1.0 collective-permute-done.20
  111.5 0.2 fusion.7
  111.8 1.3 collective-permute-start.21
  113.0 2.0 %collective-permute-start.22 = (bf16[8,8192]{1,0:T(8,128)(2,1)S(1)}, bf16[8,8192]{1,0:T(8,128)(2,1)S(1)}, u32[]{:S(2)}, u32[]{:S(2)}) collective-permute-start(bf16[8,8192]{1,0:T(8,128)(2,1)S(1)} %get-tuple-element.29), channel_id=1, source_target_pairs={{0,14},{2,0},{4,2},{6,4},{8,6},{10,8},{12,10},{14,12},{16,208},{18... | collective-permute-start | bytes 393224 | tf_op jit(solution)/shard_map/ppermute | solution.py:60
  115.1 0.6 collective-permute-start.23
  115.7 0.2 slice_reduce_fusion
  115.9 2.1 %collective-permute-done.21 = bf16[8,8192]{1,0:T(8,128)(2,1)S(1)} collective-permute-done((bf16[8,8192]{1,0:T(8,128)(2,1)S(1)}, bf16[8,8192]{1,0:T(8,128)(2,1)S(1)}, u32[]{:S(2)}, u32[]{:S(2)}) %collective-permute-start.21) | collective-permute-done | bytes 131104 | tf_op jit(solution)/shard_map/ppermute | solution.py:60
  118.0 4.7 %collective-permute-done.23 = bf16[8,8192]{1,0:T(8,128)(2,1)S(1)} collective-permute-done((bf16[8,8192]{1,0:T(8,128)(2,1)S(1)}, bf16[8,8192]{1,0:T(8,128)(2,1)S(1)}, u32[]{:S(2)}, u32[]{:S(2)}) %collective-permute-start.23) | collective-permute-done | bytes 131104 | tf_op jit(solution)/shard_map/ppermute | solution.py:60
  122.9 1.1 collective-permute-start.24
  124.0 4.6 %collective-permute-start.25 = (bf16[2,8192]{1,0:T(2,128)(2,1)S(1)}, bf16[2,8192]{1,0:T(2,128)(2,1)S(1)}, u32[]{:S(2)}, u32[]{:S(2)}) collective-permute-start(bf16[2,8192]{1,0:T(2,128)(2,1)S(1)} %get-tuple-element.32), channel_id=1, source_target_pairs={{0,8},{2,10},{4,12},{6,14},{8,0},{10,2},{12,4},{14,6},{16,24},{18,... | collective-permute-start | bytes 98312 | tf_op jit(solution)/shard_map/ppermute | solution.py:60
  128.7 1.7 %collective-permute-start.26 = (bf16[2,8192]{1,0:T(2,128)(2,1)S(1)}, bf16[2,8192]{1,0:T(2,128)(2,1)S(1)}, u32[]{:S(2)}, u32[]{:S(2)}) collective-permute-start(bf16[2,8192]{1,0:T(2,128)(2,1)S(1)} %get-tuple-element.31), channel_id=1, source_target_pairs={{0,40},{2,42},{4,44},{6,46},{8,32},{10,34},{12,36},{14,38},{16,56}... | collective-permute-start | bytes 98312 | tf_op jit(solution)/shard_map/ppermute | solution.py:60
  130.4 0.5 multiply_multiply_fusion
  130.9 1.3 collective-permute-done.25
  132.2 5.4 %collective-permute-done.26 = bf16[2,8192]{1,0:T(2,128)(2,1)S(1)} collective-permute-done((bf16[2,8192]{1,0:T(2,128)(2,1)S(1)}, bf16[2,8192]{1,0:T(2,128)(2,1)S(1)}, u32[]{:S(2)}, u32[]{:S(2)}) %collective-permute-start.26) | collective-permute-done | bytes 32800 | tf_op jit(solution)/shard_map/ppermute | solution.py:60
  137.6 0.7 fusion.5
  (30 shorter events, 0.5 us)
Async XLA Ops:
  0.6 8.7 %collective-permute-start = (bf16[2,8192]{1,0:T(2,128)(2,1)}, bf16[2,8192]{1,0:T(2,128)(2,1)S(1)}, u32[]{:S(2)}, u32[]{:S(2)}) collective-permute-start(bf16[2,8192]{1,0:T(2,128)(2,1)} %param.4), channel_id=1, source_target_pairs={{0,32},{2,34},{4,36},{6,38},{8,40},{10,42},{12,44},{14,46},{16,48}... | collective-permute-start | bytes 98312 | tf_op jit(solution)/shard_map/ppermute | solution.py:60
  1.9 9.3 %collective-permute-start.1 = (bf16[2,8192]{1,0:T(2,128)(2,1)}, bf16[2,8192]{1,0:T(2,128)(2,1)S(1)}, u32[]{:S(2)}, u32[]{:S(2)}) collective-permute-start(bf16[2,8192]{1,0:T(2,128)(2,1)} %param.4), channel_id=1, source_target_pairs={{0,8},{2,10},{4,12},{6,14},{8,0},{10,2},{12,4},{14,6},{16,24},{18,... | collective-permute-start | bytes 98312 | tf_op jit(solution)/shard_map/ppermute | solution.py:60
  9.1 8.9 %collective-permute-start.2 = (bf16[2,8192]{1,0:T(2,128)(2,1)}, bf16[2,8192]{1,0:T(2,128)(2,1)S(1)}, u32[]{:S(2)}, u32[]{:S(2)}) collective-permute-start(bf16[2,8192]{1,0:T(2,128)(2,1)} %param.4), channel_id=1, source_target_pairs={{0,40},{2,42},{4,44},{6,46},{8,32},{10,34},{12,36},{14,38},{16,56}... | collective-permute-start | bytes 98312 | tf_op jit(solution)/shard_map/ppermute | solution.py:60
  18.9 5.0 %collective-permute-start.3 = (bf16[8,8192]{1,0:T(8,128)(2,1)S(1)}, bf16[8,8192]{1,0:T(8,128)(2,1)S(1)}, u32[]{:S(2)}, u32[]{:S(2)}) collective-permute-start(bf16[8,8192]{1,0:T(8,128)(2,1)S(1)} %pad_maximum_fusion), channel_id=1, source_target_pairs={{0,14},{2,0},{4,2},{6,4},{8,6},{10,8},{12,10},{14,12},{16,208},{18... | collective-permute-start | bytes 393224 | tf_op jit(solution)/shard_map/ppermute | solution.py:60
  19.1 6.2 %collective-permute-start.4 = (bf16[8,8192]{1,0:T(8,128)(2,1)S(1)}, bf16[8,8192]{1,0:T(8,128)(2,1)S(1)}, u32[]{:S(2)}, u32[]{:S(2)}) collective-permute-start(bf16[8,8192]{1,0:T(8,128)(2,1)S(1)} %pad_maximum_fusion), channel_id=1, source_target_pairs={{0,2},{2,4},{4,6},{6,8},{8,10},{10,12},{12,14},{14,0},{16,80},{18,... | collective-permute-start | bytes 393224 | tf_op jit(solution)/shard_map/ppermute | solution.py:60
  21.1 7.3 %collective-permute-start.5 = (bf16[8,8192]{1,0:T(8,128)(2,1)S(1)}, bf16[8,8192]{1,0:T(8,128)(2,1)S(1)}, u32[]{:S(2)}, u32[]{:S(2)}) collective-permute-start(bf16[8,8192]{1,0:T(8,128)(2,1)S(1)} %pad_maximum_fusion), channel_id=1, source_target_pairs={{0,12},{2,14},{4,0},{6,2},{8,4},{10,6},{12,8},{14,10},{16,144},{18... | collective-permute-start | bytes 393224 | tf_op jit(solution)/shard_map/ppermute | solution.py:60
  29.3 15.4 %collective-permute-start.6 = (bf16[32,8192]{1,0:T(8,128)(2,1)S(1)}, bf16[32,8192]{1,0:T(8,128)(2,1)}, u32[]{:S(2)}, u32[]{:S(2)}) collective-permute-start(bf16[32,8192]{1,0:T(8,128)(2,1)S(1)} %concatenate.8.p0), channel_id=1, source_target_pairs={{0,192},{2,194},{4,196},{6,198},{8,200},{10,202},{12,204},{14,206}... | collective-permute-start | bytes 1572872 | tf_op jit(solution)/shard_map/ppermute | solution.py:60
  32.4 16.1 %collective-permute-start.7 = (bf16[32,8192]{1,0:T(8,128)(2,1)S(1)}, bf16[32,8192]{1,0:T(8,128)(2,1)}, u32[]{:S(2)}, u32[]{:S(2)}) collective-permute-start(bf16[32,8192]{1,0:T(8,128)(2,1)S(1)} %concatenate.8.p0), channel_id=1, source_target_pairs={{0,64},{2,66},{4,68},{6,70},{8,72},{10,74},{12,76},{14,78},{16,18}... | collective-permute-start | bytes 1572872 | tf_op jit(solution)/shard_map/ppermute | solution.py:60
  32.4 16.1 %collective-permute-start.8 = (bf16[32,8192]{1,0:T(8,128)(2,1)S(1)}, bf16[32,8192]{1,0:T(8,128)(2,1)}, u32[]{:S(2)}, u32[]{:S(2)}) collective-permute-start(bf16[32,8192]{1,0:T(8,128)(2,1)S(1)} %concatenate.8.p0), channel_id=1, source_target_pairs={{0,128},{2,130},{4,132},{6,134},{8,136},{10,138},{12,140},{14,142}... | collective-permute-start | bytes 1572872 | tf_op jit(solution)/shard_map/ppermute | solution.py:60
  35.7 21.0 %collective-permute-start.9 = (bf16[32,8192]{1,0:T(8,128)(2,1)S(1)}, bf16[32,8192]{1,0:T(8,128)(2,1)}, u32[]{:S(2)}, u32[]{:S(2)}) collective-permute-start(bf16[32,8192]{1,0:T(8,128)(2,1)S(1)} %concatenate.8.p0), channel_id=1, source_target_pairs={{0,16},{2,18},{4,20},{6,22},{8,24},{10,26},{12,28},{14,30},{16,0},... | collective-permute-start | bytes 1572872 | tf_op jit(solution)/shard_map/ppermute | solution.py:60
  44.7 11.9 %collective-permute-start.10 = (bf16[32,8192]{1,0:T(8,128)(2,1)}, bf16[32,8192]{1,0:T(8,128)(2,1)}, u32[]{:S(2)}, u32[]{:S(2)}) collective-permute-start(bf16[32,8192]{1,0:T(8,128)(2,1)} %collective-permute-done.6.p1), channel_id=1, source_target_pairs={{0,16},{2,18},{4,20},{6,22},{8,24},{10,26},{12,28},{14,30},{16,0},... | collective-permute-start | bytes 1572872 | tf_op jit(solution)/shard_map/ppermute | solution.py:60
  48.5 8.1 %collective-permute-start.11 = (bf16[32,8192]{1,0:T(8,128)(2,1)}, bf16[32,8192]{1,0:T(8,128)(2,1)}, u32[]{:S(2)}, u32[]{:S(2)}) collective-permute-start(bf16[32,8192]{1,0:T(8,128)(2,1)} %collective-permute-done.7.p2), channel_id=1, source_target_pairs={{0,16},{2,18},{4,20},{6,22},{8,24},{10,26},{12,28},{14,30},{16,0},... | collective-permute-start | bytes 1572872 | tf_op jit(solution)/shard_map/ppermute | solution.py:60
  48.5 8.1 %collective-permute-start.12 = (bf16[32,8192]{1,0:T(8,128)(2,1)}, bf16[32,8192]{1,0:T(8,128)(2,1)}, u32[]{:S(2)}, u32[]{:S(2)}) collective-permute-start(bf16[32,8192]{1,0:T(8,128)(2,1)} %collective-permute-done.8.p3), channel_id=1, source_target_pairs={{0,16},{2,18},{4,20},{6,22},{8,24},{10,26},{12,28},{14,30},{16,0},... | collective-permute-start | bytes 1572872 | tf_op jit(solution)/shard_map/ppermute | solution.py:60
  49.5 3.4 %copy-start = (bf16[8192,512]{1,0:T(8,128)(2,1)S(1)}, bf16[8192,512]{1,0:T(8,128)(2,1)}, u32[]{:S(2)}) copy-start(bf16[8192,512]{1,0:T(8,128)(2,1)} %w_ref.7) | copy-start | bytes 25165828
  52.9 3.8 %copy-start.1 = (bf16[8192,512]{1,0:T(8,128)(2,1)S(1)}, bf16[8192,512]{1,0:T(8,128)(2,1)}, u32[]{:S(2)}) copy-start(bf16[8192,512]{1,0:T(8,128)(2,1)} %w_ref.7) | copy-start | bytes 25165828
  61.3 2.3 %collective-permute-start.13 = (f32[3,256]{1,0:T(4,128)S(1)}, f32[3,256]{1,0:T(4,128)S(1)}, u32[]{:S(2)}, u32[]{:S(2)}) collective-permute-start(f32[3,256]{1,0:T(4,128)S(1)} %get-tuple-element.15.own_ref), channel_id=1, source_target_pairs={{0,16},{2,18},{4,20},{6,22},{8,24},{10,26},{12,28},{14,30},{16,0},... | collective-permute-start | bytes 9224 | tf_op jit(solution)/shard_map/ppermute | solution.py:60
  61.4 3.7 %collective-permute-start.14 = (f32[3,256]{1,0:T(4,128)S(1)}, f32[3,256]{1,0:T(4,128)S(1)}, u32[]{:S(2)}, u32[]{:S(2)}) collective-permute-start(f32[3,256]{1,0:T(4,128)S(1)} %get-tuple-element.15.own_ref), channel_id=1, source_target_pairs={{0,32},{2,34},{4,36},{6,38},{8,40},{10,42},{12,44},{14,46},{16,48}... | collective-permute-start | bytes 9224 | tf_op jit(solution)/shard_map/ppermute | solution.py:60
  62.4 3.0 %collective-permute-start.15 = (f32[3,256]{1,0:T(4,128)S(1)}, f32[3,256]{1,0:T(4,128)S(1)}, u32[]{:S(2)}, u32[]{:S(2)}) collective-permute-start(f32[3,256]{1,0:T(4,128)S(1)} %get-tuple-element.15.own_ref), channel_id=1, source_target_pairs={{0,48},{2,50},{4,52},{6,54},{8,56},{10,58},{12,60},{14,62},{16,32}... | collective-permute-start | bytes 9224 | tf_op jit(solution)/shard_map/ppermute | solution.py:60
  63.3 26.5 %collective-permute-start.17 = (bf16[128,8192]{1,0:T(8,128)(2,1)}, bf16[128,8192]{1,0:T(8,128)(2,1)}, u32[]{:S(2)}, u32[]{:S(2)}) collective-permute-start(bf16[128,8192]{1,0:T(8,128)(2,1)} %get-tuple-element.18), channel_id=1, source_target_pairs={{0,16},{2,18},{4,20},{6,22},{8,24},{10,26},{12,28},{14,30},{16,0},... | collective-permute-start | bytes 6291464 | tf_op jit(solution)/shard_map/ppermute | solution.py:60
  66.2 11.6 %copy-start.5 = (f32[256]{0:T(256)S(1)}, f32[256]{0:T(256)}, u32[]{:S(2)}) copy-start(f32[256]{0:T(256)} %param.7) | copy-start | bytes 3076
  71.4 18.4 %collective-permute-start.16 = (bf16[128,8192]{1,0:T(8,128)(2,1)}, bf16[128,8192]{1,0:T(8,128)(2,1)}, u32[]{:S(2)}, u32[]{:S(2)}) collective-permute-start(bf16[128,8192]{1,0:T(8,128)(2,1)} %soft.3), channel_id=1, source_target_pairs={{0,16},{2,18},{4,20},{6,22},{8,24},{10,26},{12,28},{14,30},{16,0},... | collective-permute-start | bytes 6291464 | tf_op jit(solution)/shard_map/ppermute | solution.py:60
  71.5 17.0 %all-to-all-start = ((f32[32,3,256]{2,1,0:T(4,128)}), f32[32,3,256]{2,1,0:T(4,128)S(1)}, u32[]{:S(2)}, u32[]{:S(2)}) async-start(f32[32,3,256]{2,1,0:T(4,128)} %merge.1.merged_ref), calls=%async_computation | async-start | bytes 262144 | tf_op jit(solution)/shard_map/all_to_all | solution.py:221
  78.1 3.4 %copy-start.2 = (bf16[8192,512]{1,0:T(8,128)(2,1)S(1)}, bf16[8192,512]{1,0:T(8,128)(2,1)}, u32[]{:S(2)}) copy-start(bf16[8192,512]{1,0:T(8,128)(2,1)} %w_ref.7) | copy-start | bytes 25165828
  85.3 2.0 %copy-start.3 = (f32[128,8192]{1,0:T(8,128)}, f32[128,8192]{1,0:T(8,128)S(1)}, u32[]{:S(2)}) copy-start(f32[128,8192]{1,0:T(8,128)S(1)} %soft.2.soft_own) | copy-start | bytes 12582916
  89.8 2.2 %copy-start.4 = (f32[128,8192]{1,0:T(8,128)S(1)}, f32[128,8192]{1,0:T(8,128)}, u32[]{:S(2)}) copy-start(f32[128,8192]{1,0:T(8,128)} %copy-done.3) | copy-start | bytes 12582916
  94.9 10.5 %collective-permute-start.18 = (bf16[32,8192]{1,0:T(8,128)(2,1)S(1)}, bf16[32,8192]{1,0:T(8,128)(2,1)S(1)}, u32[]{:S(2)}, u32[]{:S(2)}) collective-permute-start(bf16[32,8192]{1,0:T(8,128)(2,1)S(1)} %get-tuple-element.19), channel_id=1, source_target_pairs={{0,64},{2,66},{4,68},{6,70},{8,72},{10,74},{12,76},{14,78},{16,18}... | collective-permute-start | bytes 1572872 | tf_op jit(solution)/shard_map/ppermute | solution.py:60
  95.5 15.0 %collective-permute-start.19 = (bf16[32,8192]{1,0:T(8,128)(2,1)S(1)}, bf16[32,8192]{1,0:T(8,128)(2,1)S(1)}, u32[]{:S(2)}, u32[]{:S(2)}) collective-permute-start(bf16[32,8192]{1,0:T(8,128)(2,1)S(1)} %get-tuple-element.20), channel_id=1, source_target_pairs={{0,192},{2,194},{4,196},{6,198},{8,200},{10,202},{12,204},{14,206}... | collective-permute-start | bytes 1572872 | tf_op jit(solution)/shard_map/ppermute | solution.py:60
  100.7 10.8 %collective-permute-start.20 = (bf16[32,8192]{1,0:T(8,128)(2,1)S(1)}, bf16[32,8192]{1,0:T(8,128)(2,1)S(1)}, u32[]{:S(2)}, u32[]{:S(2)}) collective-permute-start(bf16[32,8192]{1,0:T(8,128)(2,1)S(1)} %combine.5), channel_id=1, source_target_pairs={{0,128},{2,130},{4,132},{6,134},{8,136},{10,138},{12,140},{14,142}... | collective-permute-start | bytes 1572872 | tf_op jit(solution)/shard_map/ppermute | solution.py:60
  111.8 6.3 %collective-permute-start.21 = (bf16[8,8192]{1,0:T(8,128)(2,1)S(1)}, bf16[8,8192]{1,0:T(8,128)(2,1)S(1)}, u32[]{:S(2)}, u32[]{:S(2)}) collective-permute-start(bf16[8,8192]{1,0:T(8,128)(2,1)S(1)} %get-tuple-element.27), channel_id=1, source_target_pairs={{0,2},{2,4},{4,6},{6,8},{8,10},{10,12},{12,14},{14,0},{16,80},{18,... | collective-permute-start | bytes 393224 | tf_op jit(solution)/shard_map/ppermute | solution.py:60
  113.0 5.0 %collective-permute-start.22 = (bf16[8,8192]{1,0:T(8,128)(2,1)S(1)}, bf16[8,8192]{1,0:T(8,128)(2,1)S(1)}, u32[]{:S(2)}, u32[]{:S(2)}) collective-permute-start(bf16[8,8192]{1,0:T(8,128)(2,1)S(1)} %get-tuple-element.29), channel_id=1, source_target_pairs={{0,14},{2,0},{4,2},{6,4},{8,6},{10,8},{12,10},{14,12},{16,208},{18... | collective-permute-start | bytes 393224 | tf_op jit(solution)/shard_map/ppermute | solution.py:60
  115.1 7.6 %collective-permute-start.23 = (bf16[8,8192]{1,0:T(8,128)(2,1)S(1)}, bf16[8,8192]{1,0:T(8,128)(2,1)S(1)}, u32[]{:S(2)}, u32[]{:S(2)}) collective-permute-start(bf16[8,8192]{1,0:T(8,128)(2,1)S(1)} %get-tuple-element.28), channel_id=1, source_target_pairs={{0,4},{2,6},{4,8},{6,10},{8,12},{10,14},{12,0},{14,2},{16,144},{18... | collective-permute-start | bytes 393224 | tf_op jit(solution)/shard_map/ppermute | solution.py:60
  122.9 8.0 %collective-permute-start.24 = (bf16[2,8192]{1,0:T(2,128)(2,1)S(1)}, bf16[2,8192]{1,0:T(2,128)(2,1)S(1)}, u32[]{:S(2)}, u32[]{:S(2)}) collective-permute-start(bf16[2,8192]{1,0:T(2,128)(2,1)S(1)} %get-tuple-element.30), channel_id=1, source_target_pairs={{0,32},{2,34},{4,36},{6,38},{8,40},{10,42},{12,44},{14,46},{16,48}... | collective-permute-start | bytes 98312 | tf_op jit(solution)/shard_map/ppermute | solution.py:60
  124.0 8.2 %collective-permute-start.25 = (bf16[2,8192]{1,0:T(2,128)(2,1)S(1)}, bf16[2,8192]{1,0:T(2,128)(2,1)S(1)}, u32[]{:S(2)}, u32[]{:S(2)}) collective-permute-start(bf16[2,8192]{1,0:T(2,128)(2,1)S(1)} %get-tuple-element.32), channel_id=1, source_target_pairs={{0,8},{2,10},{4,12},{6,14},{8,0},{10,2},{12,4},{14,6},{16,24},{18,... | collective-permute-start | bytes 98312 | tf_op jit(solution)/shard_map/ppermute | solution.py:60
  128.7 8.9 %collective-permute-start.26 = (bf16[2,8192]{1,0:T(2,128)(2,1)S(1)}, bf16[2,8192]{1,0:T(2,128)(2,1)S(1)}, u32[]{:S(2)}, u32[]{:S(2)}) collective-permute-start(bf16[2,8192]{1,0:T(2,128)(2,1)S(1)} %get-tuple-element.31), channel_id=1, source_target_pairs={{0,40},{2,42},{4,44},{6,46},{8,32},{10,34},{12,36},{14,38},{16,56}... | collective-permute-start | bytes 98312 | tf_op jit(solution)/shard_map/ppermute | solution.py:60

commit v4 on v3

v4 whole, which is shorter than its diff:
```python
import functools

import jax
import jax.numpy as jnp
from jax import lax
from jax.experimental import pallas as pl
from jax.experimental.pallas import tpu as pltpu
from jax.sharding import Mesh
from jax.sharding import PartitionSpec as P

zloss_coef = 0.0001
NY, NX, NC, NZ = 4, 2, 2, 8
GROUP = ("y", "x", "c", "z")
OFFSETS = (0, 1, -1, 2)
BF, F32 = jnp.bfloat16, jnp.float32
ROWS, DEPTH, WIDTH = 256, 8192, 512
CHUNK = 1024
STEPS = DEPTH // CHUNK
VMEM = pl.BlockSpec(memory_space=pltpu.VMEM)
SMEM = pl.BlockSpec(memory_space=pltpu.SMEM)


def index_of(y, x, c, z):
    return (((y % NY) * NX + x % NX) * NC + c % NC) * NZ + z % NZ


def pairs(route):
    every = [(y, x, c, z) for y in range(NY) for x in range(NX) for c in range(NC) for z in range(NZ)]
    return [(index_of(*p), index_of(*route(*p))) for p in every]


def to_x(y, x, c, z):
    return y, x + 1, c, z


def to_c(y, x, c, z):
    return y, x, c + 1, z


def to_z4(y, x, c, z):
    return y, x, c, z + 4


def to_xc(y, x, c, z):
    return y, x + 1, c + 1, z


def to_xz4(y, x, c, z):
    return y, x + 1, c, z + 4


def to_first(step):
    return lambda y, x, c, z: (y, x, c, z + step) if c == 0 else (y + step, x, c, z)


def to_second(step):
    return lambda y, x, c, z: (y + step, x, c, z) if c == 0 else (y, x, c, z + step)


def send(value, route):
    return lax.ppermute(value, GROUP, pairs(route))


def params(mib=24):
    return pltpu.CompilerParams(vmem_limit_bytes=mib << 20)


def placed(at_ref):
    y, x, c, z = (at_ref[i] for i in range(4))
    at = lax.broadcasted_iota(jnp.int32, (ROWS, 1), 0)
    r, xr, z4, q1, q2, cr = at & 1, (at >> 1) & 1, (at >> 2) & 1, (at >> 3) & 3, (at >> 5) & 3, at >> 7
    o1 = jnp.where(q1 == 2, -1, jnp.where(q1 == 3, 2, q1))
    o2 = jnp.where(q2 == 2, -1, jnp.where(q2 == 3, 2, q2))
    core = c ^ cr
    zo = jnp.where(core == 0, o1, o2) + 4 * z4
    yo = jnp.where(core == 0, o2, o1)
    rows = ((((y + yo) & 3) * 2 + (x ^ xr)) * 2 + core) * 16 + ((z + zo) & 7) * 2 + r
    return rows == lax.broadcasted_iota(jnp.int32, (ROWS, ROWS), 1)


def hits(at_ref, targets_ref, place):
    own = jnp.sum(jnp.where(place, targets_ref[...], 0), axis=1, keepdims=True) - at_ref[4]
    return lax.broadcasted_iota(jnp.int32, (ROWS, WIDTH), 1) == own


def logits_kernel(at_ref, targets_ref, p0, p1, p2, p3, p4, p5, p6, p7, w_ref, logits_ref, stats_ref):
    k = pl.program_id(0)
    left = jnp.concatenate([p[...] for p in (p0, p1, p2, p3, p4, p5, p6, p7)], axis=0)
    part = jnp.dot(left, w_ref[...], preferred_element_type=F32)

    @pl.when(k == 0)
    def _():
        logits_ref[...] = part

    @pl.when(k > 0)
    def _():
        logits_ref[...] += part

    @pl.when(k == STEPS - 1)
    def _():
        acc = logits_ref[...]
        top = jnp.max(acc, axis=1, keepdims=True)
        total = jnp.sum(jnp.exp(acc - top), axis=1, keepdims=True)
        place = placed(at_ref)
        picked = jnp.sum(jnp.where(hits(at_ref, targets_ref, place), acc, 0.0), axis=1, keepdims=True)
        for i, column in enumerate((top, total, picked)):
            stats_ref[i : i + 1, :] = jnp.sum(jnp.where(place, column, 0.0), axis=0, keepdims=True)


def times_weights(left, w_ref):
    return lax.dot_general(left, w_ref[...], (((1,), (1,)), ((), ())), preferred_element_type=F32)


def target_kernel(at_ref, targets_ref, w_ref, own_ref, other_ref, left_ref):
    @pl.when(pl.program_id(0) == 0)
    def _():
        left_ref[...] = jnp.where(hits(at_ref, targets_ref, placed(at_ref)), 1.0, 0.0).astype(BF)

    part = times_weights(left_ref[...], w_ref)
    own_ref[...] = part[: ROWS // 2].astype(BF)
    other_ref[...] = part[ROWS // 2 :].astype(BF)


def soft_kernel(start, at_ref, targets_ref, merged_ref, logits_ref, w_ref, soft_ref, left_ref):
    @pl.when(pl.program_id(0) == 0)
    def _():
        cut = slice(start, start + ROWS // 2)
        place = placed(at_ref)
        top = jnp.sum(jnp.where(place[cut], merged_ref[0, 0:1, :], 0.0), axis=1, keepdims=True)
        hit = hits(at_ref, targets_ref, place)[cut]
        left_ref[...] = jnp.where(hit, 0.0, jnp.exp(logits_ref[...] - top)).astype(BF)

    soft_ref[...] = times_weights(left_ref[...], w_ref).astype(soft_ref.dtype)


def merge_kernel(own_ref, core_ref, x_ref, both_ref, out_ref):
    refs = (own_ref, core_ref, x_ref, both_ref)
    tops = [r[0:1, :] for r in refs]
    top = jnp.maximum(jnp.maximum(tops[0], tops[1]), jnp.maximum(tops[2], tops[3]))
    total = sum(r[1:2, :] * jnp.exp(t - top) for r, t in zip(refs, tops))
    picked = sum(r[2:3, :] for r in refs)
    merged = jnp.concatenate([top, total, picked], axis=0)
    for i in range(out_ref.shape[0]):
        out_ref[i] = merged


def scales_kernel(at_ref, grad_ref, merged_ref, spread_ref, out_ref):
    place = placed(at_ref)[: ROWS // 2]

    def ordered(row):
        return jnp.sum(jnp.where(place, row, 0.0), axis=1, keepdims=True)

    tops = spread_ref[:, 0, :]
    highest = jnp.max(tops, axis=0, keepdims=True)
    total = jnp.sum(spread_ref[:, 1, :] * jnp.exp(tops - highest), axis=0, keepdims=True)
    log_total = ordered(highest + jnp.log(total))
    picked = ordered(jnp.sum(spread_ref[:, 2, :], axis=0, keepdims=True))
    top = ordered(merged_ref[0, 0:1, :])
    factor = 1.0 + 2.0 * zloss_coef * log_total
    grad = ordered(grad_ref[...])
    scale = grad * factor * jnp.exp(top - log_total)
    target = (grad * (jnp.exp(picked - log_total) * factor - 1.0)).astype(BF).astype(F32)
    lane = lax.broadcasted_iota(jnp.int32, (ROWS // 2, 128), 1)
    out_ref[...] = jnp.where(lane == 0, scale, jnp.where(lane == 1, target, jnp.where(lane == 2, log_total, picked)))


def combine_kernel(scales_ref, soft_own, soft_in, target_own, target_in, out_ref):
    soft = soft_own[...] + soft_in[...].astype(F32)
    chosen = target_own[...].astype(F32) + target_in[...].astype(F32)
    out_ref[...] = (scales_ref[:, 0:1] * soft + scales_ref[:, 1:2] * chosen).astype(out_ref.dtype)


def shards(hidden, lm_weight, targets, loss_grad):
    half = ROWS // 2
    at = jnp.stack([lax.axis_index(a) for a in GROUP] + [lax.axis_index(GROUP) * WIDTH])
    targets, loss_grad = targets.reshape(1, ROWS), loss_grad.reshape(1, ROWS)
    lm_weight = pltpu.with_memory_space_constraint(lm_weight, pltpu.HBM)
    row = pl.BlockSpec((1, ROWS), lambda k: (0, 0))
    weights = pl.BlockSpec((CHUNK, WIDTH), lambda k: (k, 0))

    block = jnp.concatenate([hidden] + [send(hidden, to) for to in (to_x, to_z4, to_xz4)])
    far, near, back = (send(block, to_first(-o)) for o in (2, 1, -1))
    block = jnp.concatenate([block, near, back, far])
    far, near, back = (send(block, to_second(-o)) for o in (2, 1, -1))

    aim, _ = lax.optimization_barrier((targets, block))
    target_own, target_out = pl.pallas_call(
        target_kernel,
        out_shape=[jax.ShapeDtypeStruct((half, DEPTH), BF)] * 2,
        grid=(STEPS,),
        in_specs=[SMEM, row, weights],
        out_specs=[pl.BlockSpec((half, CHUNK), lambda k: (0, k))] * 2,
        scratch_shapes=[pltpu.VMEM((ROWS, WIDTH), BF)],
        compiler_params=params(),
        cost_estimate=pl.CostEstimate(flops=2 * ROWS * DEPTH * WIDTH, bytes_accessed=12 << 20, transcendentals=0),
        name="target",
    )(at, aim, lm_weight)
    near, target_own, target_out = lax.optimization_barrier((near, target_own, target_out))
    pieces = [block, near, back, far]
    pieces = pieces + [send(p, to_c) for p in pieces]
    target_in = send(target_out, to_c)

    logits, stats = pl.pallas_call(
        logits_kernel,
        out_shape=(jax.ShapeDtypeStruct((ROWS, WIDTH), F32), jax.ShapeDtypeStruct((3, ROWS), F32)),
        grid=(STEPS,),
        in_specs=[SMEM, row] + [pl.BlockSpec((32, CHUNK), lambda k: (0, k))] * 8 + [weights],
        out_specs=(pl.BlockSpec((ROWS, WIDTH), lambda k: (0, 0)), pl.BlockSpec((3, ROWS), lambda k: (0, 0))),
        compiler_params=params(),
        cost_estimate=pl.CostEstimate(flops=2 * ROWS * DEPTH * WIDTH, bytes_accessed=13 << 20, transcendentals=ROWS * WIDTH),
        name="logits",
    )(at, targets, *pieces, lm_weight)
    stats = [stats] + [send(stats, to) for to in (to_c, to_x, to_xc)]
    merged = pl.pallas_call(
        merge_kernel,
        out_shape=jax.ShapeDtypeStruct((32, 3, ROWS), F32),
        in_specs=[VMEM] * 4,
        out_specs=VMEM,
        compiler_params=params(),
        name="merge",
    )(*stats)
    spread = lax.all_to_all(merged, ("y", "z"), 0, 0)

    def soft(start, dtype):
        return pl.pallas_call(
            functools.partial(soft_kernel, start),
            out_shape=jax.ShapeDtypeStruct((half, DEPTH), dtype),
            grid=(STEPS,),
            in_specs=[
                SMEM,
                row,
                pl.BlockSpec((1, 3, ROWS), lambda k: (0, 0, 0)),
                pl.BlockSpec((half, WIDTH), lambda k: (start // half, 0)),
                weights,
            ],
            out_specs=pl.BlockSpec((half, CHUNK), lambda k: (0, k)),
            scratch_shapes=[pltpu.VMEM((half, WIDTH), BF)],
            compiler_params=params(),
            cost_estimate=pl.CostEstimate(flops=1 << 20, bytes_accessed=1 << 16, transcendentals=0),
            name="soft",
        )(at, targets, merged, logits, lm_weight)

    soft_in = send(soft(half, BF), to_c)
    soft_own = soft(0, F32)
    scales = pl.pallas_call(
        scales_kernel,
        out_shape=jax.ShapeDtypeStruct((half, 128), F32),
        in_specs=[SMEM] + [VMEM] * 3,
        out_specs=VMEM,
        compiler_params=params(),
        name="scales",
    )(at, loss_grad, merged, spread)

    def combine(q, dtype):
        piece = pl.BlockSpec((32, 2 * CHUNK), lambda k: (q, k))
        return pl.pallas_call(
            combine_kernel,
            out_shape=jax.ShapeDtypeStruct((32, DEPTH), dtype),
            grid=(STEPS // 2,),
            in_specs=[pl.BlockSpec((32, 128), lambda k: (q, 0))] + [piece] * 4,
            out_specs=pl.BlockSpec((32, 2 * CHUNK), lambda k: (0, k)),
            compiler_params=params(),
            cost_estimate=pl.CostEstimate(flops=6 * 32 * DEPTH, bytes_accessed=3 << 20, transcendentals=0),
            name="combine",
        )(scales, soft_own, soft_in, target_own, target_in)

    arrived = [send(combine(k, BF), to_second(OFFSETS[k])).astype(F32) for k in (3, 1, 2)]
    part = combine(0, F32) + sum(arrived)
    log_total, target_logit = scales[:2, 2], scales[:2, 3]
    ce_loss = log_total - target_logit
    z_term = zloss_coef * log_total * log_total

    part = part.reshape(4, 8, DEPTH)
    part = part[0] + sum(send(part[k].astype(BF), to_first(OFFSETS[k])).astype(F32) for k in (3, 1, 2))
    part = [part[0:2]] + [
        send(part[2 * k : 2 * k + 2].astype(BF), to).astype(F32) for k, to in ((3, to_xz4), (2, to_z4), (1, to_x))
    ]
    part = (part[0] + part[1]) + (part[2] + part[3])
    return ce_loss, z_term, part.astype(BF)


def solution(mesh):
    mesh = Mesh(mesh.devices.reshape(NY, NX, NC, NZ, 2), (*GROUP, "dp"))
    own = ("dp", *GROUP)
    in_specs = (P(own, None), P(None, GROUP), P("dp"), P("dp"))
    out_specs = (P(own), P(own), P(own, None))
    return jax.shard_map(shards, mesh=mesh, in_specs=in_specs, out_specs=out_specs, check_vma=False)
```

time: 140 us -> 143 us (1.021)
  Pallas kernels: 27.3 us -> 46.1 us
  waiting for transfers between devices: 52.6 us -> 37.4 us
  local copies, waits for them, and re-layouts: 12.6 us -> 8.05 us
  starting transfers between devices: 41.3 us -> 45.7 us
    ppermute x27, waiting for transfers between devices: 51.3 us -> 36.5 us  [send(): return lax.ppermute(value, GROUP, pairs(route))]
    pallas_call x2, Pallas kernels: 9.06 us -> 17 us  [soft(): pl.pallas_call(functools.partial(soft_kernel, start), out_shape=jax.Shape...]
    pallas_call x1, Pallas kernels: 3.76 us -> 9.08 us  [shards(): pl.pallas_call(target_kernel, out_shape=[jax.ShapeDtypeStruct((half, DEPT...]
    unnamed x12 -> x14, local copies, waits for them, and re-layouts: 10.9 us -> 6.67 us
    pallas_call x1, Pallas kernels: 4.61 us -> 8.51 us  [shards(): pl.pallas_call(logits_kernel, out_shape=(jax.ShapeDtypeStruct((ROWS, WIDT...]
    ppermute x27, starting transfers between devices: 35.1 us -> 39 us  [send(): return lax.ppermute(value, GROUP, pairs(route))]
    pallas_call x3 -> x4, Pallas kernels: 8 us -> 9.65 us  [combine(): pl.pallas_call(combine_kernel, out_shape=jax.ShapeDtypeStruct((32, DEPTH)...]
  transfers between devices with their start and end apart: 28 -> 28, of which waited for: 17 -> 17; matrix products, arithmetic and copies ran while one was open for 2% -> 1% of each run, Pallas kernels for 14% -> 25%
where the time goes in v4:
time: 143 us; the launch traced here: 140 us
  Pallas kernels  46.1 us (32%)
  starting transfers between devices  45.7 us (32%)
  waiting for transfers between devices  37.4 us (26%)
  local copies, waits for them, and re-layouts  8.05 us (6%)
  other arithmetic  2.4 us (2%)
    ppermute x27, starting transfers between devices, send(): return lax.ppermute(value, GROUP, pairs(route))  39 us
    ppermute x27, waiting for transfers between devices, send(): return lax.ppermute(value, GROUP, pairs(route))  36.5 us
    pallas_call x2, Pallas kernels, soft(): pl.pallas_call(functools.partial(soft_kernel, start), out_shape=jax.Shape...  17 us
    pallas_call x4, Pallas kernels, combine(): pl.pallas_call(combine_kernel, out_shape=jax.ShapeDtypeStruct((32, DEPTH)...  9.65 us
    pallas_call x1, Pallas kernels, shards(): pl.pallas_call(target_kernel, out_shape=[jax.ShapeDtypeStruct((half, DEPT...  9.08 us
    pallas_call x1, Pallas kernels, shards(): pl.pallas_call(logits_kernel, out_shape=(jax.ShapeDtypeStruct((ROWS, WIDT...  8.51 us
    all_to_all x1, starting transfers between devices, shards(): spread = lax.all_to_all(merged, ('y', 'z'), 0, 0)  6.7 us
    unnamed x14, local copies, waits for them, and re-layouts  6.67 us
  transfers between devices with their start and end apart: 28, of which 17 were waited for; matrix products, arithmetic and copies ran while one was open for 1% of the time, Pallas kernels for 25%

profile of v4, /device:TPU:4, one launch (start us, length us, event | category | flops | bytes accessed | tf_op | source)
XLA Modules:
  0.0 140.4 jit_solution(13966043345938232803)
XLA Ops:
  0.6 1.3 collective-permute-start
  1.9 7.2 %collective-permute-start.1 = (bf16[2,8192]{1,0:T(2,128)(2,1)}, bf16[2,8192]{1,0:T(2,128)(2,1)S(1)}, u32[]{:S(2)}, u32[]{:S(2)}) collective-permute-start(bf16[2,8192]{1,0:T(2,128)(2,1)} %param.4), channel_id=1, source_target_pairs={{0,8},{2,10},{4,12},{6,14},{8,0},{10,2},{12,4},{14,6},{16,24},{18,... | collective-permute-start | bytes 98312 | tf_op jit(solution)/shard_map/ppermute | solution.py:61
  9.1 0.3 collective-permute-start.2
  9.4 1.9 %collective-permute-done.1 = bf16[2,8192]{1,0:T(2,128)(2,1)S(1)} collective-permute-done((bf16[2,8192]{1,0:T(2,128)(2,1)}, bf16[2,8192]{1,0:T(2,128)(2,1)S(1)}, u32[]{:S(2)}, u32[]{:S(2)}) %collective-permute-start.1) | collective-permute-done | bytes 32800 | tf_op jit(solution)/shard_map/ppermute | solution.py:61
  11.2 6.8 %collective-permute-done.2 = bf16[2,8192]{1,0:T(2,128)(2,1)S(1)} collective-permute-done((bf16[2,8192]{1,0:T(2,128)(2,1)}, bf16[2,8192]{1,0:T(2,128)(2,1)S(1)}, u32[]{:S(2)}, u32[]{:S(2)}) %collective-permute-start.2) | collective-permute-done | bytes 32800 | tf_op jit(solution)/shard_map/ppermute | solution.py:61
  18.0 0.9 pad_maximum_fusion
  18.9 0.2 collective-permute-start.3
  19.1 1.9 %collective-permute-start.4 = (bf16[8,8192]{1,0:T(8,128)(2,1)S(1)}, bf16[8,8192]{1,0:T(8,128)(2,1)S(1)}, u32[]{:S(2)}, u32[]{:S(2)}) collective-permute-start(bf16[8,8192]{1,0:T(8,128)(2,1)S(1)} %pad_maximum_fusion), channel_id=1, source_target_pairs={{0,2},{2,4},{4,6},{6,8},{8,10},{10,12},{12,14},{14,0},{16,80},{18,... | collective-permute-start | bytes 393224 | tf_op jit(solution)/shard_map/ppermute | solution.py:61
  21.1 2.9 %collective-permute-done.3 = bf16[8,8192]{1,0:T(8,128)(2,1)S(1)} collective-permute-done((bf16[8,8192]{1,0:T(8,128)(2,1)S(1)}, bf16[8,8192]{1,0:T(8,128)(2,1)S(1)}, u32[]{:S(2)}, u32[]{:S(2)}) %collective-permute-start.3) | collective-permute-done | bytes 131104 | tf_op jit(solution)/shard_map/ppermute | solution.py:61
  24.0 1.3 collective-permute-done.4
  25.3 3.0 %collective-permute-done.5 = bf16[8,8192]{1,0:T(8,128)(2,1)S(1)} collective-permute-done((bf16[8,8192]{1,0:T(8,128)(2,1)S(1)}, bf16[8,8192]{1,0:T(8,128)(2,1)S(1)}, u32[]{:S(2)}, u32[]{:S(2)}) %collective-permute-start.5) | collective-permute-done | bytes 131104 | tf_op jit(solution)/shard_map/ppermute | solution.py:61
  28.3 1.0 concatenate.8.p0
  29.3 3.1 %collective-permute-start.6 = (bf16[32,8192]{1,0:T(8,128)(2,1)S(1)}, bf16[32,8192]{1,0:T(8,128)(2,1)S(1)}, u32[]{:S(2)}, u32[]{:S(2)}) collective-permute-start(bf16[32,8192]{1,0:T(8,128)(2,1)S(1)} %concatenate.8.p0), channel_id=1, source_target_pairs={{0,192},{2,194},{4,196},{6,198},{8,200},{10,202},{12,204},{14,206}... | collective-permute-start | bytes 1572872 | tf_op jit(solution)/shard_map/ppermute | solution.py:61
  32.4 2.4 %collective-permute-start.8 = (bf16[32,8192]{1,0:T(8,128)(2,1)S(1)}, bf16[32,8192]{1,0:T(8,128)(2,1)}, u32[]{:S(2)}, u32[]{:S(2)}) collective-permute-start(bf16[32,8192]{1,0:T(8,128)(2,1)S(1)} %concatenate.8.p0), channel_id=1, source_target_pairs={{0,128},{2,130},{4,132},{6,134},{8,136},{10,138},{12,140},{14,142}... | collective-permute-start | bytes 1572872 | tf_op jit(solution)/shard_map/ppermute | solution.py:61
  34.8 0.1 stack.23.at_ref
  34.9 0.7 copy-done.4
  35.6 9.1 %target.1 = (bf16[128,8192]{1,0:T(8,128)(2,1)S(1)}, bf16[128,8192]{1,0:T(8,128)(2,1)}) custom-call(s32[5]{0:T(128)S(1)} %stack.23.at_ref, s32[1,256]{1,0:T(1,128)S(1)} %bitcast.7, bf16[8192,512]{1,0:T(8,128)(2,1)} %w_ref.7), custom_call_target="tpu_custom_call" | custom-call | flops 2147483648 | bytes 12582912 | tf_op jit(solution)/shard_map/target/pallas_call | solution.py:187
  44.7 0.5 collective-permute-start.10
  45.2 0.8 copy-done.2
  46.0 2.5 %collective-permute-done.7.p2 = bf16[32,8192]{1,0:T(8,128)(2,1)} collective-permute-done((bf16[32,8192]{1,0:T(8,128)(2,1)S(1)}, bf16[32,8192]{1,0:T(8,128)(2,1)}, u32[]{:S(2)}, u32[]{:S(2)}) %collective-permute-start.7) | collective-permute-done | bytes 524320 | tf_op jit(solution)/shard_map/ppermute | solution.py:61
  48.5 0.5 collective-permute-start.12
  49.0 1.6 %collective-permute-done.11.p6 = bf16[32,8192]{1,0:T(8,128)(2,1)S(1)} collective-permute-done((bf16[32,8192]{1,0:T(8,128)(2,1)}, bf16[32,8192]{1,0:T(8,128)(2,1)S(1)}, u32[]{:S(2)}, u32[]{:S(2)}) %collective-permute-start.11) | collective-permute-done | bytes 524320 | tf_op jit(solution)/shard_map/ppermute | solution.py:61
  50.6 0.7 collective-permute-done.12.p7
  51.4 1.0 copy-done.3
  52.4 8.5 %logits.1 = (f32[256,512]{1,0:T(8,128)S(1)}, f32[3,256]{1,0:T(4,128)S(1)}) custom-call(s32[5]{0:T(128)S(1)} %stack.23.at_ref, s32[1,256]{1,0:T(1,128)S(1)} %bitcast.8, bf16[32,8192]{1,0:T(8,128)(2,1)S(1)} %concatenate.8.p0, bf16[32,8192]{1,0:T(8,128)(2,1)S(1)} %copy-done.3, bf16[32,8192]{1,0:T(8,128)(2,1)} %collective-permute-done.7.p2, ...), custom_call_target="tpu_custom_call" | custom-call | flops 2147483648 | bytes 13631488 | tf_op jit(solution)/shard_map/logits/pallas_call | solution.py:203
  60.9 0.2 collective-permute-start.13
  61.2 1.0 collective-permute-start.14
  62.1 0.7 collective-permute-start.15
  62.9 0.4 collective-permute-start.17
  63.3 1.5 %collective-permute-done.14.x_ref = f32[3,256]{1,0:T(4,128)S(1)} collective-permute-done((f32[3,256]{1,0:T(4,128)S(1)}, f32[3,256]{1,0:T(4,128)S(1)}, u32[]{:S(2)}, u32[]{:S(2)}) %collective-permute-start.14) | collective-permute-done | bytes 3104 | tf_op jit(solution)/shard_map/ppermute | solution.py:61
  64.8 0.4 collective-permute-done.15.both_ref
  65.2 0.7 merge.1.merged_ref
  65.9 9.0 %soft.3 = bf16[128,8192]{1,0:T(8,128)(2,1)} custom-call(s32[5]{0:T(128)S(1)} %stack.23.at_ref, s32[1,256]{1,0:T(1,128)S(1)} %bitcast.9, f32[32,3,256]{2,1,0:T(4,128)} %merge.1.merged_ref, f32[256,512]{1,0:T(8,128)S(1)} %get-tuple-element.16.logits_ref, bf16[8192,512]{1,0:T(8,128)(2,1)} %w_ref.7), custom_call_target="tpu_custom_call" | custom-call | flops 1048576 | bytes 65536 | tf_op jit(solution)/shard_map/soft/pallas_call | solution.py:225
  74.8 0.1 collective-permute-start.16
  74.9 6.7 %all-to-all-start = ((f32[32,3,256]{2,1,0:T(4,128)}), f32[32,3,256]{2,1,0:T(4,128)S(1)}, u32[]{:S(2)}, u32[]{:S(2)}) async-start(f32[32,3,256]{2,1,0:T(4,128)} %merge.1.merged_ref), calls=%async_computation | async-start | bytes 262144 | tf_op jit(solution)/shard_map/all_to_all | solution.py:222
  81.7 8.0 %soft.2.soft_own = f32[128,8192]{1,0:T(8,128)S(1)} custom-call(s32[5]{0:T(128)S(1)} %stack.23.at_ref, s32[1,256]{1,0:T(1,128)S(1)} %bitcast.10, f32[32,3,256]{2,1,0:T(4,128)} %merge.1.merged_ref, f32[256,512]{1,0:T(8,128)S(1)} %get-tuple-element.16.logits_ref, bf16[8192,512]{1,0:T(8,128)(2,1)} %w_ref.7), custom_call_target="tpu_custom_call" | custom-call | flops 1048576 | bytes 65536 | tf_op jit(solution)/shard_map/soft/pallas_call | solution.py:225
  89.7 2.0 %copy-done = f32[128,8192]{1,0:T(8,128)} copy-done((f32[128,8192]{1,0:T(8,128)}, f32[128,8192]{1,0:T(8,128)S(1)}, u32[]{:S(2)}) %copy-start) | copy-done | bytes 4194328
  91.7 0.9 all-to-all-done.spread_ref
  92.6 1.2 scales.1.scales_ref
  93.8 2.2 %copy-done.1 = f32[128,8192]{1,0:T(8,128)S(1)} copy-done((f32[128,8192]{1,0:T(8,128)S(1)}, f32[128,8192]{1,0:T(8,128)}, u32[]{:S(2)}) %copy-start.1) | copy-done | bytes 4194328
  96.0 2.4 %combine.5 = bf16[32,8192]{1,0:T(8,128)(2,1)S(1)} custom-call(f32[128,128]{1,0:T(8,128)S(1)} %scales.1.scales_ref, f32[128,8192]{1,0:T(8,128)S(1)} %copy-done.1, bf16[128,8192]{1,0:T(8,128)(2,1)} %collective-permute-done.16.soft_in, bf16[128,8192]{1,0:T(8,128)(2,1)S(1)} %get-tuple-element.17.target_own, bf16[128,8192]{1,0:T(8,128)(2,1)} %collective-permute-done.17.target_in), custom_call_target="tpu_custom_call" | custom-call | flops 1572864 | bytes 3145728 | tf_op jit(solution)/shard_map/combine/pallas_call | solution.py:256
  98.4 2.5 %collective-permute-start.18 = (bf16[32,8192]{1,0:T(8,128)(2,1)S(1)}, bf16[32,8192]{1,0:T(8,128)(2,1)S(1)}, u32[]{:S(2)}, u32[]{:S(2)}) collective-permute-start(bf16[32,8192]{1,0:T(8,128)(2,1)S(1)} %combine.5), channel_id=1, source_target_pairs={{0,128},{2,130},{4,132},{6,134},{8,136},{10,138},{12,140},{14,142}... | collective-permute-start | bytes 1572872 | tf_op jit(solution)/shard_map/ppermute | solution.py:61
  100.9 2.4 %combine.6 = bf16[32,8192]{1,0:T(8,128)(2,1)S(1)} custom-call(f32[128,128]{1,0:T(8,128)S(1)} %scales.1.scales_ref, f32[128,8192]{1,0:T(8,128)S(1)} %copy-done.1, bf16[128,8192]{1,0:T(8,128)(2,1)} %collective-permute-done.16.soft_in, bf16[128,8192]{1,0:T(8,128)(2,1)S(1)} %get-tuple-element.17.target_own, bf16[128,8192]{1,0:T(8,128)(2,1)} %collective-permute-done.17.target_in), custom_call_target="tpu_custom_call" | custom-call | flops 1572864 | bytes 3145728 | tf_op jit(solution)/shard_map/combine/pallas_call | solution.py:256
  103.3 0.7 collective-permute-start.19
  104.0 2.4 %combine.7 = bf16[32,8192]{1,0:T(8,128)(2,1)S(1)} custom-call(f32[128,128]{1,0:T(8,128)S(1)} %scales.1.scales_ref, f32[128,8192]{1,0:T(8,128)S(1)} %copy-done.1, bf16[128,8192]{1,0:T(8,128)(2,1)} %collective-permute-done.16.soft_in, bf16[128,8192]{1,0:T(8,128)(2,1)S(1)} %get-tuple-element.17.target_own, bf16[128,8192]{1,0:T(8,128)(2,1)} %collective-permute-done.17.target_in), custom_call_target="tpu_custom_call" | custom-call | flops 1572864 | bytes 3145728 | tf_op jit(solution)/shard_map/combine/pallas_call | solution.py:256
  106.4 2.7 %collective-permute-start.20 = (bf16[32,8192]{1,0:T(8,128)(2,1)S(1)}, bf16[32,8192]{1,0:T(8,128)(2,1)S(1)}, u32[]{:S(2)}, u32[]{:S(2)}) collective-permute-start(bf16[32,8192]{1,0:T(8,128)(2,1)S(1)} %combine.7), channel_id=1, source_target_pairs={{0,192},{2,194},{4,196},{6,198},{8,200},{10,202},{12,204},{14,206}... | collective-permute-start | bytes 1572872 | tf_op jit(solution)/shard_map/ppermute | solution.py:61
  109.1 2.4 %combine.4 = f32[32,8192]{1,0:T(8,128)S(1)} custom-call(f32[128,128]{1,0:T(8,128)S(1)} %scales.1.scales_ref, f32[128,8192]{1,0:T(8,128)S(1)} %copy-done.1, bf16[128,8192]{1,0:T(8,128)(2,1)} %collective-permute-done.16.soft_in, bf16[128,8192]{1,0:T(8,128)(2,1)S(1)} %get-tuple-element.17.target_own, bf16[128,8192]{1,0:T(8,128)(2,1)} %collective-permute-done.17.target_in), custom_call_target="tpu_custom_call" | custom-call | flops 1572864 | bytes 3145728 | tf_op jit(solution)/shard_map/combine/pallas_call | solution.py:256
  111.5 3.2 %collective-permute-done.19 = bf16[32,8192]{1,0:T(8,128)(2,1)S(1)} collective-permute-done((bf16[32,8192]{1,0:T(8,128)(2,1)S(1)}, bf16[32,8192]{1,0:T(8,128)(2,1)S(1)}, u32[]{:S(2)}, u32[]{:S(2)}) %collective-permute-start.19) | collective-permute-done | bytes 524320 | tf_op jit(solution)/shard_map/ppermute | solution.py:61
  114.8 1.0 collective-permute-done.20
  115.8 0.2 fusion.3
  116.1 2.4 %collective-permute-start.21 = (bf16[8,8192]{1,0:T(8,128)(2,1)S(1)}, bf16[8,8192]{1,0:T(8,128)(2,1)S(1)}, u32[]{:S(2)}, u32[]{:S(2)}) collective-permute-start(bf16[8,8192]{1,0:T(8,128)(2,1)S(1)} %get-tuple-element.25), channel_id=1, source_target_pairs={{0,4},{2,6},{4,8},{6,10},{8,12},{10,14},{12,0},{14,2},{16,144},{18... | collective-permute-start | bytes 393224 | tf_op jit(solution)/shard_map/ppermute | solution.py:61
  118.5 1.5 %collective-permute-start.22 = (bf16[8,8192]{1,0:T(8,128)(2,1)S(1)}, bf16[8,8192]{1,0:T(8,128)(2,1)S(1)}, u32[]{:S(2)}, u32[]{:S(2)}) collective-permute-start(bf16[8,8192]{1,0:T(8,128)(2,1)S(1)} %get-tuple-element.27), channel_id=1, source_target_pairs={{0,2},{2,4},{4,6},{6,8},{8,10},{10,12},{12,14},{14,0},{16,80},{18,... | collective-permute-start | bytes 393224 | tf_op jit(solution)/shard_map/ppermute | solution.py:61
  120.0 1.8 %collective-permute-start.23 = (bf16[8,8192]{1,0:T(8,128)(2,1)S(1)}, bf16[8,8192]{1,0:T(8,128)(2,1)S(1)}, u32[]{:S(2)}, u32[]{:S(2)}) collective-permute-start(bf16[8,8192]{1,0:T(8,128)(2,1)S(1)} %get-tuple-element.26), channel_id=1, source_target_pairs={{0,14},{2,0},{4,2},{6,4},{8,6},{10,8},{12,10},{14,12},{16,208},{18... | collective-permute-start | bytes 393224 | tf_op jit(solution)/shard_map/ppermute | solution.py:61
  121.7 0.2 slice_reduce_fusion
  121.9 2.3 %collective-permute-done.21 = bf16[8,8192]{1,0:T(8,128)(2,1)S(1)} collective-permute-done((bf16[8,8192]{1,0:T(8,128)(2,1)S(1)}, bf16[8,8192]{1,0:T(8,128)(2,1)S(1)}, u32[]{:S(2)}, u32[]{:S(2)}) %collective-permute-start.21) | collective-permute-done | bytes 131104 | tf_op jit(solution)/shard_map/ppermute | solution.py:61
  124.2 1.8 %collective-permute-done.22 = bf16[8,8192]{1,0:T(8,128)(2,1)S(1)} collective-permute-done((bf16[8,8192]{1,0:T(8,128)(2,1)S(1)}, bf16[8,8192]{1,0:T(8,128)(2,1)S(1)}, u32[]{:S(2)}, u32[]{:S(2)}) %collective-permute-start.22) | collective-permute-done | bytes 131104 | tf_op jit(solution)/shard_map/ppermute | solution.py:61
  126.1 0.1 fusion.5
  126.2 5.1 %collective-permute-start.24 = (bf16[2,8192]{1,0:T(2,128)(2,1)S(1)}, bf16[2,8192]{1,0:T(2,128)(2,1)S(1)}, u32[]{:S(2)}, u32[]{:S(2)}) collective-permute-start(bf16[2,8192]{1,0:T(2,128)(2,1)S(1)} %get-tuple-element.28), channel_id=1, source_target_pairs={{0,40},{2,42},{4,44},{6,46},{8,32},{10,34},{12,36},{14,38},{16,56}... | collective-permute-start | bytes 98312 | tf_op jit(solution)/shard_map/ppermute | solution.py:61
  131.3 1.4 %collective-permute-start.25 = (bf16[2,8192]{1,0:T(2,128)(2,1)S(1)}, bf16[2,8192]{1,0:T(2,128)(2,1)S(1)}, u32[]{:S(2)}, u32[]{:S(2)}) collective-permute-start(bf16[2,8192]{1,0:T(2,128)(2,1)S(1)} %get-tuple-element.30), channel_id=1, source_target_pairs={{0,8},{2,10},{4,12},{6,14},{8,0},{10,2},{12,4},{14,6},{16,24},{18,... | collective-permute-start | bytes 98312 | tf_op jit(solution)/shard_map/ppermute | solution.py:61
  132.7 1.0 collective-permute-start.26
  133.7 0.5 multiply_multiply_fusion
  134.2 0.9 collective-permute-done.24
  135.1 4.6 %collective-permute-done.25 = bf16[2,8192]{1,0:T(2,128)(2,1)S(1)} collective-permute-done((bf16[2,8192]{1,0:T(2,128)(2,1)S(1)}, bf16[2,8192]{1,0:T(2,128)(2,1)S(1)}, u32[]{:S(2)}, u32[]{:S(2)}) %collective-permute-start.25) | collective-permute-done | bytes 32800 | tf_op jit(solution)/shard_map/ppermute | solution.py:61
  139.7 0.7 fusion.1
  (26 shorter events, 0.2 us)
Async XLA Ops:
  0.6 8.7 %collective-permute-start = (bf16[2,8192]{1,0:T(2,128)(2,1)}, bf16[2,8192]{1,0:T(2,128)(2,1)S(1)}, u32[]{:S(2)}, u32[]{:S(2)}) collective-permute-start(bf16[2,8192]{1,0:T(2,128)(2,1)} %param.4), channel_id=1, source_target_pairs={{0,32},{2,34},{4,36},{6,38},{8,40},{10,42},{12,44},{14,46},{16,48}... | collective-permute-start | bytes 98312 | tf_op jit(solution)/shard_map/ppermute | solution.py:61
  1.9 9.3 %collective-permute-start.1 = (bf16[2,8192]{1,0:T(2,128)(2,1)}, bf16[2,8192]{1,0:T(2,128)(2,1)S(1)}, u32[]{:S(2)}, u32[]{:S(2)}) collective-permute-start(bf16[2,8192]{1,0:T(2,128)(2,1)} %param.4), channel_id=1, source_target_pairs={{0,8},{2,10},{4,12},{6,14},{8,0},{10,2},{12,4},{14,6},{16,24},{18,... | collective-permute-start | bytes 98312 | tf_op jit(solution)/shard_map/ppermute | solution.py:61
  9.1 8.9 %collective-permute-start.2 = (bf16[2,8192]{1,0:T(2,128)(2,1)}, bf16[2,8192]{1,0:T(2,128)(2,1)S(1)}, u32[]{:S(2)}, u32[]{:S(2)}) collective-permute-start(bf16[2,8192]{1,0:T(2,128)(2,1)} %param.4), channel_id=1, source_target_pairs={{0,40},{2,42},{4,44},{6,46},{8,32},{10,34},{12,36},{14,38},{16,56}... | collective-permute-start | bytes 98312 | tf_op jit(solution)/shard_map/ppermute | solution.py:61
  18.9 5.0 %collective-permute-start.3 = (bf16[8,8192]{1,0:T(8,128)(2,1)S(1)}, bf16[8,8192]{1,0:T(8,128)(2,1)S(1)}, u32[]{:S(2)}, u32[]{:S(2)}) collective-permute-start(bf16[8,8192]{1,0:T(8,128)(2,1)S(1)} %pad_maximum_fusion), channel_id=1, source_target_pairs={{0,14},{2,0},{4,2},{6,4},{8,6},{10,8},{12,10},{14,12},{16,208},{18... | collective-permute-start | bytes 393224 | tf_op jit(solution)/shard_map/ppermute | solution.py:61
  19.1 6.2 %collective-permute-start.4 = (bf16[8,8192]{1,0:T(8,128)(2,1)S(1)}, bf16[8,8192]{1,0:T(8,128)(2,1)S(1)}, u32[]{:S(2)}, u32[]{:S(2)}) collective-permute-start(bf16[8,8192]{1,0:T(8,128)(2,1)S(1)} %pad_maximum_fusion), channel_id=1, source_target_pairs={{0,2},{2,4},{4,6},{6,8},{8,10},{10,12},{12,14},{14,0},{16,80},{18,... | collective-permute-start | bytes 393224 | tf_op jit(solution)/shard_map/ppermute | solution.py:61
  21.1 7.3 %collective-permute-start.5 = (bf16[8,8192]{1,0:T(8,128)(2,1)S(1)}, bf16[8,8192]{1,0:T(8,128)(2,1)S(1)}, u32[]{:S(2)}, u32[]{:S(2)}) collective-permute-start(bf16[8,8192]{1,0:T(8,128)(2,1)S(1)} %pad_maximum_fusion), channel_id=1, source_target_pairs={{0,12},{2,14},{4,0},{6,2},{8,4},{10,6},{12,8},{14,10},{16,144},{18... | collective-permute-start | bytes 393224 | tf_op jit(solution)/shard_map/ppermute | solution.py:61
  29.3 15.4 %collective-permute-start.6 = (bf16[32,8192]{1,0:T(8,128)(2,1)S(1)}, bf16[32,8192]{1,0:T(8,128)(2,1)S(1)}, u32[]{:S(2)}, u32[]{:S(2)}) collective-permute-start(bf16[32,8192]{1,0:T(8,128)(2,1)S(1)} %concatenate.8.p0), channel_id=1, source_target_pairs={{0,192},{2,194},{4,196},{6,198},{8,200},{10,202},{12,204},{14,206}... | collective-permute-start | bytes 1572872 | tf_op jit(solution)/shard_map/ppermute | solution.py:61
  32.4 16.1 %collective-permute-start.7 = (bf16[32,8192]{1,0:T(8,128)(2,1)S(1)}, bf16[32,8192]{1,0:T(8,128)(2,1)}, u32[]{:S(2)}, u32[]{:S(2)}) collective-permute-start(bf16[32,8192]{1,0:T(8,128)(2,1)S(1)} %concatenate.8.p0), channel_id=1, source_target_pairs={{0,64},{2,66},{4,68},{6,70},{8,72},{10,74},{12,76},{14,78},{16,18}... | collective-permute-start | bytes 1572872 | tf_op jit(solution)/shard_map/ppermute | solution.py:61
  32.4 16.1 %collective-permute-start.8 = (bf16[32,8192]{1,0:T(8,128)(2,1)S(1)}, bf16[32,8192]{1,0:T(8,128)(2,1)}, u32[]{:S(2)}, u32[]{:S(2)}) collective-permute-start(bf16[32,8192]{1,0:T(8,128)(2,1)S(1)} %concatenate.8.p0), channel_id=1, source_target_pairs={{0,128},{2,130},{4,132},{6,134},{8,136},{10,138},{12,140},{14,142}... | collective-permute-start | bytes 1572872 | tf_op jit(solution)/shard_map/ppermute | solution.py:61
  34.9 14.1 %collective-permute-start.9 = (bf16[32,8192]{1,0:T(8,128)(2,1)S(1)}, bf16[32,8192]{1,0:T(8,128)(2,1)S(1)}, u32[]{:S(2)}, u32[]{:S(2)}) collective-permute-start(bf16[32,8192]{1,0:T(8,128)(2,1)S(1)} %concatenate.8.p0), channel_id=1, source_target_pairs={{0,16},{2,18},{4,20},{6,22},{8,24},{10,26},{12,28},{14,30},{16,0},... | collective-permute-start | bytes 1572872 | tf_op jit(solution)/shard_map/ppermute | solution.py:61
  34.9 0.7 copy-start.4
  44.7 21.2 %copy-start.5 = (s32[256]{0:T(256)S(1)}, s32[256]{0:T(256)}, u32[]{:S(2)}) copy-start(s32[256]{0:T(256)} %param.6) | copy-start | bytes 3076
  44.7 4.3 %collective-permute-start.10 = (bf16[32,8192]{1,0:T(8,128)(2,1)S(1)}, bf16[32,8192]{1,0:T(8,128)(2,1)S(1)}, u32[]{:S(2)}, u32[]{:S(2)}) collective-permute-start(bf16[32,8192]{1,0:T(8,128)(2,1)S(1)} %collective-permute-done.6.p1), channel_id=1, source_target_pairs={{0,16},{2,18},{4,20},{6,22},{8,24},{10,26},{12,28},{14,30},{16,0},... | collective-permute-start | bytes 1572872 | tf_op jit(solution)/shard_map/ppermute | solution.py:61
  45.2 0.8 copy-start.2
  48.5 2.1 %collective-permute-start.11 = (bf16[32,8192]{1,0:T(8,128)(2,1)}, bf16[32,8192]{1,0:T(8,128)(2,1)S(1)}, u32[]{:S(2)}, u32[]{:S(2)}) collective-permute-start(bf16[32,8192]{1,0:T(8,128)(2,1)} %collective-permute-done.7.p2), channel_id=1, source_target_pairs={{0,16},{2,18},{4,20},{6,22},{8,24},{10,26},{12,28},{14,30},{16,0},... | collective-permute-start | bytes 1572872 | tf_op jit(solution)/shard_map/ppermute | solution.py:61
  48.5 2.9 %collective-permute-start.12 = (bf16[32,8192]{1,0:T(8,128)(2,1)}, bf16[32,8192]{1,0:T(8,128)(2,1)S(1)}, u32[]{:S(2)}, u32[]{:S(2)}) collective-permute-start(bf16[32,8192]{1,0:T(8,128)(2,1)} %collective-permute-done.8.p3), channel_id=1, source_target_pairs={{0,16},{2,18},{4,20},{6,22},{8,24},{10,26},{12,28},{14,30},{16,0},... | collective-permute-start | bytes 1572872 | tf_op jit(solution)/shard_map/ppermute | solution.py:61
  51.4 1.0 copy-start.3
  60.9 2.4 %collective-permute-start.13 = (f32[3,256]{1,0:T(4,128)S(1)}, f32[3,256]{1,0:T(4,128)S(1)}, u32[]{:S(2)}, u32[]{:S(2)}) collective-permute-start(f32[3,256]{1,0:T(4,128)S(1)} %get-tuple-element.15.own_ref), channel_id=1, source_target_pairs={{0,16},{2,18},{4,20},{6,22},{8,24},{10,26},{12,28},{14,30},{16,0},... | collective-permute-start | bytes 9224 | tf_op jit(solution)/shard_map/ppermute | solution.py:61
  61.2 3.6 %collective-permute-start.14 = (f32[3,256]{1,0:T(4,128)S(1)}, f32[3,256]{1,0:T(4,128)S(1)}, u32[]{:S(2)}, u32[]{:S(2)}) collective-permute-start(f32[3,256]{1,0:T(4,128)S(1)} %get-tuple-element.15.own_ref), channel_id=1, source_target_pairs={{0,32},{2,34},{4,36},{6,38},{8,40},{10,42},{12,44},{14,46},{16,48}... | collective-permute-start | bytes 9224 | tf_op jit(solution)/shard_map/ppermute | solution.py:61
  62.1 3.0 %collective-permute-start.15 = (f32[3,256]{1,0:T(4,128)S(1)}, f32[3,256]{1,0:T(4,128)S(1)}, u32[]{:S(2)}, u32[]{:S(2)}) collective-permute-start(f32[3,256]{1,0:T(4,128)S(1)} %get-tuple-element.15.own_ref), channel_id=1, source_target_pairs={{0,48},{2,50},{4,52},{6,54},{8,56},{10,58},{12,60},{14,62},{16,32}... | collective-permute-start | bytes 9224 | tf_op jit(solution)/shard_map/ppermute | solution.py:61
  62.9 30.9 %collective-permute-start.17 = (bf16[128,8192]{1,0:T(8,128)(2,1)}, bf16[128,8192]{1,0:T(8,128)(2,1)}, u32[]{:S(2)}, u32[]{:S(2)}) collective-permute-start(bf16[128,8192]{1,0:T(8,128)(2,1)} %get-tuple-element.18), channel_id=1, source_target_pairs={{0,16},{2,18},{4,20},{6,22},{8,24},{10,26},{12,28},{14,30},{16,0},... | collective-permute-start | bytes 6291464 | tf_op jit(solution)/shard_map/ppermute | solution.py:61
  74.8 18.9 %collective-permute-start.16 = (bf16[128,8192]{1,0:T(8,128)(2,1)}, bf16[128,8192]{1,0:T(8,128)(2,1)}, u32[]{:S(2)}, u32[]{:S(2)}) collective-permute-start(bf16[128,8192]{1,0:T(8,128)(2,1)} %soft.3), channel_id=1, source_target_pairs={{0,16},{2,18},{4,20},{6,22},{8,24},{10,26},{12,28},{14,30},{16,0},... | collective-permute-start | bytes 6291464 | tf_op jit(solution)/shard_map/ppermute | solution.py:61
  74.9 17.6 %all-to-all-start = ((f32[32,3,256]{2,1,0:T(4,128)}), f32[32,3,256]{2,1,0:T(4,128)S(1)}, u32[]{:S(2)}, u32[]{:S(2)}) async-start(f32[32,3,256]{2,1,0:T(4,128)} %merge.1.merged_ref), calls=%async_computation | async-start | bytes 262144 | tf_op jit(solution)/shard_map/all_to_all | solution.py:222
  81.7 10.9 %copy-start.6 = (f32[256]{0:T(256)S(1)}, f32[256]{0:T(256)}, u32[]{:S(2)}) copy-start(f32[256]{0:T(256)} %param.7) | copy-start | bytes 3076
  89.7 2.0 %copy-start = (f32[128,8192]{1,0:T(8,128)}, f32[128,8192]{1,0:T(8,128)S(1)}, u32[]{:S(2)}) copy-start(f32[128,8192]{1,0:T(8,128)S(1)} %soft.2.soft_own) | copy-start | bytes 12582916
  93.8 2.2 %copy-start.1 = (f32[128,8192]{1,0:T(8,128)S(1)}, f32[128,8192]{1,0:T(8,128)}, u32[]{:S(2)}) copy-start(f32[128,8192]{1,0:T(8,128)} %copy-done) | copy-start | bytes 12582916
  98.4 13.2 %collective-permute-start.18 = (bf16[32,8192]{1,0:T(8,128)(2,1)S(1)}, bf16[32,8192]{1,0:T(8,128)(2,1)S(1)}, u32[]{:S(2)}, u32[]{:S(2)}) collective-permute-start(bf16[32,8192]{1,0:T(8,128)(2,1)S(1)} %combine.5), channel_id=1, source_target_pairs={{0,128},{2,130},{4,132},{6,134},{8,136},{10,138},{12,140},{14,142}... | collective-permute-start | bytes 1572872 | tf_op jit(solution)/shard_map/ppermute | solution.py:61
  103.3 11.5 %collective-permute-start.19 = (bf16[32,8192]{1,0:T(8,128)(2,1)S(1)}, bf16[32,8192]{1,0:T(8,128)(2,1)S(1)}, u32[]{:S(2)}, u32[]{:S(2)}) collective-permute-start(bf16[32,8192]{1,0:T(8,128)(2,1)S(1)} %combine.6), channel_id=1, source_target_pairs={{0,64},{2,66},{4,68},{6,70},{8,72},{10,74},{12,76},{14,78},{16,18}... | collective-permute-start | bytes 1572872 | tf_op jit(solution)/shard_map/ppermute | solution.py:61
  106.4 9.4 %collective-permute-start.20 = (bf16[32,8192]{1,0:T(8,128)(2,1)S(1)}, bf16[32,8192]{1,0:T(8,128)(2,1)S(1)}, u32[]{:S(2)}, u32[]{:S(2)}) collective-permute-start(bf16[32,8192]{1,0:T(8,128)(2,1)S(1)} %combine.7), channel_id=1, source_target_pairs={{0,192},{2,194},{4,196},{6,198},{8,200},{10,202},{12,204},{14,206}... | collective-permute-start | bytes 1572872 | tf_op jit(solution)/shard_map/ppermute | solution.py:61
  116.1 8.2 %collective-permute-start.21 = (bf16[8,8192]{1,0:T(8,128)(2,1)S(1)}, bf16[8,8192]{1,0:T(8,128)(2,1)S(1)}, u32[]{:S(2)}, u32[]{:S(2)}) collective-permute-start(bf16[8,8192]{1,0:T(8,128)(2,1)S(1)} %get-tuple-element.25), channel_id=1, source_target_pairs={{0,4},{2,6},{4,8},{6,10},{8,12},{10,14},{12,0},{14,2},{16,144},{18... | collective-permute-start | bytes 393224 | tf_op jit(solution)/shard_map/ppermute | solution.py:61
  118.5 7.5 %collective-permute-start.22 = (bf16[8,8192]{1,0:T(8,128)(2,1)S(1)}, bf16[8,8192]{1,0:T(8,128)(2,1)S(1)}, u32[]{:S(2)}, u32[]{:S(2)}) collective-permute-start(bf16[8,8192]{1,0:T(8,128)(2,1)S(1)} %get-tuple-element.27), channel_id=1, source_target_pairs={{0,2},{2,4},{4,6},{6,8},{8,10},{10,12},{12,14},{14,0},{16,80},{18,... | collective-permute-start | bytes 393224 | tf_op jit(solution)/shard_map/ppermute | solution.py:61
  120.0 6.1 %collective-permute-start.23 = (bf16[8,8192]{1,0:T(8,128)(2,1)S(1)}, bf16[8,8192]{1,0:T(8,128)(2,1)S(1)}, u32[]{:S(2)}, u32[]{:S(2)}) collective-permute-start(bf16[8,8192]{1,0:T(8,128)(2,1)S(1)} %get-tuple-element.26), channel_id=1, source_target_pairs={{0,14},{2,0},{4,2},{6,4},{8,6},{10,8},{12,10},{14,12},{16,208},{18... | collective-permute-start | bytes 393224 | tf_op jit(solution)/shard_map/ppermute | solution.py:61
  126.2 8.9 %collective-permute-start.24 = (bf16[2,8192]{1,0:T(2,128)(2,1)S(1)}, bf16[2,8192]{1,0:T(2,128)(2,1)S(1)}, u32[]{:S(2)}, u32[]{:S(2)}) collective-permute-start(bf16[2,8192]{1,0:T(2,128)(2,1)S(1)} %get-tuple-element.28), channel_id=1, source_target_pairs={{0,40},{2,42},{4,44},{6,46},{8,32},{10,34},{12,36},{14,38},{16,56}... | collective-permute-start | bytes 98312 | tf_op jit(solution)/shard_map/ppermute | solution.py:61
  131.3 8.5 %collective-permute-start.25 = (bf16[2,8192]{1,0:T(2,128)(2,1)S(1)}, bf16[2,8192]{1,0:T(2,128)(2,1)S(1)}, u32[]{:S(2)}, u32[]{:S(2)}) collective-permute-start(bf16[2,8192]{1,0:T(2,128)(2,1)S(1)} %get-tuple-element.30), channel_id=1, source_target_pairs={{0,8},{2,10},{4,12},{6,14},{8,0},{10,2},{12,4},{14,6},{16,24},{18,... | collective-permute-start | bytes 98312 | tf_op jit(solution)/shard_map/ppermute | solution.py:61
  132.7 7.0 %collective-permute-start.26 = (bf16[2,8192]{1,0:T(2,128)(2,1)S(1)}, bf16[2,8192]{1,0:T(2,128)(2,1)S(1)}, u32[]{:S(2)}, u32[]{:S(2)}) collective-permute-start(bf16[2,8192]{1,0:T(2,128)(2,1)S(1)} %get-tuple-element.29), channel_id=1, source_target_pairs={{0,32},{2,34},{4,36},{6,38},{8,40},{10,42},{12,44},{14,46},{16,48}... | collective-permute-start | bytes 98312 | tf_op jit(solution)/shard_map/ppermute | solution.py:61

commit v5 on v4

v5 whole, which is shorter than its diff:
```python
import functools

import jax
import jax.numpy as jnp
from jax import lax
from jax.experimental import pallas as pl
from jax.experimental.pallas import tpu as pltpu
from jax.sharding import Mesh
from jax.sharding import PartitionSpec as P

zloss_coef = 0.0001
NY, NX, NC, NZ = 4, 2, 2, 8
GROUP = ("y", "x", "c", "z")
OFFSETS = (0, 1, -1, 2)
BF, F32 = jnp.bfloat16, jnp.float32
ROWS, DEPTH, WIDTH = 256, 8192, 512
CHUNK = 1024
STEPS = DEPTH // CHUNK
VMEM = pl.BlockSpec(memory_space=pltpu.VMEM)
SMEM = pl.BlockSpec(memory_space=pltpu.SMEM)
ANY = pl.BlockSpec(memory_space=pl.ANY)
HBM = pl.BlockSpec(memory_space=pltpu.HBM)


def index_of(y, x, c, z):
    return (((y % NY) * NX + x % NX) * NC + c % NC) * NZ + z % NZ


def pairs(route):
    every = [(y, x, c, z) for y in range(NY) for x in range(NX) for c in range(NC) for z in range(NZ)]
    return [(index_of(*p), index_of(*route(*p))) for p in every]


def to_x(y, x, c, z):
    return y, x + 1, c, z


def to_c(y, x, c, z):
    return y, x, c + 1, z


def to_z4(y, x, c, z):
    return y, x, c, z + 4


def to_xc(y, x, c, z):
    return y, x + 1, c + 1, z


def to_xz4(y, x, c, z):
    return y, x + 1, c, z + 4


def to_first(step):
    return lambda y, x, c, z: (y, x, c, z + step) if c == 0 else (y + step, x, c, z)


def to_second(step):
    return lambda y, x, c, z: (y + step, x, c, z) if c == 0 else (y, x, c, z + step)


def send(value, route):
    return lax.ppermute(value, GROUP, pairs(route))


def params(mib=24):
    return pltpu.CompilerParams(vmem_limit_bytes=mib << 20)


def placed(at_ref):
    y, x, c, z = (at_ref[i] for i in range(4))
    at = lax.broadcasted_iota(jnp.int32, (ROWS, 1), 0)
    r, xr, z4, q1, q2, cr = at & 1, (at >> 1) & 1, (at >> 2) & 1, (at >> 3) & 3, (at >> 5) & 3, at >> 7
    o1 = jnp.where(q1 == 2, -1, jnp.where(q1 == 3, 2, q1))
    o2 = jnp.where(q2 == 2, -1, jnp.where(q2 == 3, 2, q2))
    core = c ^ cr
    zo = jnp.where(core == 0, o1, o2) + 4 * z4
    yo = jnp.where(core == 0, o2, o1)
    rows = ((((y + yo) & 3) * 2 + (x ^ xr)) * 2 + core) * 16 + ((z + zo) & 7) * 2 + r
    return rows == lax.broadcasted_iota(jnp.int32, (ROWS, ROWS), 1)


def hits(at_ref, targets_ref, place):
    own = jnp.sum(jnp.where(place, targets_ref[...], 0), axis=1, keepdims=True) - at_ref[4]
    return lax.broadcasted_iota(jnp.int32, (ROWS, WIDTH), 1) == own


def column_copies(source, target, sems):
    cuts = [pl.ds(k * CHUNK, CHUNK) for k in range(STEPS)]
    return [pltpu.make_async_copy(source.at[:, cut], target.at[:, cut], sems.at[k]) for k, cut in enumerate(cuts)]


def weight_copies(source, target, sems):
    cuts = [pl.ds(k * CHUNK, CHUNK) for k in range(STEPS)]
    copies = [pltpu.make_async_copy(source.at[cut], target.at[cut], sems.at[k]) for k, cut in enumerate(cuts)]
    for copy in copies:
        copy.start()
    return copies


def logits_kernel(at_ref, targets_ref, p0, p1, p2, p3, p4, p5, p6, p7, w_hbm, logits_ref, stats_ref, w_ref, w_sems):
    acc = jnp.zeros((ROWS, WIDTH), F32)
    for k, copy in enumerate(weight_copies(w_hbm, w_ref, w_sems)):
        cut = slice(k * CHUNK, (k + 1) * CHUNK)
        left = jnp.concatenate([p[:, cut] for p in (p0, p1, p2, p3, p4, p5, p6, p7)], axis=0)
        copy.wait()
        acc += jnp.dot(left, w_ref[cut, :], preferred_element_type=F32)
    logits_ref[...] = acc
    top = jnp.max(acc, axis=1, keepdims=True)
    total = jnp.sum(jnp.exp(acc - top), axis=1, keepdims=True)
    place = placed(at_ref)
    picked = jnp.sum(jnp.where(hits(at_ref, targets_ref, place), acc, 0.0), axis=1, keepdims=True)
    for i, column in enumerate((top, total, picked)):
        stats_ref[i : i + 1, :] = jnp.sum(jnp.where(place, column, 0.0), axis=0, keepdims=True)


def products(left, copies, w_ref, pairs):
    for k, copy in enumerate(copies):
        cut = slice(k * CHUNK, (k + 1) * CHUNK)
        copy.wait()
        part = lax.dot_general(left, w_ref[cut, :], (((1,), (1,)), ((), ())), preferred_element_type=F32)
        first = 0
        for buffer, outs in pairs:
            buffer[:, cut] = part[first : first + buffer.shape[0]].astype(buffer.dtype)
            outs[k].start()
            first += buffer.shape[0]
    for _, outs in pairs:
        for copy in outs:
            copy.wait()


def target_kernel(at_ref, targets_ref, w_hbm, own_hbm, other_hbm, w_ref, own_ref, other_ref, w_sems, own_sems, other_sems):
    copies = weight_copies(w_hbm, w_ref, w_sems)
    left = jnp.where(hits(at_ref, targets_ref, placed(at_ref)), 1.0, 0.0).astype(BF)
    own = (own_ref, column_copies(own_ref, own_hbm, own_sems))
    other = (other_ref, column_copies(other_ref, other_hbm, other_sems))
    products(left, copies, w_ref, (own, other))


def soft_kernel(start, at_ref, targets_ref, top_ref, logits_ref, w_hbm, soft_hbm, w_ref, soft_ref, w_sems, soft_sems):
    copies = weight_copies(w_hbm, w_ref, w_sems)
    cut = slice(start, start + ROWS // 2)
    place = placed(at_ref)
    top = jnp.sum(jnp.where(place[cut], top_ref[...], 0.0), axis=1, keepdims=True)
    hit = hits(at_ref, targets_ref, place)[cut]
    left = jnp.where(hit, 0.0, jnp.exp(logits_ref[cut, :] - top)).astype(BF)
    products(left, copies, w_ref, ((soft_ref, column_copies(soft_ref, soft_hbm, soft_sems)),))


def merge_kernel(own_ref, core_ref, x_ref, both_ref, out_ref, top_ref):
    refs = (own_ref, core_ref, x_ref, both_ref)
    tops = [r[0:1, :] for r in refs]
    top = jnp.maximum(jnp.maximum(tops[0], tops[1]), jnp.maximum(tops[2], tops[3]))
    total = sum(r[1:2, :] * jnp.exp(t - top) for r, t in zip(refs, tops))
    picked = sum(r[2:3, :] for r in refs)
    merged = jnp.concatenate([top, total, picked], axis=0)
    for i in range(out_ref.shape[0]):
        out_ref[i] = merged
    top_ref[...] = top


def scales_kernel(at_ref, grad_ref, top_ref, spread_ref, out_ref):
    place = placed(at_ref)[: ROWS // 2]

    def ordered(row):
        return jnp.sum(jnp.where(place, row, 0.0), axis=1, keepdims=True)

    tops = spread_ref[:, 0, :]
    highest = jnp.max(tops, axis=0, keepdims=True)
    total = jnp.sum(spread_ref[:, 1, :] * jnp.exp(tops - highest), axis=0, keepdims=True)
    log_total = ordered(highest + jnp.log(total))
    picked = ordered(jnp.sum(spread_ref[:, 2, :], axis=0, keepdims=True))
    top = ordered(top_ref[...])
    factor = 1.0 + 2.0 * zloss_coef * log_total
    grad = ordered(grad_ref[...])
    scale = grad * factor * jnp.exp(top - log_total)
    target = (grad * (jnp.exp(picked - log_total) * factor - 1.0)).astype(BF).astype(F32)
    lane = lax.broadcasted_iota(jnp.int32, (ROWS // 2, 128), 1)
    out_ref[...] = jnp.where(lane == 0, scale, jnp.where(lane == 1, target, jnp.where(lane == 2, log_total, picked)))


def combine_kernel(parts, scales_ref, soft_own, soft_in, target_own, target_in, *refs):
    outs, (a_ref, b_ref, c_ref, d_ref, sems) = refs[: len(parts)], refs[len(parts) :]
    every = []
    for i, q in enumerate(parts):
        sources = ((soft_own, a_ref), (soft_in, b_ref), (target_own, c_ref), (target_in, d_ref))
        every.append(
            [pltpu.make_async_copy(s.at[pl.ds(32 * q, 32)], t.at[i], sems.at[i, j]) for j, (s, t) in enumerate(sources)]
        )
        for copy in every[-1]:
            copy.start()
    for i, (q, out) in enumerate(zip(parts, outs)):
        for copy in every[i]:
            copy.wait()
        scale, target = scales_ref[32 * q : 32 * q + 32, 0:1], scales_ref[32 * q : 32 * q + 32, 1:2]
        for k in range(0, DEPTH, CHUNK):
            cut = slice(k, k + CHUNK)
            soft = a_ref[i, :, cut] + b_ref[i, :, cut].astype(F32)
            chosen = c_ref[i, :, cut].astype(F32) + d_ref[i, :, cut].astype(F32)
            out[:, cut] = (scale * soft + target * chosen).astype(out.dtype)


def shards(hidden, lm_weight, targets, loss_grad):
    half = ROWS // 2
    at = jnp.stack([lax.axis_index(a) for a in GROUP] + [lax.axis_index(GROUP) * WIDTH])
    targets, loss_grad = targets.reshape(1, ROWS), loss_grad.reshape(1, ROWS)
    lm_weight = pltpu.with_memory_space_constraint(lm_weight, pltpu.HBM)
    weights = [pltpu.VMEM((DEPTH, WIDTH), BF)]
    sems = pltpu.SemaphoreType.DMA((STEPS,))

    block = jnp.concatenate([hidden] + [send(hidden, to) for to in (to_x, to_z4, to_xz4)])
    far, near, back = (send(block, to_first(-o)) for o in (2, 1, -1))
    block = jnp.concatenate([block, near, back, far])
    far, near, back = (send(block, to_second(-o)) for o in (2, 1, -1))

    aim, _ = lax.optimization_barrier((targets, block))
    target_own, target_out = pl.pallas_call(
        target_kernel,
        out_shape=[pltpu.HBM((half, DEPTH), BF)] * 2,
        in_specs=[SMEM, VMEM, ANY],
        out_specs=[HBM] * 2,
        scratch_shapes=weights + [pltpu.VMEM((half, DEPTH), BF)] * 2 + [sems] * 3,
        compiler_params=params(),
        cost_estimate=pl.CostEstimate(flops=2 * ROWS * DEPTH * WIDTH, bytes_accessed=12 << 20, transcendentals=0),
        name="target",
    )(at, aim, lm_weight)
    near, target_own, target_out = lax.optimization_barrier((near, target_own, target_out))
    pieces = [block, near, back, far]
    pieces = pieces + [send(p, to_c) for p in pieces]
    target_in = send(target_out, to_c)

    logits, stats = pl.pallas_call(
        logits_kernel,
        out_shape=(jax.ShapeDtypeStruct((ROWS, WIDTH), F32), jax.ShapeDtypeStruct((3, ROWS), F32)),
        in_specs=[SMEM] + [VMEM] * 9 + [ANY],
        out_specs=(VMEM, VMEM),
        scratch_shapes=weights + [sems],
        compiler_params=params(),
        cost_estimate=pl.CostEstimate(flops=2 * ROWS * DEPTH * WIDTH, bytes_accessed=13 << 20, transcendentals=ROWS * WIDTH),
        name="logits",
    )(at, targets, *pieces, lm_weight)
    stats = [stats] + [send(stats, to) for to in (to_c, to_x, to_xc)]
    merged, top = pl.pallas_call(
        merge_kernel,
        out_shape=(jax.ShapeDtypeStruct((32, 3, ROWS), F32), jax.ShapeDtypeStruct((1, ROWS), F32)),
        in_specs=[VMEM] * 4,
        out_specs=(VMEM, VMEM),
        compiler_params=params(),
        name="merge",
    )(*stats)
    spread = lax.all_to_all(merged, ("y", "z"), 0, 0)

    same_top = send(top, to_c)

    def soft(start, dtype):
        return pl.pallas_call(
            functools.partial(soft_kernel, start),
            out_shape=pltpu.HBM((half, DEPTH), dtype),
            in_specs=[SMEM, VMEM, VMEM, VMEM, ANY],
            out_specs=HBM,
            scratch_shapes=weights + [pltpu.VMEM((half, DEPTH), dtype)] + [sems] * 2,
            compiler_params=params(),
            cost_estimate=pl.CostEstimate(flops=ROWS * DEPTH * WIDTH, bytes_accessed=10 << 20, transcendentals=0),
            name="soft",
        )(at, targets, same_top, logits, lm_weight)

    soft_in = send(soft(half, BF), to_c)
    soft_own = soft(0, F32)
    scales = pl.pallas_call(
        scales_kernel,
        out_shape=jax.ShapeDtypeStruct((half, 128), F32),
        in_specs=[SMEM] + [VMEM] * 3,
        out_specs=VMEM,
        compiler_params=params(),
        name="scales",
    )(at, loss_grad, top, spread)

    def combine(parts, dtype):
        n = len(parts)
        return pl.pallas_call(
            functools.partial(combine_kernel, parts),
            out_shape=[jax.ShapeDtypeStruct((32, DEPTH), dtype)] * n,
            in_specs=[VMEM] + [ANY] * 4,
            out_specs=[VMEM] * n,
            scratch_shapes=[pltpu.VMEM((n, 32, DEPTH), F32)]
            + [pltpu.VMEM((n, 32, DEPTH), BF)] * 3
            + [pltpu.SemaphoreType.DMA((n, 4))],
            compiler_params=params(),
            cost_estimate=pl.CostEstimate(flops=6 * 32 * DEPTH * n, bytes_accessed=n * (3 << 20), transcendentals=0),
            name="combine",
        )(scales, soft_own, soft_in, target_own, target_in)

    far = combine((3,), BF)
    near, back = combine((1, 2), BF)
    arrived = [send(p, to_second(o)).astype(F32) for p, o in ((far[0], 2), (near, 1), (back, -1))]
    part = combine((0,), F32)[0] + sum(arrived)
    log_total, target_logit = scales[:2, 2], scales[:2, 3]
    ce_loss = log_total - target_logit
    z_term = zloss_coef * log_total * log_total

    part = part.reshape(4, 8, DEPTH)
    part = part[0] + sum(send(part[k].astype(BF), to_first(OFFSETS[k])).astype(F32) for k in (3, 1, 2))
    part = [part[0:2]] + [
        send(part[2 * k : 2 * k + 2], to) for k, to in ((3, to_xz4), (2, to_z4), (1, to_x))
    ]
    part = (part[0] + part[1]) + (part[2] + part[3])
    return ce_loss, z_term, part.astype(BF)


def solution(mesh):
    mesh = Mesh(mesh.devices.reshape(NY, NX, NC, NZ, 2), (*GROUP, "dp"))
    own = ("dp", *GROUP)
    in_specs = (P(own, None), P(None, GROUP), P("dp"), P("dp"))
    out_specs = (P(own), P(own), P(own, None))
    return jax.shard_map(shards, mesh=mesh, in_specs=in_specs, out_specs=out_specs, check_vma=False)
```

time: 143 us -> 133 us (0.930)
  Pallas kernels: 46.1 us -> 31.6 us
  waiting for transfers between devices: 37.4 us -> 48.4 us
  local copies, waits for them, and re-layouts: 8.05 us -> 4.24 us
  starting transfers between devices: 45.7 us -> 43.2 us
    pallas_call x8 -> x7, Pallas kernels: 36.4 us -> 25.6 us  [the longest x2 13 us: soft(): pl.pallas_call(functools.partial(soft_kernel, start), out_shape=pltpu.HBM...]
    ppermute x27 -> x28, waiting for transfers between devices: 36.5 us -> 44.2 us  [send(): return lax.ppermute(value, GROUP, pairs(route))]
    unnamed x14 -> x10, local copies, waits for them, and re-layouts: 6.67 us -> 2.87 us
    pallas_call x1, Pallas kernels: 8.51 us -> 5.25 us  [shards(): pl.pallas_call(logits_kernel, out_shape=(jax.ShapeDtypeStruct((ROWS, WIDT...]
    all_to_all x1, waiting for transfers between devices: 0.9 us -> 4.16 us  [shards(): spread = lax.all_to_all(merged, ('y', 'z'), 0, 0)]
    ppermute x27 -> x28, starting transfers between devices: 39 us -> 36.8 us  [send(): return lax.ppermute(value, GROUP, pairs(route))]
  transfers between devices with their start and end apart: 28 -> 29, of which waited for: 17 -> 19; matrix products, arithmetic and copies ran while one was open for 1% -> 1% of each run, Pallas kernels for 25% -> 18%
where the time goes in v5:
time: 133 us; the launch traced here: 131 us
  waiting for transfers between devices  48.4 us (36%)
  starting transfers between devices  43.2 us (32%)
  Pallas kernels  31.6 us (24%)
  local copies, waits for them, and re-layouts  4.24 us (3%)
  other arithmetic  2.39 us (2%)
    ppermute x28, waiting for transfers between devices, send(): return lax.ppermute(value, GROUP, pairs(route))  44.2 us
    ppermute x28, starting transfers between devices, send(): return lax.ppermute(value, GROUP, pairs(route))  36.8 us
    pallas_call x2, Pallas kernels, soft(): pl.pallas_call(functools.partial(soft_kernel, start), out_shape=pltpu.HBM...  13 us
    pallas_call x1, Pallas kernels, shards(): pl.pallas_call(target_kernel, out_shape=[pltpu.HBM((half, DEPTH), BF)] *...  6.56 us
    all_to_all x1, starting transfers between devices, shards(): spread = lax.all_to_all(merged, ('y', 'z'), 0, 0)  6.39 us
    pallas_call x3, Pallas kernels, combine(): pl.pallas_call(functools.partial(combine_kernel, parts), out_shape=[jax.S...  5.33 us
    pallas_call x1, Pallas kernels, shards(): pl.pallas_call(logits_kernel, out_shape=(jax.ShapeDtypeStruct((ROWS, WIDT...  5.25 us
    all_to_all x1, waiting for transfers between devices, shards(): spread = lax.all_to_all(merged, ('y', 'z'), 0, 0)  4.16 us
  transfers between devices with their start and end apart: 29, of which 19 were waited for; matrix products, arithmetic and copies ran while one was open for 1% of the time, Pallas kernels for 18%

profile of v5, /device:TPU:4, one launch (start us, length us, event | category | flops | bytes accessed | tf_op | source)
XLA Modules:
  0.0 130.7 jit_solution(3282601445046302476)
XLA Ops:
  0.6 1.3 collective-permute-start
  1.9 7.2 %collective-permute-start.1 = (bf16[2,8192]{1,0:T(2,128)(2,1)}, bf16[2,8192]{1,0:T(2,128)(2,1)S(1)}, u32[]{:S(2)}, u32[]{:S(2)}) collective-permute-start(bf16[2,8192]{1,0:T(2,128)(2,1)} %param.4), channel_id=1, source_target_pairs={{0,8},{2,10},{4,12},{6,14},{8,0},{10,2},{12,4},{14,6},{16,24},{18,... | collective-permute-start | bytes 98312 | tf_op jit(solution)/shard_map/ppermute | solution.py:63
  9.1 0.3 collective-permute-start.2
  9.4 1.9 %collective-permute-done.1 = bf16[2,8192]{1,0:T(2,128)(2,1)S(1)} collective-permute-done((bf16[2,8192]{1,0:T(2,128)(2,1)}, bf16[2,8192]{1,0:T(2,128)(2,1)S(1)}, u32[]{:S(2)}, u32[]{:S(2)}) %collective-permute-start.1) | collective-permute-done | bytes 32800 | tf_op jit(solution)/shard_map/ppermute | solution.py:63
  11.2 6.8 %collective-permute-done.2 = bf16[2,8192]{1,0:T(2,128)(2,1)S(1)} collective-permute-done((bf16[2,8192]{1,0:T(2,128)(2,1)}, bf16[2,8192]{1,0:T(2,128)(2,1)S(1)}, u32[]{:S(2)}, u32[]{:S(2)}) %collective-permute-start.2) | collective-permute-done | bytes 32800 | tf_op jit(solution)/shard_map/ppermute | solution.py:63
  18.0 0.9 pad_maximum_fusion
  18.9 0.2 collective-permute-start.3
  19.1 1.9 %collective-permute-start.4 = (bf16[8,8192]{1,0:T(8,128)(2,1)S(1)}, bf16[8,8192]{1,0:T(8,128)(2,1)S(1)}, u32[]{:S(2)}, u32[]{:S(2)}) collective-permute-start(bf16[8,8192]{1,0:T(8,128)(2,1)S(1)} %pad_maximum_fusion), channel_id=1, source_target_pairs={{0,2},{2,4},{4,6},{6,8},{8,10},{10,12},{12,14},{14,0},{16,80},{18,... | collective-permute-start | bytes 393224 | tf_op jit(solution)/shard_map/ppermute | solution.py:63
  21.1 0.1 collective-permute-start.5
  21.1 2.9 %collective-permute-done.3 = bf16[8,8192]{1,0:T(8,128)(2,1)S(1)} collective-permute-done((bf16[8,8192]{1,0:T(8,128)(2,1)S(1)}, bf16[8,8192]{1,0:T(8,128)(2,1)S(1)}, u32[]{:S(2)}, u32[]{:S(2)}) %collective-permute-start.3) | collective-permute-done | bytes 131104 | tf_op jit(solution)/shard_map/ppermute | solution.py:63
  24.0 1.3 %collective-permute-done.4 = bf16[8,8192]{1,0:T(8,128)(2,1)S(1)} collective-permute-done((bf16[8,8192]{1,0:T(8,128)(2,1)S(1)}, bf16[8,8192]{1,0:T(8,128)(2,1)S(1)}, u32[]{:S(2)}, u32[]{:S(2)}) %collective-permute-start.4) | collective-permute-done | bytes 131104 | tf_op jit(solution)/shard_map/ppermute | solution.py:63
  25.3 3.0 %collective-permute-done.5 = bf16[8,8192]{1,0:T(8,128)(2,1)S(1)} collective-permute-done((bf16[8,8192]{1,0:T(8,128)(2,1)S(1)}, bf16[8,8192]{1,0:T(8,128)(2,1)S(1)}, u32[]{:S(2)}, u32[]{:S(2)}) %collective-permute-start.5) | collective-permute-done | bytes 131104 | tf_op jit(solution)/shard_map/ppermute | solution.py:63
  28.3 1.0 concatenate.8.p0
  29.3 3.1 %collective-permute-start.6 = (bf16[32,8192]{1,0:T(8,128)(2,1)S(1)}, bf16[32,8192]{1,0:T(8,128)(2,1)S(1)}, u32[]{:S(2)}, u32[]{:S(2)}) collective-permute-start(bf16[32,8192]{1,0:T(8,128)(2,1)S(1)} %concatenate.8.p0), channel_id=1, source_target_pairs={{0,192},{2,194},{4,196},{6,198},{8,200},{10,202},{12,204},{14,206}... | collective-permute-start | bytes 1572872 | tf_op jit(solution)/shard_map/ppermute | solution.py:63
  32.4 2.4 %collective-permute-start.8 = (bf16[32,8192]{1,0:T(8,128)(2,1)S(1)}, bf16[32,8192]{1,0:T(8,128)(2,1)S(1)}, u32[]{:S(2)}, u32[]{:S(2)}) collective-permute-start(bf16[32,8192]{1,0:T(8,128)(2,1)S(1)} %concatenate.8.p0), channel_id=1, source_target_pairs={{0,128},{2,130},{4,132},{6,134},{8,136},{10,138},{12,140},{14,142}... | collective-permute-start | bytes 1572872 | tf_op jit(solution)/shard_map/ppermute | solution.py:63
  34.8 0.1 stack.23.at_ref
  34.9 0.7 copy-done.2
  35.6 6.6 %target.1 = (bf16[128,8192]{1,0:T(8,128)(2,1)}, bf16[128,8192]{1,0:T(8,128)(2,1)}) custom-call(s32[5]{0:T(128)S(1)} %stack.23.at_ref, s32[1,256]{1,0:T(1,128)S(1)} %bitcast.7, bf16[8192,512]{1,0:T(8,128)(2,1)} %w_hbm.7), custom_call_target="tpu_custom_call" | custom-call | flops 2147483648 | bytes 12582912 | tf_op jit(solution)/shard_map/target/pallas_call | solution.py:217
  42.2 2.5 %collective-permute-done.6.p1 = bf16[32,8192]{1,0:T(8,128)(2,1)S(1)} collective-permute-done((bf16[32,8192]{1,0:T(8,128)(2,1)S(1)}, bf16[32,8192]{1,0:T(8,128)(2,1)S(1)}, u32[]{:S(2)}, u32[]{:S(2)}) %collective-permute-start.6) | collective-permute-done | bytes 524320 | tf_op jit(solution)/shard_map/ppermute | solution.py:63
  44.7 3.7 %collective-permute-done.7.p2 = bf16[32,8192]{1,0:T(8,128)(2,1)S(1)} collective-permute-done((bf16[32,8192]{1,0:T(8,128)(2,1)S(1)}, bf16[32,8192]{1,0:T(8,128)(2,1)S(1)}, u32[]{:S(2)}, u32[]{:S(2)}) %collective-permute-start.7) | collective-permute-done | bytes 524320 | tf_op jit(solution)/shard_map/ppermute | solution.py:63
  48.4 0.5 collective-permute-start.12
  48.9 1.4 %collective-permute-done.11.p6 = bf16[32,8192]{1,0:T(8,128)(2,1)S(1)} collective-permute-done((bf16[32,8192]{1,0:T(8,128)(2,1)S(1)}, bf16[32,8192]{1,0:T(8,128)(2,1)S(1)}, u32[]{:S(2)}, u32[]{:S(2)}) %collective-permute-start.11) | collective-permute-done | bytes 524320 | tf_op jit(solution)/shard_map/ppermute | solution.py:63
  50.3 0.7 collective-permute-done.12.p7
  51.1 5.2 %logits.1 = (f32[256,512]{1,0:T(8,128)S(1)}, f32[3,256]{1,0:T(4,128)S(1)}) custom-call(s32[5]{0:T(128)S(1)} %stack.23.at_ref, s32[1,256]{1,0:T(1,128)S(1)} %bitcast.8, bf16[32,8192]{1,0:T(8,128)(2,1)S(1)} %concatenate.8.p0, bf16[32,8192]{1,0:T(8,128)(2,1)S(1)} %collective-permute-done.6.p1, bf16[32,8192]{1,0:T(8,128)(2,1)S(1)} %collective-permute-done.7.p2, ...), custom_call_target="tpu_custom_call" | custom-call | flops 2147483648 | bytes 13631488 | tf_op jit(solution)/shard_map/logits/pallas_call | solution.py:232
  56.3 0.2 collective-permute-start.13
  56.5 1.0 collective-permute-start.14
  57.5 0.7 collective-permute-start.15
  58.3 1.9 %collective-permute-done.14.x_ref = f32[3,256]{1,0:T(4,128)S(1)} collective-permute-done((f32[3,256]{1,0:T(4,128)S(1)}, f32[3,256]{1,0:T(4,128)S(1)}, u32[]{:S(2)}, u32[]{:S(2)}) %collective-permute-start.14) | collective-permute-done | bytes 3104 | tf_op jit(solution)/shard_map/ppermute | solution.py:63
  60.2 0.4 collective-permute-done.15.both_ref
  60.6 0.7 merge.1
  61.2 0.1 collective-permute-start.16
  61.4 0.4 collective-permute-start.18
  61.8 0.6 collective-permute-done.16.top_ref
  62.4 6.4 %soft.3 = bf16[128,8192]{1,0:T(8,128)(2,1)} custom-call(s32[5]{0:T(128)S(1)} %stack.23.at_ref, s32[1,256]{1,0:T(1,128)S(1)} %bitcast.9, f32[1,256]{1,0:T(1,128)S(1)} %collective-permute-done.16.top_ref, f32[256,512]{1,0:T(8,128)S(1)} %get-tuple-element.22.logits_ref, bf16[8192,512]{1,0:T(8,128)(2,1)} %w_hbm.7), custom_call_target="tpu_custom_call" | custom-call | flops 1073741824 | bytes 10485760 | tf_op jit(solution)/shard_map/soft/pallas_call | solution.py:256
  68.8 0.3 collective-permute-start.17
  69.1 6.4 %all-to-all-start = ((f32[32,3,256]{2,1,0:T(4,128)}), f32[32,3,256]{2,1,0:T(4,128)S(1)}, u32[]{:S(2)}, u32[]{:S(2)}) async-start(f32[32,3,256]{2,1,0:T(4,128)} %get-tuple-element.21), calls=%async_computation | async-start | bytes 262144 | tf_op jit(solution)/shard_map/all_to_all | solution.py:251
  75.5 6.6 %soft.2.soft_own = f32[128,8192]{1,0:T(8,128)} custom-call(s32[5]{0:T(128)S(1)} %stack.23.at_ref, s32[1,256]{1,0:T(1,128)S(1)} %bitcast.10, f32[1,256]{1,0:T(1,128)S(1)} %collective-permute-done.16.top_ref, f32[256,512]{1,0:T(8,128)S(1)} %get-tuple-element.22.logits_ref, bf16[8192,512]{1,0:T(8,128)(2,1)} %w_hbm.7), custom_call_target="tpu_custom_call" | custom-call | flops 1073741824 | bytes 10485760 | tf_op jit(solution)/shard_map/soft/pallas_call | solution.py:256
  82.1 4.2 %all-to-all-done.spread_ref = f32[32,3,256]{2,1,0:T(4,128)S(1)} async-done(((f32[32,3,256]{2,1,0:T(4,128)}), f32[32,3,256]{2,1,0:T(4,128)S(1)}, u32[]{:S(2)}, u32[]{:S(2)}) %all-to-all-start) | async-done | bytes 98336 | tf_op jit(solution)/shard_map/all_to_all | solution.py:251
  86.3 0.8 scales.1.scales_ref
  87.1 2.2 %copy-done = f32[128,8192]{1,0:T(8,128)S(1)} copy-done((f32[128,8192]{1,0:T(8,128)S(1)}, f32[128,8192]{1,0:T(8,128)}, u32[]{:S(2)}) %copy-start) | copy-done | bytes 4194328
  89.3 1.6 %combine.4 = bf16[32,8192]{1,0:T(8,128)(2,1)S(1)} custom-call(f32[128,128]{1,0:T(8,128)S(1)} %scales.1.scales_ref, f32[128,8192]{1,0:T(8,128)S(1)} %copy-done, bf16[128,8192]{1,0:T(8,128)(2,1)} %collective-permute-done.17.soft_in, bf16[128,8192]{1,0:T(8,128)(2,1)S(1)} %copy-done.1, bf16[128,8192]{1,0:T(8,128)(2,1)} %collective-permute-done.18.target_in), custom_call_target="tpu_custom_call" | custom-call | flops 1572864 | bytes 3145728 | tf_op jit(solution)/shard_map/combine/pallas_call | solution.py:280
  91.0 1.5 %collective-permute-start.19 = (bf16[32,8192]{1,0:T(8,128)(2,1)S(1)}, bf16[32,8192]{1,0:T(8,128)(2,1)S(1)}, u32[]{:S(2)}, u32[]{:S(2)}) collective-permute-start(bf16[32,8192]{1,0:T(8,128)(2,1)S(1)} %combine.4), channel_id=1, source_target_pairs={{0,128},{2,130},{4,132},{6,134},{8,136},{10,138},{12,140},{14,142}... | collective-permute-start | bytes 1572872 | tf_op jit(solution)/shard_map/ppermute | solution.py:63
  92.5 2.0 %combine.5 = (bf16[32,8192]{1,0:T(8,128)(2,1)S(1)}, bf16[32,8192]{1,0:T(8,128)(2,1)S(1)}) custom-call(f32[128,128]{1,0:T(8,128)S(1)} %scales.1.scales_ref, f32[128,8192]{1,0:T(8,128)S(1)} %copy-done, bf16[128,8192]{1,0:T(8,128)(2,1)} %collective-permute-done.17.soft_in, bf16[128,8192]{1,0:T(8,128)(2,1)S(1)} %copy-done.1, ...), custom_call_target="tpu_custom_call" | custom-call | flops 3145728 | bytes 6291456 | tf_op jit(solution)/shard_map/combine/pallas_call | solution.py:280
  94.5 0.9 collective-permute-start.20
  95.4 2.7 %collective-permute-start.21 = (bf16[32,8192]{1,0:T(8,128)(2,1)S(1)}, bf16[32,8192]{1,0:T(8,128)(2,1)S(1)}, u32[]{:S(2)}, u32[]{:S(2)}) collective-permute-start(bf16[32,8192]{1,0:T(8,128)(2,1)S(1)} %get-tuple-element.26), channel_id=1, source_target_pairs={{0,192},{2,194},{4,196},{6,198},{8,200},{10,202},{12,204},{14,206}... | collective-permute-start | bytes 1572872 | tf_op jit(solution)/shard_map/ppermute | solution.py:63
  98.1 1.6 %combine.3 = f32[32,8192]{1,0:T(8,128)S(1)} custom-call(f32[128,128]{1,0:T(8,128)S(1)} %scales.1.scales_ref, f32[128,8192]{1,0:T(8,128)S(1)} %copy-done, bf16[128,8192]{1,0:T(8,128)(2,1)} %collective-permute-done.17.soft_in, bf16[128,8192]{1,0:T(8,128)(2,1)S(1)} %copy-done.1, bf16[128,8192]{1,0:T(8,128)(2,1)} %collective-permute-done.18.target_in), custom_call_target="tpu_custom_call" | custom-call | flops 1572864 | bytes 3145728 | tf_op jit(solution)/shard_map/combine/pallas_call | solution.py:280
  99.7 2.1 %collective-permute-done.19 = bf16[32,8192]{1,0:T(8,128)(2,1)S(1)} collective-permute-done((bf16[32,8192]{1,0:T(8,128)(2,1)S(1)}, bf16[32,8192]{1,0:T(8,128)(2,1)S(1)}, u32[]{:S(2)}, u32[]{:S(2)}) %collective-permute-start.19) | collective-permute-done | bytes 524320 | tf_op jit(solution)/shard_map/ppermute | solution.py:63
  101.8 5.5 %collective-permute-done.20 = bf16[32,8192]{1,0:T(8,128)(2,1)S(1)} collective-permute-done((bf16[32,8192]{1,0:T(8,128)(2,1)S(1)}, bf16[32,8192]{1,0:T(8,128)(2,1)S(1)}, u32[]{:S(2)}, u32[]{:S(2)}) %collective-permute-start.20) | collective-permute-done | bytes 524320 | tf_op jit(solution)/shard_map/ppermute | solution.py:63
  107.4 0.2 fusion.2
  107.6 1.3 %collective-permute-start.22 = (bf16[8,8192]{1,0:T(8,128)(2,1)S(1)}, bf16[8,8192]{1,0:T(8,128)(2,1)S(1)}, u32[]{:S(2)}, u32[]{:S(2)}) collective-permute-start(bf16[8,8192]{1,0:T(8,128)(2,1)S(1)} %get-tuple-element.31), channel_id=1, source_target_pairs={{0,4},{2,6},{4,8},{6,10},{8,12},{10,14},{12,0},{14,2},{16,144},{18... | collective-permute-start | bytes 393224 | tf_op jit(solution)/shard_map/ppermute | solution.py:63
  109.0 0.7 collective-permute-start.23
  109.6 2.6 %collective-permute-start.24 = (bf16[8,8192]{1,0:T(8,128)(2,1)S(1)}, bf16[8,8192]{1,0:T(8,128)(2,1)S(1)}, u32[]{:S(2)}, u32[]{:S(2)}) collective-permute-start(bf16[8,8192]{1,0:T(8,128)(2,1)S(1)} %get-tuple-element.32), channel_id=1, source_target_pairs={{0,14},{2,0},{4,2},{6,4},{8,6},{10,8},{12,10},{14,12},{16,208},{18... | collective-permute-start | bytes 393224 | tf_op jit(solution)/shard_map/ppermute | solution.py:63
  112.2 0.2 slice_reduce_fusion
  112.4 2.5 %collective-permute-done.22 = bf16[8,8192]{1,0:T(8,128)(2,1)S(1)} collective-permute-done((bf16[8,8192]{1,0:T(8,128)(2,1)S(1)}, bf16[8,8192]{1,0:T(8,128)(2,1)S(1)}, u32[]{:S(2)}, u32[]{:S(2)}) %collective-permute-start.22) | collective-permute-done | bytes 131104 | tf_op jit(solution)/shard_map/ppermute | solution.py:63
  114.9 2.4 %collective-permute-done.23 = bf16[8,8192]{1,0:T(8,128)(2,1)S(1)} collective-permute-done((bf16[8,8192]{1,0:T(8,128)(2,1)S(1)}, bf16[8,8192]{1,0:T(8,128)(2,1)S(1)}, u32[]{:S(2)}, u32[]{:S(2)}) %collective-permute-start.23) | collective-permute-done | bytes 131104 | tf_op jit(solution)/shard_map/ppermute | solution.py:63
  117.3 0.1 slice_add_fusion
  117.4 0.1 fusion.4
  117.5 1.6 %collective-permute-start.25 = (f32[2,8192]{1,0:T(2,128)S(1)}, f32[2,8192]{1,0:T(2,128)S(1)}, u32[]{:S(2)}, u32[]{:S(2)}) collective-permute-start(f32[2,8192]{1,0:T(2,128)S(1)} %get-tuple-element.36), channel_id=1, source_target_pairs={{0,40},{2,42},{4,44},{6,46},{8,32},{10,34},{12,36},{14,38},{16,56}... | collective-permute-start | bytes 196616 | tf_op jit(solution)/shard_map/ppermute | solution.py:63
  119.1 4.9 %collective-permute-start.26 = (f32[2,8192]{1,0:T(2,128)S(1)}, f32[2,8192]{1,0:T(2,128)S(1)}, u32[]{:S(2)}, u32[]{:S(2)}) collective-permute-start(f32[2,8192]{1,0:T(2,128)S(1)} %get-tuple-element.35), channel_id=1, source_target_pairs={{0,8},{2,10},{4,12},{6,14},{8,0},{10,2},{12,4},{14,6},{16,24},{18,... | collective-permute-start | bytes 196616 | tf_op jit(solution)/shard_map/ppermute | solution.py:63
  124.0 1.0 collective-permute-start.27
  125.0 0.5 multiply_multiply_fusion
  125.5 2.4 %collective-permute-done.25 = f32[2,8192]{1,0:T(2,128)S(1)} collective-permute-done((f32[2,8192]{1,0:T(2,128)S(1)}, f32[2,8192]{1,0:T(2,128)S(1)}, u32[]{:S(2)}, u32[]{:S(2)}) %collective-permute-start.25) | collective-permute-done | bytes 65568 | tf_op jit(solution)/shard_map/ppermute | solution.py:63
  127.9 2.1 %collective-permute-done.26 = f32[2,8192]{1,0:T(2,128)S(1)} collective-permute-done((f32[2,8192]{1,0:T(2,128)S(1)}, f32[2,8192]{1,0:T(2,128)S(1)}, u32[]{:S(2)}, u32[]{:S(2)}) %collective-permute-start.26) | collective-permute-done | bytes 65568 | tf_op jit(solution)/shard_map/ppermute | solution.py:63
  130.0 0.7 fusion.1
  (23 shorter events, 0.1 us)
Async XLA Ops:
  0.6 8.7 %collective-permute-start = (bf16[2,8192]{1,0:T(2,128)(2,1)}, bf16[2,8192]{1,0:T(2,128)(2,1)S(1)}, u32[]{:S(2)}, u32[]{:S(2)}) collective-permute-start(bf16[2,8192]{1,0:T(2,128)(2,1)} %param.4), channel_id=1, source_target_pairs={{0,32},{2,34},{4,36},{6,38},{8,40},{10,42},{12,44},{14,46},{16,48}... | collective-permute-start | bytes 98312 | tf_op jit(solution)/shard_map/ppermute | solution.py:63
  1.9 9.3 %collective-permute-start.1 = (bf16[2,8192]{1,0:T(2,128)(2,1)}, bf16[2,8192]{1,0:T(2,128)(2,1)S(1)}, u32[]{:S(2)}, u32[]{:S(2)}) collective-permute-start(bf16[2,8192]{1,0:T(2,128)(2,1)} %param.4), channel_id=1, source_target_pairs={{0,8},{2,10},{4,12},{6,14},{8,0},{10,2},{12,4},{14,6},{16,24},{18,... | collective-permute-start | bytes 98312 | tf_op jit(solution)/shard_map/ppermute | solution.py:63
  9.1 8.9 %collective-permute-start.2 = (bf16[2,8192]{1,0:T(2,128)(2,1)}, bf16[2,8192]{1,0:T(2,128)(2,1)S(1)}, u32[]{:S(2)}, u32[]{:S(2)}) collective-permute-start(bf16[2,8192]{1,0:T(2,128)(2,1)} %param.4), channel_id=1, source_target_pairs={{0,40},{2,42},{4,44},{6,46},{8,32},{10,34},{12,36},{14,38},{16,56}... | collective-permute-start | bytes 98312 | tf_op jit(solution)/shard_map/ppermute | solution.py:63
  18.9 5.0 %collective-permute-start.3 = (bf16[8,8192]{1,0:T(8,128)(2,1)S(1)}, bf16[8,8192]{1,0:T(8,128)(2,1)S(1)}, u32[]{:S(2)}, u32[]{:S(2)}) collective-permute-start(bf16[8,8192]{1,0:T(8,128)(2,1)S(1)} %pad_maximum_fusion), channel_id=1, source_target_pairs={{0,14},{2,0},{4,2},{6,4},{8,6},{10,8},{12,10},{14,12},{16,208},{18... | collective-permute-start | bytes 393224 | tf_op jit(solution)/shard_map/ppermute | solution.py:63
  19.1 6.2 %collective-permute-start.4 = (bf16[8,8192]{1,0:T(8,128)(2,1)S(1)}, bf16[8,8192]{1,0:T(8,128)(2,1)S(1)}, u32[]{:S(2)}, u32[]{:S(2)}) collective-permute-start(bf16[8,8192]{1,0:T(8,128)(2,1)S(1)} %pad_maximum_fusion), channel_id=1, source_target_pairs={{0,2},{2,4},{4,6},{6,8},{8,10},{10,12},{12,14},{14,0},{16,80},{18,... | collective-permute-start | bytes 393224 | tf_op jit(solution)/shard_map/ppermute | solution.py:63
  21.1 7.3 %collective-permute-start.5 = (bf16[8,8192]{1,0:T(8,128)(2,1)S(1)}, bf16[8,8192]{1,0:T(8,128)(2,1)S(1)}, u32[]{:S(2)}, u32[]{:S(2)}) collective-permute-start(bf16[8,8192]{1,0:T(8,128)(2,1)S(1)} %pad_maximum_fusion), channel_id=1, source_target_pairs={{0,12},{2,14},{4,0},{6,2},{8,4},{10,6},{12,8},{14,10},{16,144},{18... | collective-permute-start | bytes 393224 | tf_op jit(solution)/shard_map/ppermute | solution.py:63
  29.3 15.4 %collective-permute-start.6 = (bf16[32,8192]{1,0:T(8,128)(2,1)S(1)}, bf16[32,8192]{1,0:T(8,128)(2,1)S(1)}, u32[]{:S(2)}, u32[]{:S(2)}) collective-permute-start(bf16[32,8192]{1,0:T(8,128)(2,1)S(1)} %concatenate.8.p0), channel_id=1, source_target_pairs={{0,192},{2,194},{4,196},{6,198},{8,200},{10,202},{12,204},{14,206}... | collective-permute-start | bytes 1572872 | tf_op jit(solution)/shard_map/ppermute | solution.py:63
  32.4 16.0 %collective-permute-start.7 = (bf16[32,8192]{1,0:T(8,128)(2,1)S(1)}, bf16[32,8192]{1,0:T(8,128)(2,1)S(1)}, u32[]{:S(2)}, u32[]{:S(2)}) collective-permute-start(bf16[32,8192]{1,0:T(8,128)(2,1)S(1)} %concatenate.8.p0), channel_id=1, source_target_pairs={{0,64},{2,66},{4,68},{6,70},{8,72},{10,74},{12,76},{14,78},{16,18}... | collective-permute-start | bytes 1572872 | tf_op jit(solution)/shard_map/ppermute | solution.py:63
  32.4 16.0 %collective-permute-start.8 = (bf16[32,8192]{1,0:T(8,128)(2,1)S(1)}, bf16[32,8192]{1,0:T(8,128)(2,1)S(1)}, u32[]{:S(2)}, u32[]{:S(2)}) collective-permute-start(bf16[32,8192]{1,0:T(8,128)(2,1)S(1)} %concatenate.8.p0), channel_id=1, source_target_pairs={{0,128},{2,130},{4,132},{6,134},{8,136},{10,138},{12,140},{14,142}... | collective-permute-start | bytes 1572872 | tf_op jit(solution)/shard_map/ppermute | solution.py:63
  34.9 14.0 %collective-permute-start.9 = (bf16[32,8192]{1,0:T(8,128)(2,1)S(1)}, bf16[32,8192]{1,0:T(8,128)(2,1)S(1)}, u32[]{:S(2)}, u32[]{:S(2)}) collective-permute-start(bf16[32,8192]{1,0:T(8,128)(2,1)S(1)} %concatenate.8.p0), channel_id=1, source_target_pairs={{0,16},{2,18},{4,20},{6,22},{8,24},{10,26},{12,28},{14,30},{16,0},... | collective-permute-start | bytes 1572872 | tf_op jit(solution)/shard_map/ppermute | solution.py:63
  34.9 0.7 copy-start.2
  35.6 15.5 %copy-start.3 = (s32[256]{0:T(256)S(1)}, s32[256]{0:T(256)}, u32[]{:S(2)}) copy-start(s32[256]{0:T(256)} %param.6) | copy-start | bytes 3076
  44.7 4.2 %collective-permute-start.10 = (bf16[32,8192]{1,0:T(8,128)(2,1)S(1)}, bf16[32,8192]{1,0:T(8,128)(2,1)S(1)}, u32[]{:S(2)}, u32[]{:S(2)}) collective-permute-start(bf16[32,8192]{1,0:T(8,128)(2,1)S(1)} %collective-permute-done.6.p1), channel_id=1, source_target_pairs={{0,16},{2,18},{4,20},{6,22},{8,24},{10,26},{12,28},{14,30},{16,0},... | collective-permute-start | bytes 1572872 | tf_op jit(solution)/shard_map/ppermute | solution.py:63
  48.4 1.9 %collective-permute-start.11 = (bf16[32,8192]{1,0:T(8,128)(2,1)S(1)}, bf16[32,8192]{1,0:T(8,128)(2,1)S(1)}, u32[]{:S(2)}, u32[]{:S(2)}) collective-permute-start(bf16[32,8192]{1,0:T(8,128)(2,1)S(1)} %collective-permute-done.7.p2), channel_id=1, source_target_pairs={{0,16},{2,18},{4,20},{6,22},{8,24},{10,26},{12,28},{14,30},{16,0},... | collective-permute-start | bytes 1572872 | tf_op jit(solution)/shard_map/ppermute | solution.py:63
  48.4 2.7 %collective-permute-start.12 = (bf16[32,8192]{1,0:T(8,128)(2,1)S(1)}, bf16[32,8192]{1,0:T(8,128)(2,1)S(1)}, u32[]{:S(2)}, u32[]{:S(2)}) collective-permute-start(bf16[32,8192]{1,0:T(8,128)(2,1)S(1)} %collective-permute-done.8.p3), channel_id=1, source_target_pairs={{0,16},{2,18},{4,20},{6,22},{8,24},{10,26},{12,28},{14,30},{16,0},... | collective-permute-start | bytes 1572872 | tf_op jit(solution)/shard_map/ppermute | solution.py:63
  56.3 2.0 %collective-permute-start.13 = (f32[3,256]{1,0:T(4,128)S(1)}, f32[3,256]{1,0:T(4,128)S(1)}, u32[]{:S(2)}, u32[]{:S(2)}) collective-permute-start(f32[3,256]{1,0:T(4,128)S(1)} %get-tuple-element.19.own_ref), channel_id=1, source_target_pairs={{0,16},{2,18},{4,20},{6,22},{8,24},{10,26},{12,28},{14,30},{16,0},... | collective-permute-start | bytes 9224 | tf_op jit(solution)/shard_map/ppermute | solution.py:63
  56.5 3.6 %collective-permute-start.14 = (f32[3,256]{1,0:T(4,128)S(1)}, f32[3,256]{1,0:T(4,128)S(1)}, u32[]{:S(2)}, u32[]{:S(2)}) collective-permute-start(f32[3,256]{1,0:T(4,128)S(1)} %get-tuple-element.19.own_ref), channel_id=1, source_target_pairs={{0,32},{2,34},{4,36},{6,38},{8,40},{10,42},{12,44},{14,46},{16,48}... | collective-permute-start | bytes 9224 | tf_op jit(solution)/shard_map/ppermute | solution.py:63
  57.5 3.0 %collective-permute-start.15 = (f32[3,256]{1,0:T(4,128)S(1)}, f32[3,256]{1,0:T(4,128)S(1)}, u32[]{:S(2)}, u32[]{:S(2)}) collective-permute-start(f32[3,256]{1,0:T(4,128)S(1)} %get-tuple-element.19.own_ref), channel_id=1, source_target_pairs={{0,48},{2,50},{4,52},{6,54},{8,56},{10,58},{12,60},{14,62},{16,32}... | collective-permute-start | bytes 9224 | tf_op jit(solution)/shard_map/ppermute | solution.py:63
  61.2 1.1 collective-permute-start.16
  61.4 25.7 %collective-permute-start.18 = (bf16[128,8192]{1,0:T(8,128)(2,1)}, bf16[128,8192]{1,0:T(8,128)(2,1)}, u32[]{:S(2)}, u32[]{:S(2)}) collective-permute-start(bf16[128,8192]{1,0:T(8,128)(2,1)} %get-tuple-element.24), channel_id=1, source_target_pairs={{0,16},{2,18},{4,20},{6,22},{8,24},{10,26},{12,28},{14,30},{16,0},... | collective-permute-start | bytes 6291464 | tf_op jit(solution)/shard_map/ppermute | solution.py:63
  68.8 18.3 %collective-permute-start.17 = (bf16[128,8192]{1,0:T(8,128)(2,1)}, bf16[128,8192]{1,0:T(8,128)(2,1)}, u32[]{:S(2)}, u32[]{:S(2)}) collective-permute-start(bf16[128,8192]{1,0:T(8,128)(2,1)} %soft.3), channel_id=1, source_target_pairs={{0,16},{2,18},{4,20},{6,22},{8,24},{10,26},{12,28},{14,30},{16,0},... | collective-permute-start | bytes 6291464 | tf_op jit(solution)/shard_map/ppermute | solution.py:63
  69.1 17.2 %all-to-all-start = ((f32[32,3,256]{2,1,0:T(4,128)}), f32[32,3,256]{2,1,0:T(4,128)S(1)}, u32[]{:S(2)}, u32[]{:S(2)}) async-start(f32[32,3,256]{2,1,0:T(4,128)} %get-tuple-element.21), calls=%async_computation | async-start | bytes 262144 | tf_op jit(solution)/shard_map/all_to_all | solution.py:251
  75.5 10.8 %copy-start.4 = (f32[256]{0:T(256)S(1)}, f32[256]{0:T(256)}, u32[]{:S(2)}) copy-start(f32[256]{0:T(256)} %param.7) | copy-start | bytes 3076
  75.5 11.6 %copy-start.1 = (bf16[128,8192]{1,0:T(8,128)(2,1)S(1)}, bf16[128,8192]{1,0:T(8,128)(2,1)}, u32[]{:S(2)}) copy-start(bf16[128,8192]{1,0:T(8,128)(2,1)} %get-tuple-element.23.target_own) | copy-start | bytes 6291460
  87.1 2.2 %copy-start = (f32[128,8192]{1,0:T(8,128)S(1)}, f32[128,8192]{1,0:T(8,128)}, u32[]{:S(2)}) copy-start(f32[128,8192]{1,0:T(8,128)} %soft.2.soft_own) | copy-start | bytes 12582916
  91.0 10.9 %collective-permute-start.19 = (bf16[32,8192]{1,0:T(8,128)(2,1)S(1)}, bf16[32,8192]{1,0:T(8,128)(2,1)S(1)}, u32[]{:S(2)}, u32[]{:S(2)}) collective-permute-start(bf16[32,8192]{1,0:T(8,128)(2,1)S(1)} %combine.4), channel_id=1, source_target_pairs={{0,128},{2,130},{4,132},{6,134},{8,136},{10,138},{12,140},{14,142}... | collective-permute-start | bytes 1572872 | tf_op jit(solution)/shard_map/ppermute | solution.py:63
  94.5 12.8 %collective-permute-start.20 = (bf16[32,8192]{1,0:T(8,128)(2,1)S(1)}, bf16[32,8192]{1,0:T(8,128)(2,1)S(1)}, u32[]{:S(2)}, u32[]{:S(2)}) collective-permute-start(bf16[32,8192]{1,0:T(8,128)(2,1)S(1)} %get-tuple-element.25), channel_id=1, source_target_pairs={{0,64},{2,66},{4,68},{6,70},{8,72},{10,74},{12,76},{14,78},{16,18}... | collective-permute-start | bytes 1572872 | tf_op jit(solution)/shard_map/ppermute | solution.py:63
  95.4 11.9 %collective-permute-start.21 = (bf16[32,8192]{1,0:T(8,128)(2,1)S(1)}, bf16[32,8192]{1,0:T(8,128)(2,1)S(1)}, u32[]{:S(2)}, u32[]{:S(2)}) collective-permute-start(bf16[32,8192]{1,0:T(8,128)(2,1)S(1)} %get-tuple-element.26), channel_id=1, source_target_pairs={{0,192},{2,194},{4,196},{6,198},{8,200},{10,202},{12,204},{14,206}... | collective-permute-start | bytes 1572872 | tf_op jit(solution)/shard_map/ppermute | solution.py:63
  107.6 7.3 %collective-permute-start.22 = (bf16[8,8192]{1,0:T(8,128)(2,1)S(1)}, bf16[8,8192]{1,0:T(8,128)(2,1)S(1)}, u32[]{:S(2)}, u32[]{:S(2)}) collective-permute-start(bf16[8,8192]{1,0:T(8,128)(2,1)S(1)} %get-tuple-element.31), channel_id=1, source_target_pairs={{0,4},{2,6},{4,8},{6,10},{8,12},{10,14},{12,0},{14,2},{16,144},{18... | collective-permute-start | bytes 393224 | tf_op jit(solution)/shard_map/ppermute | solution.py:63
  109.0 8.4 %collective-permute-start.23 = (bf16[8,8192]{1,0:T(8,128)(2,1)S(1)}, bf16[8,8192]{1,0:T(8,128)(2,1)S(1)}, u32[]{:S(2)}, u32[]{:S(2)}) collective-permute-start(bf16[8,8192]{1,0:T(8,128)(2,1)S(1)} %get-tuple-element.33), channel_id=1, source_target_pairs={{0,2},{2,4},{4,6},{6,8},{8,10},{10,12},{12,14},{14,0},{16,80},{18,... | collective-permute-start | bytes 393224 | tf_op jit(solution)/shard_map/ppermute | solution.py:63
  109.6 7.7 %collective-permute-start.24 = (bf16[8,8192]{1,0:T(8,128)(2,1)S(1)}, bf16[8,8192]{1,0:T(8,128)(2,1)S(1)}, u32[]{:S(2)}, u32[]{:S(2)}) collective-permute-start(bf16[8,8192]{1,0:T(8,128)(2,1)S(1)} %get-tuple-element.32), channel_id=1, source_target_pairs={{0,14},{2,0},{4,2},{6,4},{8,6},{10,8},{12,10},{14,12},{16,208},{18... | collective-permute-start | bytes 393224 | tf_op jit(solution)/shard_map/ppermute | solution.py:63
  117.5 10.4 %collective-permute-start.25 = (f32[2,8192]{1,0:T(2,128)S(1)}, f32[2,8192]{1,0:T(2,128)S(1)}, u32[]{:S(2)}, u32[]{:S(2)}) collective-permute-start(f32[2,8192]{1,0:T(2,128)S(1)} %get-tuple-element.36), channel_id=1, source_target_pairs={{0,40},{2,42},{4,44},{6,46},{8,32},{10,34},{12,36},{14,38},{16,56}... | collective-permute-start | bytes 196616 | tf_op jit(solution)/shard_map/ppermute | solution.py:63
  119.1 10.9 %collective-permute-start.26 = (f32[2,8192]{1,0:T(2,128)S(1)}, f32[2,8192]{1,0:T(2,128)S(1)}, u32[]{:S(2)}, u32[]{:S(2)}) collective-permute-start(f32[2,8192]{1,0:T(2,128)S(1)} %get-tuple-element.35), channel_id=1, source_target_pairs={{0,8},{2,10},{4,12},{6,14},{8,0},{10,2},{12,4},{14,6},{16,24},{18,... | collective-permute-start | bytes 196616 | tf_op jit(solution)/shard_map/ppermute | solution.py:63
  124.0 6.0 %collective-permute-start.27 = (f32[2,8192]{1,0:T(2,128)S(1)}, f32[2,8192]{1,0:T(2,128)S(1)}, u32[]{:S(2)}, u32[]{:S(2)}) collective-permute-start(f32[2,8192]{1,0:T(2,128)S(1)} %get-tuple-element.34), channel_id=1, source_target_pairs={{0,32},{2,34},{4,36},{6,38},{8,40},{10,42},{12,44},{14,46},{16,48}... | collective-permute-start | bytes 196616 | tf_op jit(solution)/shard_map/ppermute | solution.py:63

commit v6 on v5

--- a/solution.py
+++ b/solution.py
@@ -70,7 +70,8 @@
 def placed(at_ref):
     y, x, c, z = (at_ref[i] for i in range(4))
     at = lax.broadcasted_iota(jnp.int32, (ROWS, 1), 0)
-    r, xr, z4, q1, q2, cr = at & 1, (at >> 1) & 1, (at >> 2) & 1, (at >> 3) & 3, (at >> 5) & 3, at >> 7
+    r, near, q1, q2, cr = at & 1, (at >> 1) & 3, (at >> 3) & 3, (at >> 5) & 3, at >> 7
+    xr, z4 = near & 1, near >> 1
     o1 = jnp.where(q1 == 2, -1, jnp.where(q1 == 3, 2, q1))
     o2 = jnp.where(q2 == 2, -1, jnp.where(q2 == 3, 2, q2))
     core = c ^ cr
@@ -98,26 +99,31 @@
     return copies
 
 
-def logits_kernel(at_ref, targets_ref, p0, p1, p2, p3, p4, p5, p6, p7, w_hbm, logits_ref, stats_ref, w_ref, w_sems):
+def logits_kernel(at_ref, targets_ref, p0, p1, p2, p3, p4, p5, p6, p7, w_hbm, stats_ref, own_hbm, other_hbm, w_ref, own_ref, other_ref, w_sems, own_sems, other_sems):
     acc = jnp.zeros((ROWS, WIDTH), F32)
     for k, copy in enumerate(weight_copies(w_hbm, w_ref, w_sems)):
         cut = slice(k * CHUNK, (k + 1) * CHUNK)
         left = jnp.concatenate([p[:, cut] for p in (p0, p1, p2, p3, p4, p5, p6, p7)], axis=0)
         copy.wait()
         acc += jnp.dot(left, w_ref[cut, :], preferred_element_type=F32)
-    logits_ref[...] = acc
     top = jnp.max(acc, axis=1, keepdims=True)
-    total = jnp.sum(jnp.exp(acc - top), axis=1, keepdims=True)
+    soft = jnp.exp(acc - top)
+    total = jnp.sum(soft, axis=1, keepdims=True)
     place = placed(at_ref)
-    picked = jnp.sum(jnp.where(hits(at_ref, targets_ref, place), acc, 0.0), axis=1, keepdims=True)
+    hit = hits(at_ref, targets_ref, place)
+    picked = jnp.sum(jnp.where(hit, acc, 0.0), axis=1, keepdims=True)
     for i, column in enumerate((top, total, picked)):
         stats_ref[i : i + 1, :] = jnp.sum(jnp.where(place, column, 0.0), axis=0, keepdims=True)
+    own = (own_ref, column_copies(own_ref, own_hbm, own_sems))
+    other = (other_ref, column_copies(other_ref, other_hbm, other_sems))
+    products(jnp.where(hit, 0.0, soft).astype(BF), None, w_ref, (own, other))
 
 
 def products(left, copies, w_ref, pairs):
-    for k, copy in enumerate(copies):
+    for k in range(STEPS):
         cut = slice(k * CHUNK, (k + 1) * CHUNK)
-        copy.wait()
+        if copies is not None:
+            copies[k].wait()
         part = lax.dot_general(left, w_ref[cut, :], (((1,), (1,)), ((), ())), preferred_element_type=F32)
         first = 0
         for buffer, outs in pairs:
@@ -137,17 +143,7 @@
     products(left, copies, w_ref, (own, other))
 
 
-def soft_kernel(start, at_ref, targets_ref, top_ref, logits_ref, w_hbm, soft_hbm, w_ref, soft_ref, w_sems, soft_sems):
-    copies = weight_copies(w_hbm, w_ref, w_sems)
-    cut = slice(start, start + ROWS // 2)
-    place = placed(at_ref)
-    top = jnp.sum(jnp.where(place[cut], top_ref[...], 0.0), axis=1, keepdims=True)
-    hit = hits(at_ref, targets_ref, place)[cut]
-    left = jnp.where(hit, 0.0, jnp.exp(logits_ref[cut, :] - top)).astype(BF)
-    products(left, copies, w_ref, ((soft_ref, column_copies(soft_ref, soft_hbm, soft_sems)),))
-
-
-def merge_kernel(own_ref, core_ref, x_ref, both_ref, out_ref, top_ref):
+def merge_kernel(own_ref, core_ref, x_ref, both_ref, out_ref):
     refs = (own_ref, core_ref, x_ref, both_ref)
     tops = [r[0:1, :] for r in refs]
     top = jnp.maximum(jnp.maximum(tops[0], tops[1]), jnp.maximum(tops[2], tops[3]))
@@ -156,10 +152,9 @@
     merged = jnp.concatenate([top, total, picked], axis=0)
     for i in range(out_ref.shape[0]):
         out_ref[i] = merged
-    top_ref[...] = top
-
-
-def scales_kernel(at_ref, grad_ref, top_ref, spread_ref, out_ref):
+
+
+def scales_kernel(at_ref, grad_ref, own_ref, core_ref, spread_ref, out_ref):
     place = placed(at_ref)[: ROWS // 2]
 
     def ordered(row):
@@ -170,13 +165,13 @@
     total = jnp.sum(spread_ref[:, 1, :] * jnp.exp(tops - highest), axis=0, keepdims=True)
     log_total = ordered(highest + jnp.log(total))
     picked = ordered(jnp.sum(spread_ref[:, 2, :], axis=0, keepdims=True))
-    top = ordered(top_ref[...])
     factor = 1.0 + 2.0 * zloss_coef * log_total
     grad = ordered(grad_ref[...])
-    scale = grad * factor * jnp.exp(top - log_total)
     target = (grad * (jnp.exp(picked - log_total) * factor - 1.0)).astype(BF).astype(F32)
+    own, core = (grad * factor * jnp.exp(ordered(ref[0:1, :]) - log_total) for ref in (own_ref, core_ref))
     lane = lax.broadcasted_iota(jnp.int32, (ROWS // 2, 128), 1)
-    out_ref[...] = jnp.where(lane == 0, scale, jnp.where(lane == 1, target, jnp.where(lane == 2, log_total, picked)))
+    rest = jnp.where(lane == 2, target, jnp.where(lane == 3, log_total, picked))
+    out_ref[...] = jnp.where(lane == 0, own, jnp.where(lane == 1, core, rest))
 
 
 def combine_kernel(parts, scales_ref, soft_own, soft_in, target_own, target_in, *refs):
@@ -192,12 +187,12 @@
     for i, (q, out) in enumerate(zip(parts, outs)):
         for copy in every[i]:
             copy.wait()
-        scale, target = scales_ref[32 * q : 32 * q + 32, 0:1], scales_ref[32 * q : 32 * q + 32, 1:2]
+        own, core, target = (scales_ref[32 * q : 32 * q + 32, i : i + 1] for i in range(3))
         for k in range(0, DEPTH, CHUNK):
             cut = slice(k, k + CHUNK)
-            soft = a_ref[i, :, cut] + b_ref[i, :, cut].astype(F32)
+            soft = own * a_ref[i, :, cut] + core * b_ref[i, :, cut].astype(F32)
             chosen = c_ref[i, :, cut].astype(F32) + d_ref[i, :, cut].astype(F32)
-            out[:, cut] = (scale * soft + target * chosen).astype(out.dtype)
+            out[:, cut] = (soft + target * chosen).astype(out.dtype)
 
 
 def shards(hidden, lm_weight, targets, loss_grad):
@@ -209,9 +204,8 @@
     sems = pltpu.SemaphoreType.DMA((STEPS,))
 
     block = jnp.concatenate([hidden] + [send(hidden, to) for to in (to_x, to_z4, to_xz4)])
-    far, near, back = (send(block, to_first(-o)) for o in (2, 1, -1))
-    block = jnp.concatenate([block, near, back, far])
-    far, near, back = (send(block, to_second(-o)) for o in (2, 1, -1))
+    block = jnp.concatenate([block] + [send(block, to_first(-o)) for o in OFFSETS[1:]])
+    near, back, far = (send(block, to_second(-o)) for o in OFFSETS[1:])
 
     aim, _ = lax.optimization_barrier((targets, block))
     target_own, target_out = pl.pallas_call(
@@ -224,56 +218,43 @@
         cost_estimate=pl.CostEstimate(flops=2 * ROWS * DEPTH * WIDTH, bytes_accessed=12 << 20, transcendentals=0),
         name="target",
     )(at, aim, lm_weight)
-    near, target_own, target_out = lax.optimization_barrier((near, target_own, target_out))
+    far, target_own, target_out = lax.optimization_barrier((far, target_own, target_out))
     pieces = [block, near, back, far]
     pieces = pieces + [send(p, to_c) for p in pieces]
-    target_in = send(target_out, to_c)
-
-    logits, stats = pl.pallas_call(
+
+    stats, soft_own, soft_out = pl.pallas_call(
         logits_kernel,
-        out_shape=(jax.ShapeDtypeStruct((ROWS, WIDTH), F32), jax.ShapeDtypeStruct((3, ROWS), F32)),
+        out_shape=(jax.ShapeDtypeStruct((3, ROWS), F32), pltpu.HBM((half, DEPTH), F32), pltpu.HBM((half, DEPTH), BF)),
         in_specs=[SMEM] + [VMEM] * 9 + [ANY],
-        out_specs=(VMEM, VMEM),
-        scratch_shapes=weights + [sems],
-        compiler_params=params(),
-        cost_estimate=pl.CostEstimate(flops=2 * ROWS * DEPTH * WIDTH, bytes_accessed=13 << 20, transcendentals=ROWS * WIDTH),
+        out_specs=(VMEM, HBM, HBM),
+        scratch_shapes=weights + [pltpu.VMEM((half, DEPTH), F32), pltpu.VMEM((half, DEPTH), BF)] + [sems] * 3,
+        compiler_params=params(32),
+        cost_estimate=pl.CostEstimate(flops=4 * ROWS * DEPTH * WIDTH, bytes_accessed=19 << 20, transcendentals=ROWS * WIDTH),
         name="logits",
     )(at, targets, *pieces, lm_weight)
     stats = [stats] + [send(stats, to) for to in (to_c, to_x, to_xc)]
-    merged, top = pl.pallas_call(
+    merged = pl.pallas_call(
         merge_kernel,
-        out_shape=(jax.ShapeDtypeStruct((32, 3, ROWS), F32), jax.ShapeDtypeStruct((1, ROWS), F32)),
+        out_shape=jax.ShapeDtypeStruct((32, 3, ROWS), F32),
         in_specs=[VMEM] * 4,
-        out_specs=(VMEM, VMEM),
+        out_specs=VMEM,
         compiler_params=params(),
         name="merge",
     )(*stats)
+    merged, soft_out, target_out = lax.optimization_barrier((merged, soft_out, target_out))
+    soft_in, target_in = send(soft_out, to_c), send(target_out, to_c)
     spread = lax.all_to_all(merged, ("y", "z"), 0, 0)
 
-    same_top = send(top, to_c)
-
-    def soft(start, dtype):
-        return pl.pallas_call(
-            functools.partial(soft_kernel, start),
-            out_shape=pltpu.HBM((half, DEPTH), dtype),
-            in_specs=[SMEM, VMEM, VMEM, VMEM, ANY],
-            out_specs=HBM,
-            scratch_shapes=weights + [pltpu.VMEM((half, DEPTH), dtype)] + [sems] * 2,
-            compiler_params=params(),
-            cost_estimate=pl.CostEstimate(flops=ROWS * DEPTH * WIDTH, bytes_accessed=10 << 20, transcendentals=0),
-            name="soft",
-        )(at, targets, same_top, logits, lm_weight)
-
-    soft_in = send(soft(half, BF), to_c)
-    soft_own = soft(0, F32)
     scales = pl.pallas_call(
         scales_kernel,
         out_shape=jax.ShapeDtypeStruct((half, 128), F32),
-        in_specs=[SMEM] + [VMEM] * 3,
+        in_specs=[SMEM] + [VMEM] * 4,
         out_specs=VMEM,
         compiler_params=params(),
         name="scales",
-    )(at, loss_grad, top, spread)
+    )(at, loss_grad, stats[0], stats[1], spread)
+
+    soft_own, target_own = (pltpu.with_memory_space_constraint(v, pltpu.HBM) for v in (soft_own, target_own))
 
     def combine(parts, dtype):
         n = len(parts)
@@ -290,18 +271,17 @@
             name="combine",
         )(scales, soft_own, soft_in, target_own, target_in)
 
-    far = combine((3,), BF)
-    near, back = combine((1, 2), BF)
-    arrived = [send(p, to_second(o)).astype(F32) for p, o in ((far[0], 2), (near, 1), (back, -1))]
+    parts = combine((3,), BF) + combine((1, 2), BF)
+    arrived = [send(p, to_second(o)).astype(F32) for p, o in zip(parts, (2, 1, -1))]
     part = combine((0,), F32)[0] + sum(arrived)
-    log_total, target_logit = scales[:2, 2], scales[:2, 3]
+    log_total, target_logit = scales[:2, 3], scales[:2, 4]
     ce_loss = log_total - target_logit
     z_term = zloss_coef * log_total * log_total
 
     part = part.reshape(4, 8, DEPTH)
     part = part[0] + sum(send(part[k].astype(BF), to_first(OFFSETS[k])).astype(F32) for k in (3, 1, 2))
     part = [part[0:2]] + [
-        send(part[2 * k : 2 * k + 2], to) for k, to in ((3, to_xz4), (2, to_z4), (1, to_x))
+        send(part[2 * k : 2 * k + 2], to) for k, to in ((1, to_x), (2, to_z4), (3, to_xz4))
     ]
     part = (part[0] + part[1]) + (part[2] + part[3])
     return ce_loss, z_term, part.astype(BF)

time: 133 us -> 124 us (0.932)
  blocking collectives: 0 us -> 18.6 us
  waiting for transfers between devices: 48.4 us -> 36.4 us
  Pallas kernels: 31.6 us -> 21.8 us
  starting transfers between devices: 43.2 us -> 40 us
  local copies, waits for them, and re-layouts: 4.24 us -> 2.06 us
    all_to_all x0 -> x1, blocking collectives: none -> 18.6 us  [shards(): spread = lax.all_to_all(merged, ('y', 'z'), 0, 0)]
    pallas_call x4 -> x2, Pallas kernels: 18.9 us -> 8.49 us  [the longest x1 8.46 us: shards(): pl.pallas_call(logits_kernel, out_shape=(jax.ShapeDtypeStruct((3, ROWS),...]
    ppermute x28 -> x27, waiting for transfers between devices: 44.2 us -> 36.4 us  [send(): return lax.ppermute(value, GROUP, pairs(route))]
    all_to_all x1 -> x0, starting transfers between devices: 6.39 us -> none  [shards(): spread = lax.all_to_all(merged, ('y', 'z'), 0, 0)]
    all_to_all x1 -> x0, waiting for transfers between devices: 4.16 us -> none  [shards(): spread = lax.all_to_all(merged, ('y', 'z'), 0, 0)]
    ppermute x28 -> x27, starting transfers between devices: 36.8 us -> 40 us  [send(): return lax.ppermute(value, GROUP, pairs(route))]
    unnamed x10 -> x8, local copies, waits for them, and re-layouts: 2.87 us -> 0.69 us
  transfers between devices with their start and end apart: 29 -> 27, of which waited for: 19 -> 17; matrix products, arithmetic and copies ran while one was open for 1% -> 1% of each run, Pallas kernels for 18% -> 9%
where the time goes in v6:
time: 124 us; the launch traced here: 122 us
  starting transfers between devices  40 us (32%)
  waiting for transfers between devices  36.4 us (29%)
  Pallas kernels  21.8 us (18%)
  blocking collectives  18.6 us (15%)
  other arithmetic  2.4 us (2%)
  local copies, waits for them, and re-layouts  2.06 us (2%)
    ppermute x27, starting transfers between devices, send(): return lax.ppermute(value, GROUP, pairs(route))  40 us
    ppermute x27, waiting for transfers between devices, send(): return lax.ppermute(value, GROUP, pairs(route))  36.4 us
    all_to_all x1, blocking collectives, shards(): spread = lax.all_to_all(merged, ('y', 'z'), 0, 0)  18.6 us
    pallas_call x1, Pallas kernels, shards(): pl.pallas_call(logits_kernel, out_shape=(jax.ShapeDtypeStruct((3, ROWS),...  8.46 us
    pallas_call x1, Pallas kernels, shards(): pl.pallas_call(target_kernel, out_shape=[pltpu.HBM((half, DEPTH), BF)] *...  6.55 us
    pallas_call x3, Pallas kernels, combine(): pl.pallas_call(functools.partial(combine_kernel, parts), out_shape=[jax.S...  5.88 us
  transfers between devices with their start and end apart: 27, of which 17 were waited for; matrix products, arithmetic and copies ran while one was open for 1% of the time, Pallas kernels for 9%

profile of v6, /device:TPU:4, one launch (start us, length us, event | category | flops | bytes accessed | tf_op | source)
XLA Modules:
  0.0 121.9 jit_solution(5452911599973881132)
XLA Ops:
  0.6 7.9 %collective-permute-start.2 = (bf16[2,8192]{1,0:T(2,128)(2,1)}, bf16[2,8192]{1,0:T(2,128)(2,1)S(1)}, u32[]{:S(2)}, u32[]{:S(2)}) collective-permute-start(bf16[2,8192]{1,0:T(2,128)(2,1)} %param.4), channel_id=1, source_target_pairs={{0,40},{2,42},{4,44},{6,46},{8,32},{10,34},{12,36},{14,38},{16,56}... | collective-permute-start | bytes 98312 | tf_op jit(solution)/shard_map/ppermute | solution.py:63
  8.5 0.0 collective-permute-start.1
  8.5 0.8 collective-permute-start
  9.4 1.4 %collective-permute-done.2 = bf16[2,8192]{1,0:T(2,128)(2,1)S(1)} collective-permute-done((bf16[2,8192]{1,0:T(2,128)(2,1)}, bf16[2,8192]{1,0:T(2,128)(2,1)S(1)}, u32[]{:S(2)}, u32[]{:S(2)}) %collective-permute-start.2) | collective-permute-done | bytes 32800 | tf_op jit(solution)/shard_map/ppermute | solution.py:63
  10.7 6.1 %collective-permute-done.1 = bf16[2,8192]{1,0:T(2,128)(2,1)S(1)} collective-permute-done((bf16[2,8192]{1,0:T(2,128)(2,1)}, bf16[2,8192]{1,0:T(2,128)(2,1)S(1)}, u32[]{:S(2)}, u32[]{:S(2)}) %collective-permute-start.1) | collective-permute-done | bytes 32800 | tf_op jit(solution)/shard_map/ppermute | solution.py:63
  16.8 0.0 collective-permute-done
  16.8 0.9 pad_maximum_fusion
  17.8 0.9 collective-permute-start.5
  18.7 1.0 collective-permute-start.4
  19.7 2.2 %collective-permute-start.3 = (bf16[8,8192]{1,0:T(8,128)(2,1)S(1)}, bf16[8,8192]{1,0:T(8,128)(2,1)S(1)}, u32[]{:S(2)}, u32[]{:S(2)}) collective-permute-start(bf16[8,8192]{1,0:T(8,128)(2,1)S(1)} %pad_maximum_fusion), channel_id=1, source_target_pairs={{0,14},{2,0},{4,2},{6,4},{8,6},{10,8},{12,10},{14,12},{16,208},{18... | collective-permute-start | bytes 393224 | tf_op jit(solution)/shard_map/ppermute | solution.py:63
  21.9 3.3 %collective-permute-done.5 = bf16[8,8192]{1,0:T(8,128)(2,1)S(1)} collective-permute-done((bf16[8,8192]{1,0:T(8,128)(2,1)S(1)}, bf16[8,8192]{1,0:T(8,128)(2,1)S(1)}, u32[]{:S(2)}, u32[]{:S(2)}) %collective-permute-start.5) | collective-permute-done | bytes 131104 | tf_op jit(solution)/shard_map/ppermute | solution.py:63
  25.2 0.0 collective-permute-done.4
  25.2 0.6 collective-permute-done.3
  25.8 1.0 concatenate.8.p0
  26.8 3.3 %collective-permute-start.8 = (bf16[32,8192]{1,0:T(8,128)(2,1)S(1)}, bf16[32,8192]{1,0:T(8,128)(2,1)S(1)}, u32[]{:S(2)}, u32[]{:S(2)}) collective-permute-start(bf16[32,8192]{1,0:T(8,128)(2,1)S(1)} %concatenate.8.p0), channel_id=1, source_target_pairs={{0,128},{2,130},{4,132},{6,134},{8,136},{10,138},{12,140},{14,142}... | collective-permute-start | bytes 1572872 | tf_op jit(solution)/shard_map/ppermute | solution.py:63
  30.0 0.7 collective-permute-start.7
  30.7 2.6 %collective-permute-start.6 = (bf16[32,8192]{1,0:T(8,128)(2,1)S(1)}, bf16[32,8192]{1,0:T(8,128)(2,1)S(1)}, u32[]{:S(2)}, u32[]{:S(2)}) collective-permute-start(bf16[32,8192]{1,0:T(8,128)(2,1)S(1)} %concatenate.8.p0), channel_id=1, source_target_pairs={{0,192},{2,194},{4,196},{6,198},{8,200},{10,202},{12,204},{14,206}... | collective-permute-start | bytes 1572872 | tf_op jit(solution)/shard_map/ppermute | solution.py:63
  33.3 0.1 stack.23.at_ref
  33.4 0.0 collective-permute-start.9
  33.4 0.0 copy-start
  33.4 0.7 copy-done
  34.1 6.5 %target.1 = (bf16[128,8192]{1,0:T(8,128)(2,1)}, bf16[128,8192]{1,0:T(8,128)(2,1)}) custom-call(s32[5]{0:T(128)S(1)} %stack.23.at_ref, s32[1,256]{1,0:T(1,128)S(1)} %bitcast.7, bf16[8192,512]{1,0:T(8,128)(2,1)} %w_hbm.3), custom_call_target="tpu_custom_call" | custom-call | flops 2147483648 | bytes 12582912 | tf_op jit(solution)/shard_map/target/pallas_call | solution.py:211
  40.6 0.0 collective-permute-done.8.p3
  40.7 0.0 copy-start.2
  40.7 2.5 %collective-permute-done.7.p2 = bf16[32,8192]{1,0:T(8,128)(2,1)S(1)} collective-permute-done((bf16[32,8192]{1,0:T(8,128)(2,1)S(1)}, bf16[32,8192]{1,0:T(8,128)(2,1)S(1)}, u32[]{:S(2)}, u32[]{:S(2)}) %collective-permute-start.7) | collective-permute-done | bytes 524320 | tf_op jit(solution)/shard_map/ppermute | solution.py:63
  43.2 0.0 collective-permute-start.11
  43.2 0.4 collective-permute-done.6.p1
  43.5 1.5 %collective-permute-start.10 = (bf16[32,8192]{1,0:T(8,128)(2,1)S(1)}, bf16[32,8192]{1,0:T(8,128)(2,1)S(1)}, u32[]{:S(2)}, u32[]{:S(2)}) collective-permute-start(bf16[32,8192]{1,0:T(8,128)(2,1)S(1)} %collective-permute-done.6.p1), channel_id=1, source_target_pairs={{0,16},{2,18},{4,20},{6,22},{8,24},{10,26},{12,28},{14,30},{16,0},... | collective-permute-start | bytes 1572872 | tf_op jit(solution)/shard_map/ppermute | solution.py:63
  45.0 0.0 collective-permute-start.12
  45.0 0.1 collective-permute-done.11.p6
  45.1 1.5 %collective-permute-done.10.p5 = bf16[32,8192]{1,0:T(8,128)(2,1)S(1)} collective-permute-done((bf16[32,8192]{1,0:T(8,128)(2,1)S(1)}, bf16[32,8192]{1,0:T(8,128)(2,1)S(1)}, u32[]{:S(2)}, u32[]{:S(2)}) %collective-permute-start.10) | collective-permute-done | bytes 524320 | tf_op jit(solution)/shard_map/ppermute | solution.py:63
  46.5 0.7 collective-permute-done.12.p7
  47.3 8.5 %logits.1 = (f32[3,256]{1,0:T(4,128)S(1)}, f32[128,8192]{1,0:T(8,128)}, bf16[128,8192]{1,0:T(8,128)(2,1)}) custom-call(s32[5]{0:T(128)S(1)} %stack.23.at_ref, s32[1,256]{1,0:T(1,128)S(1)} %bitcast.8, bf16[32,8192]{1,0:T(8,128)(2,1)S(1)} %concatenate.8.p0, bf16[32,8192]{1,0:T(8,128)(2,1)S(1)} %collective-permute-done.6.p1, ...), custom_call_target="tpu_custom_call" | custom-call | flops 4294967296 | bytes 19922944 | tf_op jit(solution)/shard_map/logits/pallas_call | solution.py:225
  55.8 0.6 collective-permute-start.15
  56.4 1.5 %collective-permute-start.14 = (f32[3,256]{1,0:T(4,128)S(1)}, f32[3,256]{1,0:T(4,128)S(1)}, u32[]{:S(2)}, u32[]{:S(2)}) collective-permute-start(f32[3,256]{1,0:T(4,128)S(1)} %get-tuple-element.21.own_ref), channel_id=1, source_target_pairs={{0,32},{2,34},{4,36},{6,38},{8,40},{10,42},{12,44},{14,46},{16,48}... | collective-permute-start | bytes 9224 | tf_op jit(solution)/shard_map/ppermute | solution.py:63
  57.9 1.0 collective-permute-done.15.both_ref
  58.9 1.1 collective-permute-done.14.x_ref
  60.0 0.1 collective-permute-start.16
  60.2 0.5 collective-permute-start.17
  60.6 18.6 %all_to_all.5.spread_ref = f32[32,3,256]{2,1,0:T(4,128)S(1)} all-to-all(f32[32,3,256]{2,1,0:T(4,128)S(1)} %merge.1), channel_id=1, replica_groups=mesh['y'=4,'x'=2,'c'=2,'z'=8,'dp'=2] {'y','z'}, dimensions={0} | all-to-all | bytes 196608 | tf_op jit(solution)/shard_map/all_to_all | solution.py:246
  79.2 0.8 scales.1.scales_ref
  80.1 1.8 %combine.4 = bf16[32,8192]{1,0:T(8,128)(2,1)S(1)} custom-call(f32[128,128]{1,0:T(8,128)S(1)} %scales.1.scales_ref, f32[128,8192]{1,0:T(8,128)} %get-tuple-element.25.soft_own, bf16[128,8192]{1,0:T(8,128)(2,1)S(1)} %collective-permute-done.16.soft_in, bf16[128,8192]{1,0:T(8,128)(2,1)} %get-tuple-element.27.target_own, ...), custom_call_target="tpu_custom_call" | custom-call | flops 1572864 | bytes 3145728 | tf_op jit(solution)/shard_map/combine/pallas_call | solution.py:261
  81.9 1.4 %collective-permute-start.18 = (bf16[32,8192]{1,0:T(8,128)(2,1)S(1)}, bf16[32,8192]{1,0:T(8,128)(2,1)S(1)}, u32[]{:S(2)}, u32[]{:S(2)}) collective-permute-start(bf16[32,8192]{1,0:T(8,128)(2,1)S(1)} %combine.4), channel_id=1, source_target_pairs={{0,128},{2,130},{4,132},{6,134},{8,136},{10,138},{12,140},{14,142}... | collective-permute-start | bytes 1572872 | tf_op jit(solution)/shard_map/ppermute | solution.py:63
  83.3 2.3 %combine.5 = (bf16[32,8192]{1,0:T(8,128)(2,1)S(1)}, bf16[32,8192]{1,0:T(8,128)(2,1)S(1)}) custom-call(f32[128,128]{1,0:T(8,128)S(1)} %scales.1.scales_ref, f32[128,8192]{1,0:T(8,128)} %get-tuple-element.25.soft_own, bf16[128,8192]{1,0:T(8,128)(2,1)S(1)} %collective-permute-done.16.soft_in, bf16[128,8192]{1,0:T(8,128)(2,1)} %get-tuple-element.27.target_own, ...), custom_call_target="tpu_custom_call" | custom-call | flops 3145728 | bytes 6291456 | tf_op jit(solution)/shard_map/combine/pallas_call | solution.py:261
  85.6 0.8 collective-permute-start.19
  86.4 2.5 %collective-permute-start.20 = (bf16[32,8192]{1,0:T(8,128)(2,1)S(1)}, bf16[32,8192]{1,0:T(8,128)(2,1)S(1)}, u32[]{:S(2)}, u32[]{:S(2)}) collective-permute-start(bf16[32,8192]{1,0:T(8,128)(2,1)S(1)} %get-tuple-element.30), channel_id=1, source_target_pairs={{0,192},{2,194},{4,196},{6,198},{8,200},{10,202},{12,204},{14,206}... | collective-permute-start | bytes 1572872 | tf_op jit(solution)/shard_map/ppermute | solution.py:63
  88.9 1.8 %combine.3 = f32[32,8192]{1,0:T(8,128)S(1)} custom-call(f32[128,128]{1,0:T(8,128)S(1)} %scales.1.scales_ref, f32[128,8192]{1,0:T(8,128)} %get-tuple-element.25.soft_own, bf16[128,8192]{1,0:T(8,128)(2,1)S(1)} %collective-permute-done.16.soft_in, bf16[128,8192]{1,0:T(8,128)(2,1)} %get-tuple-element.27.target_own, ...), custom_call_target="tpu_custom_call" | custom-call | flops 1572864 | bytes 3145728 | tf_op jit(solution)/shard_map/combine/pallas_call | solution.py:261
  90.7 2.0 %collective-permute-done.18 = bf16[32,8192]{1,0:T(8,128)(2,1)S(1)} collective-permute-done((bf16[32,8192]{1,0:T(8,128)(2,1)S(1)}, bf16[32,8192]{1,0:T(8,128)(2,1)S(1)}, u32[]{:S(2)}, u32[]{:S(2)}) %collective-permute-start.18) | collective-permute-done | bytes 524320 | tf_op jit(solution)/shard_map/ppermute | solution.py:63
  92.7 5.5 %collective-permute-done.19 = bf16[32,8192]{1,0:T(8,128)(2,1)S(1)} collective-permute-done((bf16[32,8192]{1,0:T(8,128)(2,1)S(1)}, bf16[32,8192]{1,0:T(8,128)(2,1)S(1)}, u32[]{:S(2)}, u32[]{:S(2)}) %collective-permute-start.19) | collective-permute-done | bytes 524320 | tf_op jit(solution)/shard_map/ppermute | solution.py:63
  98.3 0.2 fusion.2
  98.5 1.6 %collective-permute-start.21 = (bf16[8,8192]{1,0:T(8,128)(2,1)S(1)}, bf16[8,8192]{1,0:T(8,128)(2,1)S(1)}, u32[]{:S(2)}, u32[]{:S(2)}) collective-permute-start(bf16[8,8192]{1,0:T(8,128)(2,1)S(1)} %get-tuple-element.35), channel_id=1, source_target_pairs={{0,4},{2,6},{4,8},{6,10},{8,12},{10,14},{12,0},{14,2},{16,144},{18... | collective-permute-start | bytes 393224 | tf_op jit(solution)/shard_map/ppermute | solution.py:63
  100.1 2.6 %collective-permute-start.23 = (bf16[8,8192]{1,0:T(8,128)(2,1)S(1)}, bf16[8,8192]{1,0:T(8,128)(2,1)S(1)}, u32[]{:S(2)}, u32[]{:S(2)}) collective-permute-start(bf16[8,8192]{1,0:T(8,128)(2,1)S(1)} %get-tuple-element.36), channel_id=1, source_target_pairs={{0,14},{2,0},{4,2},{6,4},{8,6},{10,8},{12,10},{14,12},{16,208},{18... | collective-permute-start | bytes 393224 | tf_op jit(solution)/shard_map/ppermute | solution.py:63
  102.7 0.2 slice_reduce_fusion
  102.9 3.1 %collective-permute-done.21 = bf16[8,8192]{1,0:T(8,128)(2,1)S(1)} collective-permute-done((bf16[8,8192]{1,0:T(8,128)(2,1)S(1)}, bf16[8,8192]{1,0:T(8,128)(2,1)S(1)}, u32[]{:S(2)}, u32[]{:S(2)}) %collective-permute-start.21) | collective-permute-done | bytes 131104 | tf_op jit(solution)/shard_map/ppermute | solution.py:63
  106.1 2.8 %collective-permute-done.22 = bf16[8,8192]{1,0:T(8,128)(2,1)S(1)} collective-permute-done((bf16[8,8192]{1,0:T(8,128)(2,1)S(1)}, bf16[8,8192]{1,0:T(8,128)(2,1)S(1)}, u32[]{:S(2)}, u32[]{:S(2)}) %collective-permute-start.22) | collective-permute-done | bytes 131104 | tf_op jit(solution)/shard_map/ppermute | solution.py:63
  108.9 0.1 slice_add_fusion
  109.0 0.1 fusion.4
  109.0 1.7 %collective-permute-start.26 = (f32[2,8192]{1,0:T(2,128)S(1)}, f32[2,8192]{1,0:T(2,128)S(1)}, u32[]{:S(2)}, u32[]{:S(2)}) collective-permute-start(f32[2,8192]{1,0:T(2,128)S(1)} %get-tuple-element.38), channel_id=1, source_target_pairs={{0,40},{2,42},{4,44},{6,46},{8,32},{10,34},{12,36},{14,38},{16,56}... | collective-permute-start | bytes 196616 | tf_op jit(solution)/shard_map/ppermute | solution.py:63
  110.8 4.8 %collective-permute-start.25 = (f32[2,8192]{1,0:T(2,128)S(1)}, f32[2,8192]{1,0:T(2,128)S(1)}, u32[]{:S(2)}, u32[]{:S(2)}) collective-permute-start(f32[2,8192]{1,0:T(2,128)S(1)} %get-tuple-element.39), channel_id=1, source_target_pairs={{0,8},{2,10},{4,12},{6,14},{8,0},{10,2},{12,4},{14,6},{16,24},{18,... | collective-permute-start | bytes 196616 | tf_op jit(solution)/shard_map/ppermute | solution.py:63
  115.6 1.0 collective-permute-start.24
  116.5 0.5 multiply_multiply_fusion
  117.1 2.0 %collective-permute-done.26 = f32[2,8192]{1,0:T(2,128)S(1)} collective-permute-done((f32[2,8192]{1,0:T(2,128)S(1)}, f32[2,8192]{1,0:T(2,128)S(1)}, u32[]{:S(2)}, u32[]{:S(2)}) %collective-permute-start.26) | collective-permute-done | bytes 65568 | tf_op jit(solution)/shard_map/ppermute | solution.py:63
  119.0 2.3 %collective-permute-done.25 = f32[2,8192]{1,0:T(2,128)S(1)} collective-permute-done((f32[2,8192]{1,0:T(2,128)S(1)}, f32[2,8192]{1,0:T(2,128)S(1)}, u32[]{:S(2)}, u32[]{:S(2)}) %collective-permute-start.25) | collective-permute-done | bytes 65568 | tf_op jit(solution)/shard_map/ppermute | solution.py:63
  121.3 0.7 fusion.1
  (16 shorter events, 0.1 us)
Async XLA Ops:
  0.6 10.1 %collective-permute-start.2 = (bf16[2,8192]{1,0:T(2,128)(2,1)}, bf16[2,8192]{1,0:T(2,128)(2,1)S(1)}, u32[]{:S(2)}, u32[]{:S(2)}) collective-permute-start(bf16[2,8192]{1,0:T(2,128)(2,1)} %param.4), channel_id=1, source_target_pairs={{0,40},{2,42},{4,44},{6,46},{8,32},{10,34},{12,36},{14,38},{16,56}... | collective-permute-start | bytes 98312 | tf_op jit(solution)/shard_map/ppermute | solution.py:63
  8.5 8.3 %collective-permute-start.1 = (bf16[2,8192]{1,0:T(2,128)(2,1)}, bf16[2,8192]{1,0:T(2,128)(2,1)S(1)}, u32[]{:S(2)}, u32[]{:S(2)}) collective-permute-start(bf16[2,8192]{1,0:T(2,128)(2,1)} %param.4), channel_id=1, source_target_pairs={{0,8},{2,10},{4,12},{6,14},{8,0},{10,2},{12,4},{14,6},{16,24},{18,... | collective-permute-start | bytes 98312 | tf_op jit(solution)/shard_map/ppermute | solution.py:63
  8.5 8.3 %collective-permute-start = (bf16[2,8192]{1,0:T(2,128)(2,1)}, bf16[2,8192]{1,0:T(2,128)(2,1)S(1)}, u32[]{:S(2)}, u32[]{:S(2)}) collective-permute-start(bf16[2,8192]{1,0:T(2,128)(2,1)} %param.4), channel_id=1, source_target_pairs={{0,32},{2,34},{4,36},{6,38},{8,40},{10,42},{12,44},{14,46},{16,48}... | collective-permute-start | bytes 98312 | tf_op jit(solution)/shard_map/ppermute | solution.py:63
  17.8 7.5 %collective-permute-start.5 = (bf16[8,8192]{1,0:T(8,128)(2,1)S(1)}, bf16[8,8192]{1,0:T(8,128)(2,1)S(1)}, u32[]{:S(2)}, u32[]{:S(2)}) collective-permute-start(bf16[8,8192]{1,0:T(8,128)(2,1)S(1)} %pad_maximum_fusion), channel_id=1, source_target_pairs={{0,12},{2,14},{4,0},{6,2},{8,4},{10,6},{12,8},{14,10},{16,144},{18... | collective-permute-start | bytes 393224 | tf_op jit(solution)/shard_map/ppermute | solution.py:63
  18.7 6.5 %collective-permute-start.4 = (bf16[8,8192]{1,0:T(8,128)(2,1)S(1)}, bf16[8,8192]{1,0:T(8,128)(2,1)S(1)}, u32[]{:S(2)}, u32[]{:S(2)}) collective-permute-start(bf16[8,8192]{1,0:T(8,128)(2,1)S(1)} %pad_maximum_fusion), channel_id=1, source_target_pairs={{0,2},{2,4},{4,6},{6,8},{8,10},{10,12},{12,14},{14,0},{16,80},{18,... | collective-permute-start | bytes 393224 | tf_op jit(solution)/shard_map/ppermute | solution.py:63
  19.7 6.1 %collective-permute-start.3 = (bf16[8,8192]{1,0:T(8,128)(2,1)S(1)}, bf16[8,8192]{1,0:T(8,128)(2,1)S(1)}, u32[]{:S(2)}, u32[]{:S(2)}) collective-permute-start(bf16[8,8192]{1,0:T(8,128)(2,1)S(1)} %pad_maximum_fusion), channel_id=1, source_target_pairs={{0,14},{2,0},{4,2},{6,4},{8,6},{10,8},{12,10},{14,12},{16,208},{18... | collective-permute-start | bytes 393224 | tf_op jit(solution)/shard_map/ppermute | solution.py:63
  26.8 13.9 %collective-permute-start.8 = (bf16[32,8192]{1,0:T(8,128)(2,1)S(1)}, bf16[32,8192]{1,0:T(8,128)(2,1)S(1)}, u32[]{:S(2)}, u32[]{:S(2)}) collective-permute-start(bf16[32,8192]{1,0:T(8,128)(2,1)S(1)} %concatenate.8.p0), channel_id=1, source_target_pairs={{0,128},{2,130},{4,132},{6,134},{8,136},{10,138},{12,140},{14,142}... | collective-permute-start | bytes 1572872 | tf_op jit(solution)/shard_map/ppermute | solution.py:63
  30.0 13.1 %collective-permute-start.7 = (bf16[32,8192]{1,0:T(8,128)(2,1)S(1)}, bf16[32,8192]{1,0:T(8,128)(2,1)S(1)}, u32[]{:S(2)}, u32[]{:S(2)}) collective-permute-start(bf16[32,8192]{1,0:T(8,128)(2,1)S(1)} %concatenate.8.p0), channel_id=1, source_target_pairs={{0,64},{2,66},{4,68},{6,70},{8,72},{10,74},{12,76},{14,78},{16,18}... | collective-permute-start | bytes 1572872 | tf_op jit(solution)/shard_map/ppermute | solution.py:63
  30.7 12.8 %collective-permute-start.6 = (bf16[32,8192]{1,0:T(8,128)(2,1)S(1)}, bf16[32,8192]{1,0:T(8,128)(2,1)S(1)}, u32[]{:S(2)}, u32[]{:S(2)}) collective-permute-start(bf16[32,8192]{1,0:T(8,128)(2,1)S(1)} %concatenate.8.p0), channel_id=1, source_target_pairs={{0,192},{2,194},{4,196},{6,198},{8,200},{10,202},{12,204},{14,206}... | collective-permute-start | bytes 1572872 | tf_op jit(solution)/shard_map/ppermute | solution.py:63
  33.4 11.6 %collective-permute-start.9 = (bf16[32,8192]{1,0:T(8,128)(2,1)S(1)}, bf16[32,8192]{1,0:T(8,128)(2,1)S(1)}, u32[]{:S(2)}, u32[]{:S(2)}) collective-permute-start(bf16[32,8192]{1,0:T(8,128)(2,1)S(1)} %concatenate.8.p0), channel_id=1, source_target_pairs={{0,16},{2,18},{4,20},{6,22},{8,24},{10,26},{12,28},{14,30},{16,0},... | collective-permute-start | bytes 1572872 | tf_op jit(solution)/shard_map/ppermute | solution.py:63
  33.4 0.7 copy-start
  34.1 13.2 %copy-start.1 = (s32[256]{0:T(256)S(1)}, s32[256]{0:T(256)}, u32[]{:S(2)}) copy-start(s32[256]{0:T(256)} %param.6) | copy-start | bytes 3076
  40.6 19.5 %copy-start.3 = (bf16[128,8192]{1,0:T(8,128)(2,1)S(1)}, bf16[128,8192]{1,0:T(8,128)(2,1)}, u32[]{:S(2)}) copy-start(bf16[128,8192]{1,0:T(8,128)(2,1)} %get-tuple-element.28) | copy-start | bytes 6291460
  40.7 38.6 %copy-start.2 = (f32[256]{0:T(256)S(1)}, f32[256]{0:T(256)}, u32[]{:S(2)}) copy-start(f32[256]{0:T(256)} %param.7) | copy-start | bytes 3076
  43.2 1.9 %collective-permute-start.11 = (bf16[32,8192]{1,0:T(8,128)(2,1)S(1)}, bf16[32,8192]{1,0:T(8,128)(2,1)S(1)}, u32[]{:S(2)}, u32[]{:S(2)}) collective-permute-start(bf16[32,8192]{1,0:T(8,128)(2,1)S(1)} %collective-permute-done.7.p2), channel_id=1, source_target_pairs={{0,16},{2,18},{4,20},{6,22},{8,24},{10,26},{12,28},{14,30},{16,0},... | collective-permute-start | bytes 1572872 | tf_op jit(solution)/shard_map/ppermute | solution.py:63
  43.5 3.0 %collective-permute-start.10 = (bf16[32,8192]{1,0:T(8,128)(2,1)S(1)}, bf16[32,8192]{1,0:T(8,128)(2,1)S(1)}, u32[]{:S(2)}, u32[]{:S(2)}) collective-permute-start(bf16[32,8192]{1,0:T(8,128)(2,1)S(1)} %collective-permute-done.6.p1), channel_id=1, source_target_pairs={{0,16},{2,18},{4,20},{6,22},{8,24},{10,26},{12,28},{14,30},{16,0},... | collective-permute-start | bytes 1572872 | tf_op jit(solution)/shard_map/ppermute | solution.py:63
  45.0 2.3 %collective-permute-start.12 = (bf16[32,8192]{1,0:T(8,128)(2,1)S(1)}, bf16[32,8192]{1,0:T(8,128)(2,1)S(1)}, u32[]{:S(2)}, u32[]{:S(2)}) collective-permute-start(bf16[32,8192]{1,0:T(8,128)(2,1)S(1)} %collective-permute-done.8.p3), channel_id=1, source_target_pairs={{0,16},{2,18},{4,20},{6,22},{8,24},{10,26},{12,28},{14,30},{16,0},... | collective-permute-start | bytes 1572872 | tf_op jit(solution)/shard_map/ppermute | solution.py:63
  55.8 3.1 %collective-permute-start.15 = (f32[3,256]{1,0:T(4,128)S(1)}, f32[3,256]{1,0:T(4,128)S(1)}, u32[]{:S(2)}, u32[]{:S(2)}) collective-permute-start(f32[3,256]{1,0:T(4,128)S(1)} %get-tuple-element.21.own_ref), channel_id=1, source_target_pairs={{0,48},{2,50},{4,52},{6,54},{8,56},{10,58},{12,60},{14,62},{16,32}... | collective-permute-start | bytes 9224 | tf_op jit(solution)/shard_map/ppermute | solution.py:63
  56.4 3.6 %collective-permute-start.14 = (f32[3,256]{1,0:T(4,128)S(1)}, f32[3,256]{1,0:T(4,128)S(1)}, u32[]{:S(2)}, u32[]{:S(2)}) collective-permute-start(f32[3,256]{1,0:T(4,128)S(1)} %get-tuple-element.21.own_ref), channel_id=1, source_target_pairs={{0,32},{2,34},{4,36},{6,38},{8,40},{10,42},{12,44},{14,46},{16,48}... | collective-permute-start | bytes 9224 | tf_op jit(solution)/shard_map/ppermute | solution.py:63
  57.9 2.2 %collective-permute-start.13 = (f32[3,256]{1,0:T(4,128)S(1)}, f32[3,256]{1,0:T(4,128)S(1)}, u32[]{:S(2)}, u32[]{:S(2)}) collective-permute-start(f32[3,256]{1,0:T(4,128)S(1)} %get-tuple-element.21.own_ref), channel_id=1, source_target_pairs={{0,16},{2,18},{4,20},{6,22},{8,24},{10,26},{12,28},{14,30},{16,0},... | collective-permute-start | bytes 9224 | tf_op jit(solution)/shard_map/ppermute | solution.py:63
  60.0 20.0 %collective-permute-start.16 = (bf16[128,8192]{1,0:T(8,128)(2,1)}, bf16[128,8192]{1,0:T(8,128)(2,1)S(1)}, u32[]{:S(2)}, u32[]{:S(2)}) collective-permute-start(bf16[128,8192]{1,0:T(8,128)(2,1)} %get-tuple-element.26), channel_id=1, source_target_pairs={{0,16},{2,18},{4,20},{6,22},{8,24},{10,26},{12,28},{14,30},{16,0},... | collective-permute-start | bytes 6291464 | tf_op jit(solution)/shard_map/ppermute | solution.py:63
  60.2 19.9 %collective-permute-start.17 = (bf16[128,8192]{1,0:T(8,128)(2,1)S(1)}, bf16[128,8192]{1,0:T(8,128)(2,1)S(1)}, u32[]{:S(2)}, u32[]{:S(2)}) collective-permute-start(bf16[128,8192]{1,0:T(8,128)(2,1)S(1)} %copy-done.3), channel_id=1, source_target_pairs={{0,16},{2,18},{4,20},{6,22},{8,24},{10,26},{12,28},{14,30},{16,0},... | collective-permute-start | bytes 6291464 | tf_op jit(solution)/shard_map/ppermute | solution.py:63
  81.9 10.9 %collective-permute-start.18 = (bf16[32,8192]{1,0:T(8,128)(2,1)S(1)}, bf16[32,8192]{1,0:T(8,128)(2,1)S(1)}, u32[]{:S(2)}, u32[]{:S(2)}) collective-permute-start(bf16[32,8192]{1,0:T(8,128)(2,1)S(1)} %combine.4), channel_id=1, source_target_pairs={{0,128},{2,130},{4,132},{6,134},{8,136},{10,138},{12,140},{14,142}... | collective-permute-start | bytes 1572872 | tf_op jit(solution)/shard_map/ppermute | solution.py:63
  85.6 12.7 %collective-permute-start.19 = (bf16[32,8192]{1,0:T(8,128)(2,1)S(1)}, bf16[32,8192]{1,0:T(8,128)(2,1)S(1)}, u32[]{:S(2)}, u32[]{:S(2)}) collective-permute-start(bf16[32,8192]{1,0:T(8,128)(2,1)S(1)} %get-tuple-element.29), channel_id=1, source_target_pairs={{0,64},{2,66},{4,68},{6,70},{8,72},{10,74},{12,76},{14,78},{16,18}... | collective-permute-start | bytes 1572872 | tf_op jit(solution)/shard_map/ppermute | solution.py:63
  86.4 11.9 %collective-permute-start.20 = (bf16[32,8192]{1,0:T(8,128)(2,1)S(1)}, bf16[32,8192]{1,0:T(8,128)(2,1)S(1)}, u32[]{:S(2)}, u32[]{:S(2)}) collective-permute-start(bf16[32,8192]{1,0:T(8,128)(2,1)S(1)} %get-tuple-element.30), channel_id=1, source_target_pairs={{0,192},{2,194},{4,196},{6,198},{8,200},{10,202},{12,204},{14,206}... | collective-permute-start | bytes 1572872 | tf_op jit(solution)/shard_map/ppermute | solution.py:63
  98.5 7.5 %collective-permute-start.21 = (bf16[8,8192]{1,0:T(8,128)(2,1)S(1)}, bf16[8,8192]{1,0:T(8,128)(2,1)S(1)}, u32[]{:S(2)}, u32[]{:S(2)}) collective-permute-start(bf16[8,8192]{1,0:T(8,128)(2,1)S(1)} %get-tuple-element.35), channel_id=1, source_target_pairs={{0,4},{2,6},{4,8},{6,10},{8,12},{10,14},{12,0},{14,2},{16,144},{18... | collective-permute-start | bytes 393224 | tf_op jit(solution)/shard_map/ppermute | solution.py:63
  100.1 6.0 %collective-permute-start.23 = (bf16[8,8192]{1,0:T(8,128)(2,1)S(1)}, bf16[8,8192]{1,0:T(8,128)(2,1)S(1)}, u32[]{:S(2)}, u32[]{:S(2)}) collective-permute-start(bf16[8,8192]{1,0:T(8,128)(2,1)S(1)} %get-tuple-element.36), channel_id=1, source_target_pairs={{0,14},{2,0},{4,2},{6,4},{8,6},{10,8},{12,10},{14,12},{16,208},{18... | collective-permute-start | bytes 393224 | tf_op jit(solution)/shard_map/ppermute | solution.py:63
  102.7 6.2 %collective-permute-start.22 = (bf16[8,8192]{1,0:T(8,128)(2,1)S(1)}, bf16[8,8192]{1,0:T(8,128)(2,1)S(1)}, u32[]{:S(2)}, u32[]{:S(2)}) collective-permute-start(bf16[8,8192]{1,0:T(8,128)(2,1)S(1)} %get-tuple-element.37), channel_id=1, source_target_pairs={{0,2},{2,4},{4,6},{6,8},{8,10},{10,12},{12,14},{14,0},{16,80},{18,... | collective-permute-start | bytes 393224 | tf_op jit(solution)/shard_map/ppermute | solution.py:63
  109.0 10.0 %collective-permute-start.26 = (f32[2,8192]{1,0:T(2,128)S(1)}, f32[2,8192]{1,0:T(2,128)S(1)}, u32[]{:S(2)}, u32[]{:S(2)}) collective-permute-start(f32[2,8192]{1,0:T(2,128)S(1)} %get-tuple-element.38), channel_id=1, source_target_pairs={{0,40},{2,42},{4,44},{6,46},{8,32},{10,34},{12,36},{14,38},{16,56}... | collective-permute-start | bytes 196616 | tf_op jit(solution)/shard_map/ppermute | solution.py:63
  110.8 10.5 %collective-permute-start.25 = (f32[2,8192]{1,0:T(2,128)S(1)}, f32[2,8192]{1,0:T(2,128)S(1)}, u32[]{:S(2)}, u32[]{:S(2)}) collective-permute-start(f32[2,8192]{1,0:T(2,128)S(1)} %get-tuple-element.39), channel_id=1, source_target_pairs={{0,8},{2,10},{4,12},{6,14},{8,0},{10,2},{12,4},{14,6},{16,24},{18,... | collective-permute-start | bytes 196616 | tf_op jit(solution)/shard_map/ppermute | solution.py:63
  115.6 5.7 %collective-permute-start.24 = (f32[2,8192]{1,0:T(2,128)S(1)}, f32[2,8192]{1,0:T(2,128)S(1)}, u32[]{:S(2)}, u32[]{:S(2)}) collective-permute-start(f32[2,8192]{1,0:T(2,128)S(1)} %get-tuple-element.40), channel_id=1, source_target_pairs={{0,32},{2,34},{4,36},{6,38},{8,40},{10,42},{12,44},{14,46},{16,48}... | collective-permute-start | bytes 196616 | tf_op jit(solution)/shard_map/ppermute | solution.py:63

commit v7 on v6

--- a/solution.py
+++ b/solution.py
@@ -154,45 +154,87 @@
         out_ref[i] = merged
 
 
-def scales_kernel(at_ref, grad_ref, own_ref, core_ref, spread_ref, out_ref):
-    place = placed(at_ref)[: ROWS // 2]
-
-    def ordered(row):
-        return jnp.sum(jnp.where(place, row, 0.0), axis=1, keepdims=True)
-
+def in_order(place):
+    return lambda row: jnp.sum(jnp.where(place, row, 0.0), axis=1, keepdims=True)
+
+
+def piece_copies(parts, pairs, sems):
+    every = []
+    for i, q in enumerate(parts):
+        copies = [
+            pltpu.make_async_copy(source.at[pl.ds(32 * q, 32)], buffer.at[i], sems.at[i, j])
+            for j, (source, buffer) in enumerate(pairs)
+        ]
+        for copy in copies:
+            copy.start()
+        every.append(copies)
+    return every
+
+
+def target_pair_kernel(own_hbm, in_hbm, o1, o2, o3, a_ref, b_ref, sems):
+    every = piece_copies((1, 2, 3), ((own_hbm, a_ref), (in_hbm, b_ref)), sems)
+    for i, out in enumerate((o1, o2, o3)):
+        for copy in every[i]:
+            copy.wait()
+        for k in range(0, DEPTH, CHUNK):
+            cut = slice(k, k + CHUNK)
+            out[:, cut] = (a_ref[i, :, cut].astype(F32) + b_ref[i, :, cut].astype(F32)).astype(BF)
+
+
+def soft_pair_kernel(parts, at_ref, own_stats, core_stats, merged_ref, own_hbm, in_hbm, *refs):
+    outs, (a_ref, b_ref, sems) = refs[: len(parts)], refs[len(parts) :]
+    every = piece_copies(parts, ((own_hbm, a_ref), (in_hbm, b_ref)), sems)
+    place = placed(at_ref)
+    for i, (q, out) in enumerate(zip(parts, outs)):
+        ordered = in_order(place[32 * q : 32 * q + 32])
+        own, core = (ordered(jnp.exp(r[0:1, :] - merged_ref[0, 0:1, :])) for r in (own_stats, core_stats))
+        for copy in every[i]:
+            copy.wait()
+        for k in range(0, DEPTH, CHUNK):
+            cut = slice(k, k + CHUNK)
+            out[:, cut] = (own * a_ref[i, :, cut] + core * b_ref[i, :, cut].astype(F32)).astype(BF)
+
+
+def finish_kernel(at_ref, grad_ref, own_stats, core_stats, spread_ref, *refs):
+    own_hbm, in_hbm, target_own, target_in = refs[:4]
+    soft_hbm, target_hbm = refs[4:7], refs[7:10]
+    out_ref, log_ref, a_ref, b_ref, c_ref, d_ref, soft_ref, target_ref, sems, in_sems = refs[10:]
+    first = piece_copies((0,), ((own_hbm, a_ref), (in_hbm, b_ref), (target_own, c_ref), (target_in, d_ref)), sems)[0]
+    rest = [pltpu.make_async_copy(h, soft_ref.at[i], in_sems.at[0, i]) for i, h in enumerate(soft_hbm)]
+    rest += [pltpu.make_async_copy(h, target_ref.at[i], in_sems.at[1, i]) for i, h in enumerate(target_hbm)]
+    for copy in rest:
+        copy.start()
+    ordered = in_order(placed(at_ref)[:32])
     tops = spread_ref[:, 0, :]
     highest = jnp.max(tops, axis=0, keepdims=True)
     total = jnp.sum(spread_ref[:, 1, :] * jnp.exp(tops - highest), axis=0, keepdims=True)
-    log_total = ordered(highest + jnp.log(total))
+    log_row = highest + jnp.log(total)
+    log_total = ordered(log_row)
     picked = ordered(jnp.sum(spread_ref[:, 2, :], axis=0, keepdims=True))
+    log_ref[...] = jnp.where(lax.broadcasted_iota(jnp.int32, (8, 128), 1) == 0, log_total[:8], picked[:8])
     factor = 1.0 + 2.0 * zloss_coef * log_total
     grad = ordered(grad_ref[...])
     target = (grad * (jnp.exp(picked - log_total) * factor - 1.0)).astype(BF).astype(F32)
-    own, core = (grad * factor * jnp.exp(ordered(ref[0:1, :]) - log_total) for ref in (own_ref, core_ref))
-    lane = lax.broadcasted_iota(jnp.int32, (ROWS // 2, 128), 1)
-    rest = jnp.where(lane == 2, target, jnp.where(lane == 3, log_total, picked))
-    out_ref[...] = jnp.where(lane == 0, own, jnp.where(lane == 1, core, rest))
-
-
-def combine_kernel(parts, scales_ref, soft_own, soft_in, target_own, target_in, *refs):
-    outs, (a_ref, b_ref, c_ref, d_ref, sems) = refs[: len(parts)], refs[len(parts) :]
-    every = []
-    for i, q in enumerate(parts):
-        sources = ((soft_own, a_ref), (soft_in, b_ref), (target_own, c_ref), (target_in, d_ref))
-        every.append(
-            [pltpu.make_async_copy(s.at[pl.ds(32 * q, 32)], t.at[i], sems.at[i, j]) for j, (s, t) in enumerate(sources)]
-        )
-        for copy in every[-1]:
-            copy.start()
-    for i, (q, out) in enumerate(zip(parts, outs)):
-        for copy in every[i]:
-            copy.wait()
-        own, core, target = (scales_ref[32 * q : 32 * q + 32, i : i + 1] for i in range(3))
-        for k in range(0, DEPTH, CHUNK):
-            cut = slice(k, k + CHUNK)
-            soft = own * a_ref[i, :, cut] + core * b_ref[i, :, cut].astype(F32)
-            chosen = c_ref[i, :, cut].astype(F32) + d_ref[i, :, cut].astype(F32)
-            out[:, cut] = (soft + target * chosen).astype(out.dtype)
+    y, c, z = at_ref[0], at_ref[2], at_ref[3]
+
+    def scale(top_row):
+        return grad * factor * ordered(jnp.exp(top_row - log_row))
+
+    own, core = scale(own_stats[0:1, :]), scale(core_stats[0:1, :])
+    others = []
+    for o in OFFSETS[1:]:
+        sender = jnp.where(c == 0, ((y - o) & 3) * NZ + z, y * NZ + ((z - o) & 7))
+        others.append(scale(spread_ref[sender, 0:1, :]))
+    for copy in first + rest:
+        copy.wait()
+    for k in range(0, DEPTH, CHUNK):
+        cut = slice(k, k + CHUNK)
+        soft = own * a_ref[0, :, cut] + core * b_ref[0, :, cut].astype(F32)
+        chosen = c_ref[0, :, cut].astype(F32) + d_ref[0, :, cut].astype(F32)
+        for i in range(3):
+            soft += others[i] * soft_ref[i, :, cut].astype(F32)
+            chosen += target_ref[i, :, cut].astype(F32)
+        out_ref[:, cut] = soft + target * chosen
 
 
 def shards(hidden, lm_weight, targets, loss_grad):
@@ -203,11 +245,8 @@
     weights = [pltpu.VMEM((DEPTH, WIDTH), BF)]
     sems = pltpu.SemaphoreType.DMA((STEPS,))
 
-    block = jnp.concatenate([hidden] + [send(hidden, to) for to in (to_x, to_z4, to_xz4)])
-    block = jnp.concatenate([block] + [send(block, to_first(-o)) for o in OFFSETS[1:]])
-    near, back, far = (send(block, to_second(-o)) for o in OFFSETS[1:])
-
-    aim, _ = lax.optimization_barrier((targets, block))
+    block = jnp.concatenate([hidden, send(hidden, to_x)])
+    aim, block = lax.optimization_barrier((targets, block))
     target_own, target_out = pl.pallas_call(
         target_kernel,
         out_shape=[pltpu.HBM((half, DEPTH), BF)] * 2,
@@ -218,7 +257,25 @@
         cost_estimate=pl.CostEstimate(flops=2 * ROWS * DEPTH * WIDTH, bytes_accessed=12 << 20, transcendentals=0),
         name="target",
     )(at, aim, lm_weight)
-    far, target_own, target_out = lax.optimization_barrier((far, target_own, target_out))
+    hop, target_out = lax.optimization_barrier((send(block, to_z4), target_out))
+    target_in = send(target_out, to_c)
+    block = jnp.concatenate([block, hop])
+    block = jnp.concatenate([block] + [send(block, to_first(-o)) for o in OFFSETS[1:]])
+    near, back, far = (send(block, to_second(-o)) for o in OFFSETS[1:])
+
+    target_own = pltpu.with_memory_space_constraint(target_own, pltpu.HBM)
+    target_parts = pl.pallas_call(
+        target_pair_kernel,
+        out_shape=[jax.ShapeDtypeStruct((32, DEPTH), BF)] * 3,
+        in_specs=[ANY] * 2,
+        out_specs=[VMEM] * 3,
+        scratch_shapes=[pltpu.VMEM((3, 32, DEPTH), BF)] * 2 + [pltpu.SemaphoreType.DMA((3, 2))],
+        compiler_params=params(),
+        cost_estimate=pl.CostEstimate(flops=3 * 32 * DEPTH, bytes_accessed=5 << 20, transcendentals=0),
+        name="target_pair",
+    )(target_own, target_in)
+    near, back, far, *target_parts = lax.optimization_barrier((near, back, far, *target_parts))
+    target_got = [send(p, to_second(o)) for p, o in zip(target_parts, OFFSETS[1:])]
     pieces = [block, near, back, far]
     pieces = pieces + [send(p, to_c) for p in pieces]
 
@@ -229,7 +286,7 @@
         out_specs=(VMEM, HBM, HBM),
         scratch_shapes=weights + [pltpu.VMEM((half, DEPTH), F32), pltpu.VMEM((half, DEPTH), BF)] + [sems] * 3,
         compiler_params=params(32),
-        cost_estimate=pl.CostEstimate(flops=4 * ROWS * DEPTH * WIDTH, bytes_accessed=19 << 20, transcendentals=ROWS * WIDTH),
+        cost_estimate=pl.CostEstimate(flops=1 << 20, bytes_accessed=1 << 16, transcendentals=0),
         name="logits",
     )(at, targets, *pieces, lm_weight)
     stats = [stats] + [send(stats, to) for to in (to_c, to_x, to_xc)]
@@ -241,40 +298,42 @@
         compiler_params=params(),
         name="merge",
     )(*stats)
-    merged, soft_out, target_out = lax.optimization_barrier((merged, soft_out, target_out))
-    soft_in, target_in = send(soft_out, to_c), send(target_out, to_c)
-    spread = lax.all_to_all(merged, ("y", "z"), 0, 0)
-
-    scales = pl.pallas_call(
-        scales_kernel,
-        out_shape=jax.ShapeDtypeStruct((half, 128), F32),
-        in_specs=[SMEM] + [VMEM] * 4,
-        out_specs=VMEM,
-        compiler_params=params(),
-        name="scales",
-    )(at, loss_grad, stats[0], stats[1], spread)
-
-    soft_own, target_own = (pltpu.with_memory_space_constraint(v, pltpu.HBM) for v in (soft_own, target_own))
-
-    def combine(parts, dtype):
+    soft_own = pltpu.with_memory_space_constraint(soft_own, pltpu.HBM)
+
+    def soft_pair(parts):
         n = len(parts)
         return pl.pallas_call(
-            functools.partial(combine_kernel, parts),
-            out_shape=[jax.ShapeDtypeStruct((32, DEPTH), dtype)] * n,
-            in_specs=[VMEM] + [ANY] * 4,
+            functools.partial(soft_pair_kernel, parts),
+            out_shape=[jax.ShapeDtypeStruct((32, DEPTH), BF)] * n,
+            in_specs=[SMEM] + [VMEM] * 3 + [ANY] * 2,
             out_specs=[VMEM] * n,
-            scratch_shapes=[pltpu.VMEM((n, 32, DEPTH), F32)]
-            + [pltpu.VMEM((n, 32, DEPTH), BF)] * 3
-            + [pltpu.SemaphoreType.DMA((n, 4))],
+            scratch_shapes=[pltpu.VMEM((n, 32, DEPTH), F32), pltpu.VMEM((n, 32, DEPTH), BF), pltpu.SemaphoreType.DMA((n, 2))],
             compiler_params=params(),
-            cost_estimate=pl.CostEstimate(flops=6 * 32 * DEPTH * n, bytes_accessed=n * (3 << 20), transcendentals=0),
-            name="combine",
-        )(scales, soft_own, soft_in, target_own, target_in)
-
-    parts = combine((3,), BF) + combine((1, 2), BF)
-    arrived = [send(p, to_second(o)).astype(F32) for p, o in zip(parts, (2, 1, -1))]
-    part = combine((0,), F32)[0] + sum(arrived)
-    log_total, target_logit = scales[:2, 3], scales[:2, 4]
+            cost_estimate=pl.CostEstimate(flops=4 * 32 * DEPTH * n, bytes_accessed=n * (2 << 20), transcendentals=0),
+            name="soft_pair",
+        )(at, stats[0], stats[1], merged, soft_own, soft_in)
+
+    soft_in = send(soft_out, to_c)
+    (far,) = soft_pair((3,))
+    near, back = soft_pair((1, 2))
+    merged, near, back, far = lax.optimization_barrier((merged, near, back, far))
+    soft_got = [send(p, to_second(o)) for p, o in zip((near, back, far), OFFSETS[1:])]
+    spread = lax.all_to_all(merged, ("y", "z"), 0, 0)
+
+    piece = pltpu.VMEM((1, 32, DEPTH), BF)
+    part, logs = pl.pallas_call(
+        finish_kernel,
+        out_shape=(jax.ShapeDtypeStruct((32, DEPTH), F32), jax.ShapeDtypeStruct((8, 128), F32)),
+        in_specs=[SMEM] + [VMEM] * 4 + [ANY] * 10,
+        out_specs=(VMEM, VMEM),
+        scratch_shapes=[pltpu.VMEM((1, 32, DEPTH), F32), piece, piece, piece]
+        + [pltpu.VMEM((3, 32, DEPTH), BF)] * 2
+        + [pltpu.SemaphoreType.DMA((1, 4)), pltpu.SemaphoreType.DMA((2, 3))],
+        compiler_params=params(),
+        cost_estimate=pl.CostEstimate(flops=16 * 32 * DEPTH, bytes_accessed=7 << 20, transcendentals=0),
+        name="finish",
+    )(at, loss_grad, stats[0], stats[1], spread, soft_own, soft_in, target_own, target_in, *soft_got, *target_got)
+    log_total, target_logit = logs[:2, 0], logs[:2, 1]
     ce_loss = log_total - target_logit
     z_term = zloss_coef * log_total * log_total
 

time: 124 us -> 133 us (1.073)
  the two profiles are of different devices: /device:TPU:4 before, /device:TPU:1 now
where the time goes in v7:
time: 133 us; the launch traced here: 132 us
  starting transfers between devices  50.3 us (38%)
  waiting for transfers between devices  47 us (35%)
  Pallas kernels  29 us (22%)
  local copies, waits for them, and re-layouts  2.76 us (2%)
  other arithmetic  2.21 us (2%)
    ppermute x29, starting transfers between devices, send(): return lax.ppermute(value, GROUP, pairs(route))  43.5 us
    ppermute x29, waiting for transfers between devices, send(): return lax.ppermute(value, GROUP, pairs(route))  28.2 us
    all_to_all x1, waiting for transfers between devices, shards(): spread = lax.all_to_all(merged, ('y', 'z'), 0, 0)  18.8 us
    pallas_call x1, Pallas kernels, shards(): pl.pallas_call(logits_kernel, out_shape=(jax.ShapeDtypeStruct((3, ROWS),...  8.47 us
    all_to_all x1, starting transfers between devices, shards(): spread = lax.all_to_all(merged, ('y', 'z'), 0, 0)  6.74 us
    pallas_call x2, Pallas kernels, soft_pair(): pl.pallas_call(functools.partial(soft_pair_kernel, parts), out_shape=[jax...  6.67 us
    pallas_call x1, Pallas kernels, shards(): pl.pallas_call(target_kernel, out_shape=[pltpu.HBM((half, DEPTH), BF)] *...  6.54 us
    pallas_call x1, Pallas kernels, shards(): pl.pallas_call(finish_kernel, out_shape=(jax.ShapeDtypeStruct((32, DEPTH)...  3.48 us
  transfers between devices with their start and end apart: 30, of which 13 were waited for; matrix products, arithmetic and copies ran while one was open for 1% of the time, Pallas kernels for 13%

profile of v7, /device:TPU:1, one launch (start us, length us, event | category | flops | bytes accessed | tf_op | source)
XLA Modules:
  0.0 132.1 jit_solution(8454871704861678696)
XLA Ops:
  0.6 2.1 %collective-permute-start = (bf16[2,8192]{1,0:T(2,128)(2,1)}, bf16[2,8192]{1,0:T(2,128)(2,1)S(1)}, u32[]{:S(2)}, u32[]{:S(2)}) collective-permute-start(bf16[2,8192]{1,0:T(2,128)(2,1)} %param.4), channel_id=1, source_target_pairs={{0,32},{2,34},{4,36},{6,38},{8,40},{10,42},{12,44},{14,46},{16,48}... | collective-permute-start | bytes 98312 | tf_op jit(solution)/shard_map/ppermute | solution.py:63
  2.8 0.1 stack.23.at_ref
  2.8 1.4 %collective-permute-done = bf16[2,8192]{1,0:T(2,128)(2,1)S(1)} collective-permute-done((bf16[2,8192]{1,0:T(2,128)(2,1)}, bf16[2,8192]{1,0:T(2,128)(2,1)S(1)}, u32[]{:S(2)}, u32[]{:S(2)}) %collective-permute-start) | collective-permute-done | bytes 32800 | tf_op jit(solution)/shard_map/ppermute | solution.py:63
  4.3 0.8 pad_maximum_fusion.1
  5.1 7.2 %collective-permute-start.1 = (bf16[4,8192]{1,0:T(4,128)(2,1)S(1)}, bf16[4,8192]{1,0:T(4,128)(2,1)S(1)}, u32[]{:S(2)}, u32[]{:S(2)}) collective-permute-start(bf16[4,8192]{1,0:T(4,128)(2,1)S(1)} %pad_maximum_fusion.1), channel_id=1, source_target_pairs={{0,8},{2,10},{4,12},{6,14},{8,0},{10,2},{12,4},{14,6},{16,24},{18,... | collective-permute-start | bytes 196616 | tf_op jit(solution)/shard_map/ppermute | solution.py:63
  12.4 0.7 copy-done.2
  13.0 6.5 %target.1 = (bf16[128,8192]{1,0:T(8,128)(2,1)}, bf16[128,8192]{1,0:T(8,128)(2,1)}) custom-call(s32[5]{0:T(128)S(1)} %stack.23.at_ref, s32[1,256]{1,0:T(1,128)S(1)} %bitcast.7, bf16[8192,512]{1,0:T(8,128)(2,1)} %w_hbm.3), custom_call_target="tpu_custom_call" | custom-call | flops 2147483648 | bytes 12582912 | tf_op jit(solution)/shard_map/target/pallas_call | solution.py:250
  19.6 2.2 %collective-permute-start.8 = (bf16[128,8192]{1,0:T(8,128)(2,1)}, bf16[128,8192]{1,0:T(8,128)(2,1)S(1)}, u32[]{:S(2)}, u32[]{:S(2)}) collective-permute-start(bf16[128,8192]{1,0:T(8,128)(2,1)} %get-tuple-element.34), channel_id=1, source_target_pairs={{0,16},{2,18},{4,20},{6,22},{8,24},{10,26},{12,28},{14,30},{16,0},... | collective-permute-start | bytes 6291464 | tf_op jit(solution)/shard_map/ppermute | solution.py:63
  21.8 0.1 pad_maximum_fusion
  21.9 3.0 %collective-permute-start.4 = (bf16[8,8192]{1,0:T(8,128)(2,1)S(1)}, bf16[8,8192]{1,0:T(8,128)(2,1)S(1)}, u32[]{:S(2)}, u32[]{:S(2)}) collective-permute-start(bf16[8,8192]{1,0:T(8,128)(2,1)S(1)} %pad_maximum_fusion), channel_id=1, source_target_pairs={{0,12},{2,14},{4,0},{6,2},{8,4},{10,6},{12,8},{14,10},{16,144},{18... | collective-permute-start | bytes 393224 | tf_op jit(solution)/shard_map/ppermute | solution.py:63
  24.8 0.4 collective-permute-start.3
  25.2 2.3 %collective-permute-start.2 = (bf16[8,8192]{1,0:T(8,128)(2,1)S(1)}, bf16[8,8192]{1,0:T(8,128)(2,1)S(1)}, u32[]{:S(2)}, u32[]{:S(2)}) collective-permute-start(bf16[8,8192]{1,0:T(8,128)(2,1)S(1)} %pad_maximum_fusion), channel_id=1, source_target_pairs={{0,14},{2,0},{4,2},{6,4},{8,6},{10,8},{12,10},{14,12},{16,208},{18... | collective-permute-start | bytes 393224 | tf_op jit(solution)/shard_map/ppermute | solution.py:63
  27.5 0.0 collective-permute-done.4
  27.5 2.3 %collective-permute-done.3 = bf16[8,8192]{1,0:T(8,128)(2,1)S(1)} collective-permute-done((bf16[8,8192]{1,0:T(8,128)(2,1)S(1)}, bf16[8,8192]{1,0:T(8,128)(2,1)S(1)}, u32[]{:S(2)}, u32[]{:S(2)}) %collective-permute-start.3) | collective-permute-done | bytes 131104 | tf_op jit(solution)/shard_map/ppermute | solution.py:63
  29.9 0.0 collective-permute-done.2
  29.9 0.1 concatenate.12.p0
  30.0 0.1 collective-permute-start.7
  30.1 1.3 collective-permute-start.6
  31.4 1.5 %collective-permute-start.5 = (bf16[32,8192]{1,0:T(8,128)(2,1)S(1)}, bf16[32,8192]{1,0:T(8,128)(2,1)S(1)}, u32[]{:S(2)}, u32[]{:S(2)}) collective-permute-start(bf16[32,8192]{1,0:T(8,128)(2,1)S(1)} %concatenate.12.p0), channel_id=1, source_target_pairs={{0,192},{2,194},{4,196},{6,198},{8,200},{10,202},{12,204},{14,206}... | collective-permute-start | bytes 1572872 | tf_op jit(solution)/shard_map/ppermute | solution.py:63
  32.8 3.1 %collective-permute-start.9 = (bf16[32,8192]{1,0:T(8,128)(2,1)S(1)}, bf16[32,8192]{1,0:T(8,128)(2,1)S(1)}, u32[]{:S(2)}, u32[]{:S(2)}) collective-permute-start(bf16[32,8192]{1,0:T(8,128)(2,1)S(1)} %concatenate.12.p0), channel_id=1, source_target_pairs={{0,16},{2,18},{4,20},{6,22},{8,24},{10,26},{12,28},{14,30},{16,0},... | collective-permute-start | bytes 1572872 | tf_op jit(solution)/shard_map/ppermute | solution.py:63
  36.0 3.2 %target_pair.1 = (bf16[32,8192]{1,0:T(8,128)(2,1)S(1)}, bf16[32,8192]{1,0:T(8,128)(2,1)}, bf16[32,8192]{1,0:T(8,128)(2,1)}) custom-call(bf16[128,8192]{1,0:T(8,128)(2,1)} %get-tuple-element.33.own_hbm.refs_2_, bf16[128,8192]{1,0:T(8,128)(2,1)S(1)} %collective-permute-done.8.in_hbm.refs_3_), custom_call_target="tpu_custom_call" | custom-call | flops 786432 | bytes 5242880 | tf_op jit(solution)/shard_map/target_pair/pallas_call | solution.py:267
  39.2 5.6 %collective-permute-done.7.p3 = bf16[32,8192]{1,0:T(8,128)(2,1)S(1)} collective-permute-done((bf16[32,8192]{1,0:T(8,128)(2,1)S(1)}, bf16[32,8192]{1,0:T(8,128)(2,1)S(1)}, u32[]{:S(2)}, u32[]{:S(2)}) %collective-permute-start.7) | collective-permute-done | bytes 524320 | tf_op jit(solution)/shard_map/ppermute | solution.py:63
  44.8 4.5 %collective-permute-done.5.p1 = bf16[32,8192]{1,0:T(8,128)(2,1)S(1)} collective-permute-done((bf16[32,8192]{1,0:T(8,128)(2,1)S(1)}, bf16[32,8192]{1,0:T(8,128)(2,1)S(1)}, u32[]{:S(2)}, u32[]{:S(2)}) %collective-permute-start.5) | collective-permute-done | bytes 524320 | tf_op jit(solution)/shard_map/ppermute | solution.py:63
  49.3 0.0 collective-permute-start.10
  49.3 0.5 collective-permute-start.11
  49.8 0.0 collective-permute-start.12
  49.8 1.4 %collective-permute-done.10.p5 = bf16[32,8192]{1,0:T(8,128)(2,1)S(1)} collective-permute-done((bf16[32,8192]{1,0:T(8,128)(2,1)S(1)}, bf16[32,8192]{1,0:T(8,128)(2,1)S(1)}, u32[]{:S(2)}, u32[]{:S(2)}) %collective-permute-start.10) | collective-permute-done | bytes 524320 | tf_op jit(solution)/shard_map/ppermute | solution.py:63
  51.2 0.7 collective-permute-done.11.p6
  51.9 0.7 collective-permute-done.12.p7
  52.7 8.5 %logits.1 = (f32[3,256]{1,0:T(4,128)S(1)}, f32[128,8192]{1,0:T(8,128)}, bf16[128,8192]{1,0:T(8,128)(2,1)}) custom-call(s32[5]{0:T(128)S(1)} %stack.23.at_ref, s32[1,256]{1,0:T(1,128)S(1)} %bitcast.8, bf16[32,8192]{1,0:T(8,128)(2,1)S(1)} %concatenate.12.p0, bf16[32,8192]{1,0:T(8,128)(2,1)S(1)} %collective-permute-done.5.p1, ...), custom_call_target="tpu_custom_call" | custom-call | flops 1048576 | bytes 65536 | tf_op jit(solution)/shard_map/logits/pallas_call | solution.py:282
  61.2 0.2 collective-permute-start.16
  61.4 1.3 collective-permute-start.20
  62.7 0.7 collective-permute-start.15
  63.3 0.6 collective-permute-start.14
  64.0 0.8 collective-permute-start.13
  64.8 0.9 collective-permute-done.15.both_ref
  65.7 1.4 %collective-permute-start.21 = (bf16[32,8192]{1,0:T(8,128)(2,1)}, bf16[32,8192]{1,0:T(8,128)(2,1)S(1)}, u32[]{:S(2)}, u32[]{:S(2)}) collective-permute-start(bf16[32,8192]{1,0:T(8,128)(2,1)} %get-tuple-element.51), channel_id=1, source_target_pairs={{0,192},{2,194},{4,196},{6,198},{8,200},{10,202},{12,204},{14,206}... | collective-permute-start | bytes 1572872 | tf_op jit(solution)/shard_map/ppermute | solution.py:63
  67.1 1.4 %collective-permute-start.22 = (bf16[32,8192]{1,0:T(8,128)(2,1)}, bf16[32,8192]{1,0:T(8,128)(2,1)}, u32[]{:S(2)}, u32[]{:S(2)}) collective-permute-start(bf16[32,8192]{1,0:T(8,128)(2,1)} %get-tuple-element.52), channel_id=1, source_target_pairs={{0,128},{2,130},{4,132},{6,134},{8,136},{10,138},{12,140},{14,142}... | collective-permute-start | bytes 1572872 | tf_op jit(solution)/shard_map/ppermute | solution.py:63
  68.5 0.7 merge.1.merged_ref
  69.2 3.1 %soft_pair.3 = bf16[32,8192]{1,0:T(8,128)(2,1)} custom-call(s32[5]{0:T(128)S(1)} %stack.23.at_ref, f32[3,256]{1,0:T(4,128)S(1)} %get-tuple-element.41.own_ref.own_stats, f32[3,256]{1,0:T(4,128)S(1)} %collective-permute-done.13.core_ref.core_stats, f32[32,3,256]{2,1,0:T(4,128)} %merge.1.merged_ref, f32[128,8192]{1,0:T(8,128)} %get-tuple-element.42.own_hbm.refs_0_, ...), custom_call_target="tpu_custom_call" | custom-call | flops 1048576 | bytes 2097152 | tf_op jit(solution)/shard_map/soft_pair/pallas_call | solution.py:305
  72.4 0.0 copy-start.4
  72.4 3.5 %soft_pair.2 = (bf16[32,8192]{1,0:T(8,128)(2,1)}, bf16[32,8192]{1,0:T(8,128)(2,1)}) custom-call(s32[5]{0:T(128)S(1)} %stack.23.at_ref, f32[3,256]{1,0:T(4,128)S(1)} %get-tuple-element.41.own_ref.own_stats, f32[3,256]{1,0:T(4,128)S(1)} %collective-permute-done.13.core_ref.core_stats, f32[32,3,256]{2,1,0:T(4,128)} %merge.1.merged_ref, ...), custom_call_target="tpu_custom_call" | custom-call | flops 2097152 | bytes 4194304 | tf_op jit(solution)/shard_map/soft_pair/pallas_call | solution.py:305
  75.9 1.6 %collective-permute-start.17 = (bf16[32,8192]{1,0:T(8,128)(2,1)}, bf16[32,8192]{1,0:T(8,128)(2,1)}, u32[]{:S(2)}, u32[]{:S(2)}) collective-permute-start(bf16[32,8192]{1,0:T(8,128)(2,1)} %get-tuple-element.47), channel_id=1, source_target_pairs={{0,64},{2,66},{4,68},{6,70},{8,72},{10,74},{12,76},{14,78},{16,18}... | collective-permute-start | bytes 1572872 | tf_op jit(solution)/shard_map/ppermute | solution.py:63
  77.6 1.1 collective-permute-start.18
  78.7 1.5 %collective-permute-start.19 = (bf16[32,8192]{1,0:T(8,128)(2,1)}, bf16[32,8192]{1,0:T(8,128)(2,1)}, u32[]{:S(2)}, u32[]{:S(2)}) collective-permute-start(bf16[32,8192]{1,0:T(8,128)(2,1)} %soft_pair.3), channel_id=1, source_target_pairs={{0,128},{2,130},{4,132},{6,134},{8,136},{10,138},{12,140},{14,142}... | collective-permute-start | bytes 1572872 | tf_op jit(solution)/shard_map/ppermute | solution.py:63
  80.2 6.7 %all-to-all-start = ((f32[32,3,256]{2,1,0:T(4,128)}), f32[32,3,256]{2,1,0:T(4,128)S(1)}, u32[]{:S(2)}, u32[]{:S(2)}) async-start(f32[32,3,256]{2,1,0:T(4,128)} %merge.1.merged_ref), calls=%async_computation | async-start | bytes 262144 | tf_op jit(solution)/shard_map/all_to_all | solution.py:321
  87.0 18.8 %all-to-all-done.spread_ref = f32[32,3,256]{2,1,0:T(4,128)S(1)} async-done(((f32[32,3,256]{2,1,0:T(4,128)}), f32[32,3,256]{2,1,0:T(4,128)S(1)}, u32[]{:S(2)}, u32[]{:S(2)}) %all-to-all-start) | async-done | bytes 98336 | tf_op jit(solution)/shard_map/all_to_all | solution.py:321
  105.8 1.6 %copy-done.1 = bf16[128,8192]{1,0:T(8,128)(2,1)S(1)} copy-done((bf16[128,8192]{1,0:T(8,128)(2,1)S(1)}, bf16[128,8192]{1,0:T(8,128)(2,1)}, u32[]{:S(2)}) %copy-start.1) | copy-done | bytes 2097176
  107.4 3.5 %finish.1 = (f32[32,8192]{1,0:T(8,128)S(1)}, f32[8,128]{1,0:T(8,128)S(1)}) custom-call(s32[5]{0:T(128)S(1)} %stack.23.at_ref, f32[1,256]{1,0:T(1,128)S(1)} %bitcast.9, f32[3,256]{1,0:T(4,128)S(1)} %get-tuple-element.41.own_ref.own_stats, f32[3,256]{1,0:T(4,128)S(1)} %collective-permute-done.13.core_ref.core_stats, ...), custom_call_target="tpu_custom_call" | custom-call | flops 4194304 | bytes 7340032 | tf_op jit(solution)/shard_map/finish/pallas_call | solution.py:324
  110.9 0.1 convert.5
  111.0 0.7 collective-permute-start.23
  111.7 1.7 %collective-permute-start.25 = (bf16[8,8192]{1,0:T(8,128)(2,1)S(1)}, bf16[8,8192]{1,0:T(8,128)(2,1)S(1)}, u32[]{:S(2)}, u32[]{:S(2)}) collective-permute-start(bf16[8,8192]{1,0:T(8,128)(2,1)S(1)} %get-tuple-element.58), channel_id=1, source_target_pairs={{0,14},{2,0},{4,2},{6,4},{8,6},{10,8},{12,10},{14,12},{16,208},{18... | collective-permute-start | bytes 393224 | tf_op jit(solution)/shard_map/ppermute | solution.py:63
  113.4 0.2 slice_reduce_fusion
  113.6 2.8 %collective-permute-done.23 = bf16[8,8192]{1,0:T(8,128)(2,1)S(1)} collective-permute-done((bf16[8,8192]{1,0:T(8,128)(2,1)S(1)}, bf16[8,8192]{1,0:T(8,128)(2,1)S(1)}, u32[]{:S(2)}, u32[]{:S(2)}) %collective-permute-start.23) | collective-permute-done | bytes 131104 | tf_op jit(solution)/shard_map/ppermute | solution.py:63
  116.4 2.1 %collective-permute-done.24 = bf16[8,8192]{1,0:T(8,128)(2,1)S(1)} collective-permute-done((bf16[8,8192]{1,0:T(8,128)(2,1)S(1)}, bf16[8,8192]{1,0:T(8,128)(2,1)S(1)}, u32[]{:S(2)}, u32[]{:S(2)}) %collective-permute-start.24) | collective-permute-done | bytes 131104 | tf_op jit(solution)/shard_map/ppermute | solution.py:63
  118.4 0.1 add_add_fusion
  118.5 0.1 fusion.3
  118.6 5.1 %collective-permute-start.28 = (f32[2,8192]{1,0:T(2,128)S(1)}, f32[2,8192]{1,0:T(2,128)S(1)}, u32[]{:S(2)}, u32[]{:S(2)}) collective-permute-start(f32[2,8192]{1,0:T(2,128)S(1)} %get-tuple-element.60), channel_id=1, source_target_pairs={{0,40},{2,42},{4,44},{6,46},{8,32},{10,34},{12,36},{14,38},{16,56}... | collective-permute-start | bytes 196616 | tf_op jit(solution)/shard_map/ppermute | solution.py:63
  123.7 1.3 collective-permute-start.27
  125.0 0.2 collective-permute-start.26
  125.2 0.5 multiply_multiply_fusion
  125.8 1.7 %collective-permute-done.28 = f32[2,8192]{1,0:T(2,128)S(1)} collective-permute-done((f32[2,8192]{1,0:T(2,128)S(1)}, f32[2,8192]{1,0:T(2,128)S(1)}, u32[]{:S(2)}, u32[]{:S(2)}) %collective-permute-start.28) | collective-permute-done | bytes 65568 | tf_op jit(solution)/shard_map/ppermute | solution.py:63
  127.5 4.0 %collective-permute-done.27 = f32[2,8192]{1,0:T(2,128)S(1)} collective-permute-done((f32[2,8192]{1,0:T(2,128)S(1)}, f32[2,8192]{1,0:T(2,128)S(1)}, u32[]{:S(2)}, u32[]{:S(2)}) %collective-permute-start.27) | collective-permute-done | bytes 65568 | tf_op jit(solution)/shard_map/ppermute | solution.py:63
  131.4 0.7 fusion.1
  (24 shorter events, 0.1 us)
Async XLA Ops:
  0.6 3.6 %collective-permute-start = (bf16[2,8192]{1,0:T(2,128)(2,1)}, bf16[2,8192]{1,0:T(2,128)(2,1)S(1)}, u32[]{:S(2)}, u32[]{:S(2)}) collective-permute-start(bf16[2,8192]{1,0:T(2,128)(2,1)} %param.4), channel_id=1, source_target_pairs={{0,32},{2,34},{4,36},{6,38},{8,40},{10,42},{12,44},{14,46},{16,48}... | collective-permute-start | bytes 98312 | tf_op jit(solution)/shard_map/ppermute | solution.py:63
  5.1 14.5 %collective-permute-start.1 = (bf16[4,8192]{1,0:T(4,128)(2,1)S(1)}, bf16[4,8192]{1,0:T(4,128)(2,1)S(1)}, u32[]{:S(2)}, u32[]{:S(2)}) collective-permute-start(bf16[4,8192]{1,0:T(4,128)(2,1)S(1)} %pad_maximum_fusion.1), channel_id=1, source_target_pairs={{0,8},{2,10},{4,12},{6,14},{8,0},{10,2},{12,4},{14,6},{16,24},{18,... | collective-permute-start | bytes 196616 | tf_op jit(solution)/shard_map/ppermute | solution.py:63
  12.4 0.7 copy-start.2
  19.6 16.4 %collective-permute-start.8 = (bf16[128,8192]{1,0:T(8,128)(2,1)}, bf16[128,8192]{1,0:T(8,128)(2,1)S(1)}, u32[]{:S(2)}, u32[]{:S(2)}) collective-permute-start(bf16[128,8192]{1,0:T(8,128)(2,1)} %get-tuple-element.34), channel_id=1, source_target_pairs={{0,16},{2,18},{4,20},{6,22},{8,24},{10,26},{12,28},{14,30},{16,0},... | collective-permute-start | bytes 6291464 | tf_op jit(solution)/shard_map/ppermute | solution.py:63
  21.9 5.7 %collective-permute-start.4 = (bf16[8,8192]{1,0:T(8,128)(2,1)S(1)}, bf16[8,8192]{1,0:T(8,128)(2,1)S(1)}, u32[]{:S(2)}, u32[]{:S(2)}) collective-permute-start(bf16[8,8192]{1,0:T(8,128)(2,1)S(1)} %pad_maximum_fusion), channel_id=1, source_target_pairs={{0,12},{2,14},{4,0},{6,2},{8,4},{10,6},{12,8},{14,10},{16,144},{18... | collective-permute-start | bytes 393224 | tf_op jit(solution)/shard_map/ppermute | solution.py:63
  24.8 5.0 %collective-permute-start.3 = (bf16[8,8192]{1,0:T(8,128)(2,1)S(1)}, bf16[8,8192]{1,0:T(8,128)(2,1)S(1)}, u32[]{:S(2)}, u32[]{:S(2)}) collective-permute-start(bf16[8,8192]{1,0:T(8,128)(2,1)S(1)} %pad_maximum_fusion), channel_id=1, source_target_pairs={{0,2},{2,4},{4,6},{6,8},{8,10},{10,12},{12,14},{14,0},{16,80},{18,... | collective-permute-start | bytes 393224 | tf_op jit(solution)/shard_map/ppermute | solution.py:63
  25.2 4.6 %collective-permute-start.2 = (bf16[8,8192]{1,0:T(8,128)(2,1)S(1)}, bf16[8,8192]{1,0:T(8,128)(2,1)S(1)}, u32[]{:S(2)}, u32[]{:S(2)}) collective-permute-start(bf16[8,8192]{1,0:T(8,128)(2,1)S(1)} %pad_maximum_fusion), channel_id=1, source_target_pairs={{0,14},{2,0},{4,2},{6,4},{8,6},{10,8},{12,10},{14,12},{16,208},{18... | collective-permute-start | bytes 393224 | tf_op jit(solution)/shard_map/ppermute | solution.py:63
  30.0 14.8 %collective-permute-start.7 = (bf16[32,8192]{1,0:T(8,128)(2,1)S(1)}, bf16[32,8192]{1,0:T(8,128)(2,1)S(1)}, u32[]{:S(2)}, u32[]{:S(2)}) collective-permute-start(bf16[32,8192]{1,0:T(8,128)(2,1)S(1)} %concatenate.12.p0), channel_id=1, source_target_pairs={{0,128},{2,130},{4,132},{6,134},{8,136},{10,138},{12,140},{14,142}... | collective-permute-start | bytes 1572872 | tf_op jit(solution)/shard_map/ppermute | solution.py:63
  30.1 14.7 %collective-permute-start.6 = (bf16[32,8192]{1,0:T(8,128)(2,1)S(1)}, bf16[32,8192]{1,0:T(8,128)(2,1)S(1)}, u32[]{:S(2)}, u32[]{:S(2)}) collective-permute-start(bf16[32,8192]{1,0:T(8,128)(2,1)S(1)} %concatenate.12.p0), channel_id=1, source_target_pairs={{0,64},{2,66},{4,68},{6,70},{8,72},{10,74},{12,76},{14,78},{16,18}... | collective-permute-start | bytes 1572872 | tf_op jit(solution)/shard_map/ppermute | solution.py:63
  31.4 17.9 %collective-permute-start.5 = (bf16[32,8192]{1,0:T(8,128)(2,1)S(1)}, bf16[32,8192]{1,0:T(8,128)(2,1)S(1)}, u32[]{:S(2)}, u32[]{:S(2)}) collective-permute-start(bf16[32,8192]{1,0:T(8,128)(2,1)S(1)} %concatenate.12.p0), channel_id=1, source_target_pairs={{0,192},{2,194},{4,196},{6,198},{8,200},{10,202},{12,204},{14,206}... | collective-permute-start | bytes 1572872 | tf_op jit(solution)/shard_map/ppermute | solution.py:63
  32.8 16.9 %collective-permute-start.9 = (bf16[32,8192]{1,0:T(8,128)(2,1)S(1)}, bf16[32,8192]{1,0:T(8,128)(2,1)S(1)}, u32[]{:S(2)}, u32[]{:S(2)}) collective-permute-start(bf16[32,8192]{1,0:T(8,128)(2,1)S(1)} %concatenate.12.p0), channel_id=1, source_target_pairs={{0,16},{2,18},{4,20},{6,22},{8,24},{10,26},{12,28},{14,30},{16,0},... | collective-permute-start | bytes 1572872 | tf_op jit(solution)/shard_map/ppermute | solution.py:63
  36.0 3.2 %copy-start = (bf16[128,8192]{1,0:T(8,128)(2,1)}, bf16[128,8192]{1,0:T(8,128)(2,1)S(1)}, u32[]{:S(2)}) copy-start(bf16[128,8192]{1,0:T(8,128)(2,1)S(1)} %collective-permute-done.8.in_hbm.refs_3_) | copy-start | bytes 6291460
  36.0 16.7 %copy-start.3 = (s32[256]{0:T(256)S(1)}, s32[256]{0:T(256)}, u32[]{:S(2)}) copy-start(s32[256]{0:T(256)} %param.6) | copy-start | bytes 3076
  49.3 1.9 %collective-permute-start.10 = (bf16[32,8192]{1,0:T(8,128)(2,1)S(1)}, bf16[32,8192]{1,0:T(8,128)(2,1)S(1)}, u32[]{:S(2)}, u32[]{:S(2)}) collective-permute-start(bf16[32,8192]{1,0:T(8,128)(2,1)S(1)} %collective-permute-done.5.p1), channel_id=1, source_target_pairs={{0,16},{2,18},{4,20},{6,22},{8,24},{10,26},{12,28},{14,30},{16,0},... | collective-permute-start | bytes 1572872 | tf_op jit(solution)/shard_map/ppermute | solution.py:63
  49.3 2.7 %collective-permute-start.11 = (bf16[32,8192]{1,0:T(8,128)(2,1)S(1)}, bf16[32,8192]{1,0:T(8,128)(2,1)S(1)}, u32[]{:S(2)}, u32[]{:S(2)}) collective-permute-start(bf16[32,8192]{1,0:T(8,128)(2,1)S(1)} %collective-permute-done.6.p2), channel_id=1, source_target_pairs={{0,16},{2,18},{4,20},{6,22},{8,24},{10,26},{12,28},{14,30},{16,0},... | collective-permute-start | bytes 1572872 | tf_op jit(solution)/shard_map/ppermute | solution.py:63
  49.8 2.9 %collective-permute-start.12 = (bf16[32,8192]{1,0:T(8,128)(2,1)S(1)}, bf16[32,8192]{1,0:T(8,128)(2,1)S(1)}, u32[]{:S(2)}, u32[]{:S(2)}) collective-permute-start(bf16[32,8192]{1,0:T(8,128)(2,1)S(1)} %collective-permute-done.7.p3), channel_id=1, source_target_pairs={{0,16},{2,18},{4,20},{6,22},{8,24},{10,26},{12,28},{14,30},{16,0},... | collective-permute-start | bytes 1572872 | tf_op jit(solution)/shard_map/ppermute | solution.py:63
  61.2 8.1 %collective-permute-start.16 = (bf16[128,8192]{1,0:T(8,128)(2,1)}, bf16[128,8192]{1,0:T(8,128)(2,1)S(1)}, u32[]{:S(2)}, u32[]{:S(2)}) collective-permute-start(bf16[128,8192]{1,0:T(8,128)(2,1)} %get-tuple-element.43), channel_id=1, source_target_pairs={{0,16},{2,18},{4,20},{6,22},{8,24},{10,26},{12,28},{14,30},{16,0},... | collective-permute-start | bytes 6291464 | tf_op jit(solution)/shard_map/ppermute | solution.py:63
  61.4 17.3 %collective-permute-start.20 = (bf16[32,8192]{1,0:T(8,128)(2,1)S(1)}, bf16[32,8192]{1,0:T(8,128)(2,1)S(1)}, u32[]{:S(2)}, u32[]{:S(2)}) collective-permute-start(bf16[32,8192]{1,0:T(8,128)(2,1)S(1)} %get-tuple-element.50), channel_id=1, source_target_pairs={{0,64},{2,66},{4,68},{6,70},{8,72},{10,74},{12,76},{14,78},{16,18}... | collective-permute-start | bytes 1572872 | tf_op jit(solution)/shard_map/ppermute | solution.py:63
  62.7 3.0 %collective-permute-start.15 = (f32[3,256]{1,0:T(4,128)S(1)}, f32[3,256]{1,0:T(4,128)S(1)}, u32[]{:S(2)}, u32[]{:S(2)}) collective-permute-start(f32[3,256]{1,0:T(4,128)S(1)} %get-tuple-element.41.own_ref.own_stats), channel_id=1, source_target_pairs={{0,48},{2,50},{4,52},{6,54},{8,56},{10,58},{12,60},{14,62},{16,32}... | collective-permute-start | bytes 9224 | tf_op jit(solution)/shard_map/ppermute | solution.py:63
  63.3 3.8 %collective-permute-start.14 = (f32[3,256]{1,0:T(4,128)S(1)}, f32[3,256]{1,0:T(4,128)S(1)}, u32[]{:S(2)}, u32[]{:S(2)}) collective-permute-start(f32[3,256]{1,0:T(4,128)S(1)} %get-tuple-element.41.own_ref.own_stats), channel_id=1, source_target_pairs={{0,32},{2,34},{4,36},{6,38},{8,40},{10,42},{12,44},{14,46},{16,48}... | collective-permute-start | bytes 9224 | tf_op jit(solution)/shard_map/ppermute | solution.py:63
  64.0 4.6 %collective-permute-start.13 = (f32[3,256]{1,0:T(4,128)S(1)}, f32[3,256]{1,0:T(4,128)S(1)}, u32[]{:S(2)}, u32[]{:S(2)}) collective-permute-start(f32[3,256]{1,0:T(4,128)S(1)} %get-tuple-element.41.own_ref.own_stats), channel_id=1, source_target_pairs={{0,16},{2,18},{4,20},{6,22},{8,24},{10,26},{12,28},{14,30},{16,0},... | collective-permute-start | bytes 9224 | tf_op jit(solution)/shard_map/ppermute | solution.py:63
  65.7 21.3 %collective-permute-start.21 = (bf16[32,8192]{1,0:T(8,128)(2,1)}, bf16[32,8192]{1,0:T(8,128)(2,1)S(1)}, u32[]{:S(2)}, u32[]{:S(2)}) collective-permute-start(bf16[32,8192]{1,0:T(8,128)(2,1)} %get-tuple-element.51), channel_id=1, source_target_pairs={{0,192},{2,194},{4,196},{6,198},{8,200},{10,202},{12,204},{14,206}... | collective-permute-start | bytes 1572872 | tf_op jit(solution)/shard_map/ppermute | solution.py:63
  67.1 19.9 %collective-permute-start.22 = (bf16[32,8192]{1,0:T(8,128)(2,1)}, bf16[32,8192]{1,0:T(8,128)(2,1)}, u32[]{:S(2)}, u32[]{:S(2)}) collective-permute-start(bf16[32,8192]{1,0:T(8,128)(2,1)} %get-tuple-element.52), channel_id=1, source_target_pairs={{0,128},{2,130},{4,132},{6,134},{8,136},{10,138},{12,140},{14,142}... | collective-permute-start | bytes 1572872 | tf_op jit(solution)/shard_map/ppermute | solution.py:63
  72.4 33.4 %copy-start.4 = (f32[256]{0:T(256)S(1)}, f32[256]{0:T(256)}, u32[]{:S(2)}) copy-start(f32[256]{0:T(256)} %param.7) | copy-start | bytes 3076
  75.9 29.8 %collective-permute-start.17 = (bf16[32,8192]{1,0:T(8,128)(2,1)}, bf16[32,8192]{1,0:T(8,128)(2,1)}, u32[]{:S(2)}, u32[]{:S(2)}) collective-permute-start(bf16[32,8192]{1,0:T(8,128)(2,1)} %get-tuple-element.47), channel_id=1, source_target_pairs={{0,64},{2,66},{4,68},{6,70},{8,72},{10,74},{12,76},{14,78},{16,18}... | collective-permute-start | bytes 1572872 | tf_op jit(solution)/shard_map/ppermute | solution.py:63
  77.6 28.2 %collective-permute-start.18 = (bf16[32,8192]{1,0:T(8,128)(2,1)}, bf16[32,8192]{1,0:T(8,128)(2,1)}, u32[]{:S(2)}, u32[]{:S(2)}) collective-permute-start(bf16[32,8192]{1,0:T(8,128)(2,1)} %get-tuple-element.48), channel_id=1, source_target_pairs={{0,192},{2,194},{4,196},{6,198},{8,200},{10,202},{12,204},{14,206}... | collective-permute-start | bytes 1572872 | tf_op jit(solution)/shard_map/ppermute | solution.py:63
  78.7 27.1 %collective-permute-start.19 = (bf16[32,8192]{1,0:T(8,128)(2,1)}, bf16[32,8192]{1,0:T(8,128)(2,1)}, u32[]{:S(2)}, u32[]{:S(2)}) collective-permute-start(bf16[32,8192]{1,0:T(8,128)(2,1)} %soft_pair.3), channel_id=1, source_target_pairs={{0,128},{2,130},{4,132},{6,134},{8,136},{10,138},{12,140},{14,142}... | collective-permute-start | bytes 1572872 | tf_op jit(solution)/shard_map/ppermute | solution.py:63
  80.2 25.6 %all-to-all-start = ((f32[32,3,256]{2,1,0:T(4,128)}), f32[32,3,256]{2,1,0:T(4,128)S(1)}, u32[]{:S(2)}, u32[]{:S(2)}) async-start(f32[32,3,256]{2,1,0:T(4,128)} %merge.1.merged_ref), calls=%async_computation | async-start | bytes 262144 | tf_op jit(solution)/shard_map/all_to_all | solution.py:321
  105.8 1.6 %copy-start.1 = (bf16[128,8192]{1,0:T(8,128)(2,1)S(1)}, bf16[128,8192]{1,0:T(8,128)(2,1)}, u32[]{:S(2)}) copy-start(bf16[128,8192]{1,0:T(8,128)(2,1)} %copy-done) | copy-start | bytes 6291460
  111.0 5.4 %collective-permute-start.23 = (bf16[8,8192]{1,0:T(8,128)(2,1)S(1)}, bf16[8,8192]{1,0:T(8,128)(2,1)S(1)}, u32[]{:S(2)}, u32[]{:S(2)}) collective-permute-start(bf16[8,8192]{1,0:T(8,128)(2,1)S(1)} %get-tuple-element.57), channel_id=1, source_target_pairs={{0,4},{2,6},{4,8},{6,10},{8,12},{10,14},{12,0},{14,2},{16,144},{18... | collective-permute-start | bytes 393224 | tf_op jit(solution)/shard_map/ppermute | solution.py:63
  111.7 4.7 %collective-permute-start.25 = (bf16[8,8192]{1,0:T(8,128)(2,1)S(1)}, bf16[8,8192]{1,0:T(8,128)(2,1)S(1)}, u32[]{:S(2)}, u32[]{:S(2)}) collective-permute-start(bf16[8,8192]{1,0:T(8,128)(2,1)S(1)} %get-tuple-element.58), channel_id=1, source_target_pairs={{0,14},{2,0},{4,2},{6,4},{8,6},{10,8},{12,10},{14,12},{16,208},{18... | collective-permute-start | bytes 393224 | tf_op jit(solution)/shard_map/ppermute | solution.py:63
  113.4 5.0 %collective-permute-start.24 = (bf16[8,8192]{1,0:T(8,128)(2,1)S(1)}, bf16[8,8192]{1,0:T(8,128)(2,1)S(1)}, u32[]{:S(2)}, u32[]{:S(2)}) collective-permute-start(bf16[8,8192]{1,0:T(8,128)(2,1)S(1)} %get-tuple-element.59), channel_id=1, source_target_pairs={{0,2},{2,4},{4,6},{6,8},{8,10},{10,12},{12,14},{14,0},{16,80},{18,... | collective-permute-start | bytes 393224 | tf_op jit(solution)/shard_map/ppermute | solution.py:63
  118.6 8.9 %collective-permute-start.28 = (f32[2,8192]{1,0:T(2,128)S(1)}, f32[2,8192]{1,0:T(2,128)S(1)}, u32[]{:S(2)}, u32[]{:S(2)}) collective-permute-start(f32[2,8192]{1,0:T(2,128)S(1)} %get-tuple-element.60), channel_id=1, source_target_pairs={{0,40},{2,42},{4,44},{6,46},{8,32},{10,34},{12,36},{14,38},{16,56}... | collective-permute-start | bytes 196616 | tf_op jit(solution)/shard_map/ppermute | solution.py:63
  123.7 7.8 %collective-permute-start.27 = (f32[2,8192]{1,0:T(2,128)S(1)}, f32[2,8192]{1,0:T(2,128)S(1)}, u32[]{:S(2)}, u32[]{:S(2)}) collective-permute-start(f32[2,8192]{1,0:T(2,128)S(1)} %get-tuple-element.61), channel_id=1, source_target_pairs={{0,8},{2,10},{4,12},{6,14},{8,0},{10,2},{12,4},{14,6},{16,24},{18,... | collective-permute-start | bytes 196616 | tf_op jit(solution)/shard_map/ppermute | solution.py:63
  125.0 6.4 %collective-permute-start.26 = (f32[2,8192]{1,0:T(2,128)S(1)}, f32[2,8192]{1,0:T(2,128)S(1)}, u32[]{:S(2)}, u32[]{:S(2)}) collective-permute-start(f32[2,8192]{1,0:T(2,128)S(1)} %get-tuple-element.62), channel_id=1, source_target_pairs={{0,32},{2,34},{4,36},{6,38},{8,40},{10,42},{12,44},{14,46},{16,48}... | collective-permute-start | bytes 196616 | tf_op jit(solution)/shard_map/ppermute | solution.py:63

commit v8 on v6

--- a/solution.py
+++ b/solution.py
@@ -99,12 +99,11 @@
     return copies
 
 
-def logits_kernel(at_ref, targets_ref, p0, p1, p2, p3, p4, p5, p6, p7, w_hbm, stats_ref, own_hbm, other_hbm, w_ref, own_ref, other_ref, w_sems, own_sems, other_sems):
+def logits_kernel(at_ref, targets_ref, p0, p1, p2, p3, p4, p5, p6, p7, w_ref, stats_ref, own_hbm, other_hbm, own_ref, other_ref, own_sems, other_sems):
     acc = jnp.zeros((ROWS, WIDTH), F32)
-    for k, copy in enumerate(weight_copies(w_hbm, w_ref, w_sems)):
+    for k in range(STEPS):
         cut = slice(k * CHUNK, (k + 1) * CHUNK)
         left = jnp.concatenate([p[:, cut] for p in (p0, p1, p2, p3, p4, p5, p6, p7)], axis=0)
-        copy.wait()
         acc += jnp.dot(left, w_ref[cut, :], preferred_element_type=F32)
     top = jnp.max(acc, axis=1, keepdims=True)
     soft = jnp.exp(acc - top)
@@ -154,7 +153,7 @@
         out_ref[i] = merged
 
 
-def scales_kernel(at_ref, grad_ref, own_ref, core_ref, spread_ref, out_ref):
+def row_scales(at_ref, grad_ref, own_ref, core_ref, spread_ref):
     place = placed(at_ref)[: ROWS // 2]
 
     def ordered(row):
@@ -171,23 +170,28 @@
     own, core = (grad * factor * jnp.exp(ordered(ref[0:1, :]) - log_total) for ref in (own_ref, core_ref))
     lane = lax.broadcasted_iota(jnp.int32, (ROWS // 2, 128), 1)
     rest = jnp.where(lane == 2, target, jnp.where(lane == 3, log_total, picked))
-    out_ref[...] = jnp.where(lane == 0, own, jnp.where(lane == 1, core, rest))
-
-
-def combine_kernel(parts, scales_ref, soft_own, soft_in, target_own, target_in, *refs):
-    outs, (a_ref, b_ref, c_ref, d_ref, sems) = refs[: len(parts)], refs[len(parts) :]
+    return jnp.where(lane == 0, own, jnp.where(lane == 1, core, rest))
+
+
+def combine_start(parts, sources, buffers, sems):
     every = []
     for i, q in enumerate(parts):
-        sources = ((soft_own, a_ref), (soft_in, b_ref), (target_own, c_ref), (target_in, d_ref))
-        every.append(
-            [pltpu.make_async_copy(s.at[pl.ds(32 * q, 32)], t.at[i], sems.at[i, j]) for j, (s, t) in enumerate(sources)]
-        )
-        for copy in every[-1]:
+        copies = [
+            pltpu.make_async_copy(s.at[pl.ds(32 * q, 32)], t.at[i], sems.at[i, j])
+            for j, (s, t) in enumerate(zip(sources, buffers))
+        ]
+        for copy in copies:
             copy.start()
+        every.append(copies)
+    return every
+
+
+def combine_end(parts, every, scales_ref, buffers, outs):
+    a_ref, b_ref, c_ref, d_ref = buffers
     for i, (q, out) in enumerate(zip(parts, outs)):
         for copy in every[i]:
             copy.wait()
-        own, core, target = (scales_ref[32 * q : 32 * q + 32, i : i + 1] for i in range(3))
+        own, core, target = (scales_ref[32 * q : 32 * q + 32, j : j + 1] for j in range(3))
         for k in range(0, DEPTH, CHUNK):
             cut = slice(k, k + CHUNK)
             soft = own * a_ref[i, :, cut] + core * b_ref[i, :, cut].astype(F32)
@@ -195,15 +199,28 @@
             out[:, cut] = (soft + target * chosen).astype(out.dtype)
 
 
+def first_kernel(parts, at_ref, grad_ref, own_ref, core_ref, spread_ref, *refs):
+    sources, scales_ref, outs, buffers, sems = refs[:4], refs[4], refs[5:-5], refs[-5:-1], refs[-1]
+    every = combine_start(parts, sources, buffers, sems)
+    scales_ref[...] = row_scales(at_ref, grad_ref, own_ref, core_ref, spread_ref)
+    combine_end(parts, every, scales_ref, buffers, outs)
+
+
+def combine_kernel(parts, scales_ref, *refs):
+    sources, outs, buffers, sems = refs[:4], refs[4:-5], refs[-5:-1], refs[-1]
+    combine_end(parts, combine_start(parts, sources, buffers, sems), scales_ref, buffers, outs)
+
+
 def shards(hidden, lm_weight, targets, loss_grad):
     half = ROWS // 2
     at = jnp.stack([lax.axis_index(a) for a in GROUP] + [lax.axis_index(GROUP) * WIDTH])
     targets, loss_grad = targets.reshape(1, ROWS), loss_grad.reshape(1, ROWS)
-    lm_weight = pltpu.with_memory_space_constraint(lm_weight, pltpu.HBM)
+    lm_weight_in, lm_weight = lm_weight, pltpu.with_memory_space_constraint(lm_weight, pltpu.HBM)
     weights = [pltpu.VMEM((DEPTH, WIDTH), BF)]
     sems = pltpu.SemaphoreType.DMA((STEPS,))
 
-    block = jnp.concatenate([hidden] + [send(hidden, to) for to in (to_x, to_z4, to_xz4)])
+    block = jnp.concatenate([hidden, send(hidden, to_x)])
+    block = jnp.concatenate([block, send(block, to_z4)])
     block = jnp.concatenate([block] + [send(block, to_first(-o)) for o in OFFSETS[1:]])
     near, back, far = (send(block, to_second(-o)) for o in OFFSETS[1:])
 
@@ -218,20 +235,20 @@
         cost_estimate=pl.CostEstimate(flops=2 * ROWS * DEPTH * WIDTH, bytes_accessed=12 << 20, transcendentals=0),
         name="target",
     )(at, aim, lm_weight)
-    far, target_own, target_out = lax.optimization_barrier((far, target_own, target_out))
+    near, target_out = lax.optimization_barrier((near, target_out))
     pieces = [block, near, back, far]
     pieces = pieces + [send(p, to_c) for p in pieces]
 
     stats, soft_own, soft_out = pl.pallas_call(
         logits_kernel,
         out_shape=(jax.ShapeDtypeStruct((3, ROWS), F32), pltpu.HBM((half, DEPTH), F32), pltpu.HBM((half, DEPTH), BF)),
-        in_specs=[SMEM] + [VMEM] * 9 + [ANY],
+        in_specs=[SMEM] + [VMEM] * 10,
         out_specs=(VMEM, HBM, HBM),
-        scratch_shapes=weights + [pltpu.VMEM((half, DEPTH), F32), pltpu.VMEM((half, DEPTH), BF)] + [sems] * 3,
-        compiler_params=params(32),
+        scratch_shapes=[pltpu.VMEM((half, DEPTH), F32), pltpu.VMEM((half, DEPTH), BF)] + [sems] * 2,
+        compiler_params=params(16),
         cost_estimate=pl.CostEstimate(flops=4 * ROWS * DEPTH * WIDTH, bytes_accessed=19 << 20, transcendentals=ROWS * WIDTH),
         name="logits",
-    )(at, targets, *pieces, lm_weight)
+    )(at, targets, *pieces, pltpu.with_memory_space_constraint(lm_weight_in, pltpu.VMEM))
     stats = [stats] + [send(stats, to) for to in (to_c, to_x, to_xc)]
     merged = pl.pallas_call(
         merge_kernel,
@@ -245,43 +262,37 @@
     soft_in, target_in = send(soft_out, to_c), send(target_out, to_c)
     spread = lax.all_to_all(merged, ("y", "z"), 0, 0)
 
-    scales = pl.pallas_call(
-        scales_kernel,
-        out_shape=jax.ShapeDtypeStruct((half, 128), F32),
-        in_specs=[SMEM] + [VMEM] * 4,
-        out_specs=VMEM,
-        compiler_params=params(),
-        name="scales",
-    )(at, loss_grad, stats[0], stats[1], spread)
-
     soft_own, target_own = (pltpu.with_memory_space_constraint(v, pltpu.HBM) for v in (soft_own, target_own))
-
-    def combine(parts, dtype):
+    shares = (soft_own, soft_in, target_own, target_in)
+
+    def combine(parts, dtype, kernel=combine_kernel, rows=()):
         n = len(parts)
+        first = len(rows) > 1
+        scales = [jax.ShapeDtypeStruct((half, 128), F32)] if first else []
         return pl.pallas_call(
-            functools.partial(combine_kernel, parts),
-            out_shape=[jax.ShapeDtypeStruct((32, DEPTH), dtype)] * n,
-            in_specs=[VMEM] + [ANY] * 4,
-            out_specs=[VMEM] * n,
+            functools.partial(kernel, parts),
+            out_shape=scales + [jax.ShapeDtypeStruct((32, DEPTH), dtype)] * n,
+            in_specs=([SMEM] if first else []) + [VMEM] * (len(rows) - first) + [ANY] * 4,
+            out_specs=[VMEM] * (n + first),
             scratch_shapes=[pltpu.VMEM((n, 32, DEPTH), F32)]
             + [pltpu.VMEM((n, 32, DEPTH), BF)] * 3
             + [pltpu.SemaphoreType.DMA((n, 4))],
             compiler_params=params(),
             cost_estimate=pl.CostEstimate(flops=6 * 32 * DEPTH * n, bytes_accessed=n * (3 << 20), transcendentals=0),
             name="combine",
-        )(scales, soft_own, soft_in, target_own, target_in)
-
-    parts = combine((3,), BF) + combine((1, 2), BF)
-    arrived = [send(p, to_second(o)).astype(F32) for p, o in zip(parts, (2, 1, -1))]
-    part = combine((0,), F32)[0] + sum(arrived)
+        )(*rows, *shares)
+
+    scales, far = combine((3,), BF, first_kernel, (at, loss_grad, stats[0], stats[1], spread))
+    parts = [far, *combine((1, 2), BF, rows=(scales,))]
     log_total, target_logit = scales[:2, 3], scales[:2, 4]
     ce_loss = log_total - target_logit
     z_term = zloss_coef * log_total * log_total
-
+    arrived = [send(p, to_second(o)).astype(F32) for p, o in zip(parts, (2, 1, -1))]
+    part = combine((0,), F32, rows=(scales,))[0] + sum(arrived)
     part = part.reshape(4, 8, DEPTH)
     part = part[0] + sum(send(part[k].astype(BF), to_first(OFFSETS[k])).astype(F32) for k in (3, 1, 2))
-    part = [part[0:2]] + [
-        send(part[2 * k : 2 * k + 2], to) for k, to in ((1, to_x), (2, to_z4), (3, to_xz4))
+    part = [part[0:2], send(part[2:4], to_x)] + [
+        send(part[2 * k : 2 * k + 2].astype(BF), to).astype(F32) for k, to in ((2, to_z4), (3, to_xz4))
     ]
     part = (part[0] + part[1]) + (part[2] + part[3])
     return ce_loss, z_term, part.astype(BF)

time: 124 us -> 121 us (0.976)
  blocking collectives: 18.6 us -> 15.1 us
  Pallas kernels: 21.8 us -> 19.7 us
  starting transfers between devices: 40 us -> 41.7 us
    all_to_all x1, blocking collectives: 18.6 us -> 15.1 us  [shards(): spread = lax.all_to_all(merged, ('y', 'z'), 0, 0)]
    pallas_call x1, Pallas kernels: 8.46 us -> 6.54 us  [shards(): pl.pallas_call(logits_kernel, out_shape=(jax.ShapeDtypeStruct((3, ROWS),...]
    ppermute x27 -> x26, starting transfers between devices: 40 us -> 41.7 us  [send(): return lax.ppermute(value, GROUP, pairs(route))]
    ppermute x27 -> x26, waiting for transfers between devices: 36.4 us -> 37.5 us  [send(): return lax.ppermute(value, GROUP, pairs(route))]
    pallas_call x4 -> x3, Pallas kernels: 6.72 us -> 6.42 us  [combine(): pl.pallas_call(functools.partial(kernel, parts), out_shape=scales + [jax....]
  transfers between devices with their start and end apart: 27 -> 26, of which waited for: 17 -> 18; matrix products, arithmetic and copies ran while one was open for 1% -> 1% of each run, Pallas kernels for 9% -> 9%
where the time goes in v8:
time: 121 us; the launch traced here: 120 us
  starting transfers between devices  41.7 us (34%)
  waiting for transfers between devices  37.5 us (31%)
  Pallas kernels  19.7 us (16%)
  blocking collectives  15.1 us (12%)
  other arithmetic  3.21 us (3%)
  local copies, waits for them, and re-layouts  2.01 us (2%)
    ppermute x26, starting transfers between devices, send(): return lax.ppermute(value, GROUP, pairs(route))  41.7 us
    ppermute x26, waiting for transfers between devices, send(): return lax.ppermute(value, GROUP, pairs(route))  37.5 us
    all_to_all x1, blocking collectives, shards(): spread = lax.all_to_all(merged, ('y', 'z'), 0, 0)  15.1 us
    pallas_call x1, Pallas kernels, shards(): pl.pallas_call(target_kernel, out_shape=[pltpu.HBM((half, DEPTH), BF)] *...  6.75 us
    pallas_call x1, Pallas kernels, shards(): pl.pallas_call(logits_kernel, out_shape=(jax.ShapeDtypeStruct((3, ROWS),...  6.54 us
    pallas_call x3, Pallas kernels, combine(): pl.pallas_call(functools.partial(kernel, parts), out_shape=scales + [jax....  6.42 us
  transfers between devices with their start and end apart: 26, of which 18 were waited for; matrix products, arithmetic and copies ran while one was open for 1% of the time, Pallas kernels for 9%

profile of v8, /device:TPU:4, one launch (start us, length us, event | category | flops | bytes accessed | tf_op | source)
XLA Modules:
  0.0 120.1 jit_solution(17851442600272660900)
XLA Ops:
  0.6 1.3 %collective-permute-start = (bf16[2,8192]{1,0:T(2,128)(2,1)}, bf16[2,8192]{1,0:T(2,128)(2,1)S(1)}, u32[]{:S(2)}, u32[]{:S(2)}) collective-permute-start(bf16[2,8192]{1,0:T(2,128)(2,1)} %param.4), channel_id=1, source_target_pairs={{0,32},{2,34},{4,36},{6,38},{8,40},{10,42},{12,44},{14,46},{16,48}... | collective-permute-start | bytes 98312 | tf_op jit(solution)/shard_map/ppermute | solution.py:63
  1.9 2.9 %collective-permute-done = bf16[2,8192]{1,0:T(2,128)(2,1)S(1)} collective-permute-done((bf16[2,8192]{1,0:T(2,128)(2,1)}, bf16[2,8192]{1,0:T(2,128)(2,1)S(1)}, u32[]{:S(2)}, u32[]{:S(2)}) %collective-permute-start) | collective-permute-done | bytes 32800 | tf_op jit(solution)/shard_map/ppermute | solution.py:63
  4.8 0.8 pad_maximum_fusion.1
  5.7 7.3 %collective-permute-start.1 = (bf16[4,8192]{1,0:T(4,128)(2,1)S(1)}, bf16[4,8192]{1,0:T(4,128)(2,1)S(1)}, u32[]{:S(2)}, u32[]{:S(2)}) collective-permute-start(bf16[4,8192]{1,0:T(4,128)(2,1)S(1)} %pad_maximum_fusion.1), channel_id=1, source_target_pairs={{0,8},{2,10},{4,12},{6,14},{8,0},{10,2},{12,4},{14,6},{16,24},{18,... | collective-permute-start | bytes 196616 | tf_op jit(solution)/shard_map/ppermute | solution.py:63
  13.0 2.3 %collective-permute-done.1 = bf16[4,8192]{1,0:T(4,128)(2,1)S(1)} collective-permute-done((bf16[4,8192]{1,0:T(4,128)(2,1)S(1)}, bf16[4,8192]{1,0:T(4,128)(2,1)S(1)}, u32[]{:S(2)}, u32[]{:S(2)}) %collective-permute-start.1) | collective-permute-done | bytes 65568 | tf_op jit(solution)/shard_map/ppermute | solution.py:63
  15.3 0.9 pad_maximum_fusion
  16.2 5.0 %collective-permute-start.4 = (bf16[8,8192]{1,0:T(8,128)(2,1)S(1)}, bf16[8,8192]{1,0:T(8,128)(2,1)S(1)}, u32[]{:S(2)}, u32[]{:S(2)}) collective-permute-start(bf16[8,8192]{1,0:T(8,128)(2,1)S(1)} %pad_maximum_fusion), channel_id=1, source_target_pairs={{0,12},{2,14},{4,0},{6,2},{8,4},{10,6},{12,8},{14,10},{16,144},{18... | collective-permute-start | bytes 393224 | tf_op jit(solution)/shard_map/ppermute | solution.py:63
  21.2 1.0 collective-permute-start.3
  22.2 2.2 %collective-permute-start.2 = (bf16[8,8192]{1,0:T(8,128)(2,1)S(1)}, bf16[8,8192]{1,0:T(8,128)(2,1)S(1)}, u32[]{:S(2)}, u32[]{:S(2)}) collective-permute-start(bf16[8,8192]{1,0:T(8,128)(2,1)S(1)} %pad_maximum_fusion), channel_id=1, source_target_pairs={{0,14},{2,0},{4,2},{6,4},{8,6},{10,8},{12,10},{14,12},{16,208},{18... | collective-permute-start | bytes 393224 | tf_op jit(solution)/shard_map/ppermute | solution.py:63
  24.4 0.7 collective-permute-done.4
  25.1 2.3 %collective-permute-done.3 = bf16[8,8192]{1,0:T(8,128)(2,1)S(1)} collective-permute-done((bf16[8,8192]{1,0:T(8,128)(2,1)S(1)}, bf16[8,8192]{1,0:T(8,128)(2,1)S(1)}, u32[]{:S(2)}, u32[]{:S(2)}) %collective-permute-start.3) | collective-permute-done | bytes 131104 | tf_op jit(solution)/shard_map/ppermute | solution.py:63
  27.4 1.2 %collective-permute-done.2 = bf16[8,8192]{1,0:T(8,128)(2,1)S(1)} collective-permute-done((bf16[8,8192]{1,0:T(8,128)(2,1)S(1)}, bf16[8,8192]{1,0:T(8,128)(2,1)S(1)}, u32[]{:S(2)}, u32[]{:S(2)}) %collective-permute-start.2) | collective-permute-done | bytes 131104 | tf_op jit(solution)/shard_map/ppermute | solution.py:63
  28.6 0.9 concatenate.13.p0
  29.5 3.1 %collective-permute-start.5 = (bf16[32,8192]{1,0:T(8,128)(2,1)S(1)}, bf16[32,8192]{1,0:T(8,128)(2,1)S(1)}, u32[]{:S(2)}, u32[]{:S(2)}) collective-permute-start(bf16[32,8192]{1,0:T(8,128)(2,1)S(1)} %concatenate.13.p0), channel_id=1, source_target_pairs={{0,192},{2,194},{4,196},{6,198},{8,200},{10,202},{12,204},{14,206}... | collective-permute-start | bytes 1572872 | tf_op jit(solution)/shard_map/ppermute | solution.py:63
  32.6 1.0 collective-permute-start.7
  33.5 1.3 %collective-permute-start.6 = (bf16[32,8192]{1,0:T(8,128)(2,1)S(1)}, bf16[32,8192]{1,0:T(8,128)(2,1)S(1)}, u32[]{:S(2)}, u32[]{:S(2)}) collective-permute-start(bf16[32,8192]{1,0:T(8,128)(2,1)S(1)} %concatenate.13.p0), channel_id=1, source_target_pairs={{0,64},{2,66},{4,68},{6,70},{8,72},{10,74},{12,76},{14,78},{16,18}... | collective-permute-start | bytes 1572872 | tf_op jit(solution)/shard_map/ppermute | solution.py:63
  34.9 0.1 stack.23.at_ref
  35.0 0.0 collective-permute-start.8
  35.0 0.0 copy-start.1
  35.0 0.7 copy-done.1
  35.7 6.7 %target.1 = (bf16[128,8192]{1,0:T(8,128)(2,1)}, bf16[128,8192]{1,0:T(8,128)(2,1)}) custom-call(s32[5]{0:T(128)S(1)} %stack.23.at_ref, s32[1,256]{1,0:T(1,128)S(1)} %bitcast.7, bf16[8192,512]{1,0:T(8,128)(2,1)} %w_ref.1), custom_call_target="tpu_custom_call" | custom-call | flops 2147483648 | bytes 12582912 | tf_op jit(solution)/shard_map/target/pallas_call | solution.py:228
  42.4 2.5 %collective-permute-done.5.p1 = bf16[32,8192]{1,0:T(8,128)(2,1)S(1)} collective-permute-done((bf16[32,8192]{1,0:T(8,128)(2,1)S(1)}, bf16[32,8192]{1,0:T(8,128)(2,1)S(1)}, u32[]{:S(2)}, u32[]{:S(2)}) %collective-permute-start.5) | collective-permute-done | bytes 524320 | tf_op jit(solution)/shard_map/ppermute | solution.py:63
  44.9 0.0 collective-permute-done.7.p3
  44.9 0.0 collective-permute-start.11
  44.9 4.0 %collective-permute-done.6.p2 = bf16[32,8192]{1,0:T(8,128)(2,1)S(1)} collective-permute-done((bf16[32,8192]{1,0:T(8,128)(2,1)S(1)}, bf16[32,8192]{1,0:T(8,128)(2,1)S(1)}, u32[]{:S(2)}, u32[]{:S(2)}) %collective-permute-start.6) | collective-permute-done | bytes 524320 | tf_op jit(solution)/shard_map/ppermute | solution.py:63
  48.9 0.0 collective-permute-start.10
  48.9 0.5 collective-permute-start.9
  49.4 0.0 collective-permute-done.8.p4
  49.4 0.0 collective-permute-done.11.p7
  49.4 1.4 %collective-permute-done.10.p6 = bf16[32,8192]{1,0:T(8,128)(2,1)S(1)} collective-permute-done((bf16[32,8192]{1,0:T(8,128)(2,1)S(1)}, bf16[32,8192]{1,0:T(8,128)(2,1)S(1)}, u32[]{:S(2)}, u32[]{:S(2)}) %collective-permute-start.10) | collective-permute-done | bytes 524320 | tf_op jit(solution)/shard_map/ppermute | solution.py:63
  50.8 0.7 collective-permute-done.9.p5
  51.5 6.5 %logits.1 = (f32[3,256]{1,0:T(4,128)S(1)}, f32[128,8192]{1,0:T(8,128)}, bf16[128,8192]{1,0:T(8,128)(2,1)}) custom-call(s32[5]{0:T(128)S(1)} %stack.23.at_ref, s32[1,256]{1,0:T(1,128)S(1)} %bitcast.8, bf16[32,8192]{1,0:T(8,128)(2,1)S(1)} %concatenate.13.p0, bf16[32,8192]{1,0:T(8,128)(2,1)S(1)} %collective-permute-done.5.p1, ...), custom_call_target="tpu_custom_call" | custom-call | flops 4294967296 | bytes 19922944 | tf_op jit(solution)/shard_map/logits/pallas_call | solution.py:242
  58.1 1.0 collective-permute-start.14
  59.1 0.8 collective-permute-start.13
  60.0 0.1 collective-permute-start.12
  60.0 1.2 collective-permute-done.14.both_ref
  61.2 1.5 %collective-permute-done.13.x_ref = f32[3,256]{1,0:T(4,128)S(1)} collective-permute-done((f32[3,256]{1,0:T(4,128)S(1)}, f32[3,256]{1,0:T(4,128)S(1)}, u32[]{:S(2)}, u32[]{:S(2)}) %collective-permute-start.13) | collective-permute-done | bytes 3104 | tf_op jit(solution)/shard_map/ppermute | solution.py:63
  62.8 0.1 collective-permute-start.15
  62.9 0.5 collective-permute-start.16
  63.4 15.1 %all_to_all.5.spread_ref = f32[32,3,256]{2,1,0:T(4,128)S(1)} all-to-all(f32[32,3,256]{2,1,0:T(4,128)S(1)} %merge.1), channel_id=1, replica_groups=mesh['y'=4,'x'=2,'c'=2,'z'=8,'dp'=2] {'y','z'}, dimensions={0} | all-to-all | bytes 196608 | tf_op jit(solution)/shard_map/all_to_all | solution.py:263
  78.4 2.3 %combine.3 = (f32[128,128]{1,0:T(8,128)S(1)}, bf16[32,8192]{1,0:T(8,128)(2,1)S(1)}) custom-call(s32[5]{0:T(128)S(1)} %stack.23.at_ref, f32[1,256]{1,0:T(1,128)S(1)} %bitcast.9, f32[3,256]{1,0:T(4,128)S(1)} %get-tuple-element.21.own_ref, f32[3,256]{1,0:T(4,128)S(1)} %collective-permute-done.12.core_ref, f32[32,3,256]{2,1,0:T(4,128)S(1)} %all_to_all.5.spread_ref, ...), custom_call_target="tpu_custom_call" | custom-call | flops 1572864 | bytes 3145728 | tf_op jit(solution)/shard_map/combine/pallas_call | solution.py:272
  80.8 1.4 %collective-permute-start.17 = (bf16[32,8192]{1,0:T(8,128)(2,1)S(1)}, bf16[32,8192]{1,0:T(8,128)(2,1)S(1)}, u32[]{:S(2)}, u32[]{:S(2)}) collective-permute-start(bf16[32,8192]{1,0:T(8,128)(2,1)S(1)} %get-tuple-element.30), channel_id=1, source_target_pairs={{0,128},{2,130},{4,132},{6,134},{8,136},{10,138},{12,140},{14,142}... | collective-permute-start | bytes 1572872 | tf_op jit(solution)/shard_map/ppermute | solution.py:63
  82.2 2.3 %combine.5 = (bf16[32,8192]{1,0:T(8,128)(2,1)S(1)}, bf16[32,8192]{1,0:T(8,128)(2,1)S(1)}) custom-call(f32[128,128]{1,0:T(8,128)S(1)} %get-tuple-element.29.scales_ref, f32[128,8192]{1,0:T(8,128)} %get-tuple-element.25.refs_0_, bf16[128,8192]{1,0:T(8,128)(2,1)S(1)} %collective-permute-done.15.refs_1_, bf16[128,8192]{1,0:T(8,128)(2,1)} %get-tuple-element.27.refs_2_, ...), custom_call_target="tpu_custom_call" | custom-call | flops 3145728 | bytes 6291456 | tf_op jit(solution)/shard_map/combine/pallas_call | solution.py:272
  84.5 0.8 collective-permute-start.18
  85.3 2.5 %collective-permute-start.19 = (bf16[32,8192]{1,0:T(8,128)(2,1)S(1)}, bf16[32,8192]{1,0:T(8,128)(2,1)S(1)}, u32[]{:S(2)}, u32[]{:S(2)}) collective-permute-start(bf16[32,8192]{1,0:T(8,128)(2,1)S(1)} %get-tuple-element.32), channel_id=1, source_target_pairs={{0,192},{2,194},{4,196},{6,198},{8,200},{10,202},{12,204},{14,206}... | collective-permute-start | bytes 1572872 | tf_op jit(solution)/shard_map/ppermute | solution.py:63
  87.8 1.8 %combine.4 = f32[32,8192]{1,0:T(8,128)S(1)} custom-call(f32[128,128]{1,0:T(8,128)S(1)} %get-tuple-element.29.scales_ref, f32[128,8192]{1,0:T(8,128)} %get-tuple-element.25.refs_0_, bf16[128,8192]{1,0:T(8,128)(2,1)S(1)} %collective-permute-done.15.refs_1_, bf16[128,8192]{1,0:T(8,128)(2,1)} %get-tuple-element.27.refs_2_, ...), custom_call_target="tpu_custom_call" | custom-call | flops 1572864 | bytes 3145728 | tf_op jit(solution)/shard_map/combine/pallas_call | solution.py:272
  89.6 2.0 %collective-permute-done.17 = bf16[32,8192]{1,0:T(8,128)(2,1)S(1)} collective-permute-done((bf16[32,8192]{1,0:T(8,128)(2,1)S(1)}, bf16[32,8192]{1,0:T(8,128)(2,1)S(1)}, u32[]{:S(2)}, u32[]{:S(2)}) %collective-permute-start.17) | collective-permute-done | bytes 524320 | tf_op jit(solution)/shard_map/ppermute | solution.py:63
  91.6 5.5 %collective-permute-done.18 = bf16[32,8192]{1,0:T(8,128)(2,1)S(1)} collective-permute-done((bf16[32,8192]{1,0:T(8,128)(2,1)S(1)}, bf16[32,8192]{1,0:T(8,128)(2,1)S(1)}, u32[]{:S(2)}, u32[]{:S(2)}) %collective-permute-start.18) | collective-permute-done | bytes 524320 | tf_op jit(solution)/shard_map/ppermute | solution.py:63
  97.2 0.3 fusion.3
  97.5 1.6 %collective-permute-start.20 = (bf16[8,8192]{1,0:T(8,128)(2,1)S(1)}, bf16[8,8192]{1,0:T(8,128)(2,1)S(1)}, u32[]{:S(2)}, u32[]{:S(2)}) collective-permute-start(bf16[8,8192]{1,0:T(8,128)(2,1)S(1)} %get-tuple-element.39), channel_id=1, source_target_pairs={{0,4},{2,6},{4,8},{6,10},{8,12},{10,14},{12,0},{14,2},{16,144},{18... | collective-permute-start | bytes 393224 | tf_op jit(solution)/shard_map/ppermute | solution.py:63
  99.0 2.6 %collective-permute-start.22 = (bf16[8,8192]{1,0:T(8,128)(2,1)S(1)}, bf16[8,8192]{1,0:T(8,128)(2,1)S(1)}, u32[]{:S(2)}, u32[]{:S(2)}) collective-permute-start(bf16[8,8192]{1,0:T(8,128)(2,1)S(1)} %get-tuple-element.40), channel_id=1, source_target_pairs={{0,14},{2,0},{4,2},{6,4},{8,6},{10,8},{12,10},{14,12},{16,208},{18... | collective-permute-start | bytes 393224 | tf_op jit(solution)/shard_map/ppermute | solution.py:63
  101.6 0.2 slice_reduce_fusion
  101.9 3.1 %collective-permute-done.20 = bf16[8,8192]{1,0:T(8,128)(2,1)S(1)} collective-permute-done((bf16[8,8192]{1,0:T(8,128)(2,1)S(1)}, bf16[8,8192]{1,0:T(8,128)(2,1)S(1)}, u32[]{:S(2)}, u32[]{:S(2)}) %collective-permute-start.20) | collective-permute-done | bytes 131104 | tf_op jit(solution)/shard_map/ppermute | solution.py:63
  105.0 2.8 %collective-permute-done.21 = bf16[8,8192]{1,0:T(8,128)(2,1)S(1)} collective-permute-done((bf16[8,8192]{1,0:T(8,128)(2,1)S(1)}, bf16[8,8192]{1,0:T(8,128)(2,1)S(1)}, u32[]{:S(2)}, u32[]{:S(2)}) %collective-permute-start.21) | collective-permute-done | bytes 131104 | tf_op jit(solution)/shard_map/ppermute | solution.py:63
  107.8 0.1 fusion.2
  107.9 0.1 fusion.5
  108.0 1.2 %collective-permute-start.24 = (bf16[2,8192]{1,0:T(2,128)(2,1)S(1)}, bf16[2,8192]{1,0:T(2,128)(2,1)S(1)}, u32[]{:S(2)}, u32[]{:S(2)}) collective-permute-start(bf16[2,8192]{1,0:T(2,128)(2,1)S(1)} %get-tuple-element.42), channel_id=1, source_target_pairs={{0,8},{2,10},{4,12},{6,14},{8,0},{10,2},{12,4},{14,6},{16,24},{18,... | collective-permute-start | bytes 98312 | tf_op jit(solution)/shard_map/ppermute | solution.py:63
  109.2 5.1 %collective-permute-start.25 = (bf16[2,8192]{1,0:T(2,128)(2,1)S(1)}, bf16[2,8192]{1,0:T(2,128)(2,1)S(1)}, u32[]{:S(2)}, u32[]{:S(2)}) collective-permute-start(bf16[2,8192]{1,0:T(2,128)(2,1)S(1)} %get-tuple-element.43), channel_id=1, source_target_pairs={{0,40},{2,42},{4,44},{6,46},{8,32},{10,34},{12,36},{14,38},{16,56}... | collective-permute-start | bytes 98312 | tf_op jit(solution)/shard_map/ppermute | solution.py:63
  114.3 1.3 %collective-permute-start.23 = (f32[2,8192]{1,0:T(2,128)S(1)}, f32[2,8192]{1,0:T(2,128)S(1)}, u32[]{:S(2)}, u32[]{:S(2)}) collective-permute-start(f32[2,8192]{1,0:T(2,128)S(1)} %slice.54), channel_id=1, source_target_pairs={{0,32},{2,34},{4,36},{6,38},{8,40},{10,42},{12,44},{14,46},{16,48}... | collective-permute-start | bytes 196616 | tf_op jit(solution)/shard_map/ppermute | solution.py:63
  115.6 0.5 multiply_multiply_fusion
  116.1 0.1 collective-permute-done.24
  116.2 2.1 %collective-permute-done.25 = bf16[2,8192]{1,0:T(2,128)(2,1)S(1)} collective-permute-done((bf16[2,8192]{1,0:T(2,128)(2,1)S(1)}, bf16[2,8192]{1,0:T(2,128)(2,1)S(1)}, u32[]{:S(2)}, u32[]{:S(2)}) %collective-permute-start.25) | collective-permute-done | bytes 32800 | tf_op jit(solution)/shard_map/ppermute | solution.py:63
  118.3 1.1 collective-permute-done.23
  119.4 0.7 fusion.1
  (15 shorter events, 0.1 us)
Async XLA Ops:
  0.6 4.2 %collective-permute-start = (bf16[2,8192]{1,0:T(2,128)(2,1)}, bf16[2,8192]{1,0:T(2,128)(2,1)S(1)}, u32[]{:S(2)}, u32[]{:S(2)}) collective-permute-start(bf16[2,8192]{1,0:T(2,128)(2,1)} %param.4), channel_id=1, source_target_pairs={{0,32},{2,34},{4,36},{6,38},{8,40},{10,42},{12,44},{14,46},{16,48}... | collective-permute-start | bytes 98312 | tf_op jit(solution)/shard_map/ppermute | solution.py:63
  5.7 9.6 %collective-permute-start.1 = (bf16[4,8192]{1,0:T(4,128)(2,1)S(1)}, bf16[4,8192]{1,0:T(4,128)(2,1)S(1)}, u32[]{:S(2)}, u32[]{:S(2)}) collective-permute-start(bf16[4,8192]{1,0:T(4,128)(2,1)S(1)} %pad_maximum_fusion.1), channel_id=1, source_target_pairs={{0,8},{2,10},{4,12},{6,14},{8,0},{10,2},{12,4},{14,6},{16,24},{18,... | collective-permute-start | bytes 196616 | tf_op jit(solution)/shard_map/ppermute | solution.py:63
  16.2 8.9 %collective-permute-start.4 = (bf16[8,8192]{1,0:T(8,128)(2,1)S(1)}, bf16[8,8192]{1,0:T(8,128)(2,1)S(1)}, u32[]{:S(2)}, u32[]{:S(2)}) collective-permute-start(bf16[8,8192]{1,0:T(8,128)(2,1)S(1)} %pad_maximum_fusion), channel_id=1, source_target_pairs={{0,12},{2,14},{4,0},{6,2},{8,4},{10,6},{12,8},{14,10},{16,144},{18... | collective-permute-start | bytes 393224 | tf_op jit(solution)/shard_map/ppermute | solution.py:63
  21.2 6.2 %collective-permute-start.3 = (bf16[8,8192]{1,0:T(8,128)(2,1)S(1)}, bf16[8,8192]{1,0:T(8,128)(2,1)S(1)}, u32[]{:S(2)}, u32[]{:S(2)}) collective-permute-start(bf16[8,8192]{1,0:T(8,128)(2,1)S(1)} %pad_maximum_fusion), channel_id=1, source_target_pairs={{0,2},{2,4},{4,6},{6,8},{8,10},{10,12},{12,14},{14,0},{16,80},{18,... | collective-permute-start | bytes 393224 | tf_op jit(solution)/shard_map/ppermute | solution.py:63
  22.2 6.4 %collective-permute-start.2 = (bf16[8,8192]{1,0:T(8,128)(2,1)S(1)}, bf16[8,8192]{1,0:T(8,128)(2,1)S(1)}, u32[]{:S(2)}, u32[]{:S(2)}) collective-permute-start(bf16[8,8192]{1,0:T(8,128)(2,1)S(1)} %pad_maximum_fusion), channel_id=1, source_target_pairs={{0,14},{2,0},{4,2},{6,4},{8,6},{10,8},{12,10},{14,12},{16,208},{18... | collective-permute-start | bytes 393224 | tf_op jit(solution)/shard_map/ppermute | solution.py:63
  29.5 15.4 %collective-permute-start.5 = (bf16[32,8192]{1,0:T(8,128)(2,1)S(1)}, bf16[32,8192]{1,0:T(8,128)(2,1)S(1)}, u32[]{:S(2)}, u32[]{:S(2)}) collective-permute-start(bf16[32,8192]{1,0:T(8,128)(2,1)S(1)} %concatenate.13.p0), channel_id=1, source_target_pairs={{0,192},{2,194},{4,196},{6,198},{8,200},{10,202},{12,204},{14,206}... | collective-permute-start | bytes 1572872 | tf_op jit(solution)/shard_map/ppermute | solution.py:63
  32.6 12.3 %collective-permute-start.7 = (bf16[32,8192]{1,0:T(8,128)(2,1)S(1)}, bf16[32,8192]{1,0:T(8,128)(2,1)S(1)}, u32[]{:S(2)}, u32[]{:S(2)}) collective-permute-start(bf16[32,8192]{1,0:T(8,128)(2,1)S(1)} %concatenate.13.p0), channel_id=1, source_target_pairs={{0,128},{2,130},{4,132},{6,134},{8,136},{10,138},{12,140},{14,142}... | collective-permute-start | bytes 1572872 | tf_op jit(solution)/shard_map/ppermute | solution.py:63
  33.5 15.3 %collective-permute-start.6 = (bf16[32,8192]{1,0:T(8,128)(2,1)S(1)}, bf16[32,8192]{1,0:T(8,128)(2,1)S(1)}, u32[]{:S(2)}, u32[]{:S(2)}) collective-permute-start(bf16[32,8192]{1,0:T(8,128)(2,1)S(1)} %concatenate.13.p0), channel_id=1, source_target_pairs={{0,64},{2,66},{4,68},{6,70},{8,72},{10,74},{12,76},{14,78},{16,18}... | collective-permute-start | bytes 1572872 | tf_op jit(solution)/shard_map/ppermute | solution.py:63
  35.0 14.4 %collective-permute-start.8 = (bf16[32,8192]{1,0:T(8,128)(2,1)S(1)}, bf16[32,8192]{1,0:T(8,128)(2,1)S(1)}, u32[]{:S(2)}, u32[]{:S(2)}) collective-permute-start(bf16[32,8192]{1,0:T(8,128)(2,1)S(1)} %concatenate.13.p0), channel_id=1, source_target_pairs={{0,16},{2,18},{4,20},{6,22},{8,24},{10,26},{12,28},{14,30},{16,0},... | collective-permute-start | bytes 1572872 | tf_op jit(solution)/shard_map/ppermute | solution.py:63
  35.0 0.7 copy-start.1
  35.7 15.9 %copy-start = (bf16[8192,512]{1,0:T(8,128)(2,1)S(1)}, bf16[8192,512]{1,0:T(8,128)(2,1)}, u32[]{:S(2)}) copy-start(bf16[8192,512]{1,0:T(8,128)(2,1)} %w_ref.1) | copy-start | bytes 25165828
  44.9 18.0 %copy-start.3 = (bf16[128,8192]{1,0:T(8,128)(2,1)S(1)}, bf16[128,8192]{1,0:T(8,128)(2,1)}, u32[]{:S(2)}) copy-start(bf16[128,8192]{1,0:T(8,128)(2,1)} %get-tuple-element.28) | copy-start | bytes 6291460
  44.9 33.5 %copy-start.2 = (f32[256]{0:T(256)S(1)}, f32[256]{0:T(256)}, u32[]{:S(2)}) copy-start(f32[256]{0:T(256)} %param.7) | copy-start | bytes 3076
  44.9 4.5 %collective-permute-start.11 = (bf16[32,8192]{1,0:T(8,128)(2,1)S(1)}, bf16[32,8192]{1,0:T(8,128)(2,1)S(1)}, u32[]{:S(2)}, u32[]{:S(2)}) collective-permute-start(bf16[32,8192]{1,0:T(8,128)(2,1)S(1)} %collective-permute-done.7.p3), channel_id=1, source_target_pairs={{0,16},{2,18},{4,20},{6,22},{8,24},{10,26},{12,28},{14,30},{16,0},... | collective-permute-start | bytes 1572872 | tf_op jit(solution)/shard_map/ppermute | solution.py:63
  48.9 1.9 %collective-permute-start.10 = (bf16[32,8192]{1,0:T(8,128)(2,1)S(1)}, bf16[32,8192]{1,0:T(8,128)(2,1)S(1)}, u32[]{:S(2)}, u32[]{:S(2)}) collective-permute-start(bf16[32,8192]{1,0:T(8,128)(2,1)S(1)} %collective-permute-done.6.p2), channel_id=1, source_target_pairs={{0,16},{2,18},{4,20},{6,22},{8,24},{10,26},{12,28},{14,30},{16,0},... | collective-permute-start | bytes 1572872 | tf_op jit(solution)/shard_map/ppermute | solution.py:63
  48.9 2.7 %collective-permute-start.9 = (bf16[32,8192]{1,0:T(8,128)(2,1)S(1)}, bf16[32,8192]{1,0:T(8,128)(2,1)S(1)}, u32[]{:S(2)}, u32[]{:S(2)}) collective-permute-start(bf16[32,8192]{1,0:T(8,128)(2,1)S(1)} %collective-permute-done.5.p1), channel_id=1, source_target_pairs={{0,16},{2,18},{4,20},{6,22},{8,24},{10,26},{12,28},{14,30},{16,0},... | collective-permute-start | bytes 1572872 | tf_op jit(solution)/shard_map/ppermute | solution.py:63
  58.1 3.1 %collective-permute-start.14 = (f32[3,256]{1,0:T(4,128)S(1)}, f32[3,256]{1,0:T(4,128)S(1)}, u32[]{:S(2)}, u32[]{:S(2)}) collective-permute-start(f32[3,256]{1,0:T(4,128)S(1)} %get-tuple-element.21.own_ref), channel_id=1, source_target_pairs={{0,48},{2,50},{4,52},{6,54},{8,56},{10,58},{12,60},{14,62},{16,32}... | collective-permute-start | bytes 9224 | tf_op jit(solution)/shard_map/ppermute | solution.py:63
  59.1 3.6 %collective-permute-start.13 = (f32[3,256]{1,0:T(4,128)S(1)}, f32[3,256]{1,0:T(4,128)S(1)}, u32[]{:S(2)}, u32[]{:S(2)}) collective-permute-start(f32[3,256]{1,0:T(4,128)S(1)} %get-tuple-element.21.own_ref), channel_id=1, source_target_pairs={{0,32},{2,34},{4,36},{6,38},{8,40},{10,42},{12,44},{14,46},{16,48}... | collective-permute-start | bytes 9224 | tf_op jit(solution)/shard_map/ppermute | solution.py:63
  60.0 2.8 %collective-permute-start.12 = (f32[3,256]{1,0:T(4,128)S(1)}, f32[3,256]{1,0:T(4,128)S(1)}, u32[]{:S(2)}, u32[]{:S(2)}) collective-permute-start(f32[3,256]{1,0:T(4,128)S(1)} %get-tuple-element.21.own_ref), channel_id=1, source_target_pairs={{0,16},{2,18},{4,20},{6,22},{8,24},{10,26},{12,28},{14,30},{16,0},... | collective-permute-start | bytes 9224 | tf_op jit(solution)/shard_map/ppermute | solution.py:63
  62.8 15.7 %collective-permute-start.15 = (bf16[128,8192]{1,0:T(8,128)(2,1)}, bf16[128,8192]{1,0:T(8,128)(2,1)S(1)}, u32[]{:S(2)}, u32[]{:S(2)}) collective-permute-start(bf16[128,8192]{1,0:T(8,128)(2,1)} %get-tuple-element.26), channel_id=1, source_target_pairs={{0,16},{2,18},{4,20},{6,22},{8,24},{10,26},{12,28},{14,30},{16,0},... | collective-permute-start | bytes 6291464 | tf_op jit(solution)/shard_map/ppermute | solution.py:63
  62.9 15.6 %collective-permute-start.16 = (bf16[128,8192]{1,0:T(8,128)(2,1)S(1)}, bf16[128,8192]{1,0:T(8,128)(2,1)S(1)}, u32[]{:S(2)}, u32[]{:S(2)}) collective-permute-start(bf16[128,8192]{1,0:T(8,128)(2,1)S(1)} %copy-done.3), channel_id=1, source_target_pairs={{0,16},{2,18},{4,20},{6,22},{8,24},{10,26},{12,28},{14,30},{16,0},... | collective-permute-start | bytes 6291464 | tf_op jit(solution)/shard_map/ppermute | solution.py:63
  80.8 10.9 %collective-permute-start.17 = (bf16[32,8192]{1,0:T(8,128)(2,1)S(1)}, bf16[32,8192]{1,0:T(8,128)(2,1)S(1)}, u32[]{:S(2)}, u32[]{:S(2)}) collective-permute-start(bf16[32,8192]{1,0:T(8,128)(2,1)S(1)} %get-tuple-element.30), channel_id=1, source_target_pairs={{0,128},{2,130},{4,132},{6,134},{8,136},{10,138},{12,140},{14,142}... | collective-permute-start | bytes 1572872 | tf_op jit(solution)/shard_map/ppermute | solution.py:63
  84.5 12.7 %collective-permute-start.18 = (bf16[32,8192]{1,0:T(8,128)(2,1)S(1)}, bf16[32,8192]{1,0:T(8,128)(2,1)S(1)}, u32[]{:S(2)}, u32[]{:S(2)}) collective-permute-start(bf16[32,8192]{1,0:T(8,128)(2,1)S(1)} %get-tuple-element.31), channel_id=1, source_target_pairs={{0,64},{2,66},{4,68},{6,70},{8,72},{10,74},{12,76},{14,78},{16,18}... | collective-permute-start | bytes 1572872 | tf_op jit(solution)/shard_map/ppermute | solution.py:63
  85.3 11.9 %collective-permute-start.19 = (bf16[32,8192]{1,0:T(8,128)(2,1)S(1)}, bf16[32,8192]{1,0:T(8,128)(2,1)S(1)}, u32[]{:S(2)}, u32[]{:S(2)}) collective-permute-start(bf16[32,8192]{1,0:T(8,128)(2,1)S(1)} %get-tuple-element.32), channel_id=1, source_target_pairs={{0,192},{2,194},{4,196},{6,198},{8,200},{10,202},{12,204},{14,206}... | collective-permute-start | bytes 1572872 | tf_op jit(solution)/shard_map/ppermute | solution.py:63
  97.5 7.5 %collective-permute-start.20 = (bf16[8,8192]{1,0:T(8,128)(2,1)S(1)}, bf16[8,8192]{1,0:T(8,128)(2,1)S(1)}, u32[]{:S(2)}, u32[]{:S(2)}) collective-permute-start(bf16[8,8192]{1,0:T(8,128)(2,1)S(1)} %get-tuple-element.39), channel_id=1, source_target_pairs={{0,4},{2,6},{4,8},{6,10},{8,12},{10,14},{12,0},{14,2},{16,144},{18... | collective-permute-start | bytes 393224 | tf_op jit(solution)/shard_map/ppermute | solution.py:63
  99.0 6.0 %collective-permute-start.22 = (bf16[8,8192]{1,0:T(8,128)(2,1)S(1)}, bf16[8,8192]{1,0:T(8,128)(2,1)S(1)}, u32[]{:S(2)}, u32[]{:S(2)}) collective-permute-start(bf16[8,8192]{1,0:T(8,128)(2,1)S(1)} %get-tuple-element.40), channel_id=1, source_target_pairs={{0,14},{2,0},{4,2},{6,4},{8,6},{10,8},{12,10},{14,12},{16,208},{18... | collective-permute-start | bytes 393224 | tf_op jit(solution)/shard_map/ppermute | solution.py:63
  101.6 6.2 %collective-permute-start.21 = (bf16[8,8192]{1,0:T(8,128)(2,1)S(1)}, bf16[8,8192]{1,0:T(8,128)(2,1)S(1)}, u32[]{:S(2)}, u32[]{:S(2)}) collective-permute-start(bf16[8,8192]{1,0:T(8,128)(2,1)S(1)} %get-tuple-element.41), channel_id=1, source_target_pairs={{0,2},{2,4},{4,6},{6,8},{8,10},{10,12},{12,14},{14,0},{16,80},{18,... | collective-permute-start | bytes 393224 | tf_op jit(solution)/shard_map/ppermute | solution.py:63
  108.0 8.3 %collective-permute-start.24 = (bf16[2,8192]{1,0:T(2,128)(2,1)S(1)}, bf16[2,8192]{1,0:T(2,128)(2,1)S(1)}, u32[]{:S(2)}, u32[]{:S(2)}) collective-permute-start(bf16[2,8192]{1,0:T(2,128)(2,1)S(1)} %get-tuple-element.42), channel_id=1, source_target_pairs={{0,8},{2,10},{4,12},{6,14},{8,0},{10,2},{12,4},{14,6},{16,24},{18,... | collective-permute-start | bytes 98312 | tf_op jit(solution)/shard_map/ppermute | solution.py:63
  109.2 9.1 %collective-permute-start.25 = (bf16[2,8192]{1,0:T(2,128)(2,1)S(1)}, bf16[2,8192]{1,0:T(2,128)(2,1)S(1)}, u32[]{:S(2)}, u32[]{:S(2)}) collective-permute-start(bf16[2,8192]{1,0:T(2,128)(2,1)S(1)} %get-tuple-element.43), channel_id=1, source_target_pairs={{0,40},{2,42},{4,44},{6,46},{8,32},{10,34},{12,36},{14,38},{16,56}... | collective-permute-start | bytes 98312 | tf_op jit(solution)/shard_map/ppermute | solution.py:63
  114.3 5.1 %collective-permute-start.23 = (f32[2,8192]{1,0:T(2,128)S(1)}, f32[2,8192]{1,0:T(2,128)S(1)}, u32[]{:S(2)}, u32[]{:S(2)}) collective-permute-start(f32[2,8192]{1,0:T(2,128)S(1)} %slice.54), channel_id=1, source_target_pairs={{0,32},{2,34},{4,36},{6,38},{8,40},{10,42},{12,44},{14,46},{16,48}... | collective-permute-start | bytes 196616 | tf_op jit(solution)/shard_map/ppermute | solution.py:63

commit v9 on v8

--- a/solution.py
+++ b/solution.py
@@ -219,8 +219,7 @@
     weights = [pltpu.VMEM((DEPTH, WIDTH), BF)]
     sems = pltpu.SemaphoreType.DMA((STEPS,))
 
-    block = jnp.concatenate([hidden, send(hidden, to_x)])
-    block = jnp.concatenate([block, send(block, to_z4)])
+    block = jnp.concatenate([hidden] + [send(hidden, to) for to in (to_x, to_z4, to_xz4)])
     block = jnp.concatenate([block] + [send(block, to_first(-o)) for o in OFFSETS[1:]])
     near, back, far = (send(block, to_second(-o)) for o in OFFSETS[1:])
 
@@ -235,9 +234,8 @@
         cost_estimate=pl.CostEstimate(flops=2 * ROWS * DEPTH * WIDTH, bytes_accessed=12 << 20, transcendentals=0),
         name="target",
     )(at, aim, lm_weight)
-    near, target_out = lax.optimization_barrier((near, target_out))
-    pieces = [block, near, back, far]
-    pieces = pieces + [send(p, to_c) for p in pieces]
+    own, target_out = lax.optimization_barrier((block, target_out))
+    pieces = [block, near, back, far] + [send(p, to_c) for p in (own, near, back, far)]
 
     stats, soft_own, soft_out = pl.pallas_call(
         logits_kernel,

time: 121 us -> 120 us (level)
  blocking collectives: 15.1 us -> 18.6 us
  waiting for transfers between devices: 37.5 us -> 34.2 us
    all_to_all x1, blocking collectives: 15.1 us -> 18.6 us  [shards(): spread = lax.all_to_all(merged, ('y', 'z'), 0, 0)]
    ppermute x26 -> x27, waiting for transfers between devices: 37.5 us -> 34.2 us  [send(): return lax.ppermute(value, GROUP, pairs(route))]
    ppermute x26 -> x27, starting transfers between devices: 41.7 us -> 40.6 us  [send(): return lax.ppermute(value, GROUP, pairs(route))]
  transfers between devices with their start and end apart: 26 -> 27, of which waited for: 18 -> 17; matrix products, arithmetic and copies ran while one was open for 1% -> 1% of each run, Pallas kernels for 9% -> 9%
where the time goes in v9:
time: 120 us; the launch traced here: 118 us
  starting transfers between devices  40.6 us (34%)
  waiting for transfers between devices  34.2 us (29%)
  Pallas kernels  19.7 us (16%)
  blocking collectives  18.6 us (16%)
  other arithmetic  2.43 us (2%)
  local copies, waits for them, and re-layouts  2.08 us (2%)
    ppermute x27, starting transfers between devices, send(): return lax.ppermute(value, GROUP, pairs(route))  40.6 us
    ppermute x27, waiting for transfers between devices, send(): return lax.ppermute(value, GROUP, pairs(route))  34.2 us
    all_to_all x1, blocking collectives, shards(): spread = lax.all_to_all(merged, ('y', 'z'), 0, 0)  18.6 us
    pallas_call x1, Pallas kernels, shards(): pl.pallas_call(target_kernel, out_shape=[pltpu.HBM((half, DEPTH), BF)] *...  6.76 us
    pallas_call x1, Pallas kernels, shards(): pl.pallas_call(logits_kernel, out_shape=(jax.ShapeDtypeStruct((3, ROWS),...  6.49 us
    pallas_call x3, Pallas kernels, combine(): pl.pallas_call(functools.partial(kernel, parts), out_shape=scales + [jax....  6.42 us
  transfers between devices with their start and end apart: 27, of which 17 were waited for; matrix products, arithmetic and copies ran while one was open for 1% of the time, Pallas kernels for 9%

profile of v9, /device:TPU:4, one launch (start us, length us, event | category | flops | bytes accessed | tf_op | source)
XLA Modules:
  0.0 118.4 jit_solution(1806026437598432096)
XLA Ops:
  0.6 7.9 %collective-permute-start.2 = (bf16[2,8192]{1,0:T(2,128)(2,1)}, bf16[2,8192]{1,0:T(2,128)(2,1)S(1)}, u32[]{:S(2)}, u32[]{:S(2)}) collective-permute-start(bf16[2,8192]{1,0:T(2,128)(2,1)} %param.4), channel_id=1, source_target_pairs={{0,40},{2,42},{4,44},{6,46},{8,32},{10,34},{12,36},{14,38},{16,56}... | collective-permute-start | bytes 98312 | tf_op jit(solution)/shard_map/ppermute | solution.py:63
  8.5 0.0 collective-permute-start.1
  8.5 0.8 collective-permute-start
  9.4 1.4 %collective-permute-done.2 = bf16[2,8192]{1,0:T(2,128)(2,1)S(1)} collective-permute-done((bf16[2,8192]{1,0:T(2,128)(2,1)}, bf16[2,8192]{1,0:T(2,128)(2,1)S(1)}, u32[]{:S(2)}, u32[]{:S(2)}) %collective-permute-start.2) | collective-permute-done | bytes 32800 | tf_op jit(solution)/shard_map/ppermute | solution.py:63
  10.7 6.1 %collective-permute-done.1 = bf16[2,8192]{1,0:T(2,128)(2,1)S(1)} collective-permute-done((bf16[2,8192]{1,0:T(2,128)(2,1)}, bf16[2,8192]{1,0:T(2,128)(2,1)S(1)}, u32[]{:S(2)}, u32[]{:S(2)}) %collective-permute-start.1) | collective-permute-done | bytes 32800 | tf_op jit(solution)/shard_map/ppermute | solution.py:63
  16.8 0.0 collective-permute-done
  16.8 0.9 pad_maximum_fusion
  17.8 0.9 collective-permute-start.5
  18.7 1.0 collective-permute-start.4
  19.7 2.2 %collective-permute-start.3 = (bf16[8,8192]{1,0:T(8,128)(2,1)S(1)}, bf16[8,8192]{1,0:T(8,128)(2,1)S(1)}, u32[]{:S(2)}, u32[]{:S(2)}) collective-permute-start(bf16[8,8192]{1,0:T(8,128)(2,1)S(1)} %pad_maximum_fusion), channel_id=1, source_target_pairs={{0,14},{2,0},{4,2},{6,4},{8,6},{10,8},{12,10},{14,12},{16,208},{18... | collective-permute-start | bytes 393224 | tf_op jit(solution)/shard_map/ppermute | solution.py:63
  21.9 3.3 %collective-permute-done.5 = bf16[8,8192]{1,0:T(8,128)(2,1)S(1)} collective-permute-done((bf16[8,8192]{1,0:T(8,128)(2,1)S(1)}, bf16[8,8192]{1,0:T(8,128)(2,1)S(1)}, u32[]{:S(2)}, u32[]{:S(2)}) %collective-permute-start.5) | collective-permute-done | bytes 131104 | tf_op jit(solution)/shard_map/ppermute | solution.py:63
  25.2 0.6 collective-permute-done.3
  25.8 1.0 concatenate.8.p0
  26.8 3.3 %collective-permute-start.8 = (bf16[32,8192]{1,0:T(8,128)(2,1)S(1)}, bf16[32,8192]{1,0:T(8,128)(2,1)S(1)}, u32[]{:S(2)}, u32[]{:S(2)}) collective-permute-start(bf16[32,8192]{1,0:T(8,128)(2,1)S(1)} %concatenate.8.p0), channel_id=1, source_target_pairs={{0,128},{2,130},{4,132},{6,134},{8,136},{10,138},{12,140},{14,142}... | collective-permute-start | bytes 1572872 | tf_op jit(solution)/shard_map/ppermute | solution.py:63
  30.0 0.7 collective-permute-start.7
  30.7 2.6 %collective-permute-start.6 = (bf16[32,8192]{1,0:T(8,128)(2,1)S(1)}, bf16[32,8192]{1,0:T(8,128)(2,1)S(1)}, u32[]{:S(2)}, u32[]{:S(2)}) collective-permute-start(bf16[32,8192]{1,0:T(8,128)(2,1)S(1)} %concatenate.8.p0), channel_id=1, source_target_pairs={{0,192},{2,194},{4,196},{6,198},{8,200},{10,202},{12,204},{14,206}... | collective-permute-start | bytes 1572872 | tf_op jit(solution)/shard_map/ppermute | solution.py:63
  33.3 0.1 stack.23.at_ref
  33.4 0.7 copy-done.1
  34.0 6.8 %target.1 = (bf16[128,8192]{1,0:T(8,128)(2,1)}, bf16[128,8192]{1,0:T(8,128)(2,1)}) custom-call(s32[5]{0:T(128)S(1)} %stack.23.at_ref, s32[1,256]{1,0:T(1,128)S(1)} %bitcast.7, bf16[8192,512]{1,0:T(8,128)(2,1)} %w_ref.1), custom_call_target="tpu_custom_call" | custom-call | flops 2147483648 | bytes 12582912 | tf_op jit(solution)/shard_map/target/pallas_call | solution.py:227
  40.8 0.0 copy-start.2
  40.8 0.1 collective-permute-start.9
  41.0 0.5 collective-permute-start.12
  41.4 1.7 %collective-permute-done.7.p2 = bf16[32,8192]{1,0:T(8,128)(2,1)S(1)} collective-permute-done((bf16[32,8192]{1,0:T(8,128)(2,1)S(1)}, bf16[32,8192]{1,0:T(8,128)(2,1)S(1)}, u32[]{:S(2)}, u32[]{:S(2)}) %collective-permute-start.7) | collective-permute-done | bytes 524320 | tf_op jit(solution)/shard_map/ppermute | solution.py:63
  43.2 0.4 collective-permute-done.6.p1
  43.5 1.5 %collective-permute-start.10 = (bf16[32,8192]{1,0:T(8,128)(2,1)S(1)}, bf16[32,8192]{1,0:T(8,128)(2,1)S(1)}, u32[]{:S(2)}, u32[]{:S(2)}) collective-permute-start(bf16[32,8192]{1,0:T(8,128)(2,1)S(1)} %collective-permute-done.6.p1), channel_id=1, source_target_pairs={{0,16},{2,18},{4,20},{6,22},{8,24},{10,26},{12,28},{14,30},{16,0},... | collective-permute-start | bytes 1572872 | tf_op jit(solution)/shard_map/ppermute | solution.py:63
  45.0 0.0 collective-permute-done.9.p4
  45.0 0.0 collective-permute-done.12.p7
  45.0 0.1 collective-permute-done.11.p6
  45.1 1.5 %collective-permute-done.10.p5 = bf16[32,8192]{1,0:T(8,128)(2,1)S(1)} collective-permute-done((bf16[32,8192]{1,0:T(8,128)(2,1)S(1)}, bf16[32,8192]{1,0:T(8,128)(2,1)S(1)}, u32[]{:S(2)}, u32[]{:S(2)}) %collective-permute-start.10) | collective-permute-done | bytes 524320 | tf_op jit(solution)/shard_map/ppermute | solution.py:63
  46.5 6.5 %logits.1 = (f32[3,256]{1,0:T(4,128)S(1)}, f32[128,8192]{1,0:T(8,128)}, bf16[128,8192]{1,0:T(8,128)(2,1)}) custom-call(s32[5]{0:T(128)S(1)} %stack.23.at_ref, s32[1,256]{1,0:T(1,128)S(1)} %bitcast.8, bf16[32,8192]{1,0:T(8,128)(2,1)S(1)} %concatenate.8.p0, bf16[32,8192]{1,0:T(8,128)(2,1)S(1)} %collective-permute-done.6.p1, ...), custom_call_target="tpu_custom_call" | custom-call | flops 4294967296 | bytes 19922944 | tf_op jit(solution)/shard_map/logits/pallas_call | solution.py:240
  53.0 0.6 collective-permute-start.15
  53.7 1.5 %collective-permute-start.14 = (f32[3,256]{1,0:T(4,128)S(1)}, f32[3,256]{1,0:T(4,128)S(1)}, u32[]{:S(2)}, u32[]{:S(2)}) collective-permute-start(f32[3,256]{1,0:T(4,128)S(1)} %get-tuple-element.21.own_ref), channel_id=1, source_target_pairs={{0,32},{2,34},{4,36},{6,38},{8,40},{10,42},{12,44},{14,46},{16,48}... | collective-permute-start | bytes 9224 | tf_op jit(solution)/shard_map/ppermute | solution.py:63
  55.1 0.0 collective-permute-start.13
  55.1 1.0 collective-permute-done.15.both_ref
  56.2 1.1 collective-permute-done.14.x_ref
  57.3 0.0 collective-permute-done.13.core_ref
  57.3 0.1 collective-permute-start.16
  57.4 0.5 collective-permute-start.17
  57.9 18.6 %all_to_all.5.spread_ref = f32[32,3,256]{2,1,0:T(4,128)S(1)} all-to-all(f32[32,3,256]{2,1,0:T(4,128)S(1)} %merge.1), channel_id=1, replica_groups=mesh['y'=4,'x'=2,'c'=2,'z'=8,'dp'=2] {'y','z'}, dimensions={0} | all-to-all | bytes 196608 | tf_op jit(solution)/shard_map/all_to_all | solution.py:261
  76.5 2.3 %combine.3 = (f32[128,128]{1,0:T(8,128)S(1)}, bf16[32,8192]{1,0:T(8,128)(2,1)S(1)}) custom-call(s32[5]{0:T(128)S(1)} %stack.23.at_ref, f32[1,256]{1,0:T(1,128)S(1)} %bitcast.9, f32[3,256]{1,0:T(4,128)S(1)} %get-tuple-element.21.own_ref, f32[3,256]{1,0:T(4,128)S(1)} %collective-permute-done.13.core_ref, f32[32,3,256]{2,1,0:T(4,128)S(1)} %all_to_all.5.spread_ref, ...), custom_call_target="tpu_custom_call" | custom-call | flops 1572864 | bytes 3145728 | tf_op jit(solution)/shard_map/combine/pallas_call | solution.py:270
  78.8 1.4 %collective-permute-start.18 = (bf16[32,8192]{1,0:T(8,128)(2,1)S(1)}, bf16[32,8192]{1,0:T(8,128)(2,1)S(1)}, u32[]{:S(2)}, u32[]{:S(2)}) collective-permute-start(bf16[32,8192]{1,0:T(8,128)(2,1)S(1)} %get-tuple-element.30), channel_id=1, source_target_pairs={{0,128},{2,130},{4,132},{6,134},{8,136},{10,138},{12,140},{14,142}... | collective-permute-start | bytes 1572872 | tf_op jit(solution)/shard_map/ppermute | solution.py:63
  80.2 2.3 %combine.5 = (bf16[32,8192]{1,0:T(8,128)(2,1)S(1)}, bf16[32,8192]{1,0:T(8,128)(2,1)S(1)}) custom-call(f32[128,128]{1,0:T(8,128)S(1)} %get-tuple-element.29.scales_ref, f32[128,8192]{1,0:T(8,128)} %get-tuple-element.25.refs_0_, bf16[128,8192]{1,0:T(8,128)(2,1)S(1)} %collective-permute-done.16.refs_1_, bf16[128,8192]{1,0:T(8,128)(2,1)} %get-tuple-element.27.refs_2_, ...), custom_call_target="tpu_custom_call" | custom-call | flops 3145728 | bytes 6291456 | tf_op jit(solution)/shard_map/combine/pallas_call | solution.py:270
  82.6 0.8 collective-permute-start.19
  83.3 2.5 %collective-permute-start.20 = (bf16[32,8192]{1,0:T(8,128)(2,1)S(1)}, bf16[32,8192]{1,0:T(8,128)(2,1)S(1)}, u32[]{:S(2)}, u32[]{:S(2)}) collective-permute-start(bf16[32,8192]{1,0:T(8,128)(2,1)S(1)} %get-tuple-element.32), channel_id=1, source_target_pairs={{0,192},{2,194},{4,196},{6,198},{8,200},{10,202},{12,204},{14,206}... | collective-permute-start | bytes 1572872 | tf_op jit(solution)/shard_map/ppermute | solution.py:63
  85.9 1.8 %combine.4 = f32[32,8192]{1,0:T(8,128)S(1)} custom-call(f32[128,128]{1,0:T(8,128)S(1)} %get-tuple-element.29.scales_ref, f32[128,8192]{1,0:T(8,128)} %get-tuple-element.25.refs_0_, bf16[128,8192]{1,0:T(8,128)(2,1)S(1)} %collective-permute-done.16.refs_1_, bf16[128,8192]{1,0:T(8,128)(2,1)} %get-tuple-element.27.refs_2_, ...), custom_call_target="tpu_custom_call" | custom-call | flops 1572864 | bytes 3145728 | tf_op jit(solution)/shard_map/combine/pallas_call | solution.py:270
  87.7 2.0 %collective-permute-done.18 = bf16[32,8192]{1,0:T(8,128)(2,1)S(1)} collective-permute-done((bf16[32,8192]{1,0:T(8,128)(2,1)S(1)}, bf16[32,8192]{1,0:T(8,128)(2,1)S(1)}, u32[]{:S(2)}, u32[]{:S(2)}) %collective-permute-start.18) | collective-permute-done | bytes 524320 | tf_op jit(solution)/shard_map/ppermute | solution.py:63
  89.7 5.5 %collective-permute-done.19 = bf16[32,8192]{1,0:T(8,128)(2,1)S(1)} collective-permute-done((bf16[32,8192]{1,0:T(8,128)(2,1)S(1)}, bf16[32,8192]{1,0:T(8,128)(2,1)S(1)}, u32[]{:S(2)}, u32[]{:S(2)}) %collective-permute-start.19) | collective-permute-done | bytes 524320 | tf_op jit(solution)/shard_map/ppermute | solution.py:63
  95.2 0.0 collective-permute-done.20
  95.2 0.3 fusion.3
  95.5 1.6 %collective-permute-start.21 = (bf16[8,8192]{1,0:T(8,128)(2,1)S(1)}, bf16[8,8192]{1,0:T(8,128)(2,1)S(1)}, u32[]{:S(2)}, u32[]{:S(2)}) collective-permute-start(bf16[8,8192]{1,0:T(8,128)(2,1)S(1)} %get-tuple-element.39), channel_id=1, source_target_pairs={{0,4},{2,6},{4,8},{6,10},{8,12},{10,14},{12,0},{14,2},{16,144},{18... | collective-permute-start | bytes 393224 | tf_op jit(solution)/shard_map/ppermute | solution.py:63
  97.1 2.6 %collective-permute-start.23 = (bf16[8,8192]{1,0:T(8,128)(2,1)S(1)}, bf16[8,8192]{1,0:T(8,128)(2,1)S(1)}, u32[]{:S(2)}, u32[]{:S(2)}) collective-permute-start(bf16[8,8192]{1,0:T(8,128)(2,1)S(1)} %get-tuple-element.40), channel_id=1, source_target_pairs={{0,14},{2,0},{4,2},{6,4},{8,6},{10,8},{12,10},{14,12},{16,208},{18... | collective-permute-start | bytes 393224 | tf_op jit(solution)/shard_map/ppermute | solution.py:63
  99.7 0.2 slice_reduce_fusion
  99.9 3.1 %collective-permute-done.21 = bf16[8,8192]{1,0:T(8,128)(2,1)S(1)} collective-permute-done((bf16[8,8192]{1,0:T(8,128)(2,1)S(1)}, bf16[8,8192]{1,0:T(8,128)(2,1)S(1)}, u32[]{:S(2)}, u32[]{:S(2)}) %collective-permute-start.21) | collective-permute-done | bytes 131104 | tf_op jit(solution)/shard_map/ppermute | solution.py:63
  103.1 2.8 %collective-permute-done.22 = bf16[8,8192]{1,0:T(8,128)(2,1)S(1)} collective-permute-done((bf16[8,8192]{1,0:T(8,128)(2,1)S(1)}, bf16[8,8192]{1,0:T(8,128)(2,1)S(1)}, u32[]{:S(2)}, u32[]{:S(2)}) %collective-permute-start.22) | collective-permute-done | bytes 131104 | tf_op jit(solution)/shard_map/ppermute | solution.py:63
  105.9 0.1 fusion.2
  106.0 0.1 fusion.5
  106.0 1.2 %collective-permute-start.25 = (bf16[2,8192]{1,0:T(2,128)(2,1)S(1)}, bf16[2,8192]{1,0:T(2,128)(2,1)S(1)}, u32[]{:S(2)}, u32[]{:S(2)}) collective-permute-start(bf16[2,8192]{1,0:T(2,128)(2,1)S(1)} %get-tuple-element.42), channel_id=1, source_target_pairs={{0,8},{2,10},{4,12},{6,14},{8,0},{10,2},{12,4},{14,6},{16,24},{18,... | collective-permute-start | bytes 98312 | tf_op jit(solution)/shard_map/ppermute | solution.py:63
  107.3 5.3 %collective-permute-start.26 = (bf16[2,8192]{1,0:T(2,128)(2,1)S(1)}, bf16[2,8192]{1,0:T(2,128)(2,1)S(1)}, u32[]{:S(2)}, u32[]{:S(2)}) collective-permute-start(bf16[2,8192]{1,0:T(2,128)(2,1)S(1)} %get-tuple-element.43), channel_id=1, source_target_pairs={{0,40},{2,42},{4,44},{6,46},{8,32},{10,34},{12,36},{14,38},{16,56}... | collective-permute-start | bytes 98312 | tf_op jit(solution)/shard_map/ppermute | solution.py:63
  112.6 1.1 collective-permute-start.24
  113.6 0.5 multiply_multiply_fusion
  114.1 0.1 collective-permute-done.25
  114.3 2.1 %collective-permute-done.26 = bf16[2,8192]{1,0:T(2,128)(2,1)S(1)} collective-permute-done((bf16[2,8192]{1,0:T(2,128)(2,1)S(1)}, bf16[2,8192]{1,0:T(2,128)(2,1)S(1)}, u32[]{:S(2)}, u32[]{:S(2)}) %collective-permute-start.26) | collective-permute-done | bytes 32800 | tf_op jit(solution)/shard_map/ppermute | solution.py:63
  116.4 1.3 %collective-permute-done.24 = f32[2,8192]{1,0:T(2,128)S(1)} collective-permute-done((f32[2,8192]{1,0:T(2,128)S(1)}, f32[2,8192]{1,0:T(2,128)S(1)}, u32[]{:S(2)}, u32[]{:S(2)}) %collective-permute-start.24) | collective-permute-done | bytes 65568 | tf_op jit(solution)/shard_map/ppermute | solution.py:63
  117.7 0.7 fusion.1
  (16 shorter events, 0.1 us)
Async XLA Ops:
  0.6 10.1 %collective-permute-start.2 = (bf16[2,8192]{1,0:T(2,128)(2,1)}, bf16[2,8192]{1,0:T(2,128)(2,1)S(1)}, u32[]{:S(2)}, u32[]{:S(2)}) collective-permute-start(bf16[2,8192]{1,0:T(2,128)(2,1)} %param.4), channel_id=1, source_target_pairs={{0,40},{2,42},{4,44},{6,46},{8,32},{10,34},{12,36},{14,38},{16,56}... | collective-permute-start | bytes 98312 | tf_op jit(solution)/shard_map/ppermute | solution.py:63
  8.5 8.3 %collective-permute-start.1 = (bf16[2,8192]{1,0:T(2,128)(2,1)}, bf16[2,8192]{1,0:T(2,128)(2,1)S(1)}, u32[]{:S(2)}, u32[]{:S(2)}) collective-permute-start(bf16[2,8192]{1,0:T(2,128)(2,1)} %param.4), channel_id=1, source_target_pairs={{0,8},{2,10},{4,12},{6,14},{8,0},{10,2},{12,4},{14,6},{16,24},{18,... | collective-permute-start | bytes 98312 | tf_op jit(solution)/shard_map/ppermute | solution.py:63
  8.5 8.3 %collective-permute-start = (bf16[2,8192]{1,0:T(2,128)(2,1)}, bf16[2,8192]{1,0:T(2,128)(2,1)S(1)}, u32[]{:S(2)}, u32[]{:S(2)}) collective-permute-start(bf16[2,8192]{1,0:T(2,128)(2,1)} %param.4), channel_id=1, source_target_pairs={{0,32},{2,34},{4,36},{6,38},{8,40},{10,42},{12,44},{14,46},{16,48}... | collective-permute-start | bytes 98312 | tf_op jit(solution)/shard_map/ppermute | solution.py:63
  17.8 7.5 %collective-permute-start.5 = (bf16[8,8192]{1,0:T(8,128)(2,1)S(1)}, bf16[8,8192]{1,0:T(8,128)(2,1)S(1)}, u32[]{:S(2)}, u32[]{:S(2)}) collective-permute-start(bf16[8,8192]{1,0:T(8,128)(2,1)S(1)} %pad_maximum_fusion), channel_id=1, source_target_pairs={{0,12},{2,14},{4,0},{6,2},{8,4},{10,6},{12,8},{14,10},{16,144},{18... | collective-permute-start | bytes 393224 | tf_op jit(solution)/shard_map/ppermute | solution.py:63
  18.7 6.5 %collective-permute-start.4 = (bf16[8,8192]{1,0:T(8,128)(2,1)S(1)}, bf16[8,8192]{1,0:T(8,128)(2,1)S(1)}, u32[]{:S(2)}, u32[]{:S(2)}) collective-permute-start(bf16[8,8192]{1,0:T(8,128)(2,1)S(1)} %pad_maximum_fusion), channel_id=1, source_target_pairs={{0,2},{2,4},{4,6},{6,8},{8,10},{10,12},{12,14},{14,0},{16,80},{18,... | collective-permute-start | bytes 393224 | tf_op jit(solution)/shard_map/ppermute | solution.py:63
  19.7 6.1 %collective-permute-start.3 = (bf16[8,8192]{1,0:T(8,128)(2,1)S(1)}, bf16[8,8192]{1,0:T(8,128)(2,1)S(1)}, u32[]{:S(2)}, u32[]{:S(2)}) collective-permute-start(bf16[8,8192]{1,0:T(8,128)(2,1)S(1)} %pad_maximum_fusion), channel_id=1, source_target_pairs={{0,14},{2,0},{4,2},{6,4},{8,6},{10,8},{12,10},{14,12},{16,208},{18... | collective-permute-start | bytes 393224 | tf_op jit(solution)/shard_map/ppermute | solution.py:63
  26.8 14.2 %collective-permute-start.8 = (bf16[32,8192]{1,0:T(8,128)(2,1)S(1)}, bf16[32,8192]{1,0:T(8,128)(2,1)S(1)}, u32[]{:S(2)}, u32[]{:S(2)}) collective-permute-start(bf16[32,8192]{1,0:T(8,128)(2,1)S(1)} %concatenate.8.p0), channel_id=1, source_target_pairs={{0,128},{2,130},{4,132},{6,134},{8,136},{10,138},{12,140},{14,142}... | collective-permute-start | bytes 1572872 | tf_op jit(solution)/shard_map/ppermute | solution.py:63
  30.0 13.1 %collective-permute-start.7 = (bf16[32,8192]{1,0:T(8,128)(2,1)S(1)}, bf16[32,8192]{1,0:T(8,128)(2,1)S(1)}, u32[]{:S(2)}, u32[]{:S(2)}) collective-permute-start(bf16[32,8192]{1,0:T(8,128)(2,1)S(1)} %concatenate.8.p0), channel_id=1, source_target_pairs={{0,64},{2,66},{4,68},{6,70},{8,72},{10,74},{12,76},{14,78},{16,18}... | collective-permute-start | bytes 1572872 | tf_op jit(solution)/shard_map/ppermute | solution.py:63
  30.7 12.8 %collective-permute-start.6 = (bf16[32,8192]{1,0:T(8,128)(2,1)S(1)}, bf16[32,8192]{1,0:T(8,128)(2,1)S(1)}, u32[]{:S(2)}, u32[]{:S(2)}) collective-permute-start(bf16[32,8192]{1,0:T(8,128)(2,1)S(1)} %concatenate.8.p0), channel_id=1, source_target_pairs={{0,192},{2,194},{4,196},{6,198},{8,200},{10,202},{12,204},{14,206}... | collective-permute-start | bytes 1572872 | tf_op jit(solution)/shard_map/ppermute | solution.py:63
  33.4 0.7 copy-start.1
  34.0 12.5 %copy-start = (bf16[8192,512]{1,0:T(8,128)(2,1)S(1)}, bf16[8192,512]{1,0:T(8,128)(2,1)}, u32[]{:S(2)}) copy-start(bf16[8192,512]{1,0:T(8,128)(2,1)} %w_ref.1) | copy-start | bytes 25165828
  40.8 16.6 %copy-start.3 = (bf16[128,8192]{1,0:T(8,128)(2,1)S(1)}, bf16[128,8192]{1,0:T(8,128)(2,1)}, u32[]{:S(2)}) copy-start(bf16[128,8192]{1,0:T(8,128)(2,1)} %get-tuple-element.28) | copy-start | bytes 6291460
  40.8 35.7 %copy-start.2 = (f32[256]{0:T(256)S(1)}, f32[256]{0:T(256)}, u32[]{:S(2)}) copy-start(f32[256]{0:T(256)} %param.7) | copy-start | bytes 3076
  40.8 4.2 %collective-permute-start.9 = (bf16[32,8192]{1,0:T(8,128)(2,1)S(1)}, bf16[32,8192]{1,0:T(8,128)(2,1)S(1)}, u32[]{:S(2)}, u32[]{:S(2)}) collective-permute-start(bf16[32,8192]{1,0:T(8,128)(2,1)S(1)} %concatenate.8.p0), channel_id=1, source_target_pairs={{0,16},{2,18},{4,20},{6,22},{8,24},{10,26},{12,28},{14,30},{16,0},... | collective-permute-start | bytes 1572872 | tf_op jit(solution)/shard_map/ppermute | solution.py:63
  41.0 4.1 %collective-permute-start.12 = (bf16[32,8192]{1,0:T(8,128)(2,1)S(1)}, bf16[32,8192]{1,0:T(8,128)(2,1)S(1)}, u32[]{:S(2)}, u32[]{:S(2)}) collective-permute-start(bf16[32,8192]{1,0:T(8,128)(2,1)S(1)} %collective-permute-done.8.p3), channel_id=1, source_target_pairs={{0,16},{2,18},{4,20},{6,22},{8,24},{10,26},{12,28},{14,30},{16,0},... | collective-permute-start | bytes 1572872 | tf_op jit(solution)/shard_map/ppermute | solution.py:63
  43.2 1.9 %collective-permute-start.11 = (bf16[32,8192]{1,0:T(8,128)(2,1)S(1)}, bf16[32,8192]{1,0:T(8,128)(2,1)S(1)}, u32[]{:S(2)}, u32[]{:S(2)}) collective-permute-start(bf16[32,8192]{1,0:T(8,128)(2,1)S(1)} %collective-permute-done.7.p2), channel_id=1, source_target_pairs={{0,16},{2,18},{4,20},{6,22},{8,24},{10,26},{12,28},{14,30},{16,0},... | collective-permute-start | bytes 1572872 | tf_op jit(solution)/shard_map/ppermute | solution.py:63
  43.5 3.0 %collective-permute-start.10 = (bf16[32,8192]{1,0:T(8,128)(2,1)S(1)}, bf16[32,8192]{1,0:T(8,128)(2,1)S(1)}, u32[]{:S(2)}, u32[]{:S(2)}) collective-permute-start(bf16[32,8192]{1,0:T(8,128)(2,1)S(1)} %collective-permute-done.6.p1), channel_id=1, source_target_pairs={{0,16},{2,18},{4,20},{6,22},{8,24},{10,26},{12,28},{14,30},{16,0},... | collective-permute-start | bytes 1572872 | tf_op jit(solution)/shard_map/ppermute | solution.py:63
  53.0 3.1 %collective-permute-start.15 = (f32[3,256]{1,0:T(4,128)S(1)}, f32[3,256]{1,0:T(4,128)S(1)}, u32[]{:S(2)}, u32[]{:S(2)}) collective-permute-start(f32[3,256]{1,0:T(4,128)S(1)} %get-tuple-element.21.own_ref), channel_id=1, source_target_pairs={{0,48},{2,50},{4,52},{6,54},{8,56},{10,58},{12,60},{14,62},{16,32}... | collective-permute-start | bytes 9224 | tf_op jit(solution)/shard_map/ppermute | solution.py:63
  53.7 3.6 %collective-permute-start.14 = (f32[3,256]{1,0:T(4,128)S(1)}, f32[3,256]{1,0:T(4,128)S(1)}, u32[]{:S(2)}, u32[]{:S(2)}) collective-permute-start(f32[3,256]{1,0:T(4,128)S(1)} %get-tuple-element.21.own_ref), channel_id=1, source_target_pairs={{0,32},{2,34},{4,36},{6,38},{8,40},{10,42},{12,44},{14,46},{16,48}... | collective-permute-start | bytes 9224 | tf_op jit(solution)/shard_map/ppermute | solution.py:63
  55.1 2.1 %collective-permute-start.13 = (f32[3,256]{1,0:T(4,128)S(1)}, f32[3,256]{1,0:T(4,128)S(1)}, u32[]{:S(2)}, u32[]{:S(2)}) collective-permute-start(f32[3,256]{1,0:T(4,128)S(1)} %get-tuple-element.21.own_ref), channel_id=1, source_target_pairs={{0,16},{2,18},{4,20},{6,22},{8,24},{10,26},{12,28},{14,30},{16,0},... | collective-permute-start | bytes 9224 | tf_op jit(solution)/shard_map/ppermute | solution.py:63
  57.3 19.2 %collective-permute-start.16 = (bf16[128,8192]{1,0:T(8,128)(2,1)}, bf16[128,8192]{1,0:T(8,128)(2,1)S(1)}, u32[]{:S(2)}, u32[]{:S(2)}) collective-permute-start(bf16[128,8192]{1,0:T(8,128)(2,1)} %get-tuple-element.26), channel_id=1, source_target_pairs={{0,16},{2,18},{4,20},{6,22},{8,24},{10,26},{12,28},{14,30},{16,0},... | collective-permute-start | bytes 6291464 | tf_op jit(solution)/shard_map/ppermute | solution.py:63
  57.4 19.1 %collective-permute-start.17 = (bf16[128,8192]{1,0:T(8,128)(2,1)S(1)}, bf16[128,8192]{1,0:T(8,128)(2,1)S(1)}, u32[]{:S(2)}, u32[]{:S(2)}) collective-permute-start(bf16[128,8192]{1,0:T(8,128)(2,1)S(1)} %copy-done.3), channel_id=1, source_target_pairs={{0,16},{2,18},{4,20},{6,22},{8,24},{10,26},{12,28},{14,30},{16,0},... | collective-permute-start | bytes 6291464 | tf_op jit(solution)/shard_map/ppermute | solution.py:63
  78.8 10.9 %collective-permute-start.18 = (bf16[32,8192]{1,0:T(8,128)(2,1)S(1)}, bf16[32,8192]{1,0:T(8,128)(2,1)S(1)}, u32[]{:S(2)}, u32[]{:S(2)}) collective-permute-start(bf16[32,8192]{1,0:T(8,128)(2,1)S(1)} %get-tuple-element.30), channel_id=1, source_target_pairs={{0,128},{2,130},{4,132},{6,134},{8,136},{10,138},{12,140},{14,142}... | collective-permute-start | bytes 1572872 | tf_op jit(solution)/shard_map/ppermute | solution.py:63
  82.6 12.7 %collective-permute-start.19 = (bf16[32,8192]{1,0:T(8,128)(2,1)S(1)}, bf16[32,8192]{1,0:T(8,128)(2,1)S(1)}, u32[]{:S(2)}, u32[]{:S(2)}) collective-permute-start(bf16[32,8192]{1,0:T(8,128)(2,1)S(1)} %get-tuple-element.31), channel_id=1, source_target_pairs={{0,64},{2,66},{4,68},{6,70},{8,72},{10,74},{12,76},{14,78},{16,18}... | collective-permute-start | bytes 1572872 | tf_op jit(solution)/shard_map/ppermute | solution.py:63
  83.3 11.9 %collective-permute-start.20 = (bf16[32,8192]{1,0:T(8,128)(2,1)S(1)}, bf16[32,8192]{1,0:T(8,128)(2,1)S(1)}, u32[]{:S(2)}, u32[]{:S(2)}) collective-permute-start(bf16[32,8192]{1,0:T(8,128)(2,1)S(1)} %get-tuple-element.32), channel_id=1, source_target_pairs={{0,192},{2,194},{4,196},{6,198},{8,200},{10,202},{12,204},{14,206}... | collective-permute-start | bytes 1572872 | tf_op jit(solution)/shard_map/ppermute | solution.py:63
  95.5 7.5 %collective-permute-start.21 = (bf16[8,8192]{1,0:T(8,128)(2,1)S(1)}, bf16[8,8192]{1,0:T(8,128)(2,1)S(1)}, u32[]{:S(2)}, u32[]{:S(2)}) collective-permute-start(bf16[8,8192]{1,0:T(8,128)(2,1)S(1)} %get-tuple-element.39), channel_id=1, source_target_pairs={{0,4},{2,6},{4,8},{6,10},{8,12},{10,14},{12,0},{14,2},{16,144},{18... | collective-permute-start | bytes 393224 | tf_op jit(solution)/shard_map/ppermute | solution.py:63
  97.1 6.0 %collective-permute-start.23 = (bf16[8,8192]{1,0:T(8,128)(2,1)S(1)}, bf16[8,8192]{1,0:T(8,128)(2,1)S(1)}, u32[]{:S(2)}, u32[]{:S(2)}) collective-permute-start(bf16[8,8192]{1,0:T(8,128)(2,1)S(1)} %get-tuple-element.40), channel_id=1, source_target_pairs={{0,14},{2,0},{4,2},{6,4},{8,6},{10,8},{12,10},{14,12},{16,208},{18... | collective-permute-start | bytes 393224 | tf_op jit(solution)/shard_map/ppermute | solution.py:63
  99.7 6.2 %collective-permute-start.22 = (bf16[8,8192]{1,0:T(8,128)(2,1)S(1)}, bf16[8,8192]{1,0:T(8,128)(2,1)S(1)}, u32[]{:S(2)}, u32[]{:S(2)}) collective-permute-start(bf16[8,8192]{1,0:T(8,128)(2,1)S(1)} %get-tuple-element.41), channel_id=1, source_target_pairs={{0,2},{2,4},{4,6},{6,8},{8,10},{10,12},{12,14},{14,0},{16,80},{18,... | collective-permute-start | bytes 393224 | tf_op jit(solution)/shard_map/ppermute | solution.py:63
  106.0 8.3 %collective-permute-start.25 = (bf16[2,8192]{1,0:T(2,128)(2,1)S(1)}, bf16[2,8192]{1,0:T(2,128)(2,1)S(1)}, u32[]{:S(2)}, u32[]{:S(2)}) collective-permute-start(bf16[2,8192]{1,0:T(2,128)(2,1)S(1)} %get-tuple-element.42), channel_id=1, source_target_pairs={{0,8},{2,10},{4,12},{6,14},{8,0},{10,2},{12,4},{14,6},{16,24},{18,... | collective-permute-start | bytes 98312 | tf_op jit(solution)/shard_map/ppermute | solution.py:63
  107.3 9.1 %collective-permute-start.26 = (bf16[2,8192]{1,0:T(2,128)(2,1)S(1)}, bf16[2,8192]{1,0:T(2,128)(2,1)S(1)}, u32[]{:S(2)}, u32[]{:S(2)}) collective-permute-start(bf16[2,8192]{1,0:T(2,128)(2,1)S(1)} %get-tuple-element.43), channel_id=1, source_target_pairs={{0,40},{2,42},{4,44},{6,46},{8,32},{10,34},{12,36},{14,38},{16,56}... | collective-permute-start | bytes 98312 | tf_op jit(solution)/shard_map/ppermute | solution.py:63
  112.6 5.1 %collective-permute-start.24 = (f32[2,8192]{1,0:T(2,128)S(1)}, f32[2,8192]{1,0:T(2,128)S(1)}, u32[]{:S(2)}, u32[]{:S(2)}) collective-permute-start(f32[2,8192]{1,0:T(2,128)S(1)} %slice.54), channel_id=1, source_target_pairs={{0,32},{2,34},{4,36},{6,38},{8,40},{10,42},{12,44},{14,46},{16,48}... | collective-permute-start | bytes 196616 | tf_op jit(solution)/shard_map/ppermute | solution.py:63

commit v10 on v9

--- a/solution.py
+++ b/solution.py
@@ -67,7 +67,7 @@
     return pltpu.CompilerParams(vmem_limit_bytes=mib << 20)
 
 
-def placed(at_ref):
+def row_numbers(at_ref):
     y, x, c, z = (at_ref[i] for i in range(4))
     at = lax.broadcasted_iota(jnp.int32, (ROWS, 1), 0)
     r, near, q1, q2, cr = at & 1, (at >> 1) & 3, (at >> 3) & 3, (at >> 5) & 3, at >> 7
@@ -77,8 +77,15 @@
     core = c ^ cr
     zo = jnp.where(core == 0, o1, o2) + 4 * z4
     yo = jnp.where(core == 0, o2, o1)
-    rows = ((((y + yo) & 3) * 2 + (x ^ xr)) * 2 + core) * 16 + ((z + zo) & 7) * 2 + r
-    return rows == lax.broadcasted_iota(jnp.int32, (ROWS, ROWS), 1)
+    return ((((y + yo) & 3) * 2 + (x ^ xr)) * 2 + core) * 16 + ((z + zo) & 7) * 2 + r
+
+
+def placed(rows):
+    return rows == lax.broadcasted_iota(jnp.int32, (rows.shape[0], ROWS), 1)
+
+
+def placed_in_half(rows):
+    return (rows >> 5) * 16 + (rows & 15) == lax.broadcasted_iota(jnp.int32, (rows.shape[0], ROWS // 2), 1)
 
 
 def hits(at_ref, targets_ref, place):
@@ -99,7 +106,7 @@
     return copies
 
 
-def logits_kernel(at_ref, targets_ref, p0, p1, p2, p3, p4, p5, p6, p7, w_ref, stats_ref, own_hbm, other_hbm, own_ref, other_ref, own_sems, other_sems):
+def logits_kernel(at_ref, targets_ref, p0, p1, p2, p3, p4, p5, p6, p7, w_ref, stats_ref, other_stats_ref, own_hbm, other_hbm, own_ref, other_ref, own_sems, other_sems):
     acc = jnp.zeros((ROWS, WIDTH), F32)
     for k in range(STEPS):
         cut = slice(k * CHUNK, (k + 1) * CHUNK)
@@ -108,11 +115,14 @@
     top = jnp.max(acc, axis=1, keepdims=True)
     soft = jnp.exp(acc - top)
     total = jnp.sum(soft, axis=1, keepdims=True)
-    place = placed(at_ref)
-    hit = hits(at_ref, targets_ref, place)
+    rows = row_numbers(at_ref)
+    hit = hits(at_ref, targets_ref, placed(rows))
     picked = jnp.sum(jnp.where(hit, acc, 0.0), axis=1, keepdims=True)
+    half = ROWS // 2
+    place = placed_in_half(rows)
     for i, column in enumerate((top, total, picked)):
-        stats_ref[i : i + 1, :] = jnp.sum(jnp.where(place, column, 0.0), axis=0, keepdims=True)
+        stats_ref[i : i + 1, :] = jnp.sum(jnp.where(place[:half], column[:half], 0.0), axis=0, keepdims=True)
+        other_stats_ref[i : i + 1, :] = jnp.sum(jnp.where(place[half:], column[half:], 0.0), axis=0, keepdims=True)
     own = (own_ref, column_copies(own_ref, own_hbm, own_sems))
     other = (other_ref, column_copies(other_ref, other_hbm, other_sems))
     products(jnp.where(hit, 0.0, soft).astype(BF), None, w_ref, (own, other))
@@ -136,7 +146,7 @@
 
 def target_kernel(at_ref, targets_ref, w_hbm, own_hbm, other_hbm, w_ref, own_ref, other_ref, w_sems, own_sems, other_sems):
     copies = weight_copies(w_hbm, w_ref, w_sems)
-    left = jnp.where(hits(at_ref, targets_ref, placed(at_ref)), 1.0, 0.0).astype(BF)
+    left = jnp.where(hits(at_ref, targets_ref, placed(row_numbers(at_ref))), 1.0, 0.0).astype(BF)
     own = (own_ref, column_copies(own_ref, own_hbm, own_sems))
     other = (other_ref, column_copies(other_ref, other_hbm, other_sems))
     products(left, copies, w_ref, (own, other))
@@ -154,7 +164,8 @@
 
 
 def row_scales(at_ref, grad_ref, own_ref, core_ref, spread_ref):
-    place = placed(at_ref)[: ROWS // 2]
+    rows = row_numbers(at_ref)[: ROWS // 2]
+    place = placed_in_half(rows)
 
     def ordered(row):
         return jnp.sum(jnp.where(place, row, 0.0), axis=1, keepdims=True)
@@ -165,7 +176,7 @@
     log_total = ordered(highest + jnp.log(total))
     picked = ordered(jnp.sum(spread_ref[:, 2, :], axis=0, keepdims=True))
     factor = 1.0 + 2.0 * zloss_coef * log_total
-    grad = ordered(grad_ref[...])
+    grad = jnp.sum(jnp.where(placed(rows), grad_ref[...], 0.0), axis=1, keepdims=True)
     target = (grad * (jnp.exp(picked - log_total) * factor - 1.0)).astype(BF).astype(F32)
     own, core = (grad * factor * jnp.exp(ordered(ref[0:1, :]) - log_total) for ref in (own_ref, core_ref))
     lane = lax.broadcasted_iota(jnp.int32, (ROWS // 2, 128), 1)
@@ -211,6 +222,10 @@
     combine_end(parts, combine_start(parts, sources, buffers, sems), scales_ref, buffers, outs)
 
 
+def join_kernel(a_ref, b_ref, c_ref, d_ref, out_ref):
+    out_ref[...] = jnp.concatenate([r[...] for r in (a_ref, b_ref, c_ref, d_ref)], axis=0)
+
+
 def shards(hidden, lm_weight, targets, loss_grad):
     half = ROWS // 2
     at = jnp.stack([lax.axis_index(a) for a in GROUP] + [lax.axis_index(GROUP) * WIDTH])
@@ -220,7 +235,14 @@
     sems = pltpu.SemaphoreType.DMA((STEPS,))
 
     block = jnp.concatenate([hidden] + [send(hidden, to) for to in (to_x, to_z4, to_xz4)])
-    block = jnp.concatenate([block] + [send(block, to_first(-o)) for o in OFFSETS[1:]])
+    block = pl.pallas_call(
+        join_kernel,
+        out_shape=jax.ShapeDtypeStruct((32, DEPTH), BF),
+        in_specs=[VMEM] * 4,
+        out_specs=VMEM,
+        compiler_params=params(),
+        name="join",
+    )(block, *(send(block, to_first(-o)) for o in OFFSETS[1:]))
     near, back, far = (send(block, to_second(-o)) for o in OFFSETS[1:])
 
     aim, _ = lax.optimization_barrier((targets, block))
@@ -237,20 +259,20 @@
     own, target_out = lax.optimization_barrier((block, target_out))
     pieces = [block, near, back, far] + [send(p, to_c) for p in (own, near, back, far)]
 
-    stats, soft_own, soft_out = pl.pallas_call(
+    own_stats, other_stats, soft_own, soft_out = pl.pallas_call(
         logits_kernel,
-        out_shape=(jax.ShapeDtypeStruct((3, ROWS), F32), pltpu.HBM((half, DEPTH), F32), pltpu.HBM((half, DEPTH), BF)),
+        out_shape=[jax.ShapeDtypeStruct((3, half), F32)] * 2 + [pltpu.HBM((half, DEPTH), F32), pltpu.HBM((half, DEPTH), BF)],
         in_specs=[SMEM] + [VMEM] * 10,
-        out_specs=(VMEM, HBM, HBM),
+        out_specs=(VMEM, VMEM, HBM, HBM),
         scratch_shapes=[pltpu.VMEM((half, DEPTH), F32), pltpu.VMEM((half, DEPTH), BF)] + [sems] * 2,
         compiler_params=params(16),
         cost_estimate=pl.CostEstimate(flops=4 * ROWS * DEPTH * WIDTH, bytes_accessed=19 << 20, transcendentals=ROWS * WIDTH),
         name="logits",
     )(at, targets, *pieces, pltpu.with_memory_space_constraint(lm_weight_in, pltpu.VMEM))
-    stats = [stats] + [send(stats, to) for to in (to_c, to_x, to_xc)]
+    stats = [own_stats, send(other_stats, to_c), send(own_stats, to_x), send(other_stats, to_xc)]
     merged = pl.pallas_call(
         merge_kernel,
-        out_shape=jax.ShapeDtypeStruct((32, 3, ROWS), F32),
+        out_shape=jax.ShapeDtypeStruct((32, 3, half), F32),
         in_specs=[VMEM] * 4,
         out_specs=VMEM,
         compiler_params=params(),

time: 120 us -> 124 us (1.033)
  blocking collectives: 18.6 us -> 23.2 us
  waiting for transfers between devices: 34.2 us -> 35.9 us
    all_to_all x1, blocking collectives: 18.6 us -> 23.2 us  [shards(): spread = lax.all_to_all(merged, ('y', 'z'), 0, 0)]
    ppermute x27, waiting for transfers between devices: 34.2 us -> 35.9 us  [send(): return lax.ppermute(value, GROUP, pairs(route))]
    pallas_call x2 -> x3, Pallas kernels: 6.52 us -> 6.46 us  [the longest x1 6.36 us: shards(): pl.pallas_call(logits_kernel, out_shape=[jax.ShapeDtypeStruct((3, half),...]
where the time goes in v10:
time: 124 us; the launch traced here: 123 us
  starting transfers between devices  39.5 us (32%)
  waiting for transfers between devices  35.9 us (29%)
  blocking collectives  23.2 us (19%)
  Pallas kernels  19.6 us (16%)
  other arithmetic  2.42 us (2%)
    ppermute x27, starting transfers between devices, send(): return lax.ppermute(value, GROUP, pairs(route))  39.5 us
    ppermute x27, waiting for transfers between devices, send(): return lax.ppermute(value, GROUP, pairs(route))  35.9 us
    all_to_all x1, blocking collectives, shards(): spread = lax.all_to_all(merged, ('y', 'z'), 0, 0)  23.2 us
    pallas_call x1, Pallas kernels, shards(): pl.pallas_call(target_kernel, out_shape=[pltpu.HBM((half, DEPTH), BF)] *...  6.76 us
    pallas_call x3, Pallas kernels, combine(): pl.pallas_call(functools.partial(kernel, parts), out_shape=scales + [jax....  6.42 us
    pallas_call x1, Pallas kernels, shards(): pl.pallas_call(logits_kernel, out_shape=[jax.ShapeDtypeStruct((3, half),...  6.36 us
  transfers between devices with their start and end apart: 27, of which 17 were waited for; matrix products, arithmetic and copies ran while one was open for 1% of the time, Pallas kernels for 9%

profile of v10, /device:TPU:4, one launch (start us, length us, event | category | flops | bytes accessed | tf_op | source)
XLA Modules:
  0.0 122.5 jit_solution(13861241060665119709)
XLA Ops:
  0.6 7.3 %collective-permute-start.1 = (bf16[2,8192]{1,0:T(2,128)(2,1)}, bf16[2,8192]{1,0:T(2,128)(2,1)S(1)}, u32[]{:S(2)}, u32[]{:S(2)}) collective-permute-start(bf16[2,8192]{1,0:T(2,128)(2,1)} %param.4), channel_id=1, source_target_pairs={{0,8},{2,10},{4,12},{6,14},{8,0},{10,2},{12,4},{14,6},{16,24},{18,... | collective-permute-start | bytes 98312 | tf_op jit(solution)/shard_map/ppermute | solution.py:63
  7.9 1.2 collective-permute-start
  9.1 0.4 collective-permute-start.2
  9.5 0.5 collective-permute-done.1
  10.0 2.0 %collective-permute-done = bf16[2,8192]{1,0:T(2,128)(2,1)S(1)} collective-permute-done((bf16[2,8192]{1,0:T(2,128)(2,1)}, bf16[2,8192]{1,0:T(2,128)(2,1)S(1)}, u32[]{:S(2)}, u32[]{:S(2)}) %collective-permute-start) | collective-permute-done | bytes 32800 | tf_op jit(solution)/shard_map/ppermute | solution.py:63
  12.0 6.0 %collective-permute-done.2 = bf16[2,8192]{1,0:T(2,128)(2,1)S(1)} collective-permute-done((bf16[2,8192]{1,0:T(2,128)(2,1)}, bf16[2,8192]{1,0:T(2,128)(2,1)S(1)}, u32[]{:S(2)}, u32[]{:S(2)}) %collective-permute-start.2) | collective-permute-done | bytes 32800 | tf_op jit(solution)/shard_map/ppermute | solution.py:63
  18.0 0.9 pad_maximum_fusion.a_ref
  18.9 0.1 collective-permute-start.5
  19.0 1.6 %collective-permute-start.4 = (bf16[8,8192]{1,0:T(8,128)(2,1)S(1)}, bf16[8,8192]{1,0:T(8,128)(2,1)S(1)}, u32[]{:S(2)}, u32[]{:S(2)}) collective-permute-start(bf16[8,8192]{1,0:T(8,128)(2,1)S(1)} %pad_maximum_fusion.a_ref), channel_id=1, source_target_pairs={{0,2},{2,4},{4,6},{6,8},{8,10},{10,12},{12,14},{14,0},{16,80},{18,... | collective-permute-start | bytes 393224 | tf_op jit(solution)/shard_map/ppermute | solution.py:63
  20.6 1.8 %collective-permute-start.3 = (bf16[8,8192]{1,0:T(8,128)(2,1)S(1)}, bf16[8,8192]{1,0:T(8,128)(2,1)S(1)}, u32[]{:S(2)}, u32[]{:S(2)}) collective-permute-start(bf16[8,8192]{1,0:T(8,128)(2,1)S(1)} %pad_maximum_fusion.a_ref), channel_id=1, source_target_pairs={{0,14},{2,0},{4,2},{6,4},{8,6},{10,8},{12,10},{14,12},{16,208},{18... | collective-permute-start | bytes 393224 | tf_op jit(solution)/shard_map/ppermute | solution.py:63
  22.4 4.0 %collective-permute-done.5.d_ref = bf16[8,8192]{1,0:T(8,128)(2,1)S(1)} collective-permute-done((bf16[8,8192]{1,0:T(8,128)(2,1)S(1)}, bf16[8,8192]{1,0:T(8,128)(2,1)S(1)}, u32[]{:S(2)}, u32[]{:S(2)}) %collective-permute-start.5) | collective-permute-done | bytes 131104 | tf_op jit(solution)/shard_map/ppermute | solution.py:63
  26.4 0.0 collective-permute-done.3.b_ref
  26.4 0.1 join.1.p0
  26.5 3.3 %collective-permute-start.8 = (bf16[32,8192]{1,0:T(8,128)(2,1)S(1)}, bf16[32,8192]{1,0:T(8,128)(2,1)S(1)}, u32[]{:S(2)}, u32[]{:S(2)}) collective-permute-start(bf16[32,8192]{1,0:T(8,128)(2,1)S(1)} %join.1.p0), channel_id=1, source_target_pairs={{0,128},{2,130},{4,132},{6,134},{8,136},{10,138},{12,140},{14,142}... | collective-permute-start | bytes 1572872 | tf_op jit(solution)/shard_map/ppermute | solution.py:63
  29.8 0.7 collective-permute-start.7
  30.4 2.6 %collective-permute-start.6 = (bf16[32,8192]{1,0:T(8,128)(2,1)S(1)}, bf16[32,8192]{1,0:T(8,128)(2,1)S(1)}, u32[]{:S(2)}, u32[]{:S(2)}) collective-permute-start(bf16[32,8192]{1,0:T(8,128)(2,1)S(1)} %join.1.p0), channel_id=1, source_target_pairs={{0,192},{2,194},{4,196},{6,198},{8,200},{10,202},{12,204},{14,206}... | collective-permute-start | bytes 1572872 | tf_op jit(solution)/shard_map/ppermute | solution.py:63
  33.0 0.1 stack.23.at_ref
  33.1 0.7 copy-done.1
  33.8 6.8 %target.1 = (bf16[128,8192]{1,0:T(8,128)(2,1)}, bf16[128,8192]{1,0:T(8,128)(2,1)}) custom-call(s32[5]{0:T(128)S(1)} %stack.23.at_ref, s32[1,256]{1,0:T(1,128)S(1)} %bitcast.7, bf16[8192,512]{1,0:T(8,128)(2,1)} %w_ref.1), custom_call_target="tpu_custom_call" | custom-call | flops 2147483648 | bytes 12582912 | tf_op jit(solution)/shard_map/target/pallas_call | solution.py:249
  40.6 0.0 copy-start.2
  40.6 0.1 collective-permute-start.9
  40.7 0.0 collective-permute-done.8.p3
  40.7 0.5 collective-permute-start.12
  41.2 1.7 %collective-permute-done.7.p2 = bf16[32,8192]{1,0:T(8,128)(2,1)S(1)} collective-permute-done((bf16[32,8192]{1,0:T(8,128)(2,1)S(1)}, bf16[32,8192]{1,0:T(8,128)(2,1)S(1)}, u32[]{:S(2)}, u32[]{:S(2)}) %collective-permute-start.7) | collective-permute-done | bytes 524320 | tf_op jit(solution)/shard_map/ppermute | solution.py:63
  42.9 0.0 collective-permute-start.11
  42.9 0.4 collective-permute-done.6.p1
  43.3 1.1 collective-permute-start.10
  44.4 0.0 collective-permute-done.9.p4
  44.4 0.4 collective-permute-done.11.p6
  44.8 1.2 collective-permute-done.10.p5
  46.0 6.4 %logits.1 = (f32[3,128]{1,0:T(4,128)S(1)}, f32[3,128]{1,0:T(4,128)S(1)}, f32[128,8192]{1,0:T(8,128)}, bf16[128,8192]{1,0:T(8,128)(2,1)}) custom-call(s32[5]{0:T(128)S(1)} %stack.23.at_ref, s32[1,256]{1,0:T(1,128)S(1)} %bitcast.8, bf16[32,8192]{1,0:T(8,128)(2,1)S(1)} %join.1.p0, bf16[32,8192]{1,0:T(8,128)(2,1)S(1)} %collective-permute-done.6.p1, ...), custom_call_target="tpu_custom_call" | custom-call | flops 4294967296 | bytes 19922944 | tf_op jit(solution)/shard_map/logits/pallas_call | solution.py:262
  52.3 0.9 collective-permute-start.15
  53.2 0.2 collective-permute-start.13
  53.4 1.2 collective-permute-start.14
  54.6 0.9 collective-permute-done.15.both_ref
  55.4 0.0 collective-permute-done.13.core_ref
  55.4 1.5 %collective-permute-done.14.x_ref = f32[3,128]{1,0:T(4,128)S(1)} collective-permute-done((f32[3,128]{1,0:T(4,128)S(1)}, f32[3,128]{1,0:T(4,128)S(1)}, u32[]{:S(2)}, u32[]{:S(2)}) %collective-permute-start.14) | collective-permute-done | bytes 1568 | tf_op jit(solution)/shard_map/ppermute | solution.py:63
  57.0 0.1 collective-permute-start.16
  57.1 0.5 collective-permute-start.17
  57.6 23.2 %all_to_all.5.spread_ref = f32[32,3,128]{2,1,0:T(4,128)S(1)} all-to-all(f32[32,3,128]{2,1,0:T(4,128)S(1)} %merge.1), channel_id=1, replica_groups=mesh['y'=4,'x'=2,'c'=2,'z'=8,'dp'=2] {'y','z'}, dimensions={0} | all-to-all | bytes 98304 | tf_op jit(solution)/shard_map/all_to_all | solution.py:283
  80.8 2.3 %combine.3 = (f32[128,128]{1,0:T(8,128)S(1)}, bf16[32,8192]{1,0:T(8,128)(2,1)S(1)}) custom-call(s32[5]{0:T(128)S(1)} %stack.23.at_ref, f32[1,256]{1,0:T(1,128)S(1)} %bitcast.9, f32[3,128]{1,0:T(4,128)S(1)} %get-tuple-element.22.own_ref, f32[3,128]{1,0:T(4,128)S(1)} %collective-permute-done.13.core_ref, f32[32,3,128]{2,1,0:T(4,128)S(1)} %all_to_all.5.spread_ref, ...), custom_call_target="tpu_custom_call" | custom-call | flops 1572864 | bytes 3145728 | tf_op jit(solution)/shard_map/combine/pallas_call | solution.py:292
  83.1 1.4 %collective-permute-start.18 = (bf16[32,8192]{1,0:T(8,128)(2,1)S(1)}, bf16[32,8192]{1,0:T(8,128)(2,1)S(1)}, u32[]{:S(2)}, u32[]{:S(2)}) collective-permute-start(bf16[32,8192]{1,0:T(8,128)(2,1)S(1)} %get-tuple-element.32), channel_id=1, source_target_pairs={{0,128},{2,130},{4,132},{6,134},{8,136},{10,138},{12,140},{14,142}... | collective-permute-start | bytes 1572872 | tf_op jit(solution)/shard_map/ppermute | solution.py:63
  84.5 2.3 %combine.5 = (bf16[32,8192]{1,0:T(8,128)(2,1)S(1)}, bf16[32,8192]{1,0:T(8,128)(2,1)S(1)}) custom-call(f32[128,128]{1,0:T(8,128)S(1)} %get-tuple-element.31.scales_ref, f32[128,8192]{1,0:T(8,128)} %get-tuple-element.27.refs_0_, bf16[128,8192]{1,0:T(8,128)(2,1)S(1)} %collective-permute-done.16.refs_1_, bf16[128,8192]{1,0:T(8,128)(2,1)} %get-tuple-element.29.refs_2_, ...), custom_call_target="tpu_custom_call" | custom-call | flops 3145728 | bytes 6291456 | tf_op jit(solution)/shard_map/combine/pallas_call | solution.py:292
  86.8 0.8 collective-permute-start.19
  87.6 2.5 %collective-permute-start.20 = (bf16[32,8192]{1,0:T(8,128)(2,1)S(1)}, bf16[32,8192]{1,0:T(8,128)(2,1)S(1)}, u32[]{:S(2)}, u32[]{:S(2)}) collective-permute-start(bf16[32,8192]{1,0:T(8,128)(2,1)S(1)} %get-tuple-element.34), channel_id=1, source_target_pairs={{0,192},{2,194},{4,196},{6,198},{8,200},{10,202},{12,204},{14,206}... | collective-permute-start | bytes 1572872 | tf_op jit(solution)/shard_map/ppermute | solution.py:63
  90.1 1.8 %combine.4 = f32[32,8192]{1,0:T(8,128)S(1)} custom-call(f32[128,128]{1,0:T(8,128)S(1)} %get-tuple-element.31.scales_ref, f32[128,8192]{1,0:T(8,128)} %get-tuple-element.27.refs_0_, bf16[128,8192]{1,0:T(8,128)(2,1)S(1)} %collective-permute-done.16.refs_1_, bf16[128,8192]{1,0:T(8,128)(2,1)} %get-tuple-element.29.refs_2_, ...), custom_call_target="tpu_custom_call" | custom-call | flops 1572864 | bytes 3145728 | tf_op jit(solution)/shard_map/combine/pallas_call | solution.py:292
  91.9 2.0 %collective-permute-done.18 = bf16[32,8192]{1,0:T(8,128)(2,1)S(1)} collective-permute-done((bf16[32,8192]{1,0:T(8,128)(2,1)S(1)}, bf16[32,8192]{1,0:T(8,128)(2,1)S(1)}, u32[]{:S(2)}, u32[]{:S(2)}) %collective-permute-start.18) | collective-permute-done | bytes 524320 | tf_op jit(solution)/shard_map/ppermute | solution.py:63
  94.0 5.5 %collective-permute-done.19 = bf16[32,8192]{1,0:T(8,128)(2,1)S(1)} collective-permute-done((bf16[32,8192]{1,0:T(8,128)(2,1)S(1)}, bf16[32,8192]{1,0:T(8,128)(2,1)S(1)}, u32[]{:S(2)}, u32[]{:S(2)}) %collective-permute-start.19) | collective-permute-done | bytes 524320 | tf_op jit(solution)/shard_map/ppermute | solution.py:63
  99.5 0.3 fusion.3
  99.8 1.3 %collective-permute-start.21 = (bf16[8,8192]{1,0:T(8,128)(2,1)S(1)}, bf16[8,8192]{1,0:T(8,128)(2,1)S(1)}, u32[]{:S(2)}, u32[]{:S(2)}) collective-permute-start(bf16[8,8192]{1,0:T(8,128)(2,1)S(1)} %get-tuple-element.41), channel_id=1, source_target_pairs={{0,4},{2,6},{4,8},{6,10},{8,12},{10,14},{12,0},{14,2},{16,144},{18... | collective-permute-start | bytes 393224 | tf_op jit(solution)/shard_map/ppermute | solution.py:63
  101.1 2.6 %collective-permute-start.23 = (bf16[8,8192]{1,0:T(8,128)(2,1)S(1)}, bf16[8,8192]{1,0:T(8,128)(2,1)S(1)}, u32[]{:S(2)}, u32[]{:S(2)}) collective-permute-start(bf16[8,8192]{1,0:T(8,128)(2,1)S(1)} %get-tuple-element.42), channel_id=1, source_target_pairs={{0,14},{2,0},{4,2},{6,4},{8,6},{10,8},{12,10},{14,12},{16,208},{18... | collective-permute-start | bytes 393224 | tf_op jit(solution)/shard_map/ppermute | solution.py:63
  103.7 0.2 slice_reduce_fusion
  103.9 4.1 %collective-permute-done.21 = bf16[8,8192]{1,0:T(8,128)(2,1)S(1)} collective-permute-done((bf16[8,8192]{1,0:T(8,128)(2,1)S(1)}, bf16[8,8192]{1,0:T(8,128)(2,1)S(1)}, u32[]{:S(2)}, u32[]{:S(2)}) %collective-permute-start.21) | collective-permute-done | bytes 131104 | tf_op jit(solution)/shard_map/ppermute | solution.py:63
  108.0 1.8 %collective-permute-done.22 = bf16[8,8192]{1,0:T(8,128)(2,1)S(1)} collective-permute-done((bf16[8,8192]{1,0:T(8,128)(2,1)S(1)}, bf16[8,8192]{1,0:T(8,128)(2,1)S(1)}, u32[]{:S(2)}, u32[]{:S(2)}) %collective-permute-start.22) | collective-permute-done | bytes 131104 | tf_op jit(solution)/shard_map/ppermute | solution.py:63
  109.8 0.1 fusion.2
  109.9 0.1 fusion.5
  110.0 1.4 %collective-permute-start.25 = (bf16[2,8192]{1,0:T(2,128)(2,1)S(1)}, bf16[2,8192]{1,0:T(2,128)(2,1)S(1)}, u32[]{:S(2)}, u32[]{:S(2)}) collective-permute-start(bf16[2,8192]{1,0:T(2,128)(2,1)S(1)} %get-tuple-element.44), channel_id=1, source_target_pairs={{0,8},{2,10},{4,12},{6,14},{8,0},{10,2},{12,4},{14,6},{16,24},{18,... | collective-permute-start | bytes 98312 | tf_op jit(solution)/shard_map/ppermute | solution.py:63
  111.4 5.2 %collective-permute-start.26 = (bf16[2,8192]{1,0:T(2,128)(2,1)S(1)}, bf16[2,8192]{1,0:T(2,128)(2,1)S(1)}, u32[]{:S(2)}, u32[]{:S(2)}) collective-permute-start(bf16[2,8192]{1,0:T(2,128)(2,1)S(1)} %get-tuple-element.45), channel_id=1, source_target_pairs={{0,40},{2,42},{4,44},{6,46},{8,32},{10,34},{12,36},{14,38},{16,56}... | collective-permute-start | bytes 98312 | tf_op jit(solution)/shard_map/ppermute | solution.py:63
  116.7 0.9 collective-permute-start.24
  117.6 0.5 multiply_multiply_fusion
  118.1 0.2 collective-permute-done.25
  118.3 1.9 %collective-permute-done.26 = bf16[2,8192]{1,0:T(2,128)(2,1)S(1)} collective-permute-done((bf16[2,8192]{1,0:T(2,128)(2,1)S(1)}, bf16[2,8192]{1,0:T(2,128)(2,1)S(1)}, u32[]{:S(2)}, u32[]{:S(2)}) %collective-permute-start.26) | collective-permute-done | bytes 32800 | tf_op jit(solution)/shard_map/ppermute | solution.py:63
  120.2 1.7 %collective-permute-done.24 = f32[2,8192]{1,0:T(2,128)S(1)} collective-permute-done((f32[2,8192]{1,0:T(2,128)S(1)}, f32[2,8192]{1,0:T(2,128)S(1)}, u32[]{:S(2)}, u32[]{:S(2)}) %collective-permute-start.24) | collective-permute-done | bytes 65568 | tf_op jit(solution)/shard_map/ppermute | solution.py:63
  121.9 0.7 fusion.1
  (16 shorter events, 0.1 us)
Async XLA Ops:
  0.6 9.4 %collective-permute-start.1 = (bf16[2,8192]{1,0:T(2,128)(2,1)}, bf16[2,8192]{1,0:T(2,128)(2,1)S(1)}, u32[]{:S(2)}, u32[]{:S(2)}) collective-permute-start(bf16[2,8192]{1,0:T(2,128)(2,1)} %param.4), channel_id=1, source_target_pairs={{0,8},{2,10},{4,12},{6,14},{8,0},{10,2},{12,4},{14,6},{16,24},{18,... | collective-permute-start | bytes 98312 | tf_op jit(solution)/shard_map/ppermute | solution.py:63
  7.9 4.1 %collective-permute-start = (bf16[2,8192]{1,0:T(2,128)(2,1)}, bf16[2,8192]{1,0:T(2,128)(2,1)S(1)}, u32[]{:S(2)}, u32[]{:S(2)}) collective-permute-start(bf16[2,8192]{1,0:T(2,128)(2,1)} %param.4), channel_id=1, source_target_pairs={{0,32},{2,34},{4,36},{6,38},{8,40},{10,42},{12,44},{14,46},{16,48}... | collective-permute-start | bytes 98312 | tf_op jit(solution)/shard_map/ppermute | solution.py:63
  9.1 8.9 %collective-permute-start.2 = (bf16[2,8192]{1,0:T(2,128)(2,1)}, bf16[2,8192]{1,0:T(2,128)(2,1)S(1)}, u32[]{:S(2)}, u32[]{:S(2)}) collective-permute-start(bf16[2,8192]{1,0:T(2,128)(2,1)} %param.4), channel_id=1, source_target_pairs={{0,40},{2,42},{4,44},{6,46},{8,32},{10,34},{12,36},{14,38},{16,56}... | collective-permute-start | bytes 98312 | tf_op jit(solution)/shard_map/ppermute | solution.py:63
  18.9 7.5 %collective-permute-start.5 = (bf16[8,8192]{1,0:T(8,128)(2,1)S(1)}, bf16[8,8192]{1,0:T(8,128)(2,1)S(1)}, u32[]{:S(2)}, u32[]{:S(2)}) collective-permute-start(bf16[8,8192]{1,0:T(8,128)(2,1)S(1)} %pad_maximum_fusion.a_ref), channel_id=1, source_target_pairs={{0,12},{2,14},{4,0},{6,2},{8,4},{10,6},{12,8},{14,10},{16,144},{18... | collective-permute-start | bytes 393224 | tf_op jit(solution)/shard_map/ppermute | solution.py:63
  19.0 7.4 %collective-permute-start.4 = (bf16[8,8192]{1,0:T(8,128)(2,1)S(1)}, bf16[8,8192]{1,0:T(8,128)(2,1)S(1)}, u32[]{:S(2)}, u32[]{:S(2)}) collective-permute-start(bf16[8,8192]{1,0:T(8,128)(2,1)S(1)} %pad_maximum_fusion.a_ref), channel_id=1, source_target_pairs={{0,2},{2,4},{4,6},{6,8},{8,10},{10,12},{12,14},{14,0},{16,80},{18,... | collective-permute-start | bytes 393224 | tf_op jit(solution)/shard_map/ppermute | solution.py:63
  20.6 5.8 %collective-permute-start.3 = (bf16[8,8192]{1,0:T(8,128)(2,1)S(1)}, bf16[8,8192]{1,0:T(8,128)(2,1)S(1)}, u32[]{:S(2)}, u32[]{:S(2)}) collective-permute-start(bf16[8,8192]{1,0:T(8,128)(2,1)S(1)} %pad_maximum_fusion.a_ref), channel_id=1, source_target_pairs={{0,14},{2,0},{4,2},{6,4},{8,6},{10,8},{12,10},{14,12},{16,208},{18... | collective-permute-start | bytes 393224 | tf_op jit(solution)/shard_map/ppermute | solution.py:63
  26.5 14.2 %collective-permute-start.8 = (bf16[32,8192]{1,0:T(8,128)(2,1)S(1)}, bf16[32,8192]{1,0:T(8,128)(2,1)S(1)}, u32[]{:S(2)}, u32[]{:S(2)}) collective-permute-start(bf16[32,8192]{1,0:T(8,128)(2,1)S(1)} %join.1.p0), channel_id=1, source_target_pairs={{0,128},{2,130},{4,132},{6,134},{8,136},{10,138},{12,140},{14,142}... | collective-permute-start | bytes 1572872 | tf_op jit(solution)/shard_map/ppermute | solution.py:63
  29.8 13.1 %collective-permute-start.7 = (bf16[32,8192]{1,0:T(8,128)(2,1)S(1)}, bf16[32,8192]{1,0:T(8,128)(2,1)S(1)}, u32[]{:S(2)}, u32[]{:S(2)}) collective-permute-start(bf16[32,8192]{1,0:T(8,128)(2,1)S(1)} %join.1.p0), channel_id=1, source_target_pairs={{0,64},{2,66},{4,68},{6,70},{8,72},{10,74},{12,76},{14,78},{16,18}... | collective-permute-start | bytes 1572872 | tf_op jit(solution)/shard_map/ppermute | solution.py:63
  30.4 12.8 %collective-permute-start.6 = (bf16[32,8192]{1,0:T(8,128)(2,1)S(1)}, bf16[32,8192]{1,0:T(8,128)(2,1)S(1)}, u32[]{:S(2)}, u32[]{:S(2)}) collective-permute-start(bf16[32,8192]{1,0:T(8,128)(2,1)S(1)} %join.1.p0), channel_id=1, source_target_pairs={{0,192},{2,194},{4,196},{6,198},{8,200},{10,202},{12,204},{14,206}... | collective-permute-start | bytes 1572872 | tf_op jit(solution)/shard_map/ppermute | solution.py:63
  33.1 0.7 copy-start.1
  33.8 12.2 %copy-start = (bf16[8192,512]{1,0:T(8,128)(2,1)S(1)}, bf16[8192,512]{1,0:T(8,128)(2,1)}, u32[]{:S(2)}) copy-start(bf16[8192,512]{1,0:T(8,128)(2,1)} %w_ref.1) | copy-start | bytes 25165828
  40.5 16.6 %copy-start.3 = (bf16[128,8192]{1,0:T(8,128)(2,1)S(1)}, bf16[128,8192]{1,0:T(8,128)(2,1)}, u32[]{:S(2)}) copy-start(bf16[128,8192]{1,0:T(8,128)(2,1)} %get-tuple-element.30) | copy-start | bytes 6291460
  40.6 40.2 %copy-start.2 = (f32[256]{0:T(256)S(1)}, f32[256]{0:T(256)}, u32[]{:S(2)}) copy-start(f32[256]{0:T(256)} %param.7) | copy-start | bytes 3076
  40.6 3.8 %collective-permute-start.9 = (bf16[32,8192]{1,0:T(8,128)(2,1)S(1)}, bf16[32,8192]{1,0:T(8,128)(2,1)S(1)}, u32[]{:S(2)}, u32[]{:S(2)}) collective-permute-start(bf16[32,8192]{1,0:T(8,128)(2,1)S(1)} %join.1.p0), channel_id=1, source_target_pairs={{0,16},{2,18},{4,20},{6,22},{8,24},{10,26},{12,28},{14,30},{16,0},... | collective-permute-start | bytes 1572872 | tf_op jit(solution)/shard_map/ppermute | solution.py:63
  40.7 3.7 %collective-permute-start.12 = (bf16[32,8192]{1,0:T(8,128)(2,1)S(1)}, bf16[32,8192]{1,0:T(8,128)(2,1)S(1)}, u32[]{:S(2)}, u32[]{:S(2)}) collective-permute-start(bf16[32,8192]{1,0:T(8,128)(2,1)S(1)} %collective-permute-done.8.p3), channel_id=1, source_target_pairs={{0,16},{2,18},{4,20},{6,22},{8,24},{10,26},{12,28},{14,30},{16,0},... | collective-permute-start | bytes 1572872 | tf_op jit(solution)/shard_map/ppermute | solution.py:63
  42.9 1.9 %collective-permute-start.11 = (bf16[32,8192]{1,0:T(8,128)(2,1)S(1)}, bf16[32,8192]{1,0:T(8,128)(2,1)S(1)}, u32[]{:S(2)}, u32[]{:S(2)}) collective-permute-start(bf16[32,8192]{1,0:T(8,128)(2,1)S(1)} %collective-permute-done.7.p2), channel_id=1, source_target_pairs={{0,16},{2,18},{4,20},{6,22},{8,24},{10,26},{12,28},{14,30},{16,0},... | collective-permute-start | bytes 1572872 | tf_op jit(solution)/shard_map/ppermute | solution.py:63
  43.3 2.7 %collective-permute-start.10 = (bf16[32,8192]{1,0:T(8,128)(2,1)S(1)}, bf16[32,8192]{1,0:T(8,128)(2,1)S(1)}, u32[]{:S(2)}, u32[]{:S(2)}) collective-permute-start(bf16[32,8192]{1,0:T(8,128)(2,1)S(1)} %collective-permute-done.6.p1), channel_id=1, source_target_pairs={{0,16},{2,18},{4,20},{6,22},{8,24},{10,26},{12,28},{14,30},{16,0},... | collective-permute-start | bytes 1572872 | tf_op jit(solution)/shard_map/ppermute | solution.py:63
  52.3 3.1 %collective-permute-start.15 = (f32[3,128]{1,0:T(4,128)S(1)}, f32[3,128]{1,0:T(4,128)S(1)}, u32[]{:S(2)}, u32[]{:S(2)}) collective-permute-start(f32[3,128]{1,0:T(4,128)S(1)} %get-tuple-element.23), channel_id=1, source_target_pairs={{0,48},{2,50},{4,52},{6,54},{8,56},{10,58},{12,60},{14,62},{16,32}... | collective-permute-start | bytes 4616 | tf_op jit(solution)/shard_map/ppermute | solution.py:63
  53.2 2.2 %collective-permute-start.13 = (f32[3,128]{1,0:T(4,128)S(1)}, f32[3,128]{1,0:T(4,128)S(1)}, u32[]{:S(2)}, u32[]{:S(2)}) collective-permute-start(f32[3,128]{1,0:T(4,128)S(1)} %get-tuple-element.23), channel_id=1, source_target_pairs={{0,16},{2,18},{4,20},{6,22},{8,24},{10,26},{12,28},{14,30},{16,0},... | collective-permute-start | bytes 4616 | tf_op jit(solution)/shard_map/ppermute | solution.py:63
  53.4 3.6 %collective-permute-start.14 = (f32[3,128]{1,0:T(4,128)S(1)}, f32[3,128]{1,0:T(4,128)S(1)}, u32[]{:S(2)}, u32[]{:S(2)}) collective-permute-start(f32[3,128]{1,0:T(4,128)S(1)} %get-tuple-element.22.own_ref), channel_id=1, source_target_pairs={{0,32},{2,34},{4,36},{6,38},{8,40},{10,42},{12,44},{14,46},{16,48}... | collective-permute-start | bytes 4616 | tf_op jit(solution)/shard_map/ppermute | solution.py:63
  57.0 23.8 %collective-permute-start.16 = (bf16[128,8192]{1,0:T(8,128)(2,1)}, bf16[128,8192]{1,0:T(8,128)(2,1)S(1)}, u32[]{:S(2)}, u32[]{:S(2)}) collective-permute-start(bf16[128,8192]{1,0:T(8,128)(2,1)} %get-tuple-element.28), channel_id=1, source_target_pairs={{0,16},{2,18},{4,20},{6,22},{8,24},{10,26},{12,28},{14,30},{16,0},... | collective-permute-start | bytes 6291464 | tf_op jit(solution)/shard_map/ppermute | solution.py:63
  57.1 23.7 %collective-permute-start.17 = (bf16[128,8192]{1,0:T(8,128)(2,1)S(1)}, bf16[128,8192]{1,0:T(8,128)(2,1)S(1)}, u32[]{:S(2)}, u32[]{:S(2)}) collective-permute-start(bf16[128,8192]{1,0:T(8,128)(2,1)S(1)} %copy-done.3), channel_id=1, source_target_pairs={{0,16},{2,18},{4,20},{6,22},{8,24},{10,26},{12,28},{14,30},{16,0},... | collective-permute-start | bytes 6291464 | tf_op jit(solution)/shard_map/ppermute | solution.py:63
  83.1 10.9 %collective-permute-start.18 = (bf16[32,8192]{1,0:T(8,128)(2,1)S(1)}, bf16[32,8192]{1,0:T(8,128)(2,1)S(1)}, u32[]{:S(2)}, u32[]{:S(2)}) collective-permute-start(bf16[32,8192]{1,0:T(8,128)(2,1)S(1)} %get-tuple-element.32), channel_id=1, source_target_pairs={{0,128},{2,130},{4,132},{6,134},{8,136},{10,138},{12,140},{14,142}... | collective-permute-start | bytes 1572872 | tf_op jit(solution)/shard_map/ppermute | solution.py:63
  86.8 12.7 %collective-permute-start.19 = (bf16[32,8192]{1,0:T(8,128)(2,1)S(1)}, bf16[32,8192]{1,0:T(8,128)(2,1)S(1)}, u32[]{:S(2)}, u32[]{:S(2)}) collective-permute-start(bf16[32,8192]{1,0:T(8,128)(2,1)S(1)} %get-tuple-element.33), channel_id=1, source_target_pairs={{0,64},{2,66},{4,68},{6,70},{8,72},{10,74},{12,76},{14,78},{16,18}... | collective-permute-start | bytes 1572872 | tf_op jit(solution)/shard_map/ppermute | solution.py:63
  87.6 11.9 %collective-permute-start.20 = (bf16[32,8192]{1,0:T(8,128)(2,1)S(1)}, bf16[32,8192]{1,0:T(8,128)(2,1)S(1)}, u32[]{:S(2)}, u32[]{:S(2)}) collective-permute-start(bf16[32,8192]{1,0:T(8,128)(2,1)S(1)} %get-tuple-element.34), channel_id=1, source_target_pairs={{0,192},{2,194},{4,196},{6,198},{8,200},{10,202},{12,204},{14,206}... | collective-permute-start | bytes 1572872 | tf_op jit(solution)/shard_map/ppermute | solution.py:63
  99.8 8.2 %collective-permute-start.21 = (bf16[8,8192]{1,0:T(8,128)(2,1)S(1)}, bf16[8,8192]{1,0:T(8,128)(2,1)S(1)}, u32[]{:S(2)}, u32[]{:S(2)}) collective-permute-start(bf16[8,8192]{1,0:T(8,128)(2,1)S(1)} %get-tuple-element.41), channel_id=1, source_target_pairs={{0,4},{2,6},{4,8},{6,10},{8,12},{10,14},{12,0},{14,2},{16,144},{18... | collective-permute-start | bytes 393224 | tf_op jit(solution)/shard_map/ppermute | solution.py:63
  101.1 7.0 %collective-permute-start.23 = (bf16[8,8192]{1,0:T(8,128)(2,1)S(1)}, bf16[8,8192]{1,0:T(8,128)(2,1)S(1)}, u32[]{:S(2)}, u32[]{:S(2)}) collective-permute-start(bf16[8,8192]{1,0:T(8,128)(2,1)S(1)} %get-tuple-element.42), channel_id=1, source_target_pairs={{0,14},{2,0},{4,2},{6,4},{8,6},{10,8},{12,10},{14,12},{16,208},{18... | collective-permute-start | bytes 393224 | tf_op jit(solution)/shard_map/ppermute | solution.py:63
  103.7 6.2 %collective-permute-start.22 = (bf16[8,8192]{1,0:T(8,128)(2,1)S(1)}, bf16[8,8192]{1,0:T(8,128)(2,1)S(1)}, u32[]{:S(2)}, u32[]{:S(2)}) collective-permute-start(bf16[8,8192]{1,0:T(8,128)(2,1)S(1)} %get-tuple-element.43), channel_id=1, source_target_pairs={{0,2},{2,4},{4,6},{6,8},{8,10},{10,12},{12,14},{14,0},{16,80},{18,... | collective-permute-start | bytes 393224 | tf_op jit(solution)/shard_map/ppermute | solution.py:63
  110.0 8.4 %collective-permute-start.25 = (bf16[2,8192]{1,0:T(2,128)(2,1)S(1)}, bf16[2,8192]{1,0:T(2,128)(2,1)S(1)}, u32[]{:S(2)}, u32[]{:S(2)}) collective-permute-start(bf16[2,8192]{1,0:T(2,128)(2,1)S(1)} %get-tuple-element.44), channel_id=1, source_target_pairs={{0,8},{2,10},{4,12},{6,14},{8,0},{10,2},{12,4},{14,6},{16,24},{18,... | collective-permute-start | bytes 98312 | tf_op jit(solution)/shard_map/ppermute | solution.py:63
  111.4 8.8 %collective-permute-start.26 = (bf16[2,8192]{1,0:T(2,128)(2,1)S(1)}, bf16[2,8192]{1,0:T(2,128)(2,1)S(1)}, u32[]{:S(2)}, u32[]{:S(2)}) collective-permute-start(bf16[2,8192]{1,0:T(2,128)(2,1)S(1)} %get-tuple-element.45), channel_id=1, source_target_pairs={{0,40},{2,42},{4,44},{6,46},{8,32},{10,34},{12,36},{14,38},{16,56}... | collective-permute-start | bytes 98312 | tf_op jit(solution)/shard_map/ppermute | solution.py:63
  116.7 5.2 %collective-permute-start.24 = (f32[2,8192]{1,0:T(2,128)S(1)}, f32[2,8192]{1,0:T(2,128)S(1)}, u32[]{:S(2)}, u32[]{:S(2)}) collective-permute-start(f32[2,8192]{1,0:T(2,128)S(1)} %slice.54), channel_id=1, source_target_pairs={{0,32},{2,34},{4,36},{6,38},{8,40},{10,42},{12,44},{14,46},{16,48}... | collective-permute-start | bytes 196616 | tf_op jit(solution)/shard_map/ppermute | solution.py:63

commit v11 on v10

--- a/solution.py
+++ b/solution.py
@@ -222,10 +222,6 @@
     combine_end(parts, combine_start(parts, sources, buffers, sems), scales_ref, buffers, outs)
 
 
-def join_kernel(a_ref, b_ref, c_ref, d_ref, out_ref):
-    out_ref[...] = jnp.concatenate([r[...] for r in (a_ref, b_ref, c_ref, d_ref)], axis=0)
-
-
 def shards(hidden, lm_weight, targets, loss_grad):
     half = ROWS // 2
     at = jnp.stack([lax.axis_index(a) for a in GROUP] + [lax.axis_index(GROUP) * WIDTH])
@@ -235,14 +231,7 @@
     sems = pltpu.SemaphoreType.DMA((STEPS,))
 
     block = jnp.concatenate([hidden] + [send(hidden, to) for to in (to_x, to_z4, to_xz4)])
-    block = pl.pallas_call(
-        join_kernel,
-        out_shape=jax.ShapeDtypeStruct((32, DEPTH), BF),
-        in_specs=[VMEM] * 4,
-        out_specs=VMEM,
-        compiler_params=params(),
-        name="join",
-    )(block, *(send(block, to_first(-o)) for o in OFFSETS[1:]))
+    block = jnp.concatenate([block] + [send(block, to_first(-o)) for o in OFFSETS[1:]])
     near, back, far = (send(block, to_second(-o)) for o in OFFSETS[1:])
 
     aim, _ = lax.optimization_barrier((targets, block))
@@ -312,7 +301,7 @@
     part = part.reshape(4, 8, DEPTH)
     part = part[0] + sum(send(part[k].astype(BF), to_first(OFFSETS[k])).astype(F32) for k in (3, 1, 2))
     part = [part[0:2], send(part[2:4], to_x)] + [
-        send(part[2 * k : 2 * k + 2].astype(BF), to).astype(F32) for k, to in ((2, to_z4), (3, to_xz4))
+        send(part[2 * k : 2 * k + 2].astype(BF), to).astype(F32) for k, to in ((3, to_xz4), (2, to_z4))
     ]
     part = (part[0] + part[1]) + (part[2] + part[3])
     return ce_loss, z_term, part.astype(BF)

time: 124 us -> 119 us (0.960)
  blocking collectives: 23.2 us -> 18 us
  waiting for transfers between devices: 35.9 us -> 33.7 us
    all_to_all x1, blocking collectives: 23.2 us -> 18 us  [shards(): spread = lax.all_to_all(merged, ('y', 'z'), 0, 0)]
    ppermute x27, waiting for transfers between devices: 35.9 us -> 33.7 us  [send(): return lax.ppermute(value, GROUP, pairs(route))]
where the time goes in v11:
time: 119 us; the launch traced here: 117 us
  starting transfers between devices  40.5 us (34%)
  waiting for transfers between devices  33.7 us (28%)
  Pallas kernels  19.6 us (16%)
  blocking collectives  18 us (15%)
  other arithmetic  2.43 us (2%)
  local copies, waits for them, and re-layouts  2.08 us (2%)
    ppermute x27, starting transfers between devices, send(): return lax.ppermute(value, GROUP, pairs(route))  40.5 us
    ppermute x27, waiting for transfers between devices, send(): return lax.ppermute(value, GROUP, pairs(route))  33.7 us
    all_to_all x1, blocking collectives, shards(): spread = lax.all_to_all(merged, ('y', 'z'), 0, 0)  18 us
    pallas_call x1, Pallas kernels, shards(): pl.pallas_call(target_kernel, out_shape=[pltpu.HBM((half, DEPTH), BF)] *...  6.76 us
    pallas_call x3, Pallas kernels, combine(): pl.pallas_call(functools.partial(kernel, parts), out_shape=scales + [jax....  6.42 us
    pallas_call x1, Pallas kernels, shards(): pl.pallas_call(logits_kernel, out_shape=[jax.ShapeDtypeStruct((3, half),...  6.36 us
  transfers between devices with their start and end apart: 27, of which 17 were waited for; matrix products, arithmetic and copies ran while one was open for 1% of the time, Pallas kernels for 9%

profile of v11, /device:TPU:4, one launch (start us, length us, event | category | flops | bytes accessed | tf_op | source)
XLA Modules:
  0.0 117.1 jit_solution(6328079696337342547)
XLA Ops:
  0.6 7.9 %collective-permute-start.2 = (bf16[2,8192]{1,0:T(2,128)(2,1)}, bf16[2,8192]{1,0:T(2,128)(2,1)S(1)}, u32[]{:S(2)}, u32[]{:S(2)}) collective-permute-start(bf16[2,8192]{1,0:T(2,128)(2,1)} %param.4), channel_id=1, source_target_pairs={{0,40},{2,42},{4,44},{6,46},{8,32},{10,34},{12,36},{14,38},{16,56}... | collective-permute-start | bytes 98312 | tf_op jit(solution)/shard_map/ppermute | solution.py:63
  8.5 0.0 collective-permute-start.1
  8.5 0.8 collective-permute-start
  9.4 1.4 %collective-permute-done.2 = bf16[2,8192]{1,0:T(2,128)(2,1)S(1)} collective-permute-done((bf16[2,8192]{1,0:T(2,128)(2,1)}, bf16[2,8192]{1,0:T(2,128)(2,1)S(1)}, u32[]{:S(2)}, u32[]{:S(2)}) %collective-permute-start.2) | collective-permute-done | bytes 32800 | tf_op jit(solution)/shard_map/ppermute | solution.py:63
  10.7 6.1 %collective-permute-done.1 = bf16[2,8192]{1,0:T(2,128)(2,1)S(1)} collective-permute-done((bf16[2,8192]{1,0:T(2,128)(2,1)}, bf16[2,8192]{1,0:T(2,128)(2,1)S(1)}, u32[]{:S(2)}, u32[]{:S(2)}) %collective-permute-start.1) | collective-permute-done | bytes 32800 | tf_op jit(solution)/shard_map/ppermute | solution.py:63
  16.8 0.0 collective-permute-done
  16.8 0.9 pad_maximum_fusion
  17.8 0.9 collective-permute-start.5
  18.7 1.0 collective-permute-start.4
  19.7 2.2 %collective-permute-start.3 = (bf16[8,8192]{1,0:T(8,128)(2,1)S(1)}, bf16[8,8192]{1,0:T(8,128)(2,1)S(1)}, u32[]{:S(2)}, u32[]{:S(2)}) collective-permute-start(bf16[8,8192]{1,0:T(8,128)(2,1)S(1)} %pad_maximum_fusion), channel_id=1, source_target_pairs={{0,14},{2,0},{4,2},{6,4},{8,6},{10,8},{12,10},{14,12},{16,208},{18... | collective-permute-start | bytes 393224 | tf_op jit(solution)/shard_map/ppermute | solution.py:63
  21.9 3.3 %collective-permute-done.5 = bf16[8,8192]{1,0:T(8,128)(2,1)S(1)} collective-permute-done((bf16[8,8192]{1,0:T(8,128)(2,1)S(1)}, bf16[8,8192]{1,0:T(8,128)(2,1)S(1)}, u32[]{:S(2)}, u32[]{:S(2)}) %collective-permute-start.5) | collective-permute-done | bytes 131104 | tf_op jit(solution)/shard_map/ppermute | solution.py:63
  25.2 0.0 collective-permute-done.4
  25.2 0.6 collective-permute-done.3
  25.8 1.0 concatenate.8.p0
  26.8 3.3 %collective-permute-start.8 = (bf16[32,8192]{1,0:T(8,128)(2,1)S(1)}, bf16[32,8192]{1,0:T(8,128)(2,1)S(1)}, u32[]{:S(2)}, u32[]{:S(2)}) collective-permute-start(bf16[32,8192]{1,0:T(8,128)(2,1)S(1)} %concatenate.8.p0), channel_id=1, source_target_pairs={{0,128},{2,130},{4,132},{6,134},{8,136},{10,138},{12,140},{14,142}... | collective-permute-start | bytes 1572872 | tf_op jit(solution)/shard_map/ppermute | solution.py:63
  30.0 0.7 collective-permute-start.7
  30.7 2.6 %collective-permute-start.6 = (bf16[32,8192]{1,0:T(8,128)(2,1)S(1)}, bf16[32,8192]{1,0:T(8,128)(2,1)S(1)}, u32[]{:S(2)}, u32[]{:S(2)}) collective-permute-start(bf16[32,8192]{1,0:T(8,128)(2,1)S(1)} %concatenate.8.p0), channel_id=1, source_target_pairs={{0,192},{2,194},{4,196},{6,198},{8,200},{10,202},{12,204},{14,206}... | collective-permute-start | bytes 1572872 | tf_op jit(solution)/shard_map/ppermute | solution.py:63
  33.3 0.1 stack.23.at_ref
  33.4 0.7 copy-done.1
  34.0 6.8 %target.1 = (bf16[128,8192]{1,0:T(8,128)(2,1)}, bf16[128,8192]{1,0:T(8,128)(2,1)}) custom-call(s32[5]{0:T(128)S(1)} %stack.23.at_ref, s32[1,256]{1,0:T(1,128)S(1)} %bitcast.7, bf16[8192,512]{1,0:T(8,128)(2,1)} %w_ref.1), custom_call_target="tpu_custom_call" | custom-call | flops 2147483648 | bytes 12582912 | tf_op jit(solution)/shard_map/target/pallas_call | solution.py:238
  40.8 0.0 copy-start.2
  40.8 0.1 collective-permute-start.9
  40.9 0.0 collective-permute-done.8.p3
  41.0 0.5 collective-permute-start.12
  41.4 1.7 %collective-permute-done.7.p2 = bf16[32,8192]{1,0:T(8,128)(2,1)S(1)} collective-permute-done((bf16[32,8192]{1,0:T(8,128)(2,1)S(1)}, bf16[32,8192]{1,0:T(8,128)(2,1)S(1)}, u32[]{:S(2)}, u32[]{:S(2)}) %collective-permute-start.7) | collective-permute-done | bytes 524320 | tf_op jit(solution)/shard_map/ppermute | solution.py:63
  43.2 0.4 collective-permute-done.6.p1
  43.5 1.5 %collective-permute-start.10 = (bf16[32,8192]{1,0:T(8,128)(2,1)S(1)}, bf16[32,8192]{1,0:T(8,128)(2,1)S(1)}, u32[]{:S(2)}, u32[]{:S(2)}) collective-permute-start(bf16[32,8192]{1,0:T(8,128)(2,1)S(1)} %collective-permute-done.6.p1), channel_id=1, source_target_pairs={{0,16},{2,18},{4,20},{6,22},{8,24},{10,26},{12,28},{14,30},{16,0},... | collective-permute-start | bytes 1572872 | tf_op jit(solution)/shard_map/ppermute | solution.py:63
  45.0 0.1 collective-permute-done.11.p6
  45.1 1.5 %collective-permute-done.10.p5 = bf16[32,8192]{1,0:T(8,128)(2,1)S(1)} collective-permute-done((bf16[32,8192]{1,0:T(8,128)(2,1)S(1)}, bf16[32,8192]{1,0:T(8,128)(2,1)S(1)}, u32[]{:S(2)}, u32[]{:S(2)}) %collective-permute-start.10) | collective-permute-done | bytes 524320 | tf_op jit(solution)/shard_map/ppermute | solution.py:63
  46.5 6.4 %logits.1 = (f32[3,128]{1,0:T(4,128)S(1)}, f32[3,128]{1,0:T(4,128)S(1)}, f32[128,8192]{1,0:T(8,128)}, bf16[128,8192]{1,0:T(8,128)(2,1)}) custom-call(s32[5]{0:T(128)S(1)} %stack.23.at_ref, s32[1,256]{1,0:T(1,128)S(1)} %bitcast.8, bf16[32,8192]{1,0:T(8,128)(2,1)S(1)} %concatenate.8.p0, bf16[32,8192]{1,0:T(8,128)(2,1)S(1)} %collective-permute-done.6.p1, ...), custom_call_target="tpu_custom_call" | custom-call | flops 4294967296 | bytes 19922944 | tf_op jit(solution)/shard_map/logits/pallas_call | solution.py:251
  52.9 0.6 collective-permute-start.15
  53.5 0.2 collective-permute-start.13
  53.7 1.5 %collective-permute-start.14 = (f32[3,128]{1,0:T(4,128)S(1)}, f32[3,128]{1,0:T(4,128)S(1)}, u32[]{:S(2)}, u32[]{:S(2)}) collective-permute-start(f32[3,128]{1,0:T(4,128)S(1)} %get-tuple-element.22.own_ref), channel_id=1, source_target_pairs={{0,32},{2,34},{4,36},{6,38},{8,40},{10,42},{12,44},{14,46},{16,48}... | collective-permute-start | bytes 4616 | tf_op jit(solution)/shard_map/ppermute | solution.py:63
  55.2 0.9 collective-permute-done.15.both_ref
  56.0 1.3 %collective-permute-done.14.x_ref = f32[3,128]{1,0:T(4,128)S(1)} collective-permute-done((f32[3,128]{1,0:T(4,128)S(1)}, f32[3,128]{1,0:T(4,128)S(1)}, u32[]{:S(2)}, u32[]{:S(2)}) %collective-permute-start.14) | collective-permute-done | bytes 1568 | tf_op jit(solution)/shard_map/ppermute | solution.py:63
  57.3 0.1 collective-permute-start.16
  57.4 0.5 collective-permute-start.17
  57.9 18.0 %all_to_all.5.spread_ref = f32[32,3,128]{2,1,0:T(4,128)S(1)} all-to-all(f32[32,3,128]{2,1,0:T(4,128)S(1)} %merge.1), channel_id=1, replica_groups=mesh['y'=4,'x'=2,'c'=2,'z'=8,'dp'=2] {'y','z'}, dimensions={0} | all-to-all | bytes 98304 | tf_op jit(solution)/shard_map/all_to_all | solution.py:272
  75.9 0.0 collective-permute-done.16.refs_1_
  75.9 0.0 collective-permute-done.17.refs_3_
  75.9 2.3 %combine.3 = (f32[128,128]{1,0:T(8,128)S(1)}, bf16[32,8192]{1,0:T(8,128)(2,1)S(1)}) custom-call(s32[5]{0:T(128)S(1)} %stack.23.at_ref, f32[1,256]{1,0:T(1,128)S(1)} %bitcast.9, f32[3,128]{1,0:T(4,128)S(1)} %get-tuple-element.22.own_ref, f32[3,128]{1,0:T(4,128)S(1)} %collective-permute-done.13.core_ref, f32[32,3,128]{2,1,0:T(4,128)S(1)} %all_to_all.5.spread_ref, ...), custom_call_target="tpu_custom_call" | custom-call | flops 1572864 | bytes 3145728 | tf_op jit(solution)/shard_map/combine/pallas_call | solution.py:281
  78.3 1.4 %collective-permute-start.18 = (bf16[32,8192]{1,0:T(8,128)(2,1)S(1)}, bf16[32,8192]{1,0:T(8,128)(2,1)S(1)}, u32[]{:S(2)}, u32[]{:S(2)}) collective-permute-start(bf16[32,8192]{1,0:T(8,128)(2,1)S(1)} %get-tuple-element.32), channel_id=1, source_target_pairs={{0,128},{2,130},{4,132},{6,134},{8,136},{10,138},{12,140},{14,142}... | collective-permute-start | bytes 1572872 | tf_op jit(solution)/shard_map/ppermute | solution.py:63
  79.7 2.3 %combine.5 = (bf16[32,8192]{1,0:T(8,128)(2,1)S(1)}, bf16[32,8192]{1,0:T(8,128)(2,1)S(1)}) custom-call(f32[128,128]{1,0:T(8,128)S(1)} %get-tuple-element.31.scales_ref, f32[128,8192]{1,0:T(8,128)} %get-tuple-element.27.refs_0_, bf16[128,8192]{1,0:T(8,128)(2,1)S(1)} %collective-permute-done.16.refs_1_, bf16[128,8192]{1,0:T(8,128)(2,1)} %get-tuple-element.29.refs_2_, ...), custom_call_target="tpu_custom_call" | custom-call | flops 3145728 | bytes 6291456 | tf_op jit(solution)/shard_map/combine/pallas_call | solution.py:281
  82.0 0.8 collective-permute-start.19
  82.8 2.5 %collective-permute-start.20 = (bf16[32,8192]{1,0:T(8,128)(2,1)S(1)}, bf16[32,8192]{1,0:T(8,128)(2,1)S(1)}, u32[]{:S(2)}, u32[]{:S(2)}) collective-permute-start(bf16[32,8192]{1,0:T(8,128)(2,1)S(1)} %get-tuple-element.34), channel_id=1, source_target_pairs={{0,192},{2,194},{4,196},{6,198},{8,200},{10,202},{12,204},{14,206}... | collective-permute-start | bytes 1572872 | tf_op jit(solution)/shard_map/ppermute | solution.py:63
  85.3 1.8 %combine.4 = f32[32,8192]{1,0:T(8,128)S(1)} custom-call(f32[128,128]{1,0:T(8,128)S(1)} %get-tuple-element.31.scales_ref, f32[128,8192]{1,0:T(8,128)} %get-tuple-element.27.refs_0_, bf16[128,8192]{1,0:T(8,128)(2,1)S(1)} %collective-permute-done.16.refs_1_, bf16[128,8192]{1,0:T(8,128)(2,1)} %get-tuple-element.29.refs_2_, ...), custom_call_target="tpu_custom_call" | custom-call | flops 1572864 | bytes 3145728 | tf_op jit(solution)/shard_map/combine/pallas_call | solution.py:281
  87.1 2.0 %collective-permute-done.18 = bf16[32,8192]{1,0:T(8,128)(2,1)S(1)} collective-permute-done((bf16[32,8192]{1,0:T(8,128)(2,1)S(1)}, bf16[32,8192]{1,0:T(8,128)(2,1)S(1)}, u32[]{:S(2)}, u32[]{:S(2)}) %collective-permute-start.18) | collective-permute-done | bytes 524320 | tf_op jit(solution)/shard_map/ppermute | solution.py:63
  89.1 5.5 %collective-permute-done.19 = bf16[32,8192]{1,0:T(8,128)(2,1)S(1)} collective-permute-done((bf16[32,8192]{1,0:T(8,128)(2,1)S(1)}, bf16[32,8192]{1,0:T(8,128)(2,1)S(1)}, u32[]{:S(2)}, u32[]{:S(2)}) %collective-permute-start.19) | collective-permute-done | bytes 524320 | tf_op jit(solution)/shard_map/ppermute | solution.py:63
  94.7 0.3 fusion.3
  95.0 1.3 %collective-permute-start.21 = (bf16[8,8192]{1,0:T(8,128)(2,1)S(1)}, bf16[8,8192]{1,0:T(8,128)(2,1)S(1)}, u32[]{:S(2)}, u32[]{:S(2)}) collective-permute-start(bf16[8,8192]{1,0:T(8,128)(2,1)S(1)} %get-tuple-element.41), channel_id=1, source_target_pairs={{0,4},{2,6},{4,8},{6,10},{8,12},{10,14},{12,0},{14,2},{16,144},{18... | collective-permute-start | bytes 393224 | tf_op jit(solution)/shard_map/ppermute | solution.py:63
  96.2 2.6 %collective-permute-start.23 = (bf16[8,8192]{1,0:T(8,128)(2,1)S(1)}, bf16[8,8192]{1,0:T(8,128)(2,1)S(1)}, u32[]{:S(2)}, u32[]{:S(2)}) collective-permute-start(bf16[8,8192]{1,0:T(8,128)(2,1)S(1)} %get-tuple-element.42), channel_id=1, source_target_pairs={{0,14},{2,0},{4,2},{6,4},{8,6},{10,8},{12,10},{14,12},{16,208},{18... | collective-permute-start | bytes 393224 | tf_op jit(solution)/shard_map/ppermute | solution.py:63
  98.8 0.2 slice_reduce_fusion
  99.0 4.1 %collective-permute-done.21 = bf16[8,8192]{1,0:T(8,128)(2,1)S(1)} collective-permute-done((bf16[8,8192]{1,0:T(8,128)(2,1)S(1)}, bf16[8,8192]{1,0:T(8,128)(2,1)S(1)}, u32[]{:S(2)}, u32[]{:S(2)}) %collective-permute-start.21) | collective-permute-done | bytes 131104 | tf_op jit(solution)/shard_map/ppermute | solution.py:63
  103.2 1.8 %collective-permute-done.22 = bf16[8,8192]{1,0:T(8,128)(2,1)S(1)} collective-permute-done((bf16[8,8192]{1,0:T(8,128)(2,1)S(1)}, bf16[8,8192]{1,0:T(8,128)(2,1)S(1)}, u32[]{:S(2)}, u32[]{:S(2)}) %collective-permute-start.22) | collective-permute-done | bytes 131104 | tf_op jit(solution)/shard_map/ppermute | solution.py:63
  105.0 0.1 fusion.2
  105.1 0.1 fusion.5
  105.2 1.9 %collective-permute-start.25 = (bf16[2,8192]{1,0:T(2,128)(2,1)S(1)}, bf16[2,8192]{1,0:T(2,128)(2,1)S(1)}, u32[]{:S(2)}, u32[]{:S(2)}) collective-permute-start(bf16[2,8192]{1,0:T(2,128)(2,1)S(1)} %get-tuple-element.44), channel_id=1, source_target_pairs={{0,40},{2,42},{4,44},{6,46},{8,32},{10,34},{12,36},{14,38},{16,56}... | collective-permute-start | bytes 98312 | tf_op jit(solution)/shard_map/ppermute | solution.py:63
  107.1 4.6 %collective-permute-start.26 = (bf16[2,8192]{1,0:T(2,128)(2,1)S(1)}, bf16[2,8192]{1,0:T(2,128)(2,1)S(1)}, u32[]{:S(2)}, u32[]{:S(2)}) collective-permute-start(bf16[2,8192]{1,0:T(2,128)(2,1)S(1)} %get-tuple-element.45), channel_id=1, source_target_pairs={{0,8},{2,10},{4,12},{6,14},{8,0},{10,2},{12,4},{14,6},{16,24},{18,... | collective-permute-start | bytes 98312 | tf_op jit(solution)/shard_map/ppermute | solution.py:63
  111.7 1.0 collective-permute-start.24
  112.8 0.5 multiply_multiply_fusion
  113.3 1.1 collective-permute-done.25
  114.4 0.6 collective-permute-done.26
  115.0 1.5 %collective-permute-done.24 = f32[2,8192]{1,0:T(2,128)S(1)} collective-permute-done((f32[2,8192]{1,0:T(2,128)S(1)}, f32[2,8192]{1,0:T(2,128)S(1)}, u32[]{:S(2)}, u32[]{:S(2)}) %collective-permute-start.24) | collective-permute-done | bytes 65568 | tf_op jit(solution)/shard_map/ppermute | solution.py:63
  116.4 0.7 fusion.1
  (16 shorter events, 0.1 us)
Async XLA Ops:
  0.6 10.1 %collective-permute-start.2 = (bf16[2,8192]{1,0:T(2,128)(2,1)}, bf16[2,8192]{1,0:T(2,128)(2,1)S(1)}, u32[]{:S(2)}, u32[]{:S(2)}) collective-permute-start(bf16[2,8192]{1,0:T(2,128)(2,1)} %param.4), channel_id=1, source_target_pairs={{0,40},{2,42},{4,44},{6,46},{8,32},{10,34},{12,36},{14,38},{16,56}... | collective-permute-start | bytes 98312 | tf_op jit(solution)/shard_map/ppermute | solution.py:63
  8.5 8.3 %collective-permute-start.1 = (bf16[2,8192]{1,0:T(2,128)(2,1)}, bf16[2,8192]{1,0:T(2,128)(2,1)S(1)}, u32[]{:S(2)}, u32[]{:S(2)}) collective-permute-start(bf16[2,8192]{1,0:T(2,128)(2,1)} %param.4), channel_id=1, source_target_pairs={{0,8},{2,10},{4,12},{6,14},{8,0},{10,2},{12,4},{14,6},{16,24},{18,... | collective-permute-start | bytes 98312 | tf_op jit(solution)/shard_map/ppermute | solution.py:63
  8.5 8.3 %collective-permute-start = (bf16[2,8192]{1,0:T(2,128)(2,1)}, bf16[2,8192]{1,0:T(2,128)(2,1)S(1)}, u32[]{:S(2)}, u32[]{:S(2)}) collective-permute-start(bf16[2,8192]{1,0:T(2,128)(2,1)} %param.4), channel_id=1, source_target_pairs={{0,32},{2,34},{4,36},{6,38},{8,40},{10,42},{12,44},{14,46},{16,48}... | collective-permute-start | bytes 98312 | tf_op jit(solution)/shard_map/ppermute | solution.py:63
  17.8 7.5 %collective-permute-start.5 = (bf16[8,8192]{1,0:T(8,128)(2,1)S(1)}, bf16[8,8192]{1,0:T(8,128)(2,1)S(1)}, u32[]{:S(2)}, u32[]{:S(2)}) collective-permute-start(bf16[8,8192]{1,0:T(8,128)(2,1)S(1)} %pad_maximum_fusion), channel_id=1, source_target_pairs={{0,12},{2,14},{4,0},{6,2},{8,4},{10,6},{12,8},{14,10},{16,144},{18... | collective-permute-start | bytes 393224 | tf_op jit(solution)/shard_map/ppermute | solution.py:63
  18.7 6.5 %collective-permute-start.4 = (bf16[8,8192]{1,0:T(8,128)(2,1)S(1)}, bf16[8,8192]{1,0:T(8,128)(2,1)S(1)}, u32[]{:S(2)}, u32[]{:S(2)}) collective-permute-start(bf16[8,8192]{1,0:T(8,128)(2,1)S(1)} %pad_maximum_fusion), channel_id=1, source_target_pairs={{0,2},{2,4},{4,6},{6,8},{8,10},{10,12},{12,14},{14,0},{16,80},{18,... | collective-permute-start | bytes 393224 | tf_op jit(solution)/shard_map/ppermute | solution.py:63
  19.7 6.1 %collective-permute-start.3 = (bf16[8,8192]{1,0:T(8,128)(2,1)S(1)}, bf16[8,8192]{1,0:T(8,128)(2,1)S(1)}, u32[]{:S(2)}, u32[]{:S(2)}) collective-permute-start(bf16[8,8192]{1,0:T(8,128)(2,1)S(1)} %pad_maximum_fusion), channel_id=1, source_target_pairs={{0,14},{2,0},{4,2},{6,4},{8,6},{10,8},{12,10},{14,12},{16,208},{18... | collective-permute-start | bytes 393224 | tf_op jit(solution)/shard_map/ppermute | solution.py:63
  26.8 14.2 %collective-permute-start.8 = (bf16[32,8192]{1,0:T(8,128)(2,1)S(1)}, bf16[32,8192]{1,0:T(8,128)(2,1)S(1)}, u32[]{:S(2)}, u32[]{:S(2)}) collective-permute-start(bf16[32,8192]{1,0:T(8,128)(2,1)S(1)} %concatenate.8.p0), channel_id=1, source_target_pairs={{0,128},{2,130},{4,132},{6,134},{8,136},{10,138},{12,140},{14,142}... | collective-permute-start | bytes 1572872 | tf_op jit(solution)/shard_map/ppermute | solution.py:63
  30.0 13.1 %collective-permute-start.7 = (bf16[32,8192]{1,0:T(8,128)(2,1)S(1)}, bf16[32,8192]{1,0:T(8,128)(2,1)S(1)}, u32[]{:S(2)}, u32[]{:S(2)}) collective-permute-start(bf16[32,8192]{1,0:T(8,128)(2,1)S(1)} %concatenate.8.p0), channel_id=1, source_target_pairs={{0,64},{2,66},{4,68},{6,70},{8,72},{10,74},{12,76},{14,78},{16,18}... | collective-permute-start | bytes 1572872 | tf_op jit(solution)/shard_map/ppermute | solution.py:63
  30.7 12.8 %collective-permute-start.6 = (bf16[32,8192]{1,0:T(8,128)(2,1)S(1)}, bf16[32,8192]{1,0:T(8,128)(2,1)S(1)}, u32[]{:S(2)}, u32[]{:S(2)}) collective-permute-start(bf16[32,8192]{1,0:T(8,128)(2,1)S(1)} %concatenate.8.p0), channel_id=1, source_target_pairs={{0,192},{2,194},{4,196},{6,198},{8,200},{10,202},{12,204},{14,206}... | collective-permute-start | bytes 1572872 | tf_op jit(solution)/shard_map/ppermute | solution.py:63
  33.4 0.7 copy-start.1
  34.0 12.5 %copy-start = (bf16[8192,512]{1,0:T(8,128)(2,1)S(1)}, bf16[8192,512]{1,0:T(8,128)(2,1)}, u32[]{:S(2)}) copy-start(bf16[8192,512]{1,0:T(8,128)(2,1)} %w_ref.1) | copy-start | bytes 25165828
  40.8 16.6 %copy-start.3 = (bf16[128,8192]{1,0:T(8,128)(2,1)S(1)}, bf16[128,8192]{1,0:T(8,128)(2,1)}, u32[]{:S(2)}) copy-start(bf16[128,8192]{1,0:T(8,128)(2,1)} %get-tuple-element.30) | copy-start | bytes 6291460
  40.8 35.1 %copy-start.2 = (f32[256]{0:T(256)S(1)}, f32[256]{0:T(256)}, u32[]{:S(2)}) copy-start(f32[256]{0:T(256)} %param.7) | copy-start | bytes 3076
  40.8 4.2 %collective-permute-start.9 = (bf16[32,8192]{1,0:T(8,128)(2,1)S(1)}, bf16[32,8192]{1,0:T(8,128)(2,1)S(1)}, u32[]{:S(2)}, u32[]{:S(2)}) collective-permute-start(bf16[32,8192]{1,0:T(8,128)(2,1)S(1)} %concatenate.8.p0), channel_id=1, source_target_pairs={{0,16},{2,18},{4,20},{6,22},{8,24},{10,26},{12,28},{14,30},{16,0},... | collective-permute-start | bytes 1572872 | tf_op jit(solution)/shard_map/ppermute | solution.py:63
  41.0 4.1 %collective-permute-start.12 = (bf16[32,8192]{1,0:T(8,128)(2,1)S(1)}, bf16[32,8192]{1,0:T(8,128)(2,1)S(1)}, u32[]{:S(2)}, u32[]{:S(2)}) collective-permute-start(bf16[32,8192]{1,0:T(8,128)(2,1)S(1)} %collective-permute-done.8.p3), channel_id=1, source_target_pairs={{0,16},{2,18},{4,20},{6,22},{8,24},{10,26},{12,28},{14,30},{16,0},... | collective-permute-start | bytes 1572872 | tf_op jit(solution)/shard_map/ppermute | solution.py:63
  43.2 1.9 %collective-permute-start.11 = (bf16[32,8192]{1,0:T(8,128)(2,1)S(1)}, bf16[32,8192]{1,0:T(8,128)(2,1)S(1)}, u32[]{:S(2)}, u32[]{:S(2)}) collective-permute-start(bf16[32,8192]{1,0:T(8,128)(2,1)S(1)} %collective-permute-done.7.p2), channel_id=1, source_target_pairs={{0,16},{2,18},{4,20},{6,22},{8,24},{10,26},{12,28},{14,30},{16,0},... | collective-permute-start | bytes 1572872 | tf_op jit(solution)/shard_map/ppermute | solution.py:63
  43.5 3.0 %collective-permute-start.10 = (bf16[32,8192]{1,0:T(8,128)(2,1)S(1)}, bf16[32,8192]{1,0:T(8,128)(2,1)S(1)}, u32[]{:S(2)}, u32[]{:S(2)}) collective-permute-start(bf16[32,8192]{1,0:T(8,128)(2,1)S(1)} %collective-permute-done.6.p1), channel_id=1, source_target_pairs={{0,16},{2,18},{4,20},{6,22},{8,24},{10,26},{12,28},{14,30},{16,0},... | collective-permute-start | bytes 1572872 | tf_op jit(solution)/shard_map/ppermute | solution.py:63
  52.9 3.1 %collective-permute-start.15 = (f32[3,128]{1,0:T(4,128)S(1)}, f32[3,128]{1,0:T(4,128)S(1)}, u32[]{:S(2)}, u32[]{:S(2)}) collective-permute-start(f32[3,128]{1,0:T(4,128)S(1)} %get-tuple-element.23), channel_id=1, source_target_pairs={{0,48},{2,50},{4,52},{6,54},{8,56},{10,58},{12,60},{14,62},{16,32}... | collective-permute-start | bytes 4616 | tf_op jit(solution)/shard_map/ppermute | solution.py:63
  53.5 2.5 %collective-permute-start.13 = (f32[3,128]{1,0:T(4,128)S(1)}, f32[3,128]{1,0:T(4,128)S(1)}, u32[]{:S(2)}, u32[]{:S(2)}) collective-permute-start(f32[3,128]{1,0:T(4,128)S(1)} %get-tuple-element.23), channel_id=1, source_target_pairs={{0,16},{2,18},{4,20},{6,22},{8,24},{10,26},{12,28},{14,30},{16,0},... | collective-permute-start | bytes 4616 | tf_op jit(solution)/shard_map/ppermute | solution.py:63
  53.7 3.6 %collective-permute-start.14 = (f32[3,128]{1,0:T(4,128)S(1)}, f32[3,128]{1,0:T(4,128)S(1)}, u32[]{:S(2)}, u32[]{:S(2)}) collective-permute-start(f32[3,128]{1,0:T(4,128)S(1)} %get-tuple-element.22.own_ref), channel_id=1, source_target_pairs={{0,32},{2,34},{4,36},{6,38},{8,40},{10,42},{12,44},{14,46},{16,48}... | collective-permute-start | bytes 4616 | tf_op jit(solution)/shard_map/ppermute | solution.py:63
  57.3 18.6 %collective-permute-start.16 = (bf16[128,8192]{1,0:T(8,128)(2,1)}, bf16[128,8192]{1,0:T(8,128)(2,1)S(1)}, u32[]{:S(2)}, u32[]{:S(2)}) collective-permute-start(bf16[128,8192]{1,0:T(8,128)(2,1)} %get-tuple-element.28), channel_id=1, source_target_pairs={{0,16},{2,18},{4,20},{6,22},{8,24},{10,26},{12,28},{14,30},{16,0},... | collective-permute-start | bytes 6291464 | tf_op jit(solution)/shard_map/ppermute | solution.py:63
  57.4 18.5 %collective-permute-start.17 = (bf16[128,8192]{1,0:T(8,128)(2,1)S(1)}, bf16[128,8192]{1,0:T(8,128)(2,1)S(1)}, u32[]{:S(2)}, u32[]{:S(2)}) collective-permute-start(bf16[128,8192]{1,0:T(8,128)(2,1)S(1)} %copy-done.3), channel_id=1, source_target_pairs={{0,16},{2,18},{4,20},{6,22},{8,24},{10,26},{12,28},{14,30},{16,0},... | collective-permute-start | bytes 6291464 | tf_op jit(solution)/shard_map/ppermute | solution.py:63
  78.3 10.9 %collective-permute-start.18 = (bf16[32,8192]{1,0:T(8,128)(2,1)S(1)}, bf16[32,8192]{1,0:T(8,128)(2,1)S(1)}, u32[]{:S(2)}, u32[]{:S(2)}) collective-permute-start(bf16[32,8192]{1,0:T(8,128)(2,1)S(1)} %get-tuple-element.32), channel_id=1, source_target_pairs={{0,128},{2,130},{4,132},{6,134},{8,136},{10,138},{12,140},{14,142}... | collective-permute-start | bytes 1572872 | tf_op jit(solution)/shard_map/ppermute | solution.py:63
  82.0 12.7 %collective-permute-start.19 = (bf16[32,8192]{1,0:T(8,128)(2,1)S(1)}, bf16[32,8192]{1,0:T(8,128)(2,1)S(1)}, u32[]{:S(2)}, u32[]{:S(2)}) collective-permute-start(bf16[32,8192]{1,0:T(8,128)(2,1)S(1)} %get-tuple-element.33), channel_id=1, source_target_pairs={{0,64},{2,66},{4,68},{6,70},{8,72},{10,74},{12,76},{14,78},{16,18}... | collective-permute-start | bytes 1572872 | tf_op jit(solution)/shard_map/ppermute | solution.py:63
  82.8 11.9 %collective-permute-start.20 = (bf16[32,8192]{1,0:T(8,128)(2,1)S(1)}, bf16[32,8192]{1,0:T(8,128)(2,1)S(1)}, u32[]{:S(2)}, u32[]{:S(2)}) collective-permute-start(bf16[32,8192]{1,0:T(8,128)(2,1)S(1)} %get-tuple-element.34), channel_id=1, source_target_pairs={{0,192},{2,194},{4,196},{6,198},{8,200},{10,202},{12,204},{14,206}... | collective-permute-start | bytes 1572872 | tf_op jit(solution)/shard_map/ppermute | solution.py:63
  95.0 8.2 %collective-permute-start.21 = (bf16[8,8192]{1,0:T(8,128)(2,1)S(1)}, bf16[8,8192]{1,0:T(8,128)(2,1)S(1)}, u32[]{:S(2)}, u32[]{:S(2)}) collective-permute-start(bf16[8,8192]{1,0:T(8,128)(2,1)S(1)} %get-tuple-element.41), channel_id=1, source_target_pairs={{0,4},{2,6},{4,8},{6,10},{8,12},{10,14},{12,0},{14,2},{16,144},{18... | collective-permute-start | bytes 393224 | tf_op jit(solution)/shard_map/ppermute | solution.py:63
  96.2 7.0 %collective-permute-start.23 = (bf16[8,8192]{1,0:T(8,128)(2,1)S(1)}, bf16[8,8192]{1,0:T(8,128)(2,1)S(1)}, u32[]{:S(2)}, u32[]{:S(2)}) collective-permute-start(bf16[8,8192]{1,0:T(8,128)(2,1)S(1)} %get-tuple-element.42), channel_id=1, source_target_pairs={{0,14},{2,0},{4,2},{6,4},{8,6},{10,8},{12,10},{14,12},{16,208},{18... | collective-permute-start | bytes 393224 | tf_op jit(solution)/shard_map/ppermute | solution.py:63
  98.8 6.2 %collective-permute-start.22 = (bf16[8,8192]{1,0:T(8,128)(2,1)S(1)}, bf16[8,8192]{1,0:T(8,128)(2,1)S(1)}, u32[]{:S(2)}, u32[]{:S(2)}) collective-permute-start(bf16[8,8192]{1,0:T(8,128)(2,1)S(1)} %get-tuple-element.43), channel_id=1, source_target_pairs={{0,2},{2,4},{4,6},{6,8},{8,10},{10,12},{12,14},{14,0},{16,80},{18,... | collective-permute-start | bytes 393224 | tf_op jit(solution)/shard_map/ppermute | solution.py:63
  105.2 9.3 %collective-permute-start.25 = (bf16[2,8192]{1,0:T(2,128)(2,1)S(1)}, bf16[2,8192]{1,0:T(2,128)(2,1)S(1)}, u32[]{:S(2)}, u32[]{:S(2)}) collective-permute-start(bf16[2,8192]{1,0:T(2,128)(2,1)S(1)} %get-tuple-element.44), channel_id=1, source_target_pairs={{0,40},{2,42},{4,44},{6,46},{8,32},{10,34},{12,36},{14,38},{16,56}... | collective-permute-start | bytes 98312 | tf_op jit(solution)/shard_map/ppermute | solution.py:63
  107.1 7.9 %collective-permute-start.26 = (bf16[2,8192]{1,0:T(2,128)(2,1)S(1)}, bf16[2,8192]{1,0:T(2,128)(2,1)S(1)}, u32[]{:S(2)}, u32[]{:S(2)}) collective-permute-start(bf16[2,8192]{1,0:T(2,128)(2,1)S(1)} %get-tuple-element.45), channel_id=1, source_target_pairs={{0,8},{2,10},{4,12},{6,14},{8,0},{10,2},{12,4},{14,6},{16,24},{18,... | collective-permute-start | bytes 98312 | tf_op jit(solution)/shard_map/ppermute | solution.py:63
  111.7 4.7 %collective-permute-start.24 = (f32[2,8192]{1,0:T(2,128)S(1)}, f32[2,8192]{1,0:T(2,128)S(1)}, u32[]{:S(2)}, u32[]{:S(2)}) collective-permute-start(f32[2,8192]{1,0:T(2,128)S(1)} %slice.54), channel_id=1, source_target_pairs={{0,32},{2,34},{4,36},{6,38},{8,40},{10,42},{12,44},{14,46},{16,48}... | collective-permute-start | bytes 196616 | tf_op jit(solution)/shard_map/ppermute | solution.py:63

commit v12 on v11

--- a/solution.py
+++ b/solution.py
@@ -106,7 +106,7 @@
     return copies
 
 
-def logits_kernel(at_ref, targets_ref, p0, p1, p2, p3, p4, p5, p6, p7, w_ref, stats_ref, other_stats_ref, own_hbm, other_hbm, own_ref, other_ref, own_sems, other_sems):
+def logits_kernel(at_ref, targets_ref, p0, p1, p2, p3, p4, p5, p6, p7, w_ref, stats_ref, other_stats_ref, soft_ref):
     acc = jnp.zeros((ROWS, WIDTH), F32)
     for k in range(STEPS):
         cut = slice(k * CHUNK, (k + 1) * CHUNK)
@@ -123,9 +123,13 @@
     for i, column in enumerate((top, total, picked)):
         stats_ref[i : i + 1, :] = jnp.sum(jnp.where(place[:half], column[:half], 0.0), axis=0, keepdims=True)
         other_stats_ref[i : i + 1, :] = jnp.sum(jnp.where(place[half:], column[half:], 0.0), axis=0, keepdims=True)
+    soft_ref[...] = jnp.where(hit, 0.0, soft).astype(BF)
+
+
+def soft_kernel(soft_ref, w_ref, own_hbm, other_hbm, own_ref, other_ref, own_sems, other_sems):
     own = (own_ref, column_copies(own_ref, own_hbm, own_sems))
     other = (other_ref, column_copies(other_ref, other_hbm, other_sems))
-    products(jnp.where(hit, 0.0, soft).astype(BF), None, w_ref, (own, other))
+    products(soft_ref[...], None, w_ref, (own, other))
 
 
 def products(left, copies, w_ref, pairs):
@@ -248,16 +252,26 @@
     own, target_out = lax.optimization_barrier((block, target_out))
     pieces = [block, near, back, far] + [send(p, to_c) for p in (own, near, back, far)]
 
-    own_stats, other_stats, soft_own, soft_out = pl.pallas_call(
+    near_weights = pltpu.with_memory_space_constraint(lm_weight_in, pltpu.VMEM)
+    own_stats, other_stats, soft = pl.pallas_call(
         logits_kernel,
-        out_shape=[jax.ShapeDtypeStruct((3, half), F32)] * 2 + [pltpu.HBM((half, DEPTH), F32), pltpu.HBM((half, DEPTH), BF)],
+        out_shape=[jax.ShapeDtypeStruct((3, half), F32)] * 2 + [jax.ShapeDtypeStruct((ROWS, WIDTH), BF)],
         in_specs=[SMEM] + [VMEM] * 10,
-        out_specs=(VMEM, VMEM, HBM, HBM),
+        out_specs=[VMEM] * 3,
+        compiler_params=params(16),
+        cost_estimate=pl.CostEstimate(flops=2 * ROWS * DEPTH * WIDTH, bytes_accessed=13 << 20, transcendentals=ROWS * WIDTH),
+        name="logits",
+    )(at, targets, *pieces, near_weights)
+    soft_own, soft_out = pl.pallas_call(
+        soft_kernel,
+        out_shape=(pltpu.HBM((half, DEPTH), F32), pltpu.HBM((half, DEPTH), BF)),
+        in_specs=[VMEM] * 2,
+        out_specs=(HBM, HBM),
         scratch_shapes=[pltpu.VMEM((half, DEPTH), F32), pltpu.VMEM((half, DEPTH), BF)] + [sems] * 2,
         compiler_params=params(16),
-        cost_estimate=pl.CostEstimate(flops=4 * ROWS * DEPTH * WIDTH, bytes_accessed=19 << 20, transcendentals=ROWS * WIDTH),
-        name="logits",
-    )(at, targets, *pieces, pltpu.with_memory_space_constraint(lm_weight_in, pltpu.VMEM))
+        cost_estimate=pl.CostEstimate(flops=2 * ROWS * DEPTH * WIDTH, bytes_accessed=14 << 20, transcendentals=0),
+        name="soft",
+    )(soft, near_weights)
     stats = [own_stats, send(other_stats, to_c), send(own_stats, to_x), send(other_stats, to_xc)]
     merged = pl.pallas_call(
         merge_kernel,
@@ -291,8 +305,7 @@
             name="combine",
         )(*rows, *shares)
 
-    scales, far = combine((3,), BF, first_kernel, (at, loss_grad, stats[0], stats[1], spread))
-    parts = [far, *combine((1, 2), BF, rows=(scales,))]
+    scales, *parts = combine((3, 1, 2), BF, first_kernel, (at, loss_grad, stats[0], stats[1], spread))
     log_total, target_logit = scales[:2, 3], scales[:2, 4]
     ce_loss = log_total - target_logit
     z_term = zloss_coef * log_total * log_total
@@ -300,9 +313,8 @@
     part = combine((0,), F32, rows=(scales,))[0] + sum(arrived)
     part = part.reshape(4, 8, DEPTH)
     part = part[0] + sum(send(part[k].astype(BF), to_first(OFFSETS[k])).astype(F32) for k in (3, 1, 2))
-    part = [part[0:2], send(part[2:4], to_x)] + [
-        send(part[2 * k : 2 * k + 2].astype(BF), to).astype(F32) for k, to in ((3, to_xz4), (2, to_z4))
-    ]
+    moved = [send(part[2 * k : 2 * k + 2].astype(BF), to).astype(F32) for k, to in ((3, to_xz4), (2, to_z4))]
+    part = [part[0:2], *moved, send(part[2:4], to_x)]
     part = (part[0] + part[1]) + (part[2] + part[3])
     return ce_loss, z_term, part.astype(BF)
 

time: 119 us -> 117 us (0.983)
    pallas_call x0 -> x1, Pallas kernels: none -> 3.39 us  [shards(): pl.pallas_call(soft_kernel, out_shape=(pltpu.HBM((half, DEPTH), F32), plt...]
    pallas_call x1, Pallas kernels: 6.36 us -> 3.15 us  [shards(): pl.pallas_call(logits_kernel, out_shape=[jax.ShapeDtypeStruct((3, half),...]
    pallas_call x3 -> x2, Pallas kernels: 6.42 us -> 5.17 us  [combine(): pl.pallas_call(functools.partial(kernel, parts), out_shape=scales + [jax....]
  transfers between devices with their start and end apart: 27 -> 27, of which waited for: 17 -> 15; matrix products, arithmetic and copies ran while one was open for 1% -> 1% of each run, Pallas kernels for 9% -> 10%
where the time goes in v12:
time: 117 us; the launch traced here: 116 us
  starting transfers between devices  40.4 us (35%)
  waiting for transfers between devices  33.9 us (29%)
  Pallas kernels  18.5 us (16%)
  blocking collectives  17.6 us (15%)
  other arithmetic  2.39 us (2%)
  local copies, waits for them, and re-layouts  2.07 us (2%)
    ppermute x27, starting transfers between devices, send(): return lax.ppermute(value, GROUP, pairs(route))  40.4 us
    ppermute x27, waiting for transfers between devices, send(): return lax.ppermute(value, GROUP, pairs(route))  33.9 us
    all_to_all x1, blocking collectives, shards(): spread = lax.all_to_all(merged, ('y', 'z'), 0, 0)  17.6 us
    pallas_call x1, Pallas kernels, shards(): pl.pallas_call(target_kernel, out_shape=[pltpu.HBM((half, DEPTH), BF)] *...  6.76 us
    pallas_call x2, Pallas kernels, combine(): pl.pallas_call(functools.partial(kernel, parts), out_shape=scales + [jax....  5.17 us
    pallas_call x1, Pallas kernels, shards(): pl.pallas_call(soft_kernel, out_shape=(pltpu.HBM((half, DEPTH), F32), plt...  3.39 us
    pallas_call x1, Pallas kernels, shards(): pl.pallas_call(logits_kernel, out_shape=[jax.ShapeDtypeStruct((3, half),...  3.15 us
  transfers between devices with their start and end apart: 27, of which 15 were waited for; matrix products, arithmetic and copies ran while one was open for 1% of the time, Pallas kernels for 10%

profile of v12, /device:TPU:4, one launch (start us, length us, event | category | flops | bytes accessed | tf_op | source)
XLA Modules:
  0.0 115.7 jit_solution(16342970874165033866)
XLA Ops:
  0.6 7.9 %collective-permute-start.2 = (bf16[2,8192]{1,0:T(2,128)(2,1)}, bf16[2,8192]{1,0:T(2,128)(2,1)S(1)}, u32[]{:S(2)}, u32[]{:S(2)}) collective-permute-start(bf16[2,8192]{1,0:T(2,128)(2,1)} %param.4), channel_id=1, source_target_pairs={{0,40},{2,42},{4,44},{6,46},{8,32},{10,34},{12,36},{14,38},{16,56}... | collective-permute-start | bytes 98312 | tf_op jit(solution)/shard_map/ppermute | solution.py:63
  8.5 0.0 collective-permute-start.1
  8.5 0.8 collective-permute-start
  9.4 1.4 %collective-permute-done.2 = bf16[2,8192]{1,0:T(2,128)(2,1)S(1)} collective-permute-done((bf16[2,8192]{1,0:T(2,128)(2,1)}, bf16[2,8192]{1,0:T(2,128)(2,1)S(1)}, u32[]{:S(2)}, u32[]{:S(2)}) %collective-permute-start.2) | collective-permute-done | bytes 32800 | tf_op jit(solution)/shard_map/ppermute | solution.py:63
  10.7 6.1 %collective-permute-done.1 = bf16[2,8192]{1,0:T(2,128)(2,1)S(1)} collective-permute-done((bf16[2,8192]{1,0:T(2,128)(2,1)}, bf16[2,8192]{1,0:T(2,128)(2,1)S(1)}, u32[]{:S(2)}, u32[]{:S(2)}) %collective-permute-start.1) | collective-permute-done | bytes 32800 | tf_op jit(solution)/shard_map/ppermute | solution.py:63
  16.8 0.0 collective-permute-done
  16.8 0.9 pad_maximum_fusion
  17.8 0.9 collective-permute-start.5
  18.7 1.0 collective-permute-start.4
  19.7 2.2 %collective-permute-start.3 = (bf16[8,8192]{1,0:T(8,128)(2,1)S(1)}, bf16[8,8192]{1,0:T(8,128)(2,1)S(1)}, u32[]{:S(2)}, u32[]{:S(2)}) collective-permute-start(bf16[8,8192]{1,0:T(8,128)(2,1)S(1)} %pad_maximum_fusion), channel_id=1, source_target_pairs={{0,14},{2,0},{4,2},{6,4},{8,6},{10,8},{12,10},{14,12},{16,208},{18... | collective-permute-start | bytes 393224 | tf_op jit(solution)/shard_map/ppermute | solution.py:63
  21.9 3.3 %collective-permute-done.5 = bf16[8,8192]{1,0:T(8,128)(2,1)S(1)} collective-permute-done((bf16[8,8192]{1,0:T(8,128)(2,1)S(1)}, bf16[8,8192]{1,0:T(8,128)(2,1)S(1)}, u32[]{:S(2)}, u32[]{:S(2)}) %collective-permute-start.5) | collective-permute-done | bytes 131104 | tf_op jit(solution)/shard_map/ppermute | solution.py:63
  25.2 0.0 collective-permute-done.4
  25.2 0.6 collective-permute-done.3
  25.8 1.0 concatenate.8.p0
  26.8 3.3 %collective-permute-start.8 = (bf16[32,8192]{1,0:T(8,128)(2,1)S(1)}, bf16[32,8192]{1,0:T(8,128)(2,1)S(1)}, u32[]{:S(2)}, u32[]{:S(2)}) collective-permute-start(bf16[32,8192]{1,0:T(8,128)(2,1)S(1)} %concatenate.8.p0), channel_id=1, source_target_pairs={{0,128},{2,130},{4,132},{6,134},{8,136},{10,138},{12,140},{14,142}... | collective-permute-start | bytes 1572872 | tf_op jit(solution)/shard_map/ppermute | solution.py:63
  30.0 0.7 collective-permute-start.7
  30.7 2.6 %collective-permute-start.6 = (bf16[32,8192]{1,0:T(8,128)(2,1)S(1)}, bf16[32,8192]{1,0:T(8,128)(2,1)S(1)}, u32[]{:S(2)}, u32[]{:S(2)}) collective-permute-start(bf16[32,8192]{1,0:T(8,128)(2,1)S(1)} %concatenate.8.p0), channel_id=1, source_target_pairs={{0,192},{2,194},{4,196},{6,198},{8,200},{10,202},{12,204},{14,206}... | collective-permute-start | bytes 1572872 | tf_op jit(solution)/shard_map/ppermute | solution.py:63
  33.3 0.1 stack.23.at_ref
  33.4 0.7 copy-done.1
  34.0 6.8 %target.1 = (bf16[128,8192]{1,0:T(8,128)(2,1)}, bf16[128,8192]{1,0:T(8,128)(2,1)}) custom-call(s32[5]{0:T(128)S(1)} %stack.23.at_ref, s32[1,256]{1,0:T(1,128)S(1)} %bitcast.7, bf16[8192,512]{1,0:T(8,128)(2,1)} %w_ref.3), custom_call_target="tpu_custom_call" | custom-call | flops 2147483648 | bytes 12582912 | tf_op jit(solution)/shard_map/target/pallas_call | solution.py:242
  40.8 0.1 collective-permute-start.9
  40.9 0.0 collective-permute-done.8.p3
  40.9 0.5 collective-permute-start.12
  41.4 1.7 %collective-permute-done.7.p2 = bf16[32,8192]{1,0:T(8,128)(2,1)S(1)} collective-permute-done((bf16[32,8192]{1,0:T(8,128)(2,1)S(1)}, bf16[32,8192]{1,0:T(8,128)(2,1)S(1)}, u32[]{:S(2)}, u32[]{:S(2)}) %collective-permute-start.7) | collective-permute-done | bytes 524320 | tf_op jit(solution)/shard_map/ppermute | solution.py:63
  43.2 0.0 collective-permute-start.11
  43.2 0.4 collective-permute-done.6.p1
  43.5 1.5 %collective-permute-start.10 = (bf16[32,8192]{1,0:T(8,128)(2,1)S(1)}, bf16[32,8192]{1,0:T(8,128)(2,1)S(1)}, u32[]{:S(2)}, u32[]{:S(2)}) collective-permute-start(bf16[32,8192]{1,0:T(8,128)(2,1)S(1)} %collective-permute-done.6.p1), channel_id=1, source_target_pairs={{0,16},{2,18},{4,20},{6,22},{8,24},{10,26},{12,28},{14,30},{16,0},... | collective-permute-start | bytes 1572872 | tf_op jit(solution)/shard_map/ppermute | solution.py:63
  45.0 0.1 collective-permute-done.11.p6
  45.1 1.5 %collective-permute-done.10.p5 = bf16[32,8192]{1,0:T(8,128)(2,1)S(1)} collective-permute-done((bf16[32,8192]{1,0:T(8,128)(2,1)S(1)}, bf16[32,8192]{1,0:T(8,128)(2,1)S(1)}, u32[]{:S(2)}, u32[]{:S(2)}) %collective-permute-start.10) | collective-permute-done | bytes 524320 | tf_op jit(solution)/shard_map/ppermute | solution.py:63
  46.5 3.1 %logits.1 = (f32[3,128]{1,0:T(4,128)S(1)}, f32[3,128]{1,0:T(4,128)S(1)}, bf16[256,512]{1,0:T(8,128)(2,1)S(1)}) custom-call(s32[5]{0:T(128)S(1)} %stack.23.at_ref, s32[1,256]{1,0:T(1,128)S(1)} %bitcast.8, bf16[32,8192]{1,0:T(8,128)(2,1)S(1)} %concatenate.8.p0, bf16[32,8192]{1,0:T(8,128)(2,1)S(1)} %collective-permute-done.6.p1, ...), custom_call_target="tpu_custom_call" | custom-call | flops 2147483648 | bytes 13631488 | tf_op jit(solution)/shard_map/logits/pallas_call | solution.py:256
  49.7 0.6 collective-permute-start.15
  50.3 0.2 collective-permute-start.13
  50.5 1.5 %collective-permute-start.14 = (f32[3,128]{1,0:T(4,128)S(1)}, f32[3,128]{1,0:T(4,128)S(1)}, u32[]{:S(2)}, u32[]{:S(2)}) collective-permute-start(f32[3,128]{1,0:T(4,128)S(1)} %get-tuple-element.23.own_ref), channel_id=1, source_target_pairs={{0,32},{2,34},{4,36},{6,38},{8,40},{10,42},{12,44},{14,46},{16,48}... | collective-permute-start | bytes 4616 | tf_op jit(solution)/shard_map/ppermute | solution.py:63
  52.0 3.4 %soft.1 = (f32[128,8192]{1,0:T(8,128)}, bf16[128,8192]{1,0:T(8,128)(2,1)}) custom-call(bf16[256,512]{1,0:T(8,128)(2,1)S(1)} %get-tuple-element.25.soft_ref, bf16[8192,512]{1,0:T(8,128)(2,1)S(1)} %copy-done), custom_call_target="tpu_custom_call" | custom-call | flops 2147483648 | bytes 14680064 | tf_op jit(solution)/shard_map/soft/pallas_call | solution.py:265
  55.4 0.0 collective-permute-done.15.both_ref
  55.4 0.0 collective-permute-done.14.x_ref
  55.4 0.2 collective-permute-start.16
  55.6 0.4 collective-permute-start.17
  56.0 17.6 %all_to_all.5.spread_ref = f32[32,3,128]{2,1,0:T(4,128)S(1)} all-to-all(f32[32,3,128]{2,1,0:T(4,128)S(1)} %merge.1), channel_id=1, replica_groups=mesh['y'=4,'x'=2,'c'=2,'z'=8,'dp'=2] {'y','z'}, dimensions={0} | all-to-all | bytes 98304 | tf_op jit(solution)/shard_map/all_to_all | solution.py:286
  73.7 0.0 collective-permute-done.16.refs_1_
  73.7 0.0 collective-permute-done.17.refs_3_
  73.7 3.4 %combine.2 = (f32[128,128]{1,0:T(8,128)S(1)}, bf16[32,8192]{1,0:T(8,128)(2,1)S(1)}, bf16[32,8192]{1,0:T(8,128)(2,1)S(1)}, bf16[32,8192]{1,0:T(8,128)(2,1)S(1)}) custom-call(s32[5]{0:T(128)S(1)} %stack.23.at_ref, f32[1,256]{1,0:T(1,128)S(1)} %bitcast.9, f32[3,128]{1,0:T(4,128)S(1)} %get-tuple-element.23.own_ref, ...), custom_call_target="tpu_custom_call" | custom-call | flops 4718592 | bytes 9437184 | tf_op jit(solution)/shard_map/combine/pallas_call | solution.py:295
  77.1 1.4 %collective-permute-start.18 = (bf16[32,8192]{1,0:T(8,128)(2,1)S(1)}, bf16[32,8192]{1,0:T(8,128)(2,1)S(1)}, u32[]{:S(2)}, u32[]{:S(2)}) collective-permute-start(bf16[32,8192]{1,0:T(8,128)(2,1)S(1)} %get-tuple-element.34), channel_id=1, source_target_pairs={{0,128},{2,130},{4,132},{6,134},{8,136},{10,138},{12,140},{14,142}... | collective-permute-start | bytes 1572872 | tf_op jit(solution)/shard_map/ppermute | solution.py:63
  78.5 0.7 collective-permute-start.19
  79.2 2.5 %collective-permute-start.20 = (bf16[32,8192]{1,0:T(8,128)(2,1)S(1)}, bf16[32,8192]{1,0:T(8,128)(2,1)S(1)}, u32[]{:S(2)}, u32[]{:S(2)}) collective-permute-start(bf16[32,8192]{1,0:T(8,128)(2,1)S(1)} %get-tuple-element.36), channel_id=1, source_target_pairs={{0,192},{2,194},{4,196},{6,198},{8,200},{10,202},{12,204},{14,206}... | collective-permute-start | bytes 1572872 | tf_op jit(solution)/shard_map/ppermute | solution.py:63
  81.7 1.8 %combine.3 = f32[32,8192]{1,0:T(8,128)S(1)} custom-call(f32[128,128]{1,0:T(8,128)S(1)} %get-tuple-element.33.scales_ref, f32[128,8192]{1,0:T(8,128)} %get-tuple-element.29.refs_0_, bf16[128,8192]{1,0:T(8,128)(2,1)S(1)} %collective-permute-done.16.refs_1_, bf16[128,8192]{1,0:T(8,128)(2,1)} %get-tuple-element.31.refs_2_, ...), custom_call_target="tpu_custom_call" | custom-call | flops 1572864 | bytes 3145728 | tf_op jit(solution)/shard_map/combine/pallas_call | solution.py:295
  83.5 4.4 %collective-permute-done.18 = bf16[32,8192]{1,0:T(8,128)(2,1)S(1)} collective-permute-done((bf16[32,8192]{1,0:T(8,128)(2,1)S(1)}, bf16[32,8192]{1,0:T(8,128)(2,1)S(1)}, u32[]{:S(2)}, u32[]{:S(2)}) %collective-permute-start.18) | collective-permute-done | bytes 524320 | tf_op jit(solution)/shard_map/ppermute | solution.py:63
  87.9 5.5 %collective-permute-done.19 = bf16[32,8192]{1,0:T(8,128)(2,1)S(1)} collective-permute-done((bf16[32,8192]{1,0:T(8,128)(2,1)S(1)}, bf16[32,8192]{1,0:T(8,128)(2,1)S(1)}, u32[]{:S(2)}, u32[]{:S(2)}) %collective-permute-start.19) | collective-permute-done | bytes 524320 | tf_op jit(solution)/shard_map/ppermute | solution.py:63
  93.4 0.2 fusion.3
  93.7 1.3 %collective-permute-start.21 = (bf16[8,8192]{1,0:T(8,128)(2,1)S(1)}, bf16[8,8192]{1,0:T(8,128)(2,1)S(1)}, u32[]{:S(2)}, u32[]{:S(2)}) collective-permute-start(bf16[8,8192]{1,0:T(8,128)(2,1)S(1)} %get-tuple-element.43), channel_id=1, source_target_pairs={{0,4},{2,6},{4,8},{6,10},{8,12},{10,14},{12,0},{14,2},{16,144},{18... | collective-permute-start | bytes 393224 | tf_op jit(solution)/shard_map/ppermute | solution.py:63
  95.0 2.6 %collective-permute-start.23 = (bf16[8,8192]{1,0:T(8,128)(2,1)S(1)}, bf16[8,8192]{1,0:T(8,128)(2,1)S(1)}, u32[]{:S(2)}, u32[]{:S(2)}) collective-permute-start(bf16[8,8192]{1,0:T(8,128)(2,1)S(1)} %get-tuple-element.44), channel_id=1, source_target_pairs={{0,14},{2,0},{4,2},{6,4},{8,6},{10,8},{12,10},{14,12},{16,208},{18... | collective-permute-start | bytes 393224 | tf_op jit(solution)/shard_map/ppermute | solution.py:63
  97.6 0.2 slice_reduce_fusion
  97.8 4.1 %collective-permute-done.21 = bf16[8,8192]{1,0:T(8,128)(2,1)S(1)} collective-permute-done((bf16[8,8192]{1,0:T(8,128)(2,1)S(1)}, bf16[8,8192]{1,0:T(8,128)(2,1)S(1)}, u32[]{:S(2)}, u32[]{:S(2)}) %collective-permute-start.21) | collective-permute-done | bytes 131104 | tf_op jit(solution)/shard_map/ppermute | solution.py:63
  101.9 1.8 %collective-permute-done.22 = bf16[8,8192]{1,0:T(8,128)(2,1)S(1)} collective-permute-done((bf16[8,8192]{1,0:T(8,128)(2,1)S(1)}, bf16[8,8192]{1,0:T(8,128)(2,1)S(1)}, u32[]{:S(2)}, u32[]{:S(2)}) %collective-permute-start.22) | collective-permute-done | bytes 131104 | tf_op jit(solution)/shard_map/ppermute | solution.py:63
  103.8 0.1 fusion.2
  103.8 0.1 fusion.5
  103.9 1.8 %collective-permute-start.24 = (bf16[2,8192]{1,0:T(2,128)(2,1)S(1)}, bf16[2,8192]{1,0:T(2,128)(2,1)S(1)}, u32[]{:S(2)}, u32[]{:S(2)}) collective-permute-start(bf16[2,8192]{1,0:T(2,128)(2,1)S(1)} %get-tuple-element.46), channel_id=1, source_target_pairs={{0,40},{2,42},{4,44},{6,46},{8,32},{10,34},{12,36},{14,38},{16,56}... | collective-permute-start | bytes 98312 | tf_op jit(solution)/shard_map/ppermute | solution.py:63
  105.7 4.6 %collective-permute-start.25 = (bf16[2,8192]{1,0:T(2,128)(2,1)S(1)}, bf16[2,8192]{1,0:T(2,128)(2,1)S(1)}, u32[]{:S(2)}, u32[]{:S(2)}) collective-permute-start(bf16[2,8192]{1,0:T(2,128)(2,1)S(1)} %get-tuple-element.47), channel_id=1, source_target_pairs={{0,8},{2,10},{4,12},{6,14},{8,0},{10,2},{12,4},{14,6},{16,24},{18,... | collective-permute-start | bytes 98312 | tf_op jit(solution)/shard_map/ppermute | solution.py:63
  110.4 1.1 collective-permute-start.26
  111.5 0.5 multiply_multiply_fusion
  112.0 1.1 collective-permute-done.24
  113.2 0.4 collective-permute-done.25
  113.6 1.5 %collective-permute-done.26 = f32[2,8192]{1,0:T(2,128)S(1)} collective-permute-done((f32[2,8192]{1,0:T(2,128)S(1)}, f32[2,8192]{1,0:T(2,128)S(1)}, u32[]{:S(2)}, u32[]{:S(2)}) %collective-permute-start.26) | collective-permute-done | bytes 65568 | tf_op jit(solution)/shard_map/ppermute | solution.py:63
  115.1 0.7 fusion.1
  (16 shorter events, 0.1 us)
Async XLA Ops:
  0.6 10.1 %collective-permute-start.2 = (bf16[2,8192]{1,0:T(2,128)(2,1)}, bf16[2,8192]{1,0:T(2,128)(2,1)S(1)}, u32[]{:S(2)}, u32[]{:S(2)}) collective-permute-start(bf16[2,8192]{1,0:T(2,128)(2,1)} %param.4), channel_id=1, source_target_pairs={{0,40},{2,42},{4,44},{6,46},{8,32},{10,34},{12,36},{14,38},{16,56}... | collective-permute-start | bytes 98312 | tf_op jit(solution)/shard_map/ppermute | solution.py:63
  8.5 8.3 %collective-permute-start.1 = (bf16[2,8192]{1,0:T(2,128)(2,1)}, bf16[2,8192]{1,0:T(2,128)(2,1)S(1)}, u32[]{:S(2)}, u32[]{:S(2)}) collective-permute-start(bf16[2,8192]{1,0:T(2,128)(2,1)} %param.4), channel_id=1, source_target_pairs={{0,8},{2,10},{4,12},{6,14},{8,0},{10,2},{12,4},{14,6},{16,24},{18,... | collective-permute-start | bytes 98312 | tf_op jit(solution)/shard_map/ppermute | solution.py:63
  8.5 8.3 %collective-permute-start = (bf16[2,8192]{1,0:T(2,128)(2,1)}, bf16[2,8192]{1,0:T(2,128)(2,1)S(1)}, u32[]{:S(2)}, u32[]{:S(2)}) collective-permute-start(bf16[2,8192]{1,0:T(2,128)(2,1)} %param.4), channel_id=1, source_target_pairs={{0,32},{2,34},{4,36},{6,38},{8,40},{10,42},{12,44},{14,46},{16,48}... | collective-permute-start | bytes 98312 | tf_op jit(solution)/shard_map/ppermute | solution.py:63
  17.8 7.5 %collective-permute-start.5 = (bf16[8,8192]{1,0:T(8,128)(2,1)S(1)}, bf16[8,8192]{1,0:T(8,128)(2,1)S(1)}, u32[]{:S(2)}, u32[]{:S(2)}) collective-permute-start(bf16[8,8192]{1,0:T(8,128)(2,1)S(1)} %pad_maximum_fusion), channel_id=1, source_target_pairs={{0,12},{2,14},{4,0},{6,2},{8,4},{10,6},{12,8},{14,10},{16,144},{18... | collective-permute-start | bytes 393224 | tf_op jit(solution)/shard_map/ppermute | solution.py:63
  18.7 6.5 %collective-permute-start.4 = (bf16[8,8192]{1,0:T(8,128)(2,1)S(1)}, bf16[8,8192]{1,0:T(8,128)(2,1)S(1)}, u32[]{:S(2)}, u32[]{:S(2)}) collective-permute-start(bf16[8,8192]{1,0:T(8,128)(2,1)S(1)} %pad_maximum_fusion), channel_id=1, source_target_pairs={{0,2},{2,4},{4,6},{6,8},{8,10},{10,12},{12,14},{14,0},{16,80},{18,... | collective-permute-start | bytes 393224 | tf_op jit(solution)/shard_map/ppermute | solution.py:63
  19.7 6.1 %collective-permute-start.3 = (bf16[8,8192]{1,0:T(8,128)(2,1)S(1)}, bf16[8,8192]{1,0:T(8,128)(2,1)S(1)}, u32[]{:S(2)}, u32[]{:S(2)}) collective-permute-start(bf16[8,8192]{1,0:T(8,128)(2,1)S(1)} %pad_maximum_fusion), channel_id=1, source_target_pairs={{0,14},{2,0},{4,2},{6,4},{8,6},{10,8},{12,10},{14,12},{16,208},{18... | collective-permute-start | bytes 393224 | tf_op jit(solution)/shard_map/ppermute | solution.py:63
  26.8 14.1 %collective-permute-start.8 = (bf16[32,8192]{1,0:T(8,128)(2,1)S(1)}, bf16[32,8192]{1,0:T(8,128)(2,1)S(1)}, u32[]{:S(2)}, u32[]{:S(2)}) collective-permute-start(bf16[32,8192]{1,0:T(8,128)(2,1)S(1)} %concatenate.8.p0), channel_id=1, source_target_pairs={{0,128},{2,130},{4,132},{6,134},{8,136},{10,138},{12,140},{14,142}... | collective-permute-start | bytes 1572872 | tf_op jit(solution)/shard_map/ppermute | solution.py:63
  30.0 13.1 %collective-permute-start.7 = (bf16[32,8192]{1,0:T(8,128)(2,1)S(1)}, bf16[32,8192]{1,0:T(8,128)(2,1)S(1)}, u32[]{:S(2)}, u32[]{:S(2)}) collective-permute-start(bf16[32,8192]{1,0:T(8,128)(2,1)S(1)} %concatenate.8.p0), channel_id=1, source_target_pairs={{0,64},{2,66},{4,68},{6,70},{8,72},{10,74},{12,76},{14,78},{16,18}... | collective-permute-start | bytes 1572872 | tf_op jit(solution)/shard_map/ppermute | solution.py:63
  30.7 12.8 %collective-permute-start.6 = (bf16[32,8192]{1,0:T(8,128)(2,1)S(1)}, bf16[32,8192]{1,0:T(8,128)(2,1)S(1)}, u32[]{:S(2)}, u32[]{:S(2)}) collective-permute-start(bf16[32,8192]{1,0:T(8,128)(2,1)S(1)} %concatenate.8.p0), channel_id=1, source_target_pairs={{0,192},{2,194},{4,196},{6,198},{8,200},{10,202},{12,204},{14,206}... | collective-permute-start | bytes 1572872 | tf_op jit(solution)/shard_map/ppermute | solution.py:63
  33.4 0.7 copy-start.1
  34.0 12.5 %copy-start = (bf16[8192,512]{1,0:T(8,128)(2,1)S(1)}, bf16[8192,512]{1,0:T(8,128)(2,1)}, u32[]{:S(2)}) copy-start(bf16[8192,512]{1,0:T(8,128)(2,1)} %w_ref.3) | copy-start | bytes 25165828
  40.8 4.2 %collective-permute-start.9 = (bf16[32,8192]{1,0:T(8,128)(2,1)S(1)}, bf16[32,8192]{1,0:T(8,128)(2,1)S(1)}, u32[]{:S(2)}, u32[]{:S(2)}) collective-permute-start(bf16[32,8192]{1,0:T(8,128)(2,1)S(1)} %concatenate.8.p0), channel_id=1, source_target_pairs={{0,16},{2,18},{4,20},{6,22},{8,24},{10,26},{12,28},{14,30},{16,0},... | collective-permute-start | bytes 1572872 | tf_op jit(solution)/shard_map/ppermute | solution.py:63
  40.9 4.1 %collective-permute-start.12 = (bf16[32,8192]{1,0:T(8,128)(2,1)S(1)}, bf16[32,8192]{1,0:T(8,128)(2,1)S(1)}, u32[]{:S(2)}, u32[]{:S(2)}) collective-permute-start(bf16[32,8192]{1,0:T(8,128)(2,1)S(1)} %collective-permute-done.8.p3), channel_id=1, source_target_pairs={{0,16},{2,18},{4,20},{6,22},{8,24},{10,26},{12,28},{14,30},{16,0},... | collective-permute-start | bytes 1572872 | tf_op jit(solution)/shard_map/ppermute | solution.py:63
  43.2 1.9 %collective-permute-start.11 = (bf16[32,8192]{1,0:T(8,128)(2,1)S(1)}, bf16[32,8192]{1,0:T(8,128)(2,1)S(1)}, u32[]{:S(2)}, u32[]{:S(2)}) collective-permute-start(bf16[32,8192]{1,0:T(8,128)(2,1)S(1)} %collective-permute-done.7.p2), channel_id=1, source_target_pairs={{0,16},{2,18},{4,20},{6,22},{8,24},{10,26},{12,28},{14,30},{16,0},... | collective-permute-start | bytes 1572872 | tf_op jit(solution)/shard_map/ppermute | solution.py:63
  43.5 3.0 %collective-permute-start.10 = (bf16[32,8192]{1,0:T(8,128)(2,1)S(1)}, bf16[32,8192]{1,0:T(8,128)(2,1)S(1)}, u32[]{:S(2)}, u32[]{:S(2)}) collective-permute-start(bf16[32,8192]{1,0:T(8,128)(2,1)S(1)} %collective-permute-done.6.p1), channel_id=1, source_target_pairs={{0,16},{2,18},{4,20},{6,22},{8,24},{10,26},{12,28},{14,30},{16,0},... | collective-permute-start | bytes 1572872 | tf_op jit(solution)/shard_map/ppermute | solution.py:63
  49.7 5.7 %collective-permute-start.15 = (f32[3,128]{1,0:T(4,128)S(1)}, f32[3,128]{1,0:T(4,128)S(1)}, u32[]{:S(2)}, u32[]{:S(2)}) collective-permute-start(f32[3,128]{1,0:T(4,128)S(1)} %get-tuple-element.24), channel_id=1, source_target_pairs={{0,48},{2,50},{4,52},{6,54},{8,56},{10,58},{12,60},{14,62},{16,32}... | collective-permute-start | bytes 4616 | tf_op jit(solution)/shard_map/ppermute | solution.py:63
  50.3 5.0 %collective-permute-start.13 = (f32[3,128]{1,0:T(4,128)S(1)}, f32[3,128]{1,0:T(4,128)S(1)}, u32[]{:S(2)}, u32[]{:S(2)}) collective-permute-start(f32[3,128]{1,0:T(4,128)S(1)} %get-tuple-element.24), channel_id=1, source_target_pairs={{0,16},{2,18},{4,20},{6,22},{8,24},{10,26},{12,28},{14,30},{16,0},... | collective-permute-start | bytes 4616 | tf_op jit(solution)/shard_map/ppermute | solution.py:63
  50.5 4.9 %collective-permute-start.14 = (f32[3,128]{1,0:T(4,128)S(1)}, f32[3,128]{1,0:T(4,128)S(1)}, u32[]{:S(2)}, u32[]{:S(2)}) collective-permute-start(f32[3,128]{1,0:T(4,128)S(1)} %get-tuple-element.23.own_ref), channel_id=1, source_target_pairs={{0,32},{2,34},{4,36},{6,38},{8,40},{10,42},{12,44},{14,46},{16,48}... | collective-permute-start | bytes 4616 | tf_op jit(solution)/shard_map/ppermute | solution.py:63
  52.0 3.6 %copy-start.3 = (bf16[128,8192]{1,0:T(8,128)(2,1)S(1)}, bf16[128,8192]{1,0:T(8,128)(2,1)}, u32[]{:S(2)}) copy-start(bf16[128,8192]{1,0:T(8,128)(2,1)} %get-tuple-element.32) | copy-start | bytes 6291460
  52.0 21.7 %copy-start.2 = (f32[256]{0:T(256)S(1)}, f32[256]{0:T(256)}, u32[]{:S(2)}) copy-start(f32[256]{0:T(256)} %param.7) | copy-start | bytes 3076
  55.4 18.2 %collective-permute-start.16 = (bf16[128,8192]{1,0:T(8,128)(2,1)}, bf16[128,8192]{1,0:T(8,128)(2,1)S(1)}, u32[]{:S(2)}, u32[]{:S(2)}) collective-permute-start(bf16[128,8192]{1,0:T(8,128)(2,1)} %get-tuple-element.30), channel_id=1, source_target_pairs={{0,16},{2,18},{4,20},{6,22},{8,24},{10,26},{12,28},{14,30},{16,0},... | collective-permute-start | bytes 6291464 | tf_op jit(solution)/shard_map/ppermute | solution.py:63
  55.6 18.1 %collective-permute-start.17 = (bf16[128,8192]{1,0:T(8,128)(2,1)S(1)}, bf16[128,8192]{1,0:T(8,128)(2,1)S(1)}, u32[]{:S(2)}, u32[]{:S(2)}) collective-permute-start(bf16[128,8192]{1,0:T(8,128)(2,1)S(1)} %copy-done.3), channel_id=1, source_target_pairs={{0,16},{2,18},{4,20},{6,22},{8,24},{10,26},{12,28},{14,30},{16,0},... | collective-permute-start | bytes 6291464 | tf_op jit(solution)/shard_map/ppermute | solution.py:63
  77.1 10.9 %collective-permute-start.18 = (bf16[32,8192]{1,0:T(8,128)(2,1)S(1)}, bf16[32,8192]{1,0:T(8,128)(2,1)S(1)}, u32[]{:S(2)}, u32[]{:S(2)}) collective-permute-start(bf16[32,8192]{1,0:T(8,128)(2,1)S(1)} %get-tuple-element.34), channel_id=1, source_target_pairs={{0,128},{2,130},{4,132},{6,134},{8,136},{10,138},{12,140},{14,142}... | collective-permute-start | bytes 1572872 | tf_op jit(solution)/shard_map/ppermute | solution.py:63
  78.5 15.0 %collective-permute-start.19 = (bf16[32,8192]{1,0:T(8,128)(2,1)S(1)}, bf16[32,8192]{1,0:T(8,128)(2,1)S(1)}, u32[]{:S(2)}, u32[]{:S(2)}) collective-permute-start(bf16[32,8192]{1,0:T(8,128)(2,1)S(1)} %get-tuple-element.35), channel_id=1, source_target_pairs={{0,64},{2,66},{4,68},{6,70},{8,72},{10,74},{12,76},{14,78},{16,18}... | collective-permute-start | bytes 1572872 | tf_op jit(solution)/shard_map/ppermute | solution.py:63
  79.2 14.3 %collective-permute-start.20 = (bf16[32,8192]{1,0:T(8,128)(2,1)S(1)}, bf16[32,8192]{1,0:T(8,128)(2,1)S(1)}, u32[]{:S(2)}, u32[]{:S(2)}) collective-permute-start(bf16[32,8192]{1,0:T(8,128)(2,1)S(1)} %get-tuple-element.36), channel_id=1, source_target_pairs={{0,192},{2,194},{4,196},{6,198},{8,200},{10,202},{12,204},{14,206}... | collective-permute-start | bytes 1572872 | tf_op jit(solution)/shard_map/ppermute | solution.py:63
  93.7 8.2 %collective-permute-start.21 = (bf16[8,8192]{1,0:T(8,128)(2,1)S(1)}, bf16[8,8192]{1,0:T(8,128)(2,1)S(1)}, u32[]{:S(2)}, u32[]{:S(2)}) collective-permute-start(bf16[8,8192]{1,0:T(8,128)(2,1)S(1)} %get-tuple-element.43), channel_id=1, source_target_pairs={{0,4},{2,6},{4,8},{6,10},{8,12},{10,14},{12,0},{14,2},{16,144},{18... | collective-permute-start | bytes 393224 | tf_op jit(solution)/shard_map/ppermute | solution.py:63
  95.0 7.0 %collective-permute-start.23 = (bf16[8,8192]{1,0:T(8,128)(2,1)S(1)}, bf16[8,8192]{1,0:T(8,128)(2,1)S(1)}, u32[]{:S(2)}, u32[]{:S(2)}) collective-permute-start(bf16[8,8192]{1,0:T(8,128)(2,1)S(1)} %get-tuple-element.44), channel_id=1, source_target_pairs={{0,14},{2,0},{4,2},{6,4},{8,6},{10,8},{12,10},{14,12},{16,208},{18... | collective-permute-start | bytes 393224 | tf_op jit(solution)/shard_map/ppermute | solution.py:63
  97.6 6.2 %collective-permute-start.22 = (bf16[8,8192]{1,0:T(8,128)(2,1)S(1)}, bf16[8,8192]{1,0:T(8,128)(2,1)S(1)}, u32[]{:S(2)}, u32[]{:S(2)}) collective-permute-start(bf16[8,8192]{1,0:T(8,128)(2,1)S(1)} %get-tuple-element.45), channel_id=1, source_target_pairs={{0,2},{2,4},{4,6},{6,8},{8,10},{10,12},{12,14},{14,0},{16,80},{18,... | collective-permute-start | bytes 393224 | tf_op jit(solution)/shard_map/ppermute | solution.py:63
  103.9 9.3 %collective-permute-start.24 = (bf16[2,8192]{1,0:T(2,128)(2,1)S(1)}, bf16[2,8192]{1,0:T(2,128)(2,1)S(1)}, u32[]{:S(2)}, u32[]{:S(2)}) collective-permute-start(bf16[2,8192]{1,0:T(2,128)(2,1)S(1)} %get-tuple-element.46), channel_id=1, source_target_pairs={{0,40},{2,42},{4,44},{6,46},{8,32},{10,34},{12,36},{14,38},{16,56}... | collective-permute-start | bytes 98312 | tf_op jit(solution)/shard_map/ppermute | solution.py:63
  105.7 7.9 %collective-permute-start.25 = (bf16[2,8192]{1,0:T(2,128)(2,1)S(1)}, bf16[2,8192]{1,0:T(2,128)(2,1)S(1)}, u32[]{:S(2)}, u32[]{:S(2)}) collective-permute-start(bf16[2,8192]{1,0:T(2,128)(2,1)S(1)} %get-tuple-element.47), channel_id=1, source_target_pairs={{0,8},{2,10},{4,12},{6,14},{8,0},{10,2},{12,4},{14,6},{16,24},{18,... | collective-permute-start | bytes 98312 | tf_op jit(solution)/shard_map/ppermute | solution.py:63
  110.4 4.7 %collective-permute-start.26 = (f32[2,8192]{1,0:T(2,128)S(1)}, f32[2,8192]{1,0:T(2,128)S(1)}, u32[]{:S(2)}, u32[]{:S(2)}) collective-permute-start(f32[2,8192]{1,0:T(2,128)S(1)} %slice.56), channel_id=1, source_target_pairs={{0,32},{2,34},{4,36},{6,38},{8,40},{10,42},{12,44},{14,46},{16,48}... | collective-permute-start | bytes 196616 | tf_op jit(solution)/shard_map/ppermute | solution.py:63

commit v13 on v12

--- a/solution.py
+++ b/solution.py
@@ -71,7 +71,7 @@
     y, x, c, z = (at_ref[i] for i in range(4))
     at = lax.broadcasted_iota(jnp.int32, (ROWS, 1), 0)
     r, near, q1, q2, cr = at & 1, (at >> 1) & 3, (at >> 3) & 3, (at >> 5) & 3, at >> 7
-    xr, z4 = near & 1, near >> 1
+    xr, z4 = (near ^ (near >> 1)) & 1, near >> 1
     o1 = jnp.where(q1 == 2, -1, jnp.where(q1 == 3, 2, q1))
     o2 = jnp.where(q2 == 2, -1, jnp.where(q2 == 3, 2, q2))
     core = c ^ cr
@@ -226,6 +226,10 @@
     combine_end(parts, combine_start(parts, sources, buffers, sems), scales_ref, buffers, outs)
 
 
+def join_kernel(a_ref, b_ref, c_ref, d_ref, out_ref):
+    out_ref[...] = jnp.concatenate([r[...] for r in (a_ref, b_ref, c_ref, d_ref)], axis=0)
+
+
 def shards(hidden, lm_weight, targets, loss_grad):
     half = ROWS // 2
     at = jnp.stack([lax.axis_index(a) for a in GROUP] + [lax.axis_index(GROUP) * WIDTH])
@@ -234,8 +238,15 @@
     weights = [pltpu.VMEM((DEPTH, WIDTH), BF)]
     sems = pltpu.SemaphoreType.DMA((STEPS,))
 
-    block = jnp.concatenate([hidden] + [send(hidden, to) for to in (to_x, to_z4, to_xz4)])
-    block = jnp.concatenate([block] + [send(block, to_first(-o)) for o in OFFSETS[1:]])
+    block = jnp.concatenate([hidden] + [send(hidden, to) for to in (to_x, to_xz4, to_z4)])
+    block = pl.pallas_call(
+        join_kernel,
+        out_shape=jax.ShapeDtypeStruct((32, DEPTH), BF),
+        in_specs=[VMEM] * 4,
+        out_specs=VMEM,
+        compiler_params=params(),
+        name="join",
+    )(block, *(send(block, to_first(-o)) for o in OFFSETS[1:]))
     near, back, far = (send(block, to_second(-o)) for o in OFFSETS[1:])
 
     aim, _ = lax.optimization_barrier((targets, block))
@@ -313,7 +324,7 @@
     part = combine((0,), F32, rows=(scales,))[0] + sum(arrived)
     part = part.reshape(4, 8, DEPTH)
     part = part[0] + sum(send(part[k].astype(BF), to_first(OFFSETS[k])).astype(F32) for k in (3, 1, 2))
-    moved = [send(part[2 * k : 2 * k + 2].astype(BF), to).astype(F32) for k, to in ((3, to_xz4), (2, to_z4))]
+    moved = [send(part[2 * k : 2 * k + 2].astype(BF), to).astype(F32) for k, to in ((2, to_xz4), (3, to_z4))]
     part = [part[0:2], *moved, send(part[2:4], to_x)]
     part = (part[0] + part[1]) + (part[2] + part[3])
     return ce_loss, z_term, part.astype(BF)

time: 117 us -> 122 us (1.043)
  blocking collectives: 17.6 us -> 23 us
    all_to_all x1, blocking collectives: 17.6 us -> 23 us  [shards(): spread = lax.all_to_all(merged, ('y', 'z'), 0, 0)]
where the time goes in v13:
time: 122 us; the launch traced here: 120 us
  starting transfers between devices  39.3 us (32%)
  waiting for transfers between devices  35.1 us (29%)
  blocking collectives  23 us (19%)
  Pallas kernels  18.6 us (15%)
  other arithmetic  2.39 us (2%)
    ppermute x27, starting transfers between devices, send(): return lax.ppermute(value, GROUP, pairs(route))  39.3 us
    ppermute x27, waiting for transfers between devices, send(): return lax.ppermute(value, GROUP, pairs(route))  35.1 us
    all_to_all x1, blocking collectives, shards(): spread = lax.all_to_all(merged, ('y', 'z'), 0, 0)  23 us
    pallas_call x1, Pallas kernels, shards(): pl.pallas_call(target_kernel, out_shape=[pltpu.HBM((half, DEPTH), BF)] *...  6.79 us
    pallas_call x2, Pallas kernels, combine(): pl.pallas_call(functools.partial(kernel, parts), out_shape=scales + [jax....  5.17 us
    pallas_call x1, Pallas kernels, shards(): pl.pallas_call(soft_kernel, out_shape=(pltpu.HBM((half, DEPTH), F32), plt...  3.39 us
    pallas_call x1, Pallas kernels, shards(): pl.pallas_call(logits_kernel, out_shape=[jax.ShapeDtypeStruct((3, half),...  3.15 us
  transfers between devices with their start and end apart: 27, of which 15 were waited for; matrix products, arithmetic and copies ran while one was open for 1% of the time, Pallas kernels for 10%

profile of v13, /device:TPU:4, one launch (start us, length us, event | category | flops | bytes accessed | tf_op | source)
XLA Modules:
  0.0 120.3 jit_solution(16819354694004285385)
XLA Ops:
  0.6 7.9 %collective-permute-start.1 = (bf16[2,8192]{1,0:T(2,128)(2,1)}, bf16[2,8192]{1,0:T(2,128)(2,1)S(1)}, u32[]{:S(2)}, u32[]{:S(2)}) collective-permute-start(bf16[2,8192]{1,0:T(2,128)(2,1)} %param.4), channel_id=1, source_target_pairs={{0,40},{2,42},{4,44},{6,46},{8,32},{10,34},{12,36},{14,38},{16,56}... | collective-permute-start | bytes 98312 | tf_op jit(solution)/shard_map/ppermute | solution.py:63
  8.5 0.8 collective-permute-start
  9.4 0.0 collective-permute-start.2
  9.4 1.4 %collective-permute-done.1 = bf16[2,8192]{1,0:T(2,128)(2,1)S(1)} collective-permute-done((bf16[2,8192]{1,0:T(2,128)(2,1)}, bf16[2,8192]{1,0:T(2,128)(2,1)S(1)}, u32[]{:S(2)}, u32[]{:S(2)}) %collective-permute-start.1) | collective-permute-done | bytes 32800 | tf_op jit(solution)/shard_map/ppermute | solution.py:63
  10.7 1.9 %collective-permute-done = bf16[2,8192]{1,0:T(2,128)(2,1)S(1)} collective-permute-done((bf16[2,8192]{1,0:T(2,128)(2,1)}, bf16[2,8192]{1,0:T(2,128)(2,1)S(1)}, u32[]{:S(2)}, u32[]{:S(2)}) %collective-permute-start) | collective-permute-done | bytes 32800 | tf_op jit(solution)/shard_map/ppermute | solution.py:63
  12.7 4.7 %collective-permute-done.2 = bf16[2,8192]{1,0:T(2,128)(2,1)S(1)} collective-permute-done((bf16[2,8192]{1,0:T(2,128)(2,1)}, bf16[2,8192]{1,0:T(2,128)(2,1)S(1)}, u32[]{:S(2)}, u32[]{:S(2)}) %collective-permute-start.2) | collective-permute-done | bytes 32800 | tf_op jit(solution)/shard_map/ppermute | solution.py:63
  17.4 0.9 pad_maximum_fusion.a_ref
  18.3 0.1 collective-permute-start.5
  18.4 1.6 %collective-permute-start.4 = (bf16[8,8192]{1,0:T(8,128)(2,1)S(1)}, bf16[8,8192]{1,0:T(8,128)(2,1)S(1)}, u32[]{:S(2)}, u32[]{:S(2)}) collective-permute-start(bf16[8,8192]{1,0:T(8,128)(2,1)S(1)} %pad_maximum_fusion.a_ref), channel_id=1, source_target_pairs={{0,2},{2,4},{4,6},{6,8},{8,10},{10,12},{12,14},{14,0},{16,80},{18,... | collective-permute-start | bytes 393224 | tf_op jit(solution)/shard_map/ppermute | solution.py:63
  20.0 1.8 %collective-permute-start.3 = (bf16[8,8192]{1,0:T(8,128)(2,1)S(1)}, bf16[8,8192]{1,0:T(8,128)(2,1)S(1)}, u32[]{:S(2)}, u32[]{:S(2)}) collective-permute-start(bf16[8,8192]{1,0:T(8,128)(2,1)S(1)} %pad_maximum_fusion.a_ref), channel_id=1, source_target_pairs={{0,14},{2,0},{4,2},{6,4},{8,6},{10,8},{12,10},{14,12},{16,208},{18... | collective-permute-start | bytes 393224 | tf_op jit(solution)/shard_map/ppermute | solution.py:63
  21.7 4.0 %collective-permute-done.5.d_ref = bf16[8,8192]{1,0:T(8,128)(2,1)S(1)} collective-permute-done((bf16[8,8192]{1,0:T(8,128)(2,1)S(1)}, bf16[8,8192]{1,0:T(8,128)(2,1)S(1)}, u32[]{:S(2)}, u32[]{:S(2)}) %collective-permute-start.5) | collective-permute-done | bytes 131104 | tf_op jit(solution)/shard_map/ppermute | solution.py:63
  25.8 0.0 collective-permute-done.4.c_ref
  25.8 0.0 collective-permute-done.3.b_ref
  25.8 0.1 join.1.p0
  25.9 3.3 %collective-permute-start.8 = (bf16[32,8192]{1,0:T(8,128)(2,1)S(1)}, bf16[32,8192]{1,0:T(8,128)(2,1)S(1)}, u32[]{:S(2)}, u32[]{:S(2)}) collective-permute-start(bf16[32,8192]{1,0:T(8,128)(2,1)S(1)} %join.1.p0), channel_id=1, source_target_pairs={{0,128},{2,130},{4,132},{6,134},{8,136},{10,138},{12,140},{14,142}... | collective-permute-start | bytes 1572872 | tf_op jit(solution)/shard_map/ppermute | solution.py:63
  29.1 0.7 collective-permute-start.7
  29.8 2.6 %collective-permute-start.6 = (bf16[32,8192]{1,0:T(8,128)(2,1)S(1)}, bf16[32,8192]{1,0:T(8,128)(2,1)S(1)}, u32[]{:S(2)}, u32[]{:S(2)}) collective-permute-start(bf16[32,8192]{1,0:T(8,128)(2,1)S(1)} %join.1.p0), channel_id=1, source_target_pairs={{0,192},{2,194},{4,196},{6,198},{8,200},{10,202},{12,204},{14,206}... | collective-permute-start | bytes 1572872 | tf_op jit(solution)/shard_map/ppermute | solution.py:63
  32.4 0.1 stack.23.at_ref
  32.5 0.7 copy-done.1
  33.1 6.8 %target.1 = (bf16[128,8192]{1,0:T(8,128)(2,1)}, bf16[128,8192]{1,0:T(8,128)(2,1)}) custom-call(s32[5]{0:T(128)S(1)} %stack.23.at_ref, s32[1,256]{1,0:T(1,128)S(1)} %bitcast.7, bf16[8192,512]{1,0:T(8,128)(2,1)} %w_ref.3), custom_call_target="tpu_custom_call" | custom-call | flops 2147483648 | bytes 12582912 | tf_op jit(solution)/shard_map/target/pallas_call | solution.py:253
  39.9 0.1 collective-permute-start.9
  40.0 0.0 collective-permute-done.8.p3
  40.0 0.5 collective-permute-start.12
  40.5 1.7 %collective-permute-done.7.p2 = bf16[32,8192]{1,0:T(8,128)(2,1)S(1)} collective-permute-done((bf16[32,8192]{1,0:T(8,128)(2,1)S(1)}, bf16[32,8192]{1,0:T(8,128)(2,1)S(1)}, u32[]{:S(2)}, u32[]{:S(2)}) %collective-permute-start.7) | collective-permute-done | bytes 524320 | tf_op jit(solution)/shard_map/ppermute | solution.py:63
  42.2 0.0 collective-permute-start.11
  42.2 0.4 collective-permute-done.6.p1
  42.6 1.1 collective-permute-start.10
  43.7 0.4 collective-permute-done.11.p6
  44.2 1.1 collective-permute-done.10.p5
  45.3 3.1 %logits.1 = (f32[3,128]{1,0:T(4,128)S(1)}, f32[3,128]{1,0:T(4,128)S(1)}, bf16[256,512]{1,0:T(8,128)(2,1)S(1)}) custom-call(s32[5]{0:T(128)S(1)} %stack.23.at_ref, s32[1,256]{1,0:T(1,128)S(1)} %bitcast.8, bf16[32,8192]{1,0:T(8,128)(2,1)S(1)} %join.1.p0, bf16[32,8192]{1,0:T(8,128)(2,1)S(1)} %collective-permute-done.6.p1, ...), custom_call_target="tpu_custom_call" | custom-call | flops 2147483648 | bytes 13631488 | tf_op jit(solution)/shard_map/logits/pallas_call | solution.py:267
  48.4 1.3 %collective-permute-start.15 = (f32[3,128]{1,0:T(4,128)S(1)}, f32[3,128]{1,0:T(4,128)S(1)}, u32[]{:S(2)}, u32[]{:S(2)}) collective-permute-start(f32[3,128]{1,0:T(4,128)S(1)} %get-tuple-element.24), channel_id=1, source_target_pairs={{0,48},{2,50},{4,52},{6,54},{8,56},{10,58},{12,60},{14,62},{16,32}... | collective-permute-start | bytes 4616 | tf_op jit(solution)/shard_map/ppermute | solution.py:63
  49.7 0.2 collective-permute-start.13
  49.8 0.8 collective-permute-start.14
  50.7 3.4 %soft.1 = (f32[128,8192]{1,0:T(8,128)}, bf16[128,8192]{1,0:T(8,128)(2,1)}) custom-call(bf16[256,512]{1,0:T(8,128)(2,1)S(1)} %get-tuple-element.25.soft_ref, bf16[8192,512]{1,0:T(8,128)(2,1)S(1)} %copy-done), custom_call_target="tpu_custom_call" | custom-call | flops 2147483648 | bytes 14680064 | tf_op jit(solution)/shard_map/soft/pallas_call | solution.py:276
  54.1 0.0 collective-permute-done.15.both_ref
  54.1 0.0 collective-permute-done.14.x_ref
  54.1 0.2 collective-permute-start.16
  54.3 0.4 collective-permute-start.17
  54.7 23.0 %all_to_all.5.spread_ref = f32[32,3,128]{2,1,0:T(4,128)S(1)} all-to-all(f32[32,3,128]{2,1,0:T(4,128)S(1)} %merge.1), channel_id=1, replica_groups=mesh['y'=4,'x'=2,'c'=2,'z'=8,'dp'=2] {'y','z'}, dimensions={0} | all-to-all | bytes 98304 | tf_op jit(solution)/shard_map/all_to_all | solution.py:297
  77.8 0.0 collective-permute-done.16.refs_1_
  77.8 0.0 collective-permute-done.17.refs_3_
  77.8 3.4 %combine.2 = (f32[128,128]{1,0:T(8,128)S(1)}, bf16[32,8192]{1,0:T(8,128)(2,1)S(1)}, bf16[32,8192]{1,0:T(8,128)(2,1)S(1)}, bf16[32,8192]{1,0:T(8,128)(2,1)S(1)}) custom-call(s32[5]{0:T(128)S(1)} %stack.23.at_ref, f32[1,256]{1,0:T(1,128)S(1)} %bitcast.9, f32[3,128]{1,0:T(4,128)S(1)} %get-tuple-element.23.own_ref, ...), custom_call_target="tpu_custom_call" | custom-call | flops 4718592 | bytes 9437184 | tf_op jit(solution)/shard_map/combine/pallas_call | solution.py:306
  81.2 1.4 %collective-permute-start.18 = (bf16[32,8192]{1,0:T(8,128)(2,1)S(1)}, bf16[32,8192]{1,0:T(8,128)(2,1)S(1)}, u32[]{:S(2)}, u32[]{:S(2)}) collective-permute-start(bf16[32,8192]{1,0:T(8,128)(2,1)S(1)} %get-tuple-element.34), channel_id=1, source_target_pairs={{0,128},{2,130},{4,132},{6,134},{8,136},{10,138},{12,140},{14,142}... | collective-permute-start | bytes 1572872 | tf_op jit(solution)/shard_map/ppermute | solution.py:63
  82.6 0.7 collective-permute-start.19
  83.3 2.5 %collective-permute-start.20 = (bf16[32,8192]{1,0:T(8,128)(2,1)S(1)}, bf16[32,8192]{1,0:T(8,128)(2,1)S(1)}, u32[]{:S(2)}, u32[]{:S(2)}) collective-permute-start(bf16[32,8192]{1,0:T(8,128)(2,1)S(1)} %get-tuple-element.36), channel_id=1, source_target_pairs={{0,192},{2,194},{4,196},{6,198},{8,200},{10,202},{12,204},{14,206}... | collective-permute-start | bytes 1572872 | tf_op jit(solution)/shard_map/ppermute | solution.py:63
  85.8 1.8 %combine.3 = f32[32,8192]{1,0:T(8,128)S(1)} custom-call(f32[128,128]{1,0:T(8,128)S(1)} %get-tuple-element.33.scales_ref, f32[128,8192]{1,0:T(8,128)} %get-tuple-element.29.refs_0_, bf16[128,8192]{1,0:T(8,128)(2,1)S(1)} %collective-permute-done.16.refs_1_, bf16[128,8192]{1,0:T(8,128)(2,1)} %get-tuple-element.31.refs_2_, ...), custom_call_target="tpu_custom_call" | custom-call | flops 1572864 | bytes 3145728 | tf_op jit(solution)/shard_map/combine/pallas_call | solution.py:306
  87.6 4.4 %collective-permute-done.18 = bf16[32,8192]{1,0:T(8,128)(2,1)S(1)} collective-permute-done((bf16[32,8192]{1,0:T(8,128)(2,1)S(1)}, bf16[32,8192]{1,0:T(8,128)(2,1)S(1)}, u32[]{:S(2)}, u32[]{:S(2)}) %collective-permute-start.18) | collective-permute-done | bytes 524320 | tf_op jit(solution)/shard_map/ppermute | solution.py:63
  92.0 5.5 %collective-permute-done.19 = bf16[32,8192]{1,0:T(8,128)(2,1)S(1)} collective-permute-done((bf16[32,8192]{1,0:T(8,128)(2,1)S(1)}, bf16[32,8192]{1,0:T(8,128)(2,1)S(1)}, u32[]{:S(2)}, u32[]{:S(2)}) %collective-permute-start.19) | collective-permute-done | bytes 524320 | tf_op jit(solution)/shard_map/ppermute | solution.py:63
  97.6 0.2 fusion.3
  97.8 1.3 %collective-permute-start.21 = (bf16[8,8192]{1,0:T(8,128)(2,1)S(1)}, bf16[8,8192]{1,0:T(8,128)(2,1)S(1)}, u32[]{:S(2)}, u32[]{:S(2)}) collective-permute-start(bf16[8,8192]{1,0:T(8,128)(2,1)S(1)} %get-tuple-element.43), channel_id=1, source_target_pairs={{0,4},{2,6},{4,8},{6,10},{8,12},{10,14},{12,0},{14,2},{16,144},{18... | collective-permute-start | bytes 393224 | tf_op jit(solution)/shard_map/ppermute | solution.py:63
  99.1 2.6 %collective-permute-start.23 = (bf16[8,8192]{1,0:T(8,128)(2,1)S(1)}, bf16[8,8192]{1,0:T(8,128)(2,1)S(1)}, u32[]{:S(2)}, u32[]{:S(2)}) collective-permute-start(bf16[8,8192]{1,0:T(8,128)(2,1)S(1)} %get-tuple-element.44), channel_id=1, source_target_pairs={{0,14},{2,0},{4,2},{6,4},{8,6},{10,8},{12,10},{14,12},{16,208},{18... | collective-permute-start | bytes 393224 | tf_op jit(solution)/shard_map/ppermute | solution.py:63
  101.7 0.2 slice_reduce_fusion
  101.9 4.1 %collective-permute-done.21 = bf16[8,8192]{1,0:T(8,128)(2,1)S(1)} collective-permute-done((bf16[8,8192]{1,0:T(8,128)(2,1)S(1)}, bf16[8,8192]{1,0:T(8,128)(2,1)S(1)}, u32[]{:S(2)}, u32[]{:S(2)}) %collective-permute-start.21) | collective-permute-done | bytes 131104 | tf_op jit(solution)/shard_map/ppermute | solution.py:63
  106.1 1.8 %collective-permute-done.22 = bf16[8,8192]{1,0:T(8,128)(2,1)S(1)} collective-permute-done((bf16[8,8192]{1,0:T(8,128)(2,1)S(1)}, bf16[8,8192]{1,0:T(8,128)(2,1)S(1)}, u32[]{:S(2)}, u32[]{:S(2)}) %collective-permute-start.22) | collective-permute-done | bytes 131104 | tf_op jit(solution)/shard_map/ppermute | solution.py:63
  107.9 0.1 fusion.2
  108.0 0.1 fusion.5
  108.0 2.3 %collective-permute-start.24 = (bf16[2,8192]{1,0:T(2,128)(2,1)S(1)}, bf16[2,8192]{1,0:T(2,128)(2,1)S(1)}, u32[]{:S(2)}, u32[]{:S(2)}) collective-permute-start(bf16[2,8192]{1,0:T(2,128)(2,1)S(1)} %get-tuple-element.46), channel_id=1, source_target_pairs={{0,40},{2,42},{4,44},{6,46},{8,32},{10,34},{12,36},{14,38},{16,56}... | collective-permute-start | bytes 98312 | tf_op jit(solution)/shard_map/ppermute | solution.py:63
  110.3 4.6 %collective-permute-start.25 = (bf16[2,8192]{1,0:T(2,128)(2,1)S(1)}, bf16[2,8192]{1,0:T(2,128)(2,1)S(1)}, u32[]{:S(2)}, u32[]{:S(2)}) collective-permute-start(bf16[2,8192]{1,0:T(2,128)(2,1)S(1)} %get-tuple-element.47), channel_id=1, source_target_pairs={{0,8},{2,10},{4,12},{6,14},{8,0},{10,2},{12,4},{14,6},{16,24},{18,... | collective-permute-start | bytes 98312 | tf_op jit(solution)/shard_map/ppermute | solution.py:63
  114.9 0.7 collective-permute-start.26
  115.6 0.5 multiply_multiply_fusion
  116.1 1.1 collective-permute-done.24
  117.3 0.9 collective-permute-done.25
  118.2 1.4 %collective-permute-done.26 = f32[2,8192]{1,0:T(2,128)S(1)} collective-permute-done((f32[2,8192]{1,0:T(2,128)S(1)}, f32[2,8192]{1,0:T(2,128)S(1)}, u32[]{:S(2)}, u32[]{:S(2)}) %collective-permute-start.26) | collective-permute-done | bytes 65568 | tf_op jit(solution)/shard_map/ppermute | solution.py:63
  119.6 0.7 fusion.1
  (16 shorter events, 0.1 us)
Async XLA Ops:
  0.6 10.1 %collective-permute-start.1 = (bf16[2,8192]{1,0:T(2,128)(2,1)}, bf16[2,8192]{1,0:T(2,128)(2,1)S(1)}, u32[]{:S(2)}, u32[]{:S(2)}) collective-permute-start(bf16[2,8192]{1,0:T(2,128)(2,1)} %param.4), channel_id=1, source_target_pairs={{0,40},{2,42},{4,44},{6,46},{8,32},{10,34},{12,36},{14,38},{16,56}... | collective-permute-start | bytes 98312 | tf_op jit(solution)/shard_map/ppermute | solution.py:63
  8.5 4.1 %collective-permute-start = (bf16[2,8192]{1,0:T(2,128)(2,1)}, bf16[2,8192]{1,0:T(2,128)(2,1)S(1)}, u32[]{:S(2)}, u32[]{:S(2)}) collective-permute-start(bf16[2,8192]{1,0:T(2,128)(2,1)} %param.4), channel_id=1, source_target_pairs={{0,32},{2,34},{4,36},{6,38},{8,40},{10,42},{12,44},{14,46},{16,48}... | collective-permute-start | bytes 98312 | tf_op jit(solution)/shard_map/ppermute | solution.py:63
  9.4 8.0 %collective-permute-start.2 = (bf16[2,8192]{1,0:T(2,128)(2,1)}, bf16[2,8192]{1,0:T(2,128)(2,1)S(1)}, u32[]{:S(2)}, u32[]{:S(2)}) collective-permute-start(bf16[2,8192]{1,0:T(2,128)(2,1)} %param.4), channel_id=1, source_target_pairs={{0,8},{2,10},{4,12},{6,14},{8,0},{10,2},{12,4},{14,6},{16,24},{18,... | collective-permute-start | bytes 98312 | tf_op jit(solution)/shard_map/ppermute | solution.py:63
  18.3 7.5 %collective-permute-start.5 = (bf16[8,8192]{1,0:T(8,128)(2,1)S(1)}, bf16[8,8192]{1,0:T(8,128)(2,1)S(1)}, u32[]{:S(2)}, u32[]{:S(2)}) collective-permute-start(bf16[8,8192]{1,0:T(8,128)(2,1)S(1)} %pad_maximum_fusion.a_ref), channel_id=1, source_target_pairs={{0,12},{2,14},{4,0},{6,2},{8,4},{10,6},{12,8},{14,10},{16,144},{18... | collective-permute-start | bytes 393224 | tf_op jit(solution)/shard_map/ppermute | solution.py:63
  18.4 7.4 %collective-permute-start.4 = (bf16[8,8192]{1,0:T(8,128)(2,1)S(1)}, bf16[8,8192]{1,0:T(8,128)(2,1)S(1)}, u32[]{:S(2)}, u32[]{:S(2)}) collective-permute-start(bf16[8,8192]{1,0:T(8,128)(2,1)S(1)} %pad_maximum_fusion.a_ref), channel_id=1, source_target_pairs={{0,2},{2,4},{4,6},{6,8},{8,10},{10,12},{12,14},{14,0},{16,80},{18,... | collective-permute-start | bytes 393224 | tf_op jit(solution)/shard_map/ppermute | solution.py:63
  20.0 5.8 %collective-permute-start.3 = (bf16[8,8192]{1,0:T(8,128)(2,1)S(1)}, bf16[8,8192]{1,0:T(8,128)(2,1)S(1)}, u32[]{:S(2)}, u32[]{:S(2)}) collective-permute-start(bf16[8,8192]{1,0:T(8,128)(2,1)S(1)} %pad_maximum_fusion.a_ref), channel_id=1, source_target_pairs={{0,14},{2,0},{4,2},{6,4},{8,6},{10,8},{12,10},{14,12},{16,208},{18... | collective-permute-start | bytes 393224 | tf_op jit(solution)/shard_map/ppermute | solution.py:63
  25.9 14.2 %collective-permute-start.8 = (bf16[32,8192]{1,0:T(8,128)(2,1)S(1)}, bf16[32,8192]{1,0:T(8,128)(2,1)S(1)}, u32[]{:S(2)}, u32[]{:S(2)}) collective-permute-start(bf16[32,8192]{1,0:T(8,128)(2,1)S(1)} %join.1.p0), channel_id=1, source_target_pairs={{0,128},{2,130},{4,132},{6,134},{8,136},{10,138},{12,140},{14,142}... | collective-permute-start | bytes 1572872 | tf_op jit(solution)/shard_map/ppermute | solution.py:63
  29.1 13.1 %collective-permute-start.7 = (bf16[32,8192]{1,0:T(8,128)(2,1)S(1)}, bf16[32,8192]{1,0:T(8,128)(2,1)S(1)}, u32[]{:S(2)}, u32[]{:S(2)}) collective-permute-start(bf16[32,8192]{1,0:T(8,128)(2,1)S(1)} %join.1.p0), channel_id=1, source_target_pairs={{0,64},{2,66},{4,68},{6,70},{8,72},{10,74},{12,76},{14,78},{16,18}... | collective-permute-start | bytes 1572872 | tf_op jit(solution)/shard_map/ppermute | solution.py:63
  29.8 12.8 %collective-permute-start.6 = (bf16[32,8192]{1,0:T(8,128)(2,1)S(1)}, bf16[32,8192]{1,0:T(8,128)(2,1)S(1)}, u32[]{:S(2)}, u32[]{:S(2)}) collective-permute-start(bf16[32,8192]{1,0:T(8,128)(2,1)S(1)} %join.1.p0), channel_id=1, source_target_pairs={{0,192},{2,194},{4,196},{6,198},{8,200},{10,202},{12,204},{14,206}... | collective-permute-start | bytes 1572872 | tf_op jit(solution)/shard_map/ppermute | solution.py:63
  32.5 0.7 copy-start.1
  33.1 12.1 %copy-start = (bf16[8192,512]{1,0:T(8,128)(2,1)S(1)}, bf16[8192,512]{1,0:T(8,128)(2,1)}, u32[]{:S(2)}) copy-start(bf16[8192,512]{1,0:T(8,128)(2,1)} %w_ref.3) | copy-start | bytes 25165828
  39.9 3.8 %collective-permute-start.9 = (bf16[32,8192]{1,0:T(8,128)(2,1)S(1)}, bf16[32,8192]{1,0:T(8,128)(2,1)S(1)}, u32[]{:S(2)}, u32[]{:S(2)}) collective-permute-start(bf16[32,8192]{1,0:T(8,128)(2,1)S(1)} %join.1.p0), channel_id=1, source_target_pairs={{0,16},{2,18},{4,20},{6,22},{8,24},{10,26},{12,28},{14,30},{16,0},... | collective-permute-start | bytes 1572872 | tf_op jit(solution)/shard_map/ppermute | solution.py:63
  40.0 3.7 %collective-permute-start.12 = (bf16[32,8192]{1,0:T(8,128)(2,1)S(1)}, bf16[32,8192]{1,0:T(8,128)(2,1)S(1)}, u32[]{:S(2)}, u32[]{:S(2)}) collective-permute-start(bf16[32,8192]{1,0:T(8,128)(2,1)S(1)} %collective-permute-done.8.p3), channel_id=1, source_target_pairs={{0,16},{2,18},{4,20},{6,22},{8,24},{10,26},{12,28},{14,30},{16,0},... | collective-permute-start | bytes 1572872 | tf_op jit(solution)/shard_map/ppermute | solution.py:63
  42.2 1.9 %collective-permute-start.11 = (bf16[32,8192]{1,0:T(8,128)(2,1)S(1)}, bf16[32,8192]{1,0:T(8,128)(2,1)S(1)}, u32[]{:S(2)}, u32[]{:S(2)}) collective-permute-start(bf16[32,8192]{1,0:T(8,128)(2,1)S(1)} %collective-permute-done.7.p2), channel_id=1, source_target_pairs={{0,16},{2,18},{4,20},{6,22},{8,24},{10,26},{12,28},{14,30},{16,0},... | collective-permute-start | bytes 1572872 | tf_op jit(solution)/shard_map/ppermute | solution.py:63
  42.6 2.6 %collective-permute-start.10 = (bf16[32,8192]{1,0:T(8,128)(2,1)S(1)}, bf16[32,8192]{1,0:T(8,128)(2,1)S(1)}, u32[]{:S(2)}, u32[]{:S(2)}) collective-permute-start(bf16[32,8192]{1,0:T(8,128)(2,1)S(1)} %collective-permute-done.6.p1), channel_id=1, source_target_pairs={{0,16},{2,18},{4,20},{6,22},{8,24},{10,26},{12,28},{14,30},{16,0},... | collective-permute-start | bytes 1572872 | tf_op jit(solution)/shard_map/ppermute | solution.py:63
  48.4 5.7 %collective-permute-start.15 = (f32[3,128]{1,0:T(4,128)S(1)}, f32[3,128]{1,0:T(4,128)S(1)}, u32[]{:S(2)}, u32[]{:S(2)}) collective-permute-start(f32[3,128]{1,0:T(4,128)S(1)} %get-tuple-element.24), channel_id=1, source_target_pairs={{0,48},{2,50},{4,52},{6,54},{8,56},{10,58},{12,60},{14,62},{16,32}... | collective-permute-start | bytes 4616 | tf_op jit(solution)/shard_map/ppermute | solution.py:63
  49.7 4.4 %collective-permute-start.13 = (f32[3,128]{1,0:T(4,128)S(1)}, f32[3,128]{1,0:T(4,128)S(1)}, u32[]{:S(2)}, u32[]{:S(2)}) collective-permute-start(f32[3,128]{1,0:T(4,128)S(1)} %get-tuple-element.24), channel_id=1, source_target_pairs={{0,16},{2,18},{4,20},{6,22},{8,24},{10,26},{12,28},{14,30},{16,0},... | collective-permute-start | bytes 4616 | tf_op jit(solution)/shard_map/ppermute | solution.py:63
  49.8 4.3 %collective-permute-start.14 = (f32[3,128]{1,0:T(4,128)S(1)}, f32[3,128]{1,0:T(4,128)S(1)}, u32[]{:S(2)}, u32[]{:S(2)}) collective-permute-start(f32[3,128]{1,0:T(4,128)S(1)} %get-tuple-element.23.own_ref), channel_id=1, source_target_pairs={{0,32},{2,34},{4,36},{6,38},{8,40},{10,42},{12,44},{14,46},{16,48}... | collective-permute-start | bytes 4616 | tf_op jit(solution)/shard_map/ppermute | solution.py:63
  50.7 3.6 %copy-start.3 = (bf16[128,8192]{1,0:T(8,128)(2,1)S(1)}, bf16[128,8192]{1,0:T(8,128)(2,1)}, u32[]{:S(2)}) copy-start(bf16[128,8192]{1,0:T(8,128)(2,1)} %get-tuple-element.32) | copy-start | bytes 6291460
  50.7 27.1 %copy-start.2 = (f32[256]{0:T(256)S(1)}, f32[256]{0:T(256)}, u32[]{:S(2)}) copy-start(f32[256]{0:T(256)} %param.7) | copy-start | bytes 3076
  54.1 23.6 %collective-permute-start.16 = (bf16[128,8192]{1,0:T(8,128)(2,1)}, bf16[128,8192]{1,0:T(8,128)(2,1)S(1)}, u32[]{:S(2)}, u32[]{:S(2)}) collective-permute-start(bf16[128,8192]{1,0:T(8,128)(2,1)} %get-tuple-element.30), channel_id=1, source_target_pairs={{0,16},{2,18},{4,20},{6,22},{8,24},{10,26},{12,28},{14,30},{16,0},... | collective-permute-start | bytes 6291464 | tf_op jit(solution)/shard_map/ppermute | solution.py:63
  54.3 23.5 %collective-permute-start.17 = (bf16[128,8192]{1,0:T(8,128)(2,1)S(1)}, bf16[128,8192]{1,0:T(8,128)(2,1)S(1)}, u32[]{:S(2)}, u32[]{:S(2)}) collective-permute-start(bf16[128,8192]{1,0:T(8,128)(2,1)S(1)} %copy-done.3), channel_id=1, source_target_pairs={{0,16},{2,18},{4,20},{6,22},{8,24},{10,26},{12,28},{14,30},{16,0},... | collective-permute-start | bytes 6291464 | tf_op jit(solution)/shard_map/ppermute | solution.py:63
  81.2 10.9 %collective-permute-start.18 = (bf16[32,8192]{1,0:T(8,128)(2,1)S(1)}, bf16[32,8192]{1,0:T(8,128)(2,1)S(1)}, u32[]{:S(2)}, u32[]{:S(2)}) collective-permute-start(bf16[32,8192]{1,0:T(8,128)(2,1)S(1)} %get-tuple-element.34), channel_id=1, source_target_pairs={{0,128},{2,130},{4,132},{6,134},{8,136},{10,138},{12,140},{14,142}... | collective-permute-start | bytes 1572872 | tf_op jit(solution)/shard_map/ppermute | solution.py:63
  82.6 15.0 %collective-permute-start.19 = (bf16[32,8192]{1,0:T(8,128)(2,1)S(1)}, bf16[32,8192]{1,0:T(8,128)(2,1)S(1)}, u32[]{:S(2)}, u32[]{:S(2)}) collective-permute-start(bf16[32,8192]{1,0:T(8,128)(2,1)S(1)} %get-tuple-element.35), channel_id=1, source_target_pairs={{0,64},{2,66},{4,68},{6,70},{8,72},{10,74},{12,76},{14,78},{16,18}... | collective-permute-start | bytes 1572872 | tf_op jit(solution)/shard_map/ppermute | solution.py:63
  83.3 14.3 %collective-permute-start.20 = (bf16[32,8192]{1,0:T(8,128)(2,1)S(1)}, bf16[32,8192]{1,0:T(8,128)(2,1)S(1)}, u32[]{:S(2)}, u32[]{:S(2)}) collective-permute-start(bf16[32,8192]{1,0:T(8,128)(2,1)S(1)} %get-tuple-element.36), channel_id=1, source_target_pairs={{0,192},{2,194},{4,196},{6,198},{8,200},{10,202},{12,204},{14,206}... | collective-permute-start | bytes 1572872 | tf_op jit(solution)/shard_map/ppermute | solution.py:63
  97.8 8.2 %collective-permute-start.21 = (bf16[8,8192]{1,0:T(8,128)(2,1)S(1)}, bf16[8,8192]{1,0:T(8,128)(2,1)S(1)}, u32[]{:S(2)}, u32[]{:S(2)}) collective-permute-start(bf16[8,8192]{1,0:T(8,128)(2,1)S(1)} %get-tuple-element.43), channel_id=1, source_target_pairs={{0,4},{2,6},{4,8},{6,10},{8,12},{10,14},{12,0},{14,2},{16,144},{18... | collective-permute-start | bytes 393224 | tf_op jit(solution)/shard_map/ppermute | solution.py:63
  99.1 7.0 %collective-permute-start.23 = (bf16[8,8192]{1,0:T(8,128)(2,1)S(1)}, bf16[8,8192]{1,0:T(8,128)(2,1)S(1)}, u32[]{:S(2)}, u32[]{:S(2)}) collective-permute-start(bf16[8,8192]{1,0:T(8,128)(2,1)S(1)} %get-tuple-element.44), channel_id=1, source_target_pairs={{0,14},{2,0},{4,2},{6,4},{8,6},{10,8},{12,10},{14,12},{16,208},{18... | collective-permute-start | bytes 393224 | tf_op jit(solution)/shard_map/ppermute | solution.py:63
  101.7 6.2 %collective-permute-start.22 = (bf16[8,8192]{1,0:T(8,128)(2,1)S(1)}, bf16[8,8192]{1,0:T(8,128)(2,1)S(1)}, u32[]{:S(2)}, u32[]{:S(2)}) collective-permute-start(bf16[8,8192]{1,0:T(8,128)(2,1)S(1)} %get-tuple-element.45), channel_id=1, source_target_pairs={{0,2},{2,4},{4,6},{6,8},{8,10},{10,12},{12,14},{14,0},{16,80},{18,... | collective-permute-start | bytes 393224 | tf_op jit(solution)/shard_map/ppermute | solution.py:63
  108.0 9.3 %collective-permute-start.24 = (bf16[2,8192]{1,0:T(2,128)(2,1)S(1)}, bf16[2,8192]{1,0:T(2,128)(2,1)S(1)}, u32[]{:S(2)}, u32[]{:S(2)}) collective-permute-start(bf16[2,8192]{1,0:T(2,128)(2,1)S(1)} %get-tuple-element.46), channel_id=1, source_target_pairs={{0,40},{2,42},{4,44},{6,46},{8,32},{10,34},{12,36},{14,38},{16,56}... | collective-permute-start | bytes 98312 | tf_op jit(solution)/shard_map/ppermute | solution.py:63
  110.3 7.9 %collective-permute-start.25 = (bf16[2,8192]{1,0:T(2,128)(2,1)S(1)}, bf16[2,8192]{1,0:T(2,128)(2,1)S(1)}, u32[]{:S(2)}, u32[]{:S(2)}) collective-permute-start(bf16[2,8192]{1,0:T(2,128)(2,1)S(1)} %get-tuple-element.47), channel_id=1, source_target_pairs={{0,8},{2,10},{4,12},{6,14},{8,0},{10,2},{12,4},{14,6},{16,24},{18,... | collective-permute-start | bytes 98312 | tf_op jit(solution)/shard_map/ppermute | solution.py:63
  114.9 4.7 %collective-permute-start.26 = (f32[2,8192]{1,0:T(2,128)S(1)}, f32[2,8192]{1,0:T(2,128)S(1)}, u32[]{:S(2)}, u32[]{:S(2)}) collective-permute-start(f32[2,8192]{1,0:T(2,128)S(1)} %slice.56), channel_id=1, source_target_pairs={{0,32},{2,34},{4,36},{6,38},{8,40},{10,42},{12,44},{14,46},{16,48}... | collective-permute-start | bytes 196616 | tf_op jit(solution)/shard_map/ppermute | solution.py:63

commit v14 on v12

--- a/solution.py
+++ b/solution.py
@@ -313,8 +313,10 @@
     part = combine((0,), F32, rows=(scales,))[0] + sum(arrived)
     part = part.reshape(4, 8, DEPTH)
     part = part[0] + sum(send(part[k].astype(BF), to_first(OFFSETS[k])).astype(F32) for k in (3, 1, 2))
-    moved = [send(part[2 * k : 2 * k + 2].astype(BF), to).astype(F32) for k, to in ((3, to_xz4), (2, to_z4))]
-    part = [part[0:2], *moved, send(part[2:4], to_x)]
+    moved = [
+        send(part[2 * k : 2 * k + 2].astype(BF), to).astype(F32) for k, to in ((3, to_xz4), (2, to_z4), (1, to_x))
+    ]
+    part = [part[0:2], *moved]
     part = (part[0] + part[1]) + (part[2] + part[3])
     return ce_loss, z_term, part.astype(BF)
 

time: 117 us -> 118 us (level)
  transfers between devices with their start and end apart: 27 -> 27, of which waited for: 15 -> 14; matrix products, arithmetic and copies ran while one was open for 1% -> 1% of each run, Pallas kernels for 10% -> 10%
where the time goes in v14:
time: 118 us; the launch traced here: 116 us
  starting transfers between devices  40.3 us (34%)
  waiting for transfers between devices  34.7 us (29%)
  Pallas kernels  18.5 us (16%)
  blocking collectives  17.6 us (15%)
  other arithmetic  2.4 us (2%)
  local copies, waits for them, and re-layouts  2.07 us (2%)
    ppermute x27, starting transfers between devices, send(): return lax.ppermute(value, GROUP, pairs(route))  40.3 us
    ppermute x27, waiting for transfers between devices, send(): return lax.ppermute(value, GROUP, pairs(route))  34.7 us
    all_to_all x1, blocking collectives, shards(): spread = lax.all_to_all(merged, ('y', 'z'), 0, 0)  17.6 us
    pallas_call x1, Pallas kernels, shards(): pl.pallas_call(target_kernel, out_shape=[pltpu.HBM((half, DEPTH), BF)] *...  6.76 us
    pallas_call x2, Pallas kernels, combine(): pl.pallas_call(functools.partial(kernel, parts), out_shape=scales + [jax....  5.17 us
    pallas_call x1, Pallas kernels, shards(): pl.pallas_call(soft_kernel, out_shape=(pltpu.HBM((half, DEPTH), F32), plt...  3.39 us
    pallas_call x1, Pallas kernels, shards(): pl.pallas_call(logits_kernel, out_shape=[jax.ShapeDtypeStruct((3, half),...  3.15 us
  transfers between devices with their start and end apart: 27, of which 14 were waited for; matrix products, arithmetic and copies ran while one was open for 1% of the time, Pallas kernels for 10%

profile of v14, /device:TPU:4, one launch (start us, length us, event | category | flops | bytes accessed | tf_op | source)
XLA Modules:
  0.0 116.4 jit_solution(1113312551649454443)
XLA Ops:
  0.6 7.9 %collective-permute-start.2 = (bf16[2,8192]{1,0:T(2,128)(2,1)}, bf16[2,8192]{1,0:T(2,128)(2,1)S(1)}, u32[]{:S(2)}, u32[]{:S(2)}) collective-permute-start(bf16[2,8192]{1,0:T(2,128)(2,1)} %param.4), channel_id=1, source_target_pairs={{0,40},{2,42},{4,44},{6,46},{8,32},{10,34},{12,36},{14,38},{16,56}... | collective-permute-start | bytes 98312 | tf_op jit(solution)/shard_map/ppermute | solution.py:63
  8.5 0.0 collective-permute-start.1
  8.5 0.8 collective-permute-start
  9.4 1.4 %collective-permute-done.2 = bf16[2,8192]{1,0:T(2,128)(2,1)S(1)} collective-permute-done((bf16[2,8192]{1,0:T(2,128)(2,1)}, bf16[2,8192]{1,0:T(2,128)(2,1)S(1)}, u32[]{:S(2)}, u32[]{:S(2)}) %collective-permute-start.2) | collective-permute-done | bytes 32800 | tf_op jit(solution)/shard_map/ppermute | solution.py:63
  10.7 6.1 %collective-permute-done.1 = bf16[2,8192]{1,0:T(2,128)(2,1)S(1)} collective-permute-done((bf16[2,8192]{1,0:T(2,128)(2,1)}, bf16[2,8192]{1,0:T(2,128)(2,1)S(1)}, u32[]{:S(2)}, u32[]{:S(2)}) %collective-permute-start.1) | collective-permute-done | bytes 32800 | tf_op jit(solution)/shard_map/ppermute | solution.py:63
  16.8 0.0 collective-permute-done
  16.8 0.9 pad_maximum_fusion
  17.8 0.9 collective-permute-start.5
  18.7 1.0 collective-permute-start.4
  19.7 2.2 %collective-permute-start.3 = (bf16[8,8192]{1,0:T(8,128)(2,1)S(1)}, bf16[8,8192]{1,0:T(8,128)(2,1)S(1)}, u32[]{:S(2)}, u32[]{:S(2)}) collective-permute-start(bf16[8,8192]{1,0:T(8,128)(2,1)S(1)} %pad_maximum_fusion), channel_id=1, source_target_pairs={{0,14},{2,0},{4,2},{6,4},{8,6},{10,8},{12,10},{14,12},{16,208},{18... | collective-permute-start | bytes 393224 | tf_op jit(solution)/shard_map/ppermute | solution.py:63
  21.9 3.3 %collective-permute-done.5 = bf16[8,8192]{1,0:T(8,128)(2,1)S(1)} collective-permute-done((bf16[8,8192]{1,0:T(8,128)(2,1)S(1)}, bf16[8,8192]{1,0:T(8,128)(2,1)S(1)}, u32[]{:S(2)}, u32[]{:S(2)}) %collective-permute-start.5) | collective-permute-done | bytes 131104 | tf_op jit(solution)/shard_map/ppermute | solution.py:63
  25.2 0.6 collective-permute-done.3
  25.8 1.0 concatenate.8.p0
  26.8 3.3 %collective-permute-start.8 = (bf16[32,8192]{1,0:T(8,128)(2,1)S(1)}, bf16[32,8192]{1,0:T(8,128)(2,1)S(1)}, u32[]{:S(2)}, u32[]{:S(2)}) collective-permute-start(bf16[32,8192]{1,0:T(8,128)(2,1)S(1)} %concatenate.8.p0), channel_id=1, source_target_pairs={{0,128},{2,130},{4,132},{6,134},{8,136},{10,138},{12,140},{14,142}... | collective-permute-start | bytes 1572872 | tf_op jit(solution)/shard_map/ppermute | solution.py:63
  30.0 0.7 collective-permute-start.7
  30.7 2.6 %collective-permute-start.6 = (bf16[32,8192]{1,0:T(8,128)(2,1)S(1)}, bf16[32,8192]{1,0:T(8,128)(2,1)S(1)}, u32[]{:S(2)}, u32[]{:S(2)}) collective-permute-start(bf16[32,8192]{1,0:T(8,128)(2,1)S(1)} %concatenate.8.p0), channel_id=1, source_target_pairs={{0,192},{2,194},{4,196},{6,198},{8,200},{10,202},{12,204},{14,206}... | collective-permute-start | bytes 1572872 | tf_op jit(solution)/shard_map/ppermute | solution.py:63
  33.3 0.1 stack.23.at_ref
  33.4 0.7 copy-done.1
  34.0 6.8 %target.1 = (bf16[128,8192]{1,0:T(8,128)(2,1)}, bf16[128,8192]{1,0:T(8,128)(2,1)}) custom-call(s32[5]{0:T(128)S(1)} %stack.23.at_ref, s32[1,256]{1,0:T(1,128)S(1)} %bitcast.7, bf16[8192,512]{1,0:T(8,128)(2,1)} %w_ref.3), custom_call_target="tpu_custom_call" | custom-call | flops 2147483648 | bytes 12582912 | tf_op jit(solution)/shard_map/target/pallas_call | solution.py:242
  40.8 0.1 collective-permute-start.9
  40.9 0.0 collective-permute-done.8.p3
  40.9 0.5 collective-permute-start.12
  41.4 1.7 %collective-permute-done.7.p2 = bf16[32,8192]{1,0:T(8,128)(2,1)S(1)} collective-permute-done((bf16[32,8192]{1,0:T(8,128)(2,1)S(1)}, bf16[32,8192]{1,0:T(8,128)(2,1)S(1)}, u32[]{:S(2)}, u32[]{:S(2)}) %collective-permute-start.7) | collective-permute-done | bytes 524320 | tf_op jit(solution)/shard_map/ppermute | solution.py:63
  43.2 0.4 collective-permute-done.6.p1
  43.5 1.5 %collective-permute-start.10 = (bf16[32,8192]{1,0:T(8,128)(2,1)S(1)}, bf16[32,8192]{1,0:T(8,128)(2,1)S(1)}, u32[]{:S(2)}, u32[]{:S(2)}) collective-permute-start(bf16[32,8192]{1,0:T(8,128)(2,1)S(1)} %collective-permute-done.6.p1), channel_id=1, source_target_pairs={{0,16},{2,18},{4,20},{6,22},{8,24},{10,26},{12,28},{14,30},{16,0},... | collective-permute-start | bytes 1572872 | tf_op jit(solution)/shard_map/ppermute | solution.py:63
  45.0 0.0 collective-permute-done.9.p4
  45.0 0.0 collective-permute-done.12.p7
  45.0 0.1 collective-permute-done.11.p6
  45.1 1.5 %collective-permute-done.10.p5 = bf16[32,8192]{1,0:T(8,128)(2,1)S(1)} collective-permute-done((bf16[32,8192]{1,0:T(8,128)(2,1)S(1)}, bf16[32,8192]{1,0:T(8,128)(2,1)S(1)}, u32[]{:S(2)}, u32[]{:S(2)}) %collective-permute-start.10) | collective-permute-done | bytes 524320 | tf_op jit(solution)/shard_map/ppermute | solution.py:63
  46.5 3.1 %logits.1 = (f32[3,128]{1,0:T(4,128)S(1)}, f32[3,128]{1,0:T(4,128)S(1)}, bf16[256,512]{1,0:T(8,128)(2,1)S(1)}) custom-call(s32[5]{0:T(128)S(1)} %stack.23.at_ref, s32[1,256]{1,0:T(1,128)S(1)} %bitcast.8, bf16[32,8192]{1,0:T(8,128)(2,1)S(1)} %concatenate.8.p0, bf16[32,8192]{1,0:T(8,128)(2,1)S(1)} %collective-permute-done.6.p1, ...), custom_call_target="tpu_custom_call" | custom-call | flops 2147483648 | bytes 13631488 | tf_op jit(solution)/shard_map/logits/pallas_call | solution.py:256
  49.7 0.6 collective-permute-start.15
  50.3 0.2 collective-permute-start.13
  50.5 1.5 %collective-permute-start.14 = (f32[3,128]{1,0:T(4,128)S(1)}, f32[3,128]{1,0:T(4,128)S(1)}, u32[]{:S(2)}, u32[]{:S(2)}) collective-permute-start(f32[3,128]{1,0:T(4,128)S(1)} %get-tuple-element.23.own_ref), channel_id=1, source_target_pairs={{0,32},{2,34},{4,36},{6,38},{8,40},{10,42},{12,44},{14,46},{16,48}... | collective-permute-start | bytes 4616 | tf_op jit(solution)/shard_map/ppermute | solution.py:63
  52.0 3.4 %soft.1 = (f32[128,8192]{1,0:T(8,128)}, bf16[128,8192]{1,0:T(8,128)(2,1)}) custom-call(bf16[256,512]{1,0:T(8,128)(2,1)S(1)} %get-tuple-element.25.soft_ref, bf16[8192,512]{1,0:T(8,128)(2,1)S(1)} %copy-done), custom_call_target="tpu_custom_call" | custom-call | flops 2147483648 | bytes 14680064 | tf_op jit(solution)/shard_map/soft/pallas_call | solution.py:265
  55.4 0.0 collective-permute-done.15.both_ref
  55.4 0.0 collective-permute-done.13.core_ref
  55.4 0.2 collective-permute-start.16
  55.6 0.4 collective-permute-start.17
  56.0 17.6 %all_to_all.5.spread_ref = f32[32,3,128]{2,1,0:T(4,128)S(1)} all-to-all(f32[32,3,128]{2,1,0:T(4,128)S(1)} %merge.1), channel_id=1, replica_groups=mesh['y'=4,'x'=2,'c'=2,'z'=8,'dp'=2] {'y','z'}, dimensions={0} | all-to-all | bytes 98304 | tf_op jit(solution)/shard_map/all_to_all | solution.py:286
  73.7 0.0 collective-permute-done.16.refs_1_
  73.7 0.0 collective-permute-done.17.refs_3_
  73.7 3.4 %combine.2 = (f32[128,128]{1,0:T(8,128)S(1)}, bf16[32,8192]{1,0:T(8,128)(2,1)S(1)}, bf16[32,8192]{1,0:T(8,128)(2,1)S(1)}, bf16[32,8192]{1,0:T(8,128)(2,1)S(1)}) custom-call(s32[5]{0:T(128)S(1)} %stack.23.at_ref, f32[1,256]{1,0:T(1,128)S(1)} %bitcast.9, f32[3,128]{1,0:T(4,128)S(1)} %get-tuple-element.23.own_ref, ...), custom_call_target="tpu_custom_call" | custom-call | flops 4718592 | bytes 9437184 | tf_op jit(solution)/shard_map/combine/pallas_call | solution.py:295
  77.1 1.4 %collective-permute-start.18 = (bf16[32,8192]{1,0:T(8,128)(2,1)S(1)}, bf16[32,8192]{1,0:T(8,128)(2,1)S(1)}, u32[]{:S(2)}, u32[]{:S(2)}) collective-permute-start(bf16[32,8192]{1,0:T(8,128)(2,1)S(1)} %get-tuple-element.34), channel_id=1, source_target_pairs={{0,128},{2,130},{4,132},{6,134},{8,136},{10,138},{12,140},{14,142}... | collective-permute-start | bytes 1572872 | tf_op jit(solution)/shard_map/ppermute | solution.py:63
  78.5 0.7 collective-permute-start.19
  79.2 2.5 %collective-permute-start.20 = (bf16[32,8192]{1,0:T(8,128)(2,1)S(1)}, bf16[32,8192]{1,0:T(8,128)(2,1)S(1)}, u32[]{:S(2)}, u32[]{:S(2)}) collective-permute-start(bf16[32,8192]{1,0:T(8,128)(2,1)S(1)} %get-tuple-element.36), channel_id=1, source_target_pairs={{0,192},{2,194},{4,196},{6,198},{8,200},{10,202},{12,204},{14,206}... | collective-permute-start | bytes 1572872 | tf_op jit(solution)/shard_map/ppermute | solution.py:63
  81.7 1.8 %combine.3 = f32[32,8192]{1,0:T(8,128)S(1)} custom-call(f32[128,128]{1,0:T(8,128)S(1)} %get-tuple-element.33.scales_ref, f32[128,8192]{1,0:T(8,128)} %get-tuple-element.29.refs_0_, bf16[128,8192]{1,0:T(8,128)(2,1)S(1)} %collective-permute-done.16.refs_1_, bf16[128,8192]{1,0:T(8,128)(2,1)} %get-tuple-element.31.refs_2_, ...), custom_call_target="tpu_custom_call" | custom-call | flops 1572864 | bytes 3145728 | tf_op jit(solution)/shard_map/combine/pallas_call | solution.py:295
  83.5 4.4 %collective-permute-done.18 = bf16[32,8192]{1,0:T(8,128)(2,1)S(1)} collective-permute-done((bf16[32,8192]{1,0:T(8,128)(2,1)S(1)}, bf16[32,8192]{1,0:T(8,128)(2,1)S(1)}, u32[]{:S(2)}, u32[]{:S(2)}) %collective-permute-start.18) | collective-permute-done | bytes 524320 | tf_op jit(solution)/shard_map/ppermute | solution.py:63
  87.9 5.5 %collective-permute-done.19 = bf16[32,8192]{1,0:T(8,128)(2,1)S(1)} collective-permute-done((bf16[32,8192]{1,0:T(8,128)(2,1)S(1)}, bf16[32,8192]{1,0:T(8,128)(2,1)S(1)}, u32[]{:S(2)}, u32[]{:S(2)}) %collective-permute-start.19) | collective-permute-done | bytes 524320 | tf_op jit(solution)/shard_map/ppermute | solution.py:63
  93.4 0.0 collective-permute-done.20
  93.4 0.2 fusion.3
  93.7 1.3 %collective-permute-start.21 = (bf16[8,8192]{1,0:T(8,128)(2,1)S(1)}, bf16[8,8192]{1,0:T(8,128)(2,1)S(1)}, u32[]{:S(2)}, u32[]{:S(2)}) collective-permute-start(bf16[8,8192]{1,0:T(8,128)(2,1)S(1)} %get-tuple-element.43), channel_id=1, source_target_pairs={{0,4},{2,6},{4,8},{6,10},{8,12},{10,14},{12,0},{14,2},{16,144},{18... | collective-permute-start | bytes 393224 | tf_op jit(solution)/shard_map/ppermute | solution.py:63
  95.0 2.6 %collective-permute-start.23 = (bf16[8,8192]{1,0:T(8,128)(2,1)S(1)}, bf16[8,8192]{1,0:T(8,128)(2,1)S(1)}, u32[]{:S(2)}, u32[]{:S(2)}) collective-permute-start(bf16[8,8192]{1,0:T(8,128)(2,1)S(1)} %get-tuple-element.44), channel_id=1, source_target_pairs={{0,14},{2,0},{4,2},{6,4},{8,6},{10,8},{12,10},{14,12},{16,208},{18... | collective-permute-start | bytes 393224 | tf_op jit(solution)/shard_map/ppermute | solution.py:63
  97.6 0.2 slice_reduce_fusion
  97.8 4.1 %collective-permute-done.21 = bf16[8,8192]{1,0:T(8,128)(2,1)S(1)} collective-permute-done((bf16[8,8192]{1,0:T(8,128)(2,1)S(1)}, bf16[8,8192]{1,0:T(8,128)(2,1)S(1)}, u32[]{:S(2)}, u32[]{:S(2)}) %collective-permute-start.21) | collective-permute-done | bytes 131104 | tf_op jit(solution)/shard_map/ppermute | solution.py:63
  101.9 1.8 %collective-permute-done.22 = bf16[8,8192]{1,0:T(8,128)(2,1)S(1)} collective-permute-done((bf16[8,8192]{1,0:T(8,128)(2,1)S(1)}, bf16[8,8192]{1,0:T(8,128)(2,1)S(1)}, u32[]{:S(2)}, u32[]{:S(2)}) %collective-permute-start.22) | collective-permute-done | bytes 131104 | tf_op jit(solution)/shard_map/ppermute | solution.py:63
  103.8 0.1 fusion.2
  103.8 0.1 fusion.5
  103.9 1.8 %collective-permute-start.24 = (bf16[2,8192]{1,0:T(2,128)(2,1)S(1)}, bf16[2,8192]{1,0:T(2,128)(2,1)S(1)}, u32[]{:S(2)}, u32[]{:S(2)}) collective-permute-start(bf16[2,8192]{1,0:T(2,128)(2,1)S(1)} %get-tuple-element.46), channel_id=1, source_target_pairs={{0,40},{2,42},{4,44},{6,46},{8,32},{10,34},{12,36},{14,38},{16,56}... | collective-permute-start | bytes 98312 | tf_op jit(solution)/shard_map/ppermute | solution.py:63
  105.7 1.1 collective-permute-start.26
  106.8 4.6 %collective-permute-start.25 = (bf16[2,8192]{1,0:T(2,128)(2,1)S(1)}, bf16[2,8192]{1,0:T(2,128)(2,1)S(1)}, u32[]{:S(2)}, u32[]{:S(2)}) collective-permute-start(bf16[2,8192]{1,0:T(2,128)(2,1)S(1)} %get-tuple-element.48), channel_id=1, source_target_pairs={{0,8},{2,10},{4,12},{6,14},{8,0},{10,2},{12,4},{14,6},{16,24},{18,... | collective-permute-start | bytes 98312 | tf_op jit(solution)/shard_map/ppermute | solution.py:63
  111.4 0.5 multiply_multiply_fusion
  111.9 1.2 %collective-permute-done.24 = bf16[2,8192]{1,0:T(2,128)(2,1)S(1)} collective-permute-done((bf16[2,8192]{1,0:T(2,128)(2,1)S(1)}, bf16[2,8192]{1,0:T(2,128)(2,1)S(1)}, u32[]{:S(2)}, u32[]{:S(2)}) %collective-permute-start.24) | collective-permute-done | bytes 32800 | tf_op jit(solution)/shard_map/ppermute | solution.py:63
  113.1 2.6 %collective-permute-done.25 = bf16[2,8192]{1,0:T(2,128)(2,1)S(1)} collective-permute-done((bf16[2,8192]{1,0:T(2,128)(2,1)S(1)}, bf16[2,8192]{1,0:T(2,128)(2,1)S(1)}, u32[]{:S(2)}, u32[]{:S(2)}) %collective-permute-start.25) | collective-permute-done | bytes 32800 | tf_op jit(solution)/shard_map/ppermute | solution.py:63
  115.7 0.7 fusion.1
  (15 shorter events, 0.1 us)
Async XLA Ops:
  0.6 10.1 %collective-permute-start.2 = (bf16[2,8192]{1,0:T(2,128)(2,1)}, bf16[2,8192]{1,0:T(2,128)(2,1)S(1)}, u32[]{:S(2)}, u32[]{:S(2)}) collective-permute-start(bf16[2,8192]{1,0:T(2,128)(2,1)} %param.4), channel_id=1, source_target_pairs={{0,40},{2,42},{4,44},{6,46},{8,32},{10,34},{12,36},{14,38},{16,56}... | collective-permute-start | bytes 98312 | tf_op jit(solution)/shard_map/ppermute | solution.py:63
  8.5 8.3 %collective-permute-start.1 = (bf16[2,8192]{1,0:T(2,128)(2,1)}, bf16[2,8192]{1,0:T(2,128)(2,1)S(1)}, u32[]{:S(2)}, u32[]{:S(2)}) collective-permute-start(bf16[2,8192]{1,0:T(2,128)(2,1)} %param.4), channel_id=1, source_target_pairs={{0,8},{2,10},{4,12},{6,14},{8,0},{10,2},{12,4},{14,6},{16,24},{18,... | collective-permute-start | bytes 98312 | tf_op jit(solution)/shard_map/ppermute | solution.py:63
  8.5 8.3 %collective-permute-start = (bf16[2,8192]{1,0:T(2,128)(2,1)}, bf16[2,8192]{1,0:T(2,128)(2,1)S(1)}, u32[]{:S(2)}, u32[]{:S(2)}) collective-permute-start(bf16[2,8192]{1,0:T(2,128)(2,1)} %param.4), channel_id=1, source_target_pairs={{0,32},{2,34},{4,36},{6,38},{8,40},{10,42},{12,44},{14,46},{16,48}... | collective-permute-start | bytes 98312 | tf_op jit(solution)/shard_map/ppermute | solution.py:63
  17.8 7.5 %collective-permute-start.5 = (bf16[8,8192]{1,0:T(8,128)(2,1)S(1)}, bf16[8,8192]{1,0:T(8,128)(2,1)S(1)}, u32[]{:S(2)}, u32[]{:S(2)}) collective-permute-start(bf16[8,8192]{1,0:T(8,128)(2,1)S(1)} %pad_maximum_fusion), channel_id=1, source_target_pairs={{0,12},{2,14},{4,0},{6,2},{8,4},{10,6},{12,8},{14,10},{16,144},{18... | collective-permute-start | bytes 393224 | tf_op jit(solution)/shard_map/ppermute | solution.py:63
  18.7 6.5 %collective-permute-start.4 = (bf16[8,8192]{1,0:T(8,128)(2,1)S(1)}, bf16[8,8192]{1,0:T(8,128)(2,1)S(1)}, u32[]{:S(2)}, u32[]{:S(2)}) collective-permute-start(bf16[8,8192]{1,0:T(8,128)(2,1)S(1)} %pad_maximum_fusion), channel_id=1, source_target_pairs={{0,2},{2,4},{4,6},{6,8},{8,10},{10,12},{12,14},{14,0},{16,80},{18,... | collective-permute-start | bytes 393224 | tf_op jit(solution)/shard_map/ppermute | solution.py:63
  19.7 6.1 %collective-permute-start.3 = (bf16[8,8192]{1,0:T(8,128)(2,1)S(1)}, bf16[8,8192]{1,0:T(8,128)(2,1)S(1)}, u32[]{:S(2)}, u32[]{:S(2)}) collective-permute-start(bf16[8,8192]{1,0:T(8,128)(2,1)S(1)} %pad_maximum_fusion), channel_id=1, source_target_pairs={{0,14},{2,0},{4,2},{6,4},{8,6},{10,8},{12,10},{14,12},{16,208},{18... | collective-permute-start | bytes 393224 | tf_op jit(solution)/shard_map/ppermute | solution.py:63
  26.8 14.1 %collective-permute-start.8 = (bf16[32,8192]{1,0:T(8,128)(2,1)S(1)}, bf16[32,8192]{1,0:T(8,128)(2,1)S(1)}, u32[]{:S(2)}, u32[]{:S(2)}) collective-permute-start(bf16[32,8192]{1,0:T(8,128)(2,1)S(1)} %concatenate.8.p0), channel_id=1, source_target_pairs={{0,128},{2,130},{4,132},{6,134},{8,136},{10,138},{12,140},{14,142}... | collective-permute-start | bytes 1572872 | tf_op jit(solution)/shard_map/ppermute | solution.py:63
  30.0 13.1 %collective-permute-start.7 = (bf16[32,8192]{1,0:T(8,128)(2,1)S(1)}, bf16[32,8192]{1,0:T(8,128)(2,1)S(1)}, u32[]{:S(2)}, u32[]{:S(2)}) collective-permute-start(bf16[32,8192]{1,0:T(8,128)(2,1)S(1)} %concatenate.8.p0), channel_id=1, source_target_pairs={{0,64},{2,66},{4,68},{6,70},{8,72},{10,74},{12,76},{14,78},{16,18}... | collective-permute-start | bytes 1572872 | tf_op jit(solution)/shard_map/ppermute | solution.py:63
  30.7 12.8 %collective-permute-start.6 = (bf16[32,8192]{1,0:T(8,128)(2,1)S(1)}, bf16[32,8192]{1,0:T(8,128)(2,1)S(1)}, u32[]{:S(2)}, u32[]{:S(2)}) collective-permute-start(bf16[32,8192]{1,0:T(8,128)(2,1)S(1)} %concatenate.8.p0), channel_id=1, source_target_pairs={{0,192},{2,194},{4,196},{6,198},{8,200},{10,202},{12,204},{14,206}... | collective-permute-start | bytes 1572872 | tf_op jit(solution)/shard_map/ppermute | solution.py:63
  33.4 0.7 copy-start.1
  34.0 12.5 %copy-start = (bf16[8192,512]{1,0:T(8,128)(2,1)S(1)}, bf16[8192,512]{1,0:T(8,128)(2,1)}, u32[]{:S(2)}) copy-start(bf16[8192,512]{1,0:T(8,128)(2,1)} %w_ref.3) | copy-start | bytes 25165828
  40.8 4.2 %collective-permute-start.9 = (bf16[32,8192]{1,0:T(8,128)(2,1)S(1)}, bf16[32,8192]{1,0:T(8,128)(2,1)S(1)}, u32[]{:S(2)}, u32[]{:S(2)}) collective-permute-start(bf16[32,8192]{1,0:T(8,128)(2,1)S(1)} %concatenate.8.p0), channel_id=1, source_target_pairs={{0,16},{2,18},{4,20},{6,22},{8,24},{10,26},{12,28},{14,30},{16,0},... | collective-permute-start | bytes 1572872 | tf_op jit(solution)/shard_map/ppermute | solution.py:63
  40.9 4.1 %collective-permute-start.12 = (bf16[32,8192]{1,0:T(8,128)(2,1)S(1)}, bf16[32,8192]{1,0:T(8,128)(2,1)S(1)}, u32[]{:S(2)}, u32[]{:S(2)}) collective-permute-start(bf16[32,8192]{1,0:T(8,128)(2,1)S(1)} %collective-permute-done.8.p3), channel_id=1, source_target_pairs={{0,16},{2,18},{4,20},{6,22},{8,24},{10,26},{12,28},{14,30},{16,0},... | collective-permute-start | bytes 1572872 | tf_op jit(solution)/shard_map/ppermute | solution.py:63
  43.2 1.9 %collective-permute-start.11 = (bf16[32,8192]{1,0:T(8,128)(2,1)S(1)}, bf16[32,8192]{1,0:T(8,128)(2,1)S(1)}, u32[]{:S(2)}, u32[]{:S(2)}) collective-permute-start(bf16[32,8192]{1,0:T(8,128)(2,1)S(1)} %collective-permute-done.7.p2), channel_id=1, source_target_pairs={{0,16},{2,18},{4,20},{6,22},{8,24},{10,26},{12,28},{14,30},{16,0},... | collective-permute-start | bytes 1572872 | tf_op jit(solution)/shard_map/ppermute | solution.py:63
  43.5 3.0 %collective-permute-start.10 = (bf16[32,8192]{1,0:T(8,128)(2,1)S(1)}, bf16[32,8192]{1,0:T(8,128)(2,1)S(1)}, u32[]{:S(2)}, u32[]{:S(2)}) collective-permute-start(bf16[32,8192]{1,0:T(8,128)(2,1)S(1)} %collective-permute-done.6.p1), channel_id=1, source_target_pairs={{0,16},{2,18},{4,20},{6,22},{8,24},{10,26},{12,28},{14,30},{16,0},... | collective-permute-start | bytes 1572872 | tf_op jit(solution)/shard_map/ppermute | solution.py:63
  49.7 5.7 %collective-permute-start.15 = (f32[3,128]{1,0:T(4,128)S(1)}, f32[3,128]{1,0:T(4,128)S(1)}, u32[]{:S(2)}, u32[]{:S(2)}) collective-permute-start(f32[3,128]{1,0:T(4,128)S(1)} %get-tuple-element.24), channel_id=1, source_target_pairs={{0,48},{2,50},{4,52},{6,54},{8,56},{10,58},{12,60},{14,62},{16,32}... | collective-permute-start | bytes 4616 | tf_op jit(solution)/shard_map/ppermute | solution.py:63
  50.3 5.0 %collective-permute-start.13 = (f32[3,128]{1,0:T(4,128)S(1)}, f32[3,128]{1,0:T(4,128)S(1)}, u32[]{:S(2)}, u32[]{:S(2)}) collective-permute-start(f32[3,128]{1,0:T(4,128)S(1)} %get-tuple-element.24), channel_id=1, source_target_pairs={{0,16},{2,18},{4,20},{6,22},{8,24},{10,26},{12,28},{14,30},{16,0},... | collective-permute-start | bytes 4616 | tf_op jit(solution)/shard_map/ppermute | solution.py:63
  50.5 4.9 %collective-permute-start.14 = (f32[3,128]{1,0:T(4,128)S(1)}, f32[3,128]{1,0:T(4,128)S(1)}, u32[]{:S(2)}, u32[]{:S(2)}) collective-permute-start(f32[3,128]{1,0:T(4,128)S(1)} %get-tuple-element.23.own_ref), channel_id=1, source_target_pairs={{0,32},{2,34},{4,36},{6,38},{8,40},{10,42},{12,44},{14,46},{16,48}... | collective-permute-start | bytes 4616 | tf_op jit(solution)/shard_map/ppermute | solution.py:63
  52.0 3.6 %copy-start.3 = (bf16[128,8192]{1,0:T(8,128)(2,1)S(1)}, bf16[128,8192]{1,0:T(8,128)(2,1)}, u32[]{:S(2)}) copy-start(bf16[128,8192]{1,0:T(8,128)(2,1)} %get-tuple-element.32) | copy-start | bytes 6291460
  52.0 21.7 %copy-start.2 = (f32[256]{0:T(256)S(1)}, f32[256]{0:T(256)}, u32[]{:S(2)}) copy-start(f32[256]{0:T(256)} %param.7) | copy-start | bytes 3076
  55.4 18.2 %collective-permute-start.16 = (bf16[128,8192]{1,0:T(8,128)(2,1)}, bf16[128,8192]{1,0:T(8,128)(2,1)S(1)}, u32[]{:S(2)}, u32[]{:S(2)}) collective-permute-start(bf16[128,8192]{1,0:T(8,128)(2,1)} %get-tuple-element.30), channel_id=1, source_target_pairs={{0,16},{2,18},{4,20},{6,22},{8,24},{10,26},{12,28},{14,30},{16,0},... | collective-permute-start | bytes 6291464 | tf_op jit(solution)/shard_map/ppermute | solution.py:63
  55.6 18.1 %collective-permute-start.17 = (bf16[128,8192]{1,0:T(8,128)(2,1)S(1)}, bf16[128,8192]{1,0:T(8,128)(2,1)S(1)}, u32[]{:S(2)}, u32[]{:S(2)}) collective-permute-start(bf16[128,8192]{1,0:T(8,128)(2,1)S(1)} %copy-done.3), channel_id=1, source_target_pairs={{0,16},{2,18},{4,20},{6,22},{8,24},{10,26},{12,28},{14,30},{16,0},... | collective-permute-start | bytes 6291464 | tf_op jit(solution)/shard_map/ppermute | solution.py:63
  77.1 10.9 %collective-permute-start.18 = (bf16[32,8192]{1,0:T(8,128)(2,1)S(1)}, bf16[32,8192]{1,0:T(8,128)(2,1)S(1)}, u32[]{:S(2)}, u32[]{:S(2)}) collective-permute-start(bf16[32,8192]{1,0:T(8,128)(2,1)S(1)} %get-tuple-element.34), channel_id=1, source_target_pairs={{0,128},{2,130},{4,132},{6,134},{8,136},{10,138},{12,140},{14,142}... | collective-permute-start | bytes 1572872 | tf_op jit(solution)/shard_map/ppermute | solution.py:63
  78.5 15.0 %collective-permute-start.19 = (bf16[32,8192]{1,0:T(8,128)(2,1)S(1)}, bf16[32,8192]{1,0:T(8,128)(2,1)S(1)}, u32[]{:S(2)}, u32[]{:S(2)}) collective-permute-start(bf16[32,8192]{1,0:T(8,128)(2,1)S(1)} %get-tuple-element.35), channel_id=1, source_target_pairs={{0,64},{2,66},{4,68},{6,70},{8,72},{10,74},{12,76},{14,78},{16,18}... | collective-permute-start | bytes 1572872 | tf_op jit(solution)/shard_map/ppermute | solution.py:63
  79.2 14.3 %collective-permute-start.20 = (bf16[32,8192]{1,0:T(8,128)(2,1)S(1)}, bf16[32,8192]{1,0:T(8,128)(2,1)S(1)}, u32[]{:S(2)}, u32[]{:S(2)}) collective-permute-start(bf16[32,8192]{1,0:T(8,128)(2,1)S(1)} %get-tuple-element.36), channel_id=1, source_target_pairs={{0,192},{2,194},{4,196},{6,198},{8,200},{10,202},{12,204},{14,206}... | collective-permute-start | bytes 1572872 | tf_op jit(solution)/shard_map/ppermute | solution.py:63
  93.7 8.2 %collective-permute-start.21 = (bf16[8,8192]{1,0:T(8,128)(2,1)S(1)}, bf16[8,8192]{1,0:T(8,128)(2,1)S(1)}, u32[]{:S(2)}, u32[]{:S(2)}) collective-permute-start(bf16[8,8192]{1,0:T(8,128)(2,1)S(1)} %get-tuple-element.43), channel_id=1, source_target_pairs={{0,4},{2,6},{4,8},{6,10},{8,12},{10,14},{12,0},{14,2},{16,144},{18... | collective-permute-start | bytes 393224 | tf_op jit(solution)/shard_map/ppermute | solution.py:63
  95.0 7.0 %collective-permute-start.23 = (bf16[8,8192]{1,0:T(8,128)(2,1)S(1)}, bf16[8,8192]{1,0:T(8,128)(2,1)S(1)}, u32[]{:S(2)}, u32[]{:S(2)}) collective-permute-start(bf16[8,8192]{1,0:T(8,128)(2,1)S(1)} %get-tuple-element.44), channel_id=1, source_target_pairs={{0,14},{2,0},{4,2},{6,4},{8,6},{10,8},{12,10},{14,12},{16,208},{18... | collective-permute-start | bytes 393224 | tf_op jit(solution)/shard_map/ppermute | solution.py:63
  97.6 6.2 %collective-permute-start.22 = (bf16[8,8192]{1,0:T(8,128)(2,1)S(1)}, bf16[8,8192]{1,0:T(8,128)(2,1)S(1)}, u32[]{:S(2)}, u32[]{:S(2)}) collective-permute-start(bf16[8,8192]{1,0:T(8,128)(2,1)S(1)} %get-tuple-element.45), channel_id=1, source_target_pairs={{0,2},{2,4},{4,6},{6,8},{8,10},{10,12},{12,14},{14,0},{16,80},{18,... | collective-permute-start | bytes 393224 | tf_op jit(solution)/shard_map/ppermute | solution.py:63
  103.9 9.2 %collective-permute-start.24 = (bf16[2,8192]{1,0:T(2,128)(2,1)S(1)}, bf16[2,8192]{1,0:T(2,128)(2,1)S(1)}, u32[]{:S(2)}, u32[]{:S(2)}) collective-permute-start(bf16[2,8192]{1,0:T(2,128)(2,1)S(1)} %get-tuple-element.46), channel_id=1, source_target_pairs={{0,40},{2,42},{4,44},{6,46},{8,32},{10,34},{12,36},{14,38},{16,56}... | collective-permute-start | bytes 98312 | tf_op jit(solution)/shard_map/ppermute | solution.py:63
  105.7 7.4 %collective-permute-start.26 = (bf16[2,8192]{1,0:T(2,128)(2,1)S(1)}, bf16[2,8192]{1,0:T(2,128)(2,1)S(1)}, u32[]{:S(2)}, u32[]{:S(2)}) collective-permute-start(bf16[2,8192]{1,0:T(2,128)(2,1)S(1)} %get-tuple-element.47), channel_id=1, source_target_pairs={{0,32},{2,34},{4,36},{6,38},{8,40},{10,42},{12,44},{14,46},{16,48}... | collective-permute-start | bytes 98312 | tf_op jit(solution)/shard_map/ppermute | solution.py:63
  106.8 8.9 %collective-permute-start.25 = (bf16[2,8192]{1,0:T(2,128)(2,1)S(1)}, bf16[2,8192]{1,0:T(2,128)(2,1)S(1)}, u32[]{:S(2)}, u32[]{:S(2)}) collective-permute-start(bf16[2,8192]{1,0:T(2,128)(2,1)S(1)} %get-tuple-element.48), channel_id=1, source_target_pairs={{0,8},{2,10},{4,12},{6,14},{8,0},{10,2},{12,4},{14,6},{16,24},{18,... | collective-permute-start | bytes 98312 | tf_op jit(solution)/shard_map/ppermute | solution.py:63
